TPU v7x, 32 devices: a whole 2x2x4 slice. The times are simulated.
32 devices in a mesh: groups: 2 (over x), frames: 16 (over z, y, core).
Axes of the slice: x: 2, y: 2, z: 4, core: 2. Of those that a mesh axis runs over, the one named last changes fastest.
Arguments:
- latents: bfloat16 [256, 32, 512], P(('groups', 'frames')), parts along dimension 0, may hold values from -6 to 6
- timestep: int32 [256], P(('groups', 'frames')), parts along dimension 0, may hold values from 0 to 49, as said below
- lookback: int32 [256], P(('groups', 'frames')), parts along dimension 0, may hold values from 1 to 8, as said below
- modulation: bfloat16 [2, 50, 4, 512], replicated, may hold values from -2.390625 to 2.390625
- input_weight: bfloat16 [2, 512, 2304], replicated, may hold values from -0.25 to 0.25
- step_weight: bfloat16 [2, 512, 16], replicated, may hold values from -0.25 to 0.25
- conv_weight: float32 [2, 4, 1280], replicated, may hold values from -3 to 3
- step_bias: float32 [2, 50, 16], replicated, may hold values from -3 to 2
- decay_log: float32 [2, 16], replicated
- skip_gain: float32 [2, 16], replicated, may hold values from -2 to 2
- norm_gain: float32 [2, 1024], replicated, may hold values from 0.1 to 1.9
- output_weight: bfloat16 [2, 1024, 512], replicated, may hold values from -0.1875 to 0.1875
- query_weight: bfloat16 [2, 512, 512], replicated
- memory_weight: bfloat16 [2, 512, 1024], replicated
- merge_weight: bfloat16 [2, 512, 512], replicated, may hold values from -0.25 to 0.25
Outputs:
- denoised: float32 [256, 32, 512], P(('groups', 'frames')), parts along dimension 0
There are 2 independent parts, one for each index of `groups`. A program takes and returns all parts, laid end to end along the dimension named above; an argument that names none is the same for every part. Nothing has to cross between parts.
Inputs may be any that keep to these rules, and one draw needn't show every extreme that they name: timestep is the same for all frames of each aligned run of 8 frames. lookback[f] counts the preceding frames that frame f attends to; 8 occurs in every draw.
All inputs are finite; a program needn't handle non-finite values.
Results may differ from a plain program's by a relative error of at most 0.01.
Values may be sent and summed in bfloat16 or wider, within the bound.
No kernel may reach another device: no remote copies, remote signals or barrier semaphores. Data moves between devices by JAX's collectives and lax.ppermute only.
A program may use at most 128 MiB of HBM per device.

v0:
```python
import jax
import jax.numpy as jnp
from jax import lax
from jax.sharding import PartitionSpec as P

HEADS = 16
HEAD_DIM = 64
STATE = 128
ATT_HEADS = 8
NSTEPS = 50
LAYERS = 2
CONV = 4
SPAN = 128
WINDOW = 8


EPS = 1e-06
HEAD_EPS = 1e-05


def from_behind(value, axis, steps):
    count = lax.axis_size(axis)
    initial, last = (max(0, -steps), min(count, count - steps))
    return lax.ppermute(value, axis, [(source, source + steps) for source in range(initial, last)])


def carried_in(value, axis, combine, identity):
    devices, place = (lax.axis_size(axis), lax.axis_index(axis))
    everything = jax.tree.map(
        lambda part, kind: lax.all_gather(part.astype(kind), axis),
        value,
        (jnp.bfloat16, jnp.bfloat16),
    )
    start = jax.tree.map(
        lambda part, zero: jnp.broadcast_to(jnp.asarray(zero, part.dtype), part.shape),
        value,
        identity,
    )

    def hop(k, before):
        reached = k < place
        new = combine(
            before, jax.tree.map(lambda part, own: part[k].astype(own.dtype), everything, value)
        )
        return jax.tree.map(lambda a, b: jnp.where(reached, a, b), new, before)

    return lax.fori_loop(0, devices, hop, start)


def rms_rows(values):
    return values * lax.rsqrt(jnp.mean(values * values, axis=-1, keepdims=True) + EPS)


def modulated(resid, shift, scale):
    normed = rms_rows(resid)
    return (normed * (1.0 + scale[:, None, :]) + shift[:, None, :]).astype(jnp.bfloat16)


def conv_silu(extended, weights, count):
    total = weights[0][None, :] * extended[0:count].astype(jnp.float32)
    for offset in range(1, CONV):
        total = total + weights[offset][None, :] * extended[offset : offset + count].astype(
            jnp.float32
        )
    return jax.nn.silu(total).astype(jnp.bfloat16)


def span_terms(values, input_map, output_map, log_decay, step_size):
    count = values.shape[0] // SPAN
    by_head = values.reshape(count, SPAN, HEADS, HEAD_DIM)
    in_blocks = input_map.reshape(count, SPAN, STATE)
    out_blocks = output_map.reshape(count, SPAN, STATE)
    cumulated = jnp.cumsum(log_decay.reshape(count, SPAN, HEADS), axis=1).transpose(0, 2, 1)
    steps = step_size.reshape(count, SPAN, HEADS).transpose(0, 2, 1)
    affinity = jnp.einsum("cqn,csn->cqs", out_blocks, in_blocks, preferred_element_type=jnp.float32)
    position = jnp.arange(SPAN)
    lower = position[:, None] >= position[None, :]
    gaps = cumulated[:, :, :, None] - cumulated[:, :, None, :]
    gaps = jnp.where(lower[None, None], gaps, -jnp.inf)
    mixing = (affinity[:, None] * jnp.exp(gaps) * steps[:, :, None, :]).astype(jnp.bfloat16)
    y_local = jnp.einsum("chqs,cshp->cqhp", mixing, by_head, preferred_element_type=jnp.float32)
    edge = jnp.exp(cumulated[:, :, -1:] - cumulated) * steps
    weighted = (in_blocks[:, None, :, :].astype(jnp.float32) * edge[:, :, :, None]).astype(
        jnp.bfloat16
    )
    states = jnp.einsum("cshp,chsn->chpn", by_head, weighted, preferred_element_type=jnp.float32)
    return (y_local, states, cumulated, out_blocks)


def finish_mixer(resid, y_total, values, gate_half, skip, gain, weight):
    rows = values.shape[0]
    mixed = y_total.reshape(rows, HEADS * HEAD_DIM) + jnp.repeat(skip, HEAD_DIM)[
        None, :
    ] * values.astype(jnp.float32)
    gated = (mixed * jax.nn.silu(gate_half.astype(jnp.float32))).reshape(rows, HEADS, HEAD_DIM)
    gated = gated * lax.rsqrt(jnp.mean(gated * gated, axis=-1, keepdims=True) + HEAD_EPS)
    normed = (gated.reshape(rows, HEADS * HEAD_DIM) * gain[None, :]).astype(jnp.bfloat16)
    update = jnp.dot(normed, weight, preferred_element_type=jnp.float32)
    return resid + update.reshape(resid.shape)


def combine_states(earlier, later):
    return (earlier[0] * later[0], later[0][:, None, None] * earlier[1] + later[1])


def attend(query_block, key_block, query_frame, key_frame, reach):
    count, tok_frame, attn = query_block.shape
    heads = attn // HEAD_DIM
    queries = query_block.reshape(count * tok_frame, heads, HEAD_DIM)
    key_rows = key_block[:, :, :attn].reshape(-1, heads, HEAD_DIM)
    value_rows = key_block[:, :, attn:].reshape(-1, heads, HEAD_DIM)
    scores = jnp.einsum(
        "qhd,khd->hqk", queries, key_rows, preferred_element_type=jnp.float32
    ) * HEAD_DIM ** (-0.5)
    allowed = (
        (key_frame[None, :] >= 0)
        & (key_frame[None, :] <= query_frame[:, None])
        & (key_frame[None, :] >= query_frame[:, None] - reach[:, None])
    )
    allowed = jnp.repeat(jnp.repeat(allowed, tok_frame, axis=0), tok_frame, axis=1)
    scores = jnp.where(allowed[None], scores, -1e30)
    top = jnp.max(scores, axis=-1, keepdims=True)
    weights = jnp.exp(scores - top)
    probs = (weights / jnp.sum(weights, axis=-1, keepdims=True)).astype(jnp.bfloat16)
    mixed = jnp.einsum("hqk,khd->qhd", probs, value_rows, preferred_element_type=jnp.float32)
    return mixed.astype(jnp.bfloat16).reshape(count, tok_frame, attn)


def shards(
    latents,
    timestep,
    lookback,
    modulation,
    input_weight,
    step_weight,
    conv_weight,
    step_bias,
    decay_log,
    skip_gain,
    norm_gain,
    output_weight,
    query_weight,
    memory_weight,
    merge_weight,
):
    frames_dev, tok_frame, width = latents.shape
    inner = HEADS * HEAD_DIM
    attn = ATT_HEADS * HEAD_DIM
    base = lax.axis_index("frames") * frames_dev
    onehot = (timestep[:, None] == jnp.arange(NSTEPS, dtype=jnp.int32)[None, :]).astype(
        jnp.bfloat16
    )
    onehot_wide = onehot.astype(jnp.float32)
    resid = latents.astype(jnp.float32)
    for layer in range(LAYERS):
        mods = jnp.dot(
            onehot, modulation[layer].reshape(NSTEPS, 4 * width), preferred_element_type=jnp.float32
        ).reshape(frames_dev, 4, width)
        frame_bias = jnp.dot(onehot_wide, step_bias[layer], precision=lax.Precision.HIGHEST)
        u_rows = modulated(resid, mods[:, 0], mods[:, 1]).reshape(-1, width)
        projected = jnp.dot(u_rows, input_weight[layer], preferred_element_type=jnp.float32).astype(
            jnp.bfloat16
        )
        gate_half = projected[:, :inner]
        mixed_in = projected[:, inner:]
        step_raw = jnp.dot(u_rows, step_weight[layer], preferred_element_type=jnp.float32)
        step_raw = (
            step_raw.reshape(frames_dev, tok_frame, HEADS) + frame_bias[:, None, :]
        ).reshape(-1, HEADS)
        rows = mixed_in.shape[0]
        tail = from_behind(mixed_in[rows - (CONV - 1) :], "frames", 1)
        extended = jnp.concatenate([tail, mixed_in], axis=0)
        act = conv_silu(extended, conv_weight[layer], rows)
        values = act[:, :inner]
        input_map = act[:, inner : inner + STATE]
        output_map = act[:, inner + STATE :]
        step_size = jax.nn.softplus(step_raw)
        log_decay = -jnp.exp(decay_log[layer])[None, :] * step_size
        y_local, states, cumulated, out_blocks = span_terms(
            values, input_map, output_map, log_decay, step_size
        )
        ends = cumulated[:, :, -1]

        def walk(carry, item):
            state, end_log = item
            return (jnp.exp(end_log)[:, None, None] * carry + state, carry)

        dev_state, before = lax.scan(
            walk, jnp.zeros((HEADS, HEAD_DIM, STATE), jnp.float32), (states, ends)
        )
        dev_decay = jnp.exp(jnp.sum(ends, axis=0))
        scanned = carried_in(
            (dev_decay, dev_state),
            "frames",
            combine_states,
            (jnp.ones_like(dev_decay), jnp.zeros_like(dev_state)),
        )
        incoming = scanned[1]
        prefix = jnp.exp(jnp.cumsum(ends, axis=0) - ends)
        entering = before + prefix[:, :, None, None] * incoming[None]
        y_carry = jnp.einsum(
            "cqn,chpn->cqhp",
            out_blocks.astype(jnp.float32),
            entering,
            precision=lax.Precision.HIGHEST,
        )
        y_carry = y_carry * jnp.exp(cumulated).transpose(0, 2, 1)[:, :, :, None]
        hidden = finish_mixer(
            resid,
            y_local + y_carry,
            values,
            gate_half,
            skip_gain[layer],
            norm_gain[layer],
            output_weight[layer],
        )
        a_rows = modulated(hidden, mods[:, 2], mods[:, 3]).reshape(-1, width)
        queries = (
            jnp.dot(a_rows, query_weight[layer], preferred_element_type=jnp.float32)
            .astype(jnp.bfloat16)
            .reshape(frames_dev, tok_frame, attn)
        )
        memory = (
            jnp.dot(a_rows, memory_weight[layer], preferred_element_type=jnp.float32)
            .astype(jnp.bfloat16)
            .reshape(frames_dev, tok_frame, 2 * attn)
        )
        memory_tail = from_behind(memory, "frames", 1)
        keyed = jnp.concatenate([memory_tail, memory], axis=0)
        query_frame = base + 0 + jnp.arange(WINDOW, dtype=jnp.int32)
        key_frame = base + 0 - WINDOW + jnp.arange(2 * WINDOW, dtype=jnp.int32)
        outputs = attend(queries, keyed, query_frame, key_frame, lookback)
        attended = outputs.reshape(-1, attn)
        update = jnp.dot(attended, merge_weight[layer], preferred_element_type=jnp.float32)
        resid = hidden + update.reshape(hidden.shape)
    return resid


def solution(mesh):
    return jax.shard_map(
        shards,
        mesh=mesh,
        in_specs=(
            P(("groups", "frames"), None, None),
            P(("groups", "frames")),
            P(("groups", "frames")),
            P(),
            P(),
            P(),
            P(),
            P(),
            P(),
            P(),
            P(),
            P(),
            P(),
            P(),
            P(),
        ),
        out_specs=P(("groups", "frames"), None, None),
        check_vma=False,
    )
```

profile of v0, /device:TPU:8, one launch (start us, length us, event | category | flops | bytes accessed | tf_op | source)
XLA Modules:
  0.0 265.0 jit_solution(11436102423662947714)
XLA Ops:
  6.5 1.9 slice_bitcast_fusion
  9.9 2.5 convolution_convert_fusion.1
  12.4 1.9 collective-permute-start
  23.0 1.7 while.54
  25.7 1.3 dynamic-slice
  28.4 25.8 %all-reduce = bf16[256]{0:T(256)(128)(2,1)S(1)} all-reduce(bf16[256]{0:T(256)(128)(2,1)S(1)} %dynamic-update-slice), channel_id=2, replica_groups=mesh['groups'=2,'frames'=16] {'frames'}, use_global_device_ids=true, to_apply=%add | all-reduce | flops 256 | bytes 1024
  55.0 1.3 slice_bitcast_fusion.6
  60.2 1.9 convolution_bitcast_fusion.1
  62.1 15.9 %all-gather.7.cloned.1.call-done = bf16[256,64,128]{2,1,0:T(8,128)(2,1)} async-done(((bf16[16,64,128]{2,1,0:T(8,128)(2,1)}), bf16[256,64,128]{2,1,0:T(8,128)(2,1)}) %all-gather.7.cloned.1.call-update) | async-done | bytes 4194320 | tf_op jit(solution)/shard_map/all_gather | solution.py:30
  78.0 18.1 %while.55 = (s32[]{:T(128)}, f32[16,64,128]{2,1,0:T(8,128)S(1)}, s32[]{:T(128)}, bf16[16,16]{1,0:T(8,128)(2,1)S(1)}, bf16[16,16,64,128]{3,2,1,0:T(8,128)(2,1)}, /*index=5*/s32[]{:T(128)}, s32[]{:T(128)}) while((s32[]{:T(128)}, f32[16,64,128]{2,1,0:T(8,128)S(1)}, s32[]{:T(128)}, bf16[16,16]{1,0:T(8,128)(2,1)S(1)}, ...), condition=%wide.region_7.8_spmd.clone, body=%wide.region_6.7_spmd.clone.sunk | while | flops 655380 | bytes 1310985 | solution.py:47
  79.1 1.1 fusion.166
  80.2 1.1 fusion.166
  81.4 1.1 fusion.166
  82.5 1.1 fusion.166
  83.6 1.1 fusion.166
  84.8 1.1 fusion.166
  85.9 1.1 fusion.166
  87.0 1.1 fusion.166
  88.2 1.1 fusion.166
  89.3 1.1 fusion.166
  91.6 1.1 fusion.166
  92.7 1.1 fusion.166
  93.8 1.1 fusion.166
  95.0 1.1 fusion.166
  96.1 2.0 fusion.23
  98.0 2.1 copy.224
  100.1 2.0 reshape.376
  102.1 2.4 fusion.129
  104.6 1.6 copy.193
  107.3 1.6 copy.194
  108.9 1.6 multiply_convert_fusion.11
  112.6 2.3 collective-permute-start.1
  116.9 1.3 convolution_convert_fusion.5
  118.4 5.7 %collective-permute-done.1 = bf16[8,32,1024]{2,1,0:T(8,128)(2,1)S(1)} collective-permute-done((bf16[8,32,1024]{2,1,0:T(8,128)(2,1)S(1)}, bf16[8,32,1024]{2,1,0:T(8,128)(2,1)S(1)}, u32[]{:S(2)}, u32[]{:S(2)}) %collective-permute-start.1) | collective-permute-done | bytes 524320 | tf_op jit(solution)/shard_map/ppermute | solution.py:24
  124.7 1.5 reshape.332
  127.2 2.1 fusion.133
  133.7 2.5 convolution_convert_fusion
  136.2 1.9 collective-permute-start.2
  138.9 3.2 %collective-permute-done.2 = bf16[3,1280]{1,0:T(4,128)(2,1)S(1)} collective-permute-done((bf16[3,1280]{1,0:T(4,128)(2,1)S(1)}, bf16[3,1280]{1,0:T(4,128)(2,1)S(1)}, u32[]{:S(2)}, u32[]{:S(2)}) %collective-permute-start.2) | collective-permute-done | bytes 7712 | tf_op jit(solution)/shard_map/ppermute | solution.py:24
  144.6 1.8 fusion.37
  146.4 1.1 broadcast.160
  147.5 3.3 %while.56 = (s32[]{:T(128)}, f32[16,64,128]{2,1,0:T(8,128)S(1)}, f32[2,16,64,128]{3,2,1,0:T(8,128)}, f32[2,16]{1,0:T(2,128)}, f32[2,16,64,128]{3,2,1,0:T(8,128)S(1)}, /*index=5*/s32[]{:T(128)}, s32[]{:T(128)}) while((s32[]{:T(128)}, f32[16,64,128]{2,1,0:T(8,128)S(1)}, f32[2,16,64,128]{3,2,1,0:T(8,128)}, f32[2,16]{1,0:T(2,128)}, ...), condition=%wide.region_15.16_spmd.clone, body=%wide.region_14.15_spmd.clone.sunk | while | flops 524291 | bytes 2622240 | solution.py:188
  154.6 23.5 %all-reduce.1 = bf16[256]{0:T(256)(128)(2,1)S(1)} all-reduce(bf16[256]{0:T(256)(128)(2,1)S(1)} %dynamic-update-slice.1), channel_id=4, replica_groups=mesh['groups'=2,'frames'=16] {'frames'}, use_global_device_ids=true, to_apply=%add.1 | all-reduce | flops 256 | bytes 1024
  178.8 1.3 subtract_exponential_fusion.2
  180.3 2.6 convolution_bitcast_fusion
  182.9 18.0 %all-gather.9.cloned.1.call-done = bf16[256,64,128]{2,1,0:T(8,128)(2,1)} async-done(((bf16[16,64,128]{2,1,0:T(8,128)(2,1)}), bf16[256,64,128]{2,1,0:T(8,128)(2,1)}) %all-gather.9.cloned.1.call-update) | async-done | bytes 4194320 | tf_op jit(solution)/shard_map/all_gather | solution.py:30
  200.9 18.1 %while.57 = (s32[]{:T(128)}, f32[16,64,128]{2,1,0:T(8,128)S(1)}, s32[]{:T(128)}, bf16[16,16]{1,0:T(8,128)(2,1)S(1)}, bf16[16,16,64,128]{3,2,1,0:T(8,128)(2,1)}, /*index=5*/s32[]{:T(128)}, s32[]{:T(128)}) while((s32[]{:T(128)}, f32[16,64,128]{2,1,0:T(8,128)S(1)}, s32[]{:T(128)}, bf16[16,16]{1,0:T(8,128)(2,1)S(1)}, ...), condition=%wide.region_19.20_spmd.clone, body=%wide.region_18.19_spmd.clone.sunk | while | flops 655380 | bytes 1310985 | solution.py:47
  200.9 1.1 fusion.168
  202.0 1.1 fusion.168
  203.2 1.1 fusion.168
  204.3 1.1 fusion.168
  205.4 1.1 fusion.168
  219.0 2.3 fusion.22
  221.3 2.1 copy.225
  223.4 2.0 reshape.377
  225.4 2.4 fusion.128
  227.8 1.6 copy.216
  230.6 1.6 copy.217
  232.2 1.6 multiply_convert_fusion.10
  235.9 2.2 collective-permute-start.3
  238.5 8.8 %collective-permute-done.3 = bf16[8,32,1024]{2,1,0:T(8,128)(2,1)S(1)} collective-permute-done((bf16[8,32,1024]{2,1,0:T(8,128)(2,1)S(1)}, bf16[8,32,1024]{2,1,0:T(8,128)(2,1)S(1)}, u32[]{:S(2)}, u32[]{:S(2)}) %collective-permute-start.3) | collective-permute-done | bytes 524320 | tf_op jit(solution)/shard_map/ppermute | solution.py:24
  248.9 3.7 %fusion.134 = (f32[8,256]{1,0:T(8,128)S(1)}, f32[8,256,512]{2,1,0:T(8,128)}) fusion(f32[8,256,512]{2,1,0:T(8,128)S(1)} %fusion.43, pred[256,512]{1,0:T(8,128)(4,1)S(1)} %copy-done.12), kind=kOutput, calls=%fused_computation.246 | output fusion | flops 6291967 | bytes 8527872 | tf_op jit(solution)/shard_map/sub | solution.py:123
  253.2 3.2 %fusion.27 = bf16[256,8,64]{0,2,1:T(8,128)(2,1)S(1)} fusion(f32[8,256,512]{2,1,0:T(8,128)} %get-tuple-element.416, f32[8,256]{1,0:T(8,128)S(1)} %get-tuple-element.415, bf16[512,8,64]{2,1,0:T(8,128)(2,1)S(1)} %reshape.343), kind=kOutput, calls=%fused_computation.67 | convolution fusion | flops 136445952 | bytes 4988928 | tf_op jit(solution)/shard_map/hqk,khd->qhd/dot_general | solution.py:125
  257.0 1.1 convolution_add_fusion.2
  (279 shorter events, 61.0 us)
Async XLA Ops:
  6.5 2.1 copy-start.36
  6.5 3.0 %copy-start.7 = (bf16[8,32,512]{2,1,0:T(8,128)(2,1)S(1)}, bf16[8,32,512]{2,1,0:T(8,128)(2,1)}, u32[]{:S(2)}) copy-start(bf16[8,32,512]{2,1,0:T(8,128)(2,1)} %param.23) | copy-start | bytes 786436
  6.5 71.4 %all-gather.7.cloned.1.call-start = ((), (), s32[]{:S(2)}) async-start(), calls=%async_computation | async-start | bytes 4456448 | tf_op jit(solution)/shard_map/all_gather | solution.py:30
  9.8 4.5 %copy-start.45 = (f32[2,50,16]{1,2,0:T(8,128)S(1)}, f32[2,50,16]{1,2,0:T(8,128)}, u32[]{:S(2)}) copy-start(f32[2,50,16]{1,2,0:T(8,128)} %param.30) | copy-start | bytes 19204
  9.8 4.7 %copy-start.25 = (bf16[2,512,16]{1,2,0:T(8,128)(2,1)S(1)}, bf16[2,512,16]{1,2,0:T(8,128)(2,1)}, u32[]{:S(2)}) copy-start(bf16[2,512,16]{1,2,0:T(8,128)(2,1)} %param.28) | copy-start | bytes 98308
  9.8 5.1 %copy-start.39 = (f32[2,16]{1,0:T(2,128)S(1)}, f32[2,16]{1,0:T(2,128)}, u32[]{:S(2)}) copy-start(f32[2,16]{1,0:T(2,128)} %param.31) | copy-start | bytes 388
  9.9 7.9 %copy-start.19 = (f32[2,4,1280]{2,1,0:T(4,128)S(1)}, f32[2,4,1280]{2,1,0:T(4,128)}, u32[]{:S(2)}) copy-start(f32[2,4,1280]{2,1,0:T(4,128)} %param.29) | copy-start | bytes 122884
  12.3 6.1 %copy-start = (bf16[256,2304]{1,0:T(8,128)(2,1)}, bf16[256,2304]{1,0:T(8,128)(2,1)S(1)}, u32[]{:S(2)}) copy-start(bf16[256,2304]{1,0:T(8,128)(2,1)S(1)} %convolution_convert_fusion.1) | copy-start | bytes 3538948
  12.4 6.2 %collective-permute-start = (bf16[3,1280]{1,0:T(4,128)(2,1)S(1)}, bf16[3,1280]{1,0:T(4,128)(2,1)S(1)}, u32[]{:S(2)}, u32[]{:S(2)}) collective-permute-start(bf16[3,1280]{1,0:T(4,128)(2,1)S(1)} %slice.272), channel_id=1, source_target_pairs={{0,1},{1,2},{2,3},{3,4},{4,5},{5,6},{6,7},{7,8},{8,9},{9,10},{10,1... | collective-permute-start | bytes 23048 | tf_op jit(solution)/shard_map/ppermute | solution.py:24
  17.1 0.6 copy-start.29
  21.0 0.8 copy-start.2
  24.7 33.6 %copy-start.40 = (s32[8]{0:T(128)S(1)}, s32[8]{0:T(128)}, u32[]{:S(2)}) copy-start(s32[8]{0:T(128)} %param.25) | copy-start | bytes 100
  24.8 33.6 %copy-start.30 = (f32[2,16]{1,0:T(2,128)S(1)}, f32[2,16]{1,0:T(2,128)}, u32[]{:S(2)}) copy-start(f32[2,16]{1,0:T(2,128)} %get-tuple-element.639) | copy-start | bytes 388
  24.8 33.6 %copy-start.37 = (s32[8]{0:T(128)S(1)}, s32[8]{0:T(128)}, u32[]{:S(2)}) copy-start(s32[8]{0:T(128)} %param.24) | copy-start | bytes 100
  24.8 33.6 %copy-start.46 = (f32[2,50,16]{1,2,0:T(8,128)S(1)}, f32[2,50,16]{1,2,0:T(8,128)}, u32[]{:S(2)}) copy-start(f32[2,50,16]{1,2,0:T(8,128)} %param.30) | copy-start | bytes 19204
  24.8 34.4 %copy-start.33 = (f32[2,1024]{1,0:T(2,128)S(1)}, f32[2,1024]{1,0:T(2,128)}, u32[]{:S(2)}) copy-start(f32[2,1024]{1,0:T(2,128)} %param.33) | copy-start | bytes 24580
  24.8 35.4 %copy-start.3 = (bf16[2,128,16,64]{1,3,2,0:T(8,128)(2,1)S(1)}, bf16[2,128,16,64]{1,3,2,0:T(8,128)(2,1)}, u32[]{:S(2)}) copy-start(bf16[2,128,16,64]{1,3,2,0:T(8,128)(2,1)} %copy-done.2) | copy-start | bytes 1572868
  24.8 35.4 %copy-start.28 = (f32[2,16,128]{2,1,0:T(8,128)S(1)}, f32[2,16,128]{2,1,0:T(8,128)}, u32[]{:S(2)}) copy-start(f32[2,16,128]{2,1,0:T(8,128)} %get-tuple-element.400) | copy-start | bytes 49156
  25.6 175.3 %all-gather.9.cloned.1.call-start = ((), (), s32[]{:S(2)}) async-start(), calls=%async_computation.1 | async-start | bytes 4456448 | tf_op jit(solution)/shard_map/all_gather | solution.py:30
  58.3 3.8 %copy-start.32 = (pred[128,128]{1,0:T(8,128)(4,1)}, pred[128,128]{1,0:T(8,128)(4,1)S(1)}, u32[]{:S(2)}) copy-start(pred[128,128]{1,0:T(8,128)(4,1)S(1)} %iota_compare_fusion) | copy-start | bytes 49156
  108.9 1.7 copy-start.8
  108.9 1.8 copy-start.9
  110.5 0.8 copy-start.14
  110.5 0.8 copy-start.15
  110.5 1.6 copy-start.42
  111.2 3.8 %copy-start.41 = (s32[16]{0:T(128)S(1)}, s32[16]{0:T(128)}, u32[]{:S(2)}) copy-start(s32[16]{0:T(128)} %iota_add_fusion.1) | copy-start | bytes 196
  112.6 11.4 %collective-permute-start.1 = (bf16[8,32,1024]{2,1,0:T(8,128)(2,1)S(1)}, bf16[8,32,1024]{2,1,0:T(8,128)(2,1)S(1)}, u32[]{:S(2)}, u32[]{:S(2)}) collective-permute-start(bf16[8,32,1024]{2,1,0:T(8,128)(2,1)S(1)} %bitcast.253), channel_id=1, source_target_pairs={{0,1},{1,2},{2,3},{3,4},{4,5},{5,6},{6,7},{7,8},{8,9},{9,10},{10,1... | collective-permute-start | bytes 1572872 | tf_op jit(solution)/shard_map/ppermute | solution.py:24
  126.3 0.9 copy-start.11
  127.2 2.1 copy-start.6
  129.3 1.7 copy-start.4
  130.3 1.1 copy-start.18
  130.3 1.2 copy-start.26
  130.3 1.2 copy-start.34
  130.6 1.3 copy-start.38
  133.7 4.5 %copy-start.31 = (f32[2,16]{1,0:T(2,128)}, f32[2,16]{1,0:T(2,128)S(1)}, u32[]{:S(2)}) copy-start(f32[2,16]{1,0:T(2,128)S(1)} %get-tuple-element.588) | copy-start | bytes 388
  133.7 8.4 %copy-start.21 = (f32[1280]{0:T(1024)S(1)}, f32[1280]{0:T(1024)}, u32[]{:S(2)}) copy-start(f32[1280]{0:T(1024)} %get-tuple-element.327) | copy-start | bytes 15364
  133.7 8.4 %copy-start.22 = (f32[1280]{0:T(1024)S(1)}, f32[1280]{0:T(1024)}, u32[]{:S(2)}) copy-start(f32[1280]{0:T(1024)} %get-tuple-element.328) | copy-start | bytes 15364
  133.7 8.4 %copy-start.23 = (f32[1280]{0:T(1024)S(1)}, f32[1280]{0:T(1024)}, u32[]{:S(2)}) copy-start(f32[1280]{0:T(1024)} %get-tuple-element.333) | copy-start | bytes 15364
  133.7 8.4 %copy-start.24 = (f32[1280]{0:T(1024)S(1)}, f32[1280]{0:T(1024)}, u32[]{:S(2)}) copy-start(f32[1280]{0:T(1024)} %get-tuple-element.334) | copy-start | bytes 15364
  136.2 6.9 %copy-start.1 = (bf16[256,2304]{1,0:T(8,128)(2,1)}, bf16[256,2304]{1,0:T(8,128)(2,1)S(1)}, u32[]{:S(2)}) copy-start(bf16[256,2304]{1,0:T(8,128)(2,1)S(1)} %convolution_convert_fusion) | copy-start | bytes 3538948
  136.2 5.9 %collective-permute-start.2 = (bf16[3,1280]{1,0:T(4,128)(2,1)S(1)}, bf16[3,1280]{1,0:T(4,128)(2,1)S(1)}, u32[]{:S(2)}, u32[]{:S(2)}) collective-permute-start(bf16[3,1280]{1,0:T(4,128)(2,1)S(1)} %slice.289), channel_id=1, source_target_pairs={{0,1},{1,2},{2,3},{3,4},{4,5},{5,6},{6,7},{7,8},{8,9},{9,10},{10,1... | collective-permute-start | bytes 23048 | tf_op jit(solution)/shard_map/ppermute | solution.py:24
  200.9 18.1 %copy-start.13 = (f32[2,128,16]{1,2,0:T(8,128)S(1)}, f32[2,128,16]{1,2,0:T(8,128)}, u32[]{:S(2)}) copy-start(f32[2,128,16]{1,2,0:T(8,128)} %copy.213) | copy-start | bytes 49156
  200.9 18.1 %copy-start.35 = (f32[2,16]{1,0:T(2,128)S(1)}, f32[2,16]{1,0:T(2,128)}, u32[]{:S(2)}) copy-start(f32[2,16]{1,0:T(2,128)} %subtract_exponential_fusion.2) | copy-start | bytes 388
  223.4 2.0 copy-start.20
  229.4 2.8 %copy-start.27 = (f32[1,1024]{1,0:T(1,128)S(1)}, f32[1,1024]{1,0:T(1,128)}, u32[]{:S(2)}) copy-start(f32[1,1024]{1,0:T(1,128)} %get-tuple-element.401) | copy-start | bytes 12292
  232.2 1.8 copy-start.10
  233.8 0.7 copy-start.16
  233.8 0.7 copy-start.17
  233.8 1.6 copy-start.43
  234.4 3.7 %copy-start.44 = (bf16[2,512,512]{2,1,0:T(8,128)(2,1)S(1)}, bf16[2,512,512]{2,1,0:T(8,128)(2,1)}, u32[]{:S(2)}) copy-start(bf16[2,512,512]{2,1,0:T(8,128)(2,1)} %param.35) | copy-start | bytes 3145732
  235.9 11.4 %collective-permute-start.3 = (bf16[8,32,1024]{2,1,0:T(8,128)(2,1)S(1)}, bf16[8,32,1024]{2,1,0:T(8,128)(2,1)S(1)}, u32[]{:S(2)}, u32[]{:S(2)}) collective-permute-start(bf16[8,32,1024]{2,1,0:T(8,128)(2,1)S(1)} %bitcast.255), channel_id=1, source_target_pairs={{0,1},{1,2},{2,3},{3,4},{4,5},{5,6},{6,7},{7,8},{8,9},{9,10},{10,1... | collective-permute-start | bytes 1572872 | tf_op jit(solution)/shard_map/ppermute | solution.py:24
  248.0 0.9 copy-start.12
  253.2 3.9 %copy-start.5 = (bf16[2,512,512]{2,1,0:T(8,128)(2,1)S(1)}, bf16[2,512,512]{2,1,0:T(8,128)(2,1)}, u32[]{:S(2)}) copy-start(bf16[2,512,512]{2,1,0:T(8,128)(2,1)} %param.37) | copy-start | bytes 3145732
Sparse Core Ops, SparseCore 0:
  25.7 52.2 all-gather.6
  151.7 49.1 all-gather.8
where the time goes:
time: 267 us; the launch traced here: 265 us
  other arithmetic  66 us (25%)
  waiting for transfers between devices  51.6 us (19%)
  blocking collectives  49.2 us (18%)
  local copies, waits for them, and re-layouts  44 us (16%)
  matrix products  29.5 us (11%)
  between operations  15.2 us (6%)
  starting transfers between devices  8.4 us (3%)
    unnamed x2, blocking collectives  49.2 us
    select_n x32, other arithmetic, hop(): return jax.tree.map(lambda a, b: jnp.where(reached, a, b), new, before)  34.9 us
    all_gather x2, waiting for transfers between devices, carried_in(): lax.all_gather(part.astype(kind), axis)  33.9 us
    ppermute x4, waiting for transfers between devices, from_behind(): lax.ppermute(value, axis, [(source, source + steps) for source in range(i...  17.7 us
    unnamed x104, local copies, waits for them, and re-layouts  8.46 us
    ppermute x4, starting transfers between devices, from_behind(): lax.ppermute(value, axis, [(source, source + steps) for source in range(i...  8.36 us
    reshape x4, local copies, waits for them, and re-layouts, finish_mixer(): y_total.reshape(rows, HEADS * HEAD_DIM)  8.18 us
    sub x2, other arithmetic, attend(): weights = jnp.exp(scores - top)  5.78 us
  transfers between devices with their start and end apart: 6, of which 5 were waited for; matrix products, arithmetic and copies ran while one was open for 10% of the time, Pallas kernels for 0%

commit v1 on v0

v1 whole, which is shorter than its diff:
```python
import functools

import jax
import jax.numpy as jnp
from jax import lax
from jax.experimental import pallas as pl
from jax.experimental.pallas import tpu as pltpu
from jax.sharding import PartitionSpec as P

HEADS = 16
HEAD_DIM = 64
STATE = 128
ATT_HEADS = 8
LAYERS = 2
CONV = 4
SPAN = 128
WINDOW = 8
EPS = 1e-06
HEAD_EPS = 1e-05
INNER = HEADS * HEAD_DIM
ATTN = ATT_HEADS * HEAD_DIM
PAD = 16
LANES = 128
TAIL = 16
F32 = jnp.float32
BF16 = jnp.bfloat16


def dot(a, b, dims=((1,), (0,)), precision=None):
    return lax.dot_general(a, b, (dims, ((), ())), precision=precision, preferred_element_type=F32)


def rms_mod(x, shift, scale):
    normed = x * lax.rsqrt(jnp.mean(x * x, axis=-1, keepdims=True) + EPS)
    return (normed * (1.0 + scale) + shift).astype(BF16)


def spread(per_head):
    high = per_head.astype(BF16)
    rest = per_head - high.astype(F32)
    middle = rest.astype(BF16)
    low = (rest - middle.astype(F32)).astype(BF16)
    row = lax.broadcasted_iota(jnp.int32, (HEADS, INNER), 0)
    head = lax.broadcasted_iota(jnp.int32, (HEADS, INNER), 1) // HEAD_DIM
    sel = jnp.where(row == head, 1.0, 0.0).astype(BF16)
    return dot(high, sel) + dot(middle, sel) + dot(low, sel)


def first_kernel(x_ref, mods_ref, u_ref, tail_ref):
    rows = x_ref.shape[0]
    u = rms_mod(x_ref[...].astype(F32), mods_ref[0:1, :], mods_ref[1:2, :])
    u_ref[...] = u
    tail_ref[...] = u[rows - TAIL :]


def local_kernel(
    parts,
    u_ref,
    tail_ref,
    w_ref,
    sw_ref,
    conv_ref,
    bias_ref,
    decay_ref,
    skip_ref,
    gate_ref,
    y_ref,
    out_map_ref,
    cum_ref,
    send_ref,
    ext_ref,
    act_ref,
):
    rows = u_ref.shape[0]
    u = u_ref[...]
    tail = tail_ref[...]
    chunk = 256
    for c in range(0, INNER, chunk):
        gate_ref[:, c : c + chunk] = dot(u, w_ref[:, c : c + chunk]).astype(BF16)
    for c in range(0, INNER + 2 * STATE, chunk):
        w = w_ref[:, INNER + c : INNER + c + chunk]
        ext_ref[0:TAIL, :] = dot(tail, w).astype(BF16).astype(F32)
        ext_ref[TAIL:, :] = dot(u, w).astype(BF16).astype(F32)
        total = None
        for k in range(CONV):
            start = TAIL - (CONV - 1) + k
            term = conv_ref[k : k + 1, c : c + chunk] * ext_ref[start : start + rows, :]
            total = term if total is None else total + term
        act_ref[:, c : c + chunk] = (total * jax.nn.sigmoid(total)).astype(BF16)

    raw = dot(u, sw_ref[...]) + bias_ref[...]
    step = jnp.maximum(raw, 0.0) + jnp.log1p(jnp.exp(-jnp.abs(raw)))
    log_decay = -jnp.exp(decay_ref[...]) * step
    log_step = jnp.log(step)

    q_pos = lax.broadcasted_iota(jnp.int32, (SPAN, SPAN), 0)
    s_pos = lax.broadcasted_iota(jnp.int32, (SPAN, SPAN), 1)
    lower = q_pos >= s_pos
    lower_f = jnp.where(lower, 1.0, 0.0).astype(F32)
    lane = lax.broadcasted_iota(jnp.int32, (SPAN, LANES), 1)
    left = lane < HEAD_DIM
    zero = jnp.zeros((SPAN, LANES), BF16)
    skip = skip_ref[...]

    before = jnp.zeros((1, HEADS), F32)
    state = None
    for b in range(rows // SPAN):
        r = slice(b * SPAN, (b + 1) * SPAN)
        cum = dot(lower_f, log_decay[r], precision=lax.Precision.HIGHEST)
        end = cum[SPAN - 1 : SPAN, :]
        cum_ref[r, :] = cum + before
        before = before + end
        shifted = (cum - log_step[r]).T
        edge = jnp.exp(end - cum) * step[r]
        in_map = act_ref[r, INNER : INNER + STATE]
        out_map = act_ref[r, INNER + STATE :]
        out_map_ref[r, :] = out_map
        affinity = dot(out_map, in_map, ((1,), (1,)))
        if state is not None:
            entering = dot(out_map, state.astype(BF16)) * spread(jnp.exp(cum))
        for pair in range(HEADS // 2):
            cols = slice(pair * LANES, (pair + 1) * LANES)
            values = act_ref[r, cols]
            mixing = []
            for h in (2 * pair, 2 * pair + 1):
                gap = cum[:, h : h + 1] - shifted[h : h + 1, :]
                mixing.append(jnp.where(lower, affinity * jnp.exp(gap), 0.0).astype(BF16))
            both = jnp.concatenate(mixing, axis=1)
            stacked = jnp.concatenate(
                [jnp.where(left, values, zero), jnp.where(left, zero, values)], axis=0
            )
            y = dot(both, stacked) + skip[:, cols] * values.astype(F32)
            if state is not None:
                y = y + entering[:, cols]
            y_ref[r, cols] = y
        scaled = (act_ref[r, 0:INNER].astype(F32) * spread(edge)).astype(BF16)
        term = dot(in_map, scaled, ((0,), (0,)))
        if state is None:
            state = term
        else:
            state = spread(jnp.broadcast_to(jnp.exp(end), (8, HEADS)))[0:1, :] * state + term

    part_rows = INNER // parts
    held = max(1, part_rows // HEAD_DIM)
    pad_row = lax.broadcasted_iota(jnp.int32, (PAD, LANES), 0)
    for pair in range(HEADS // 2):
        turned = state[:, pair * LANES : (pair + 1) * LANES].T.astype(BF16)
        for k in range(LANES // min(part_rows, LANES)):
            first = pair * LANES + k * min(part_rows, LANES)
            part, at = first // part_rows, first % part_rows
            size = min(part_rows, LANES)
            send_ref[part, at : at + size, :] = turned[k * size : (k + 1) * size, :]
    for part in range(parts):
        pad = jnp.zeros((PAD, LANES), F32)
        for i in range(held):
            h = part * part_rows // HEAD_DIM + i
            decay = jnp.broadcast_to(before[:, h : h + 1], (PAD, LANES))
            high = decay.astype(BF16).astype(F32)
            pad = jnp.where(pad_row == 2 * i, high, jnp.where(pad_row == 2 * i + 1, decay - high, pad))
        send_ref[part, part_rows:, :] = pad.astype(BF16)


def scan_kernel(got_ref, back_ref):
    parts, padded, _ = got_ref.shape
    part_rows = padded - PAD
    held = max(1, part_rows // HEAD_DIM)
    size = part_rows // held
    carry = [jnp.zeros((size, LANES), F32) for _ in range(held)]
    for d in range(parts):
        pad = got_ref[d, part_rows:, :].astype(F32)
        for i in range(held):
            rows = slice(i * size, (i + 1) * size)
            back_ref[d, rows, :] = carry[i].astype(BF16)
            decay = jnp.exp(pad[2 * i : 2 * i + 1, :] + pad[2 * i + 1 : 2 * i + 2, :])
            carry[i] = decay * carry[i] + got_ref[d, rows, :].astype(F32)


def finish_kernel(
    enter_ref,
    out_map_ref,
    cum_ref,
    y_ref,
    gate_ref,
    resid_ref,
    w_ref,
    gain_ref,
    mods_ref,
    hidden_ref,
    a_ref,
    normed_ref,
):
    out_map = out_map_ref[...]
    scale = jnp.exp(cum_ref[...])
    chunk = 256
    row = lax.broadcasted_iota(jnp.int32, (chunk, chunk), 0) // HEAD_DIM
    col = lax.broadcasted_iota(jnp.int32, (chunk, chunk), 1) // HEAD_DIM
    same = jnp.where(row == col, 1.0 / HEAD_DIM, 0.0).astype(BF16)
    wide = spread(scale)
    for c in range(0, INNER, chunk):
        cols = slice(c, c + chunk)
        carried = dot(out_map, enter_ref[cols, :], ((1,), (1,)))
        gate = gate_ref[:, cols].astype(F32)
        total = (y_ref[:, cols] + carried * wide[:, cols]) * (gate * jax.nn.sigmoid(gate))
        square = total * total
        high = square.astype(BF16)
        low = (square - high.astype(F32)).astype(BF16)
        mean = dot(high, same) + dot(low, same)
        normed_ref[:, cols] = (total * lax.rsqrt(mean + HEAD_EPS) * gain_ref[:, cols]).astype(BF16)
    hidden = resid_ref[...].astype(F32) + dot(normed_ref[...], w_ref[...])
    hidden_ref[...] = hidden
    a_ref[...] = rms_mod(hidden, mods_ref[2:3, :], mods_ref[3:4, :])


def memory_kernel(a_ref, wq_ref, wm_ref, q_ref, kv_ref):
    a = a_ref[...]
    q_ref[...] = (dot(a, wq_ref[...]).astype(BF16).astype(F32) * HEAD_DIM**-0.5).astype(BF16)
    kv_ref[...] = dot(a, wm_ref[...]).astype(BF16)


def attend_kernel(
    last,
    tok_frame,
    base_ref,
    reach_ref,
    q_ref,
    kv_ref,
    prev_ref,
    wm_ref,
    merge_ref,
    hidden_ref,
    mods_ref,
    *rest,
):
    if last:
        resid_ref, keyed_ref, bias_ref, out_ref = rest
    else:
        resid_ref, u_ref, tail_ref, keyed_ref, bias_ref, out_ref = rest
    rows = q_ref.shape[0]
    keyed_ref[0:rows, :] = dot(prev_ref[...], wm_ref[...]).astype(BF16)
    keyed_ref[rows:, :] = kv_ref[...]
    key_frame = lax.broadcasted_iota(jnp.int32, (tok_frame, 2 * rows), 1) // tok_frame
    first = WINDOW - base_ref[0]
    for f in range(WINDOW):
        low = jnp.maximum(first, f + WINDOW - reach_ref[f])
        seen = (key_frame >= low) & (key_frame <= f + WINDOW)
        bias_ref[f * tok_frame : (f + 1) * tok_frame, :] = jnp.where(seen, 0.0, -1e30)
    half = rows // 2
    span = rows + half
    q_left = lax.broadcasted_iota(jnp.int32, (half, LANES), 1) < HEAD_DIM
    k_left = lax.broadcasted_iota(jnp.int32, (span, LANES), 1) < HEAD_DIM
    one = jnp.ones((span, LANES), BF16)
    zero = jnp.zeros((half, LANES), BF16)
    for part in range(2):
        r = slice(part * half, (part + 1) * half)
        k_rows = slice(part * half, part * half + span)
        bias = bias_ref[r, k_rows]
        for pair in range(ATT_HEADS // 2):
            cols = slice(pair * LANES, (pair + 1) * LANES)
            query = q_ref[r, cols]
            keys = keyed_ref[k_rows, cols]
            values = keyed_ref[k_rows, ATTN + pair * LANES : ATTN + (pair + 1) * LANES]
            sides = []
            for side in range(2):
                mine = q_left if side == 0 else ~q_left
                own = k_left if side == 0 else ~k_left
                scores = dot(jnp.where(mine, query, zero), keys, ((1,), (1,))) + bias
                top = jnp.max(scores, axis=-1, keepdims=True)
                weights = jnp.exp(scores - top).astype(BF16)
                sides.append(dot(weights, jnp.where(own, values, one)))
            number = jnp.where(q_left, sides[0], sides[1])
            total = pltpu.roll(jnp.where(q_left, sides[1], sides[0]), HEAD_DIM, 1)
            out_ref[r, cols] = (number / total).astype(BF16)
    resid = hidden_ref[...] + dot(out_ref[...], merge_ref[...])
    resid_ref[...] = resid
    if not last:
        u = rms_mod(resid, mods_ref[0:1, :], mods_ref[1:2, :])
        u_ref[...] = u
        tail_ref[...] = u[rows - TAIL :]


def whole(array):
    zeros = (0,) * array.ndim
    return pl.BlockSpec(array.shape, lambda i: zeros)


def layer_of(array, layer):
    zeros = (0,) * (array.ndim - 1)
    return pl.BlockSpec((None,) + array.shape[1:], lambda i: (layer,) + zeros)


SCALARS = pl.BlockSpec(memory_space=pltpu.SMEM)


def run(kernel, specs, operands, outs, scratch=(), name=None):
    return pl.pallas_call(
        kernel,
        grid=(1,),
        in_specs=specs,
        out_specs=[whole(o) for o in outs],
        out_shape=list(outs),
        scratch_shapes=list(scratch),
        compiler_params=pltpu.CompilerParams(vmem_limit_bytes=40 * 1024 * 1024),
        name=name,
    )(*operands)


def shape(dims, dtype):
    return jax.ShapeDtypeStruct(dims, dtype)


def from_behind(value, axis):
    count = lax.axis_size(axis)
    return lax.ppermute(value, axis, [(i, i + 1) for i in range(count - 1)])


def shards(
    latents,
    timestep,
    lookback,
    modulation,
    input_weight,
    step_weight,
    conv_weight,
    step_bias,
    decay_log,
    skip_gain,
    norm_gain,
    output_weight,
    query_weight,
    memory_weight,
    merge_weight,
):
    frames_dev, tok_frame, width = latents.shape
    rows = frames_dev * tok_frame
    parts = lax.axis_size("frames")
    part_rows = INNER // parts
    base = (lax.axis_index("frames") * frames_dev).astype(jnp.int32).reshape(1)
    mods = modulation[:, timestep[0]].astype(F32)
    bias = step_bias[:, timestep[0]][:, None, :]
    decay_log = decay_log[:, None, :]
    skip = jnp.repeat(skip_gain, HEAD_DIM, axis=1)[:, None, :]
    gain = norm_gain[:, None, :]
    resid = latents.reshape(rows, width)
    u, tail = run(
        first_kernel,
        [whole(resid), layer_of(mods, 0)],
        (resid, mods),
        [shape((rows, width), BF16), shape((TAIL, width), BF16)],
        name="first",
    )
    for layer in range(LAYERS):
        tail = from_behind(tail, "frames")
        per_layer = (input_weight, step_weight, conv_weight, bias, decay_log, skip)
        gate, y, out_map, cum, send = run(
            functools.partial(local_kernel, parts),
            [whole(u), whole(tail)] + [layer_of(p, layer) for p in per_layer],
            (u, tail) + per_layer,
            [
                shape((rows, INNER), BF16),
                shape((rows, INNER), F32),
                shape((rows, STATE), BF16),
                shape((rows, HEADS), F32),
                shape((parts, part_rows + PAD, LANES), BF16),
            ],
            [pltpu.VMEM((rows + TAIL, 256), F32), pltpu.VMEM((rows, INNER + 2 * STATE), BF16)],
            name="local",
        )
        got = lax.all_to_all(send, "frames", 0, 0)
        (back,) = run(
            scan_kernel,
            [whole(got)],
            (got,),
            [shape((parts, part_rows, LANES), BF16)],
            name="scan",
        )
        enter = lax.all_to_all(back, "frames", 0, 0).reshape(INNER, LANES)
        hidden, a = run(
            finish_kernel,
            [whole(enter), whole(out_map), whole(cum), whole(y), whole(gate), whole(resid)]
            + [layer_of(output_weight, layer), layer_of(gain, layer), layer_of(mods, layer)],
            (enter, out_map, cum, y, gate, resid, output_weight, gain, mods),
            [shape((rows, width), F32), shape((rows, width), BF16)],
            [pltpu.VMEM((rows, INNER), BF16)],
            name="finish",
        )
        prev = from_behind(a, "frames")
        q, kv = run(
            memory_kernel,
            [whole(a), layer_of(query_weight, layer), layer_of(memory_weight, layer)],
            (a, query_weight, memory_weight),
            [shape((rows, ATTN), BF16), shape((rows, 2 * ATTN), BF16)],
            name="memory",
        )
        last = layer == LAYERS - 1
        outs = [shape((rows, width), F32)]
        if not last:
            outs += [shape((rows, width), BF16), shape((TAIL, width), BF16)]
        result = run(
            functools.partial(attend_kernel, last, tok_frame),
            [SCALARS, SCALARS, whole(q), whole(kv), whole(prev)]
            + [layer_of(memory_weight, layer), layer_of(merge_weight, layer), whole(hidden)]
            + [layer_of(mods, min(layer + 1, LAYERS - 1))],
            (base, lookback, q, kv, prev, memory_weight, merge_weight, hidden, mods),
            outs,
            [
                pltpu.VMEM((2 * rows, 2 * ATTN), BF16),
                pltpu.VMEM((rows, 2 * rows), F32),
                pltpu.VMEM((rows, ATTN), BF16),
            ],
            name="attend",
        )
        resid = result[0]
        if not last:
            u, tail = result[1:]
    return resid.reshape(latents.shape)


def solution(mesh):
    sharded = P(("groups", "frames"))
    return jax.shard_map(
        shards,
        mesh=mesh,
        in_specs=(P(("groups", "frames"), None, None), sharded, sharded) + (P(),) * 12,
        out_specs=P(("groups", "frames"), None, None),
        check_vma=False,
    )
```

time: 267 us -> 131 us (0.49)
  other arithmetic: 66 us -> 0.7 us
  matrix products: 29.5 us -> 0 us
  waiting for transfers between devices: 51.6 us -> 23.6 us
  Pallas kernels: 0 us -> 27.5 us
  local copies, waits for them, and re-layouts: 44 us -> 19.6 us
  between operations: 15.2 us -> 2.14 us
  blocking collectives: 49.2 us -> 41.3 us
  starting transfers between devices: 8.4 us -> 14.7 us
    unnamed x2 -> x0, blocking collectives: 49.2 us -> none
    all_to_all x0 -> x3, blocking collectives: none -> 41.3 us  [the longest x2 28.5 us: shards(): got = lax.all_to_all(send, 'frames', 0, 0)]
    select_n x32 -> x0, other arithmetic: 34.9 us -> none  [hop(): return jax.tree.map(lambda a, b: jnp.where(reached, a, b), new, before)]
    all_gather x2 -> x0, waiting for transfers between devices: 33.9 us -> none  [carried_in(): lax.all_gather(part.astype(kind), axis)]
    dot_general x28 -> x0, matrix products: 29.5 us -> none  [the longest x2 4.96 us: shards(): jnp.dot(u_rows, input_weight[layer], preferred_element_type=jnp.float32)]
    pallas_call x0 -> x11, Pallas kernels: none -> 27.5 us  [run(): pl.pallas_call(kernel, grid=(1,), in_specs=specs, out_specs=[whole(o) for...]
    reshape x15 -> x0, local copies, waits for them, and re-layouts: 14.6 us -> none  [the longest x4 8.18 us: finish_mixer(): y_total.reshape(rows, HEADS * HEAD_DIM)]
    unnamed x104 -> x54, local copies, waits for them, and re-layouts: 8.46 us -> 18.7 us
  transfers between devices with their start and end apart: 6 -> 5, of which waited for: 5 -> 5; matrix products, arithmetic and copies ran while one was open for 10% -> 1% of each run, Pallas kernels for 0% -> 2%
where the time goes in v1:
time: 131 us; the launch traced here: 129 us
  blocking collectives  41.3 us (32%)
  Pallas kernels  27.5 us (21%)
  waiting for transfers between devices  23.6 us (18%)
  local copies, waits for them, and re-layouts  19.6 us (15%)
  starting transfers between devices  14.7 us (11%)
  between operations  2.14 us (2%)
    all_to_all x2, blocking collectives, shards(): got = lax.all_to_all(send, 'frames', 0, 0)  28.5 us
    pallas_call x11, Pallas kernels, run(): pl.pallas_call(kernel, grid=(1,), in_specs=specs, out_specs=[whole(o) for...  27.5 us
    unnamed x54, local copies, waits for them, and re-layouts  18.7 us
    ppermute x4, waiting for transfers between devices, from_behind(): return lax.ppermute(value, axis, [(i, i + 1) for i in range(count - 1)])  15.7 us
    all_to_all x1, blocking collectives, shards(): enter = lax.all_to_all(back, 'frames', 0, 0).reshape(INNER, LANES)  12.8 us
    ppermute x4, starting transfers between devices, from_behind(): return lax.ppermute(value, axis, [(i, i + 1) for i in range(count - 1)])  9.59 us
    all_to_all x1, waiting for transfers between devices, shards(): enter = lax.all_to_all(back, 'frames', 0, 0).reshape(INNER, LANES)  7.89 us
    all_to_all x1, starting transfers between devices, shards(): enter = lax.all_to_all(back, 'frames', 0, 0).reshape(INNER, LANES)  5.09 us
  transfers between devices with their start and end apart: 5, of which 5 were waited for; matrix products, arithmetic and copies ran while one was open for 1% of the time, Pallas kernels for 2%

profile of v1, /device:TPU:8, one launch (start us, length us, event | category | flops | bytes accessed | tf_op | source)
XLA Modules:
  0.0 129.5 jit_solution(2076129357353821840)
XLA Ops:
  0.0 0.0 copy-start
  2.0 0.7 bitcast_convert_fusion.mods_ref
  2.7 0.0 copy-start.8
  2.7 0.9 copy-done.8
  3.6 0.2 first.1
  3.8 1.9 %collective-permute-start = (bf16[16,512]{1,0:T(8,128)(2,1)S(1)}, bf16[16,512]{1,0:T(8,128)(2,1)S(1)}, u32[]{:S(2)}, u32[]{:S(2)}) collective-permute-start(bf16[16,512]{1,0:T(8,128)(2,1)S(1)} %get-tuple-element.29), channel_id=1, source_target_pairs={{0,1},{1,2},{2,3},{3,4},{4,5},{5,6},{6,7},{7,8},{8,9},{9,10},{10,1... | collective-permute-start | bytes 49160 | tf_op jit(solution)/shard_map/ppermute | solution.py:313
  5.7 0.0 copy-done
  5.7 0.1 constant_dynamic-slice_fusion
  5.8 0.1 copy.23.bias_ref
  5.9 0.8 broadcast_in_dim.10
  6.6 0.1 broadcast_in_dim_reshape.3.skip_ref
  6.7 0.9 copy.18.sw_ref
  7.6 2.1 %collective-permute-done.tail_ref = bf16[16,512]{1,0:T(8,128)(2,1)S(1)} collective-permute-done((bf16[16,512]{1,0:T(8,128)(2,1)S(1)}, bf16[16,512]{1,0:T(8,128)(2,1)S(1)}, u32[]{:S(2)}, u32[]{:S(2)}) %collective-permute-start) | collective-permute-done | bytes 16416 | tf_op jit(solution)/shard_map/ppermute | solution.py:313
  9.7 0.0 copy-start.2
  9.7 2.3 %copy-done.2 = bf16[2,512,2304]{2,1,0:T(8,128)(2,1)S(1)} copy-done((bf16[2,512,2304]{2,1,0:T(8,128)(2,1)S(1)}, bf16[2,512,2304]{2,1,0:T(8,128)(2,1)}, u32[]{:S(2)}) %copy-start.2) | copy-done | bytes 4718616
  12.1 0.8 copy-done.18
  12.9 0.7 copy-done.22
  13.5 4.2 %local.2 = (bf16[256,1024]{1,0:T(8,128)(2,1)S(1)}, f32[256,1024]{1,0:T(8,128)S(1)}, bf16[256,128]{1,0:T(8,128)(2,1)S(1)}, f32[256,16]{1,0:T(8,128)S(1)}, bf16[16,80,128]{2,1,0:T(8,128)(2,1)S(1)}) custom-call(bf16[256,512]{1,0:T(8,128)(2,1)S(1)} %get-tuple-element.28.u_ref, bf16[16,512]{1,0:T(8,128)(2,1)S(1)} %collective-permute-done.tail_ref, ...), custom_call_target="tpu_custom_call" | custom-call | tf_op jit(solution)/shard_map/local/pallas_call | solution.py:295
  17.7 0.0 copy-start.12
  17.7 1.0 copy-done.12
  18.7 0.8 copy-done.14
  19.5 0.7 copy-done.20
  20.1 14.6 %all_to_all.20.got_ref = bf16[16,80,128]{2,1,0:T(8,128)(2,1)S(1)} all-to-all(bf16[16,80,128]{2,1,0:T(8,128)(2,1)S(1)} %get-tuple-element.30), channel_id=1, replica_groups=mesh['groups'=2,'frames'=16] {'frames'}, dimensions={0} | all-to-all | bytes 655360 | tf_op jit(solution)/shard_map/all_to_all | solution.py:368
  34.8 0.8 scan.2
  35.5 5.1 %all-to-all-start.1 = ((bf16[16,64,128]{2,1,0:T(8,128)(2,1)}), bf16[16,64,128]{2,1,0:T(8,128)(2,1)S(1)}, u32[]{:S(2)}, u32[]{:S(2)}) async-start(bf16[16,64,128]{2,1,0:T(8,128)(2,1)} %scan.2), calls=%async_computation.1 | async-start | bytes 524288 | tf_op jit(solution)/shard_map/all_to_all | solution.py:376
  40.6 0.0 copy-done.25
  40.6 7.9 %all-to-all-done.1 = bf16[16,64,128]{2,1,0:T(8,128)(2,1)S(1)} async-done(((bf16[16,64,128]{2,1,0:T(8,128)(2,1)}), bf16[16,64,128]{2,1,0:T(8,128)(2,1)S(1)}, u32[]{:S(2)}, u32[]{:S(2)}) %all-to-all-start.1) | async-done | bytes 262176 | tf_op jit(solution)/shard_map/all_to_all | solution.py:376
  48.5 0.7 copy-done.10
  49.2 1.6 %copy-done.4 = bf16[2,1024,512]{2,1,0:T(8,128)(2,1)S(1)} copy-done((bf16[2,1024,512]{2,1,0:T(8,128)(2,1)S(1)}, bf16[2,1024,512]{2,1,0:T(8,128)(2,1)}, u32[]{:S(2)}) %copy-start.4) | copy-done | bytes 2097176
  50.8 0.9 copy-done.9
  51.8 0.9 copy-done.11
  52.7 1.2 copy-done.13
  53.9 1.0 copy-done.15
  55.0 0.9 copy-done.21
  55.9 2.3 %finish.2 = (f32[256,512]{1,0:T(8,128)S(1)}, bf16[256,512]{1,0:T(8,128)(2,1)}) custom-call(bf16[1024,128]{1,0:T(8,128)(2,1)S(1)} %bitcast.17, bf16[256,128]{1,0:T(8,128)(2,1)S(1)} %get-tuple-element.31.out_map_ref, f32[256,16]{1,0:T(8,128)S(1)} %copy-done.21, f32[256,1024]{1,0:T(8,128)S(1)} %copy-done.13, bf16[256,1024]{1,0:T(8,128)(2,1)S(1)} %copy-done.15, ...), custom_call_target="tpu_custom_call" | custom-call | tf_op jit(solution)/shard_map/finish/pallas_call | solution.py:295
  58.2 0.8 copy-done.16
  59.0 3.0 %collective-permute-start.1 = (bf16[256,512]{1,0:T(8,128)(2,1)}, bf16[256,512]{1,0:T(8,128)(2,1)}, u32[]{:S(2)}, u32[]{:S(2)}) collective-permute-start(bf16[256,512]{1,0:T(8,128)(2,1)} %get-tuple-element.35.a_ref), channel_id=1, source_target_pairs={{0,1},{1,2},{2,3},{3,4},{4,5},{5,6},{6,7},{7,8},{8,9},{9,10},{10,1... | collective-permute-start | bytes 786440 | tf_op jit(solution)/shard_map/ppermute | solution.py:313
  62.0 0.0 copy-done.1
  62.0 0.0 copy-done.6
  62.0 0.0 copy-start.7
  62.0 0.0 copy-start.17
  62.0 1.6 %memory.2 = (bf16[256,512]{1,0:T(8,128)(2,1)S(1)}, bf16[256,1024]{1,0:T(8,128)(2,1)S(1)}) custom-call(bf16[256,512]{1,0:T(8,128)(2,1)} %get-tuple-element.35.a_ref, bf16[2,512,512]{2,1,0:T(8,128)(2,1)S(1)} %copy-done.6, bf16[2,512,1024]{2,1,0:T(8,128)(2,1)S(1)} %copy-done.1), custom_call_target="tpu_custom_call" | custom-call | tf_op jit(solution)/shard_map/memory/pallas_call | solution.py:295
  63.6 4.3 %collective-permute-done.1.prev_ref = bf16[256,512]{1,0:T(8,128)(2,1)} collective-permute-done((bf16[256,512]{1,0:T(8,128)(2,1)}, bf16[256,512]{1,0:T(8,128)(2,1)}, u32[]{:S(2)}, u32[]{:S(2)}) %collective-permute-start.1) | collective-permute-done | bytes 262176 | tf_op jit(solution)/shard_map/ppermute | solution.py:313
  68.0 0.0 copy-done.24
  68.0 0.0 copy-done.7
  68.0 0.0 copy-done.17
  68.0 0.0 copy-start.19
  68.0 0.0 copy-start.23
  68.0 5.9 %attend.2 = (f32[256,512]{1,0:T(8,128)S(1)}, bf16[256,512]{1,0:T(8,128)(2,1)S(1)}, bf16[16,512]{1,0:T(8,128)(2,1)S(1)}) custom-call(s32[1]{0:T(128)} %bitcast.base_ref, s32[8]{0:T(128)S(1)} %copy-done.24, bf16[256,512]{1,0:T(8,128)(2,1)S(1)} %get-tuple-element.36.q_ref, bf16[256,1024]{1,0:T(8,128)(2,1)S(1)} %get-tuple-element.37.kv_ref, ...), custom_call_target="tpu_custom_call" | custom-call | tf_op jit(solution)/shard_map/attend/pallas_call | solution.py:295
  73.9 2.1 %collective-permute-start.2 = (bf16[16,512]{1,0:T(8,128)(2,1)S(1)}, bf16[16,512]{1,0:T(8,128)(2,1)S(1)}, u32[]{:S(2)}, u32[]{:S(2)}) collective-permute-start(bf16[16,512]{1,0:T(8,128)(2,1)S(1)} %get-tuple-element.40), channel_id=1, source_target_pairs={{0,1},{1,2},{2,3},{3,4},{4,5},{5,6},{6,7},{7,8},{8,9},{9,10},{10,1... | collective-permute-start | bytes 49160 | tf_op jit(solution)/shard_map/ppermute | solution.py:313
  76.0 3.8 %collective-permute-done.2.tail_ref = bf16[16,512]{1,0:T(8,128)(2,1)S(1)} collective-permute-done((bf16[16,512]{1,0:T(8,128)(2,1)S(1)}, bf16[16,512]{1,0:T(8,128)(2,1)S(1)}, u32[]{:S(2)}, u32[]{:S(2)}) %collective-permute-start.2) | collective-permute-done | bytes 16416 | tf_op jit(solution)/shard_map/ppermute | solution.py:313
  79.9 0.0 copy-done.19
  79.9 0.0 copy-done.23
  79.9 2.3 %copy-done.3 = bf16[2,512,2304]{2,1,0:T(8,128)(2,1)S(1)} copy-done((bf16[2,512,2304]{2,1,0:T(8,128)(2,1)S(1)}, bf16[2,512,2304]{2,1,0:T(8,128)(2,1)}, u32[]{:S(2)}) %copy-start.3) | copy-done | bytes 4718616
  82.2 4.2 %local.3 = (bf16[256,1024]{1,0:T(8,128)(2,1)S(1)}, f32[256,1024]{1,0:T(8,128)S(1)}, bf16[256,128]{1,0:T(8,128)(2,1)S(1)}, f32[256,16]{1,0:T(8,128)S(1)}, bf16[16,80,128]{2,1,0:T(8,128)(2,1)S(1)}) custom-call(bf16[256,512]{1,0:T(8,128)(2,1)S(1)} %get-tuple-element.39.u_ref, bf16[16,512]{1,0:T(8,128)(2,1)S(1)} %collective-permute-done.2.tail_ref, ...), custom_call_target="tpu_custom_call" | custom-call | tf_op jit(solution)/shard_map/local/pallas_call | solution.py:295
  86.4 13.8 %all_to_all.21.got_ref = bf16[16,80,128]{2,1,0:T(8,128)(2,1)S(1)} all-to-all(bf16[16,80,128]{2,1,0:T(8,128)(2,1)S(1)} %get-tuple-element.41), channel_id=1, replica_groups=mesh['groups'=2,'frames'=16] {'frames'}, dimensions={0} | all-to-all | bytes 655360 | tf_op jit(solution)/shard_map/all_to_all | solution.py:368
  100.2 0.1 scan.3
  100.3 12.8 %all_to_all.22 = bf16[16,64,128]{2,1,0:T(8,128)(2,1)S(1)} all-to-all(bf16[16,64,128]{2,1,0:T(8,128)(2,1)S(1)} %scan.3), channel_id=1, replica_groups=mesh['groups'=2,'frames'=16] {'frames'}, dimensions={0} | all-to-all | bytes 524288 | tf_op jit(solution)/shard_map/all_to_all | solution.py:376
  113.1 0.0 copy-done.5
  113.1 1.6 %finish.3 = (f32[256,512]{1,0:T(8,128)S(1)}, bf16[256,512]{1,0:T(8,128)(2,1)S(1)}) custom-call(bf16[1024,128]{1,0:T(8,128)(2,1)S(1)} %bitcast.18, bf16[256,128]{1,0:T(8,128)(2,1)S(1)} %get-tuple-element.42.out_map_ref, f32[256,16]{1,0:T(8,128)S(1)} %get-tuple-element.43.cum_ref, f32[256,1024]{1,0:T(8,128)S(1)} %get-tuple-element.44.y_ref, ...), custom_call_target="tpu_custom_call" | custom-call | tf_op jit(solution)/shard_map/finish/pallas_call | solution.py:295
  114.8 2.6 %collective-permute-start.3 = (bf16[256,512]{1,0:T(8,128)(2,1)S(1)}, bf16[256,512]{1,0:T(8,128)(2,1)S(1)}, u32[]{:S(2)}, u32[]{:S(2)}) collective-permute-start(bf16[256,512]{1,0:T(8,128)(2,1)S(1)} %get-tuple-element.47.a_ref), channel_id=1, source_target_pairs={{0,1},{1,2},{2,3},{3,4},{4,5},{5,6},{6,7},{7,8},{8,9},{9,10},{10,1... | collective-permute-start | bytes 786440 | tf_op jit(solution)/shard_map/ppermute | solution.py:313
  117.4 0.6 memory.3
  117.9 5.4 %collective-permute-done.3.prev_ref = bf16[256,512]{1,0:T(8,128)(2,1)S(1)} collective-permute-done((bf16[256,512]{1,0:T(8,128)(2,1)S(1)}, bf16[256,512]{1,0:T(8,128)(2,1)S(1)}, u32[]{:S(2)}, u32[]{:S(2)}) %collective-permute-start.3) | collective-permute-done | bytes 262176 | tf_op jit(solution)/shard_map/ppermute | solution.py:313
  123.4 6.1 %attend.3 = f32[256,512]{1,0:T(8,128)} custom-call(s32[1]{0:T(128)} %bitcast.base_ref, s32[8]{0:T(128)S(1)} %copy-done.24, bf16[256,512]{1,0:T(8,128)(2,1)S(1)} %get-tuple-element.48.q_ref, bf16[256,1024]{1,0:T(8,128)(2,1)S(1)} %get-tuple-element.49.kv_ref, bf16[256,512]{1,0:T(8,128)(2,1)S(1)} %collective-permute-done.3.prev_ref, ...), custom_call_target="tpu_custom_call" | custom-call | tf_op jit(solution)/shard_map/attend/pallas_call | solution.py:295
  (19 shorter events, 0.0 us)
Async XLA Ops:
  0.0 5.7 %copy-start = (f32[2,50,16]{1,2,0:T(8,128)S(1)}, f32[2,50,16]{1,2,0:T(8,128)}, u32[]{:S(2)}) copy-start(f32[2,50,16]{1,2,0:T(8,128)} %param.22) | copy-start | bytes 19204
  2.7 0.9 copy-start.8
  3.8 6.0 %collective-permute-start = (bf16[16,512]{1,0:T(8,128)(2,1)S(1)}, bf16[16,512]{1,0:T(8,128)(2,1)S(1)}, u32[]{:S(2)}, u32[]{:S(2)}) collective-permute-start(bf16[16,512]{1,0:T(8,128)(2,1)S(1)} %get-tuple-element.29), channel_id=1, source_target_pairs={{0,1},{1,2},{2,3},{3,4},{4,5},{5,6},{6,7},{7,8},{8,9},{9,10},{10,1... | collective-permute-start | bytes 49160 | tf_op jit(solution)/shard_map/ppermute | solution.py:313
  9.7 2.3 %copy-start.2 = (bf16[2,512,2304]{2,1,0:T(8,128)(2,1)S(1)}, bf16[2,512,2304]{2,1,0:T(8,128)(2,1)}, u32[]{:S(2)}) copy-start(bf16[2,512,2304]{2,1,0:T(8,128)(2,1)} %w_ref.6) | copy-start | bytes 14155780
  12.1 0.8 copy-start.18
  12.9 0.7 copy-start.22
  13.5 27.1 %copy-start.25 = (f32[2,1024]{1,0:T(2,128)S(1)}, f32[2,1024]{1,0:T(2,128)}, u32[]{:S(2)}) copy-start(f32[2,1024]{1,0:T(2,128)} %param.25) | copy-start | bytes 24580
  17.7 1.0 copy-start.12
  18.7 0.8 copy-start.14
  19.5 0.7 copy-start.20
  35.5 13.0 %all-to-all-start.1 = ((bf16[16,64,128]{2,1,0:T(8,128)(2,1)}), bf16[16,64,128]{2,1,0:T(8,128)(2,1)S(1)}, u32[]{:S(2)}, u32[]{:S(2)}) async-start(bf16[16,64,128]{2,1,0:T(8,128)(2,1)} %scan.2), calls=%async_computation.1 | async-start | bytes 524288 | tf_op jit(solution)/shard_map/all_to_all | solution.py:376
  48.5 0.7 copy-start.10
  49.2 1.6 %copy-start.4 = (bf16[2,1024,512]{2,1,0:T(8,128)(2,1)S(1)}, bf16[2,1024,512]{2,1,0:T(8,128)(2,1)}, u32[]{:S(2)}) copy-start(bf16[2,1024,512]{2,1,0:T(8,128)(2,1)} %w_ref.7) | copy-start | bytes 6291460
  50.8 0.9 copy-start.9
  51.8 0.9 copy-start.11
  52.7 1.2 copy-start.13
  53.9 1.0 copy-start.15
  55.0 0.9 copy-start.21
  55.9 6.1 %copy-start.1 = (bf16[2,512,1024]{2,1,0:T(8,128)(2,1)S(1)}, bf16[2,512,1024]{2,1,0:T(8,128)(2,1)}, u32[]{:S(2)}) copy-start(bf16[2,512,1024]{2,1,0:T(8,128)(2,1)} %wm_ref.7) | copy-start | bytes 6291460
  55.9 6.1 %copy-start.6 = (bf16[2,512,512]{2,1,0:T(8,128)(2,1)S(1)}, bf16[2,512,512]{2,1,0:T(8,128)(2,1)}, u32[]{:S(2)}) copy-start(bf16[2,512,512]{2,1,0:T(8,128)(2,1)} %wq_ref.3) | copy-start | bytes 3145732
  58.2 0.8 copy-start.16
  59.0 9.0 %copy-start.24 = (s32[8]{0:T(128)S(1)}, s32[8]{0:T(128)}, u32[]{:S(2)}) copy-start(s32[8]{0:T(128)} %reach_ref.3) | copy-start | bytes 100
  59.0 9.0 %collective-permute-start.1 = (bf16[256,512]{1,0:T(8,128)(2,1)}, bf16[256,512]{1,0:T(8,128)(2,1)}, u32[]{:S(2)}, u32[]{:S(2)}) collective-permute-start(bf16[256,512]{1,0:T(8,128)(2,1)} %get-tuple-element.35.a_ref), channel_id=1, source_target_pairs={{0,1},{1,2},{2,3},{3,4},{4,5},{5,6},{6,7},{7,8},{8,9},{9,10},{10,1... | collective-permute-start | bytes 786440 | tf_op jit(solution)/shard_map/ppermute | solution.py:313
  62.0 6.0 %copy-start.7 = (bf16[2,512,512]{2,1,0:T(8,128)(2,1)S(1)}, bf16[2,512,512]{2,1,0:T(8,128)(2,1)}, u32[]{:S(2)}) copy-start(bf16[2,512,512]{2,1,0:T(8,128)(2,1)} %merge_ref.3) | copy-start | bytes 3145732
  62.0 6.0 %copy-start.17 = (f32[256,512]{1,0:T(8,128)S(1)}, f32[256,512]{1,0:T(8,128)}, u32[]{:S(2)}) copy-start(f32[256,512]{1,0:T(8,128)} %copy-done.16) | copy-start | bytes 1572868
  68.0 11.9 %copy-start.19 = (f32[2,4,1280]{2,1,0:T(4,128)S(1)}, f32[2,4,1280]{2,1,0:T(4,128)}, u32[]{:S(2)}) copy-start(f32[2,4,1280]{2,1,0:T(4,128)} %conv_ref.3) | copy-start | bytes 122884
  68.0 11.9 %copy-start.23 = (f32[2,16]{1,0:T(2,128)S(1)}, f32[2,16]{1,0:T(2,128)}, u32[]{:S(2)}) copy-start(f32[2,16]{1,0:T(2,128)} %param.23) | copy-start | bytes 388
  73.9 6.0 %collective-permute-start.2 = (bf16[16,512]{1,0:T(8,128)(2,1)S(1)}, bf16[16,512]{1,0:T(8,128)(2,1)S(1)}, u32[]{:S(2)}, u32[]{:S(2)}) collective-permute-start(bf16[16,512]{1,0:T(8,128)(2,1)S(1)} %get-tuple-element.40), channel_id=1, source_target_pairs={{0,1},{1,2},{2,3},{3,4},{4,5},{5,6},{6,7},{7,8},{8,9},{9,10},{10,1... | collective-permute-start | bytes 49160 | tf_op jit(solution)/shard_map/ppermute | solution.py:313
  79.9 2.3 %copy-start.3 = (bf16[2,512,2304]{2,1,0:T(8,128)(2,1)S(1)}, bf16[2,512,2304]{2,1,0:T(8,128)(2,1)}, u32[]{:S(2)}) copy-start(bf16[2,512,2304]{2,1,0:T(8,128)(2,1)} %w_ref.6) | copy-start | bytes 14155780
  82.2 30.9 %copy-start.5 = (bf16[2,1024,512]{2,1,0:T(8,128)(2,1)S(1)}, bf16[2,1024,512]{2,1,0:T(8,128)(2,1)}, u32[]{:S(2)}) copy-start(bf16[2,1024,512]{2,1,0:T(8,128)(2,1)} %w_ref.7) | copy-start | bytes 6291460
  114.8 8.6 %collective-permute-start.3 = (bf16[256,512]{1,0:T(8,128)(2,1)S(1)}, bf16[256,512]{1,0:T(8,128)(2,1)S(1)}, u32[]{:S(2)}, u32[]{:S(2)}) collective-permute-start(bf16[256,512]{1,0:T(8,128)(2,1)S(1)} %get-tuple-element.47.a_ref), channel_id=1, source_target_pairs={{0,1},{1,2},{2,3},{3,4},{4,5},{5,6},{6,7},{7,8},{8,9},{9,10},{10,1... | collective-permute-start | bytes 786440 | tf_op jit(solution)/shard_map/ppermute | solution.py:313

commit v2 on v1

v2 whole, which is shorter than its diff:
```python
import functools

import jax
import jax.numpy as jnp
from jax import lax
from jax.experimental import pallas as pl
from jax.experimental.pallas import tpu as pltpu
from jax.sharding import PartitionSpec as P

HEADS = 16
HEAD_DIM = 64
STATE = 128
ATT_HEADS = 8
LAYERS = 2
CONV = 4
SPAN = 128
WINDOW = 8
EPS = 1e-06
HEAD_EPS = 1e-05
INNER = HEADS * HEAD_DIM
ATTN = ATT_HEADS * HEAD_DIM
PAD = 16
LANES = 128
TAIL = 16
F32 = jnp.float32
BF16 = jnp.bfloat16


def dot(a, b, dims=((1,), (0,)), precision=None):
    return lax.dot_general(a, b, (dims, ((), ())), precision=precision, preferred_element_type=F32)


def rms_mod(x, shift, scale):
    normed = x * lax.rsqrt(jnp.mean(x * x, axis=-1, keepdims=True) + EPS)
    return (normed * (1.0 + scale) + shift).astype(BF16)


def spread(per_head):
    high = per_head.astype(BF16)
    low = (per_head - high.astype(F32)).astype(BF16)
    row = lax.broadcasted_iota(jnp.int32, (2 * HEADS, INNER), 0) % HEADS
    head = lax.broadcasted_iota(jnp.int32, (2 * HEADS, INNER), 1) // HEAD_DIM
    sel = jnp.where(row == head, 1.0, 0.0).astype(BF16)
    return dot(jnp.concatenate([high, low], axis=1), sel)


def spread_row(per_head):
    return spread(jnp.broadcast_to(per_head, (16, HEADS)))[0:1, :]


def mod_rows(mods_ref, layer, step, which):
    mods = mods_ref[layer, step].astype(F32)
    return mods[which : which + 1, :], mods[which + 1 : which + 2, :]


def first_kernel(step_ref, x_ref, mods_ref, u_ref, tail_ref):
    rows = x_ref.shape[0]
    u = rms_mod(x_ref[...].astype(F32), *mod_rows(mods_ref, 0, step_ref[0], 0))
    u_ref[...] = u
    tail_ref[...] = u[rows - TAIL :]


def local_kernel(
    layer,
    parts,
    step_ref,
    u_ref,
    tail_ref,
    w_ref,
    sw_ref,
    conv_ref,
    bias_ref,
    decay_ref,
    act_ref,
    cum_ref,
    shifted_ref,
    state_ref,
    send_ref,
    ext_ref,
):
    rows = u_ref.shape[0]
    u = u_ref[...]
    tail = tail_ref[...]
    nsteps = bias_ref.shape[-1]
    chosen = lax.broadcasted_iota(jnp.int32, (8, nsteps), 1) == step_ref[0]
    bias = dot(
        jnp.where(chosen, 1.0, 0.0).astype(F32),
        bias_ref[layer],
        ((1,), (1,)),
        precision=lax.Precision.HIGHEST,
    )[0:1, :]
    raw = dot(u, sw_ref[layer], ((1,), (1,))) + bias
    step = jnp.maximum(raw, 0.0) + jnp.log1p(jnp.exp(-jnp.abs(raw)))
    log_decay = -jnp.exp(decay_ref[layer : layer + 1, :]) * step
    log_step = jnp.log(step)
    q_pos = lax.broadcasted_iota(jnp.int32, (SPAN, SPAN), 0)
    s_pos = lax.broadcasted_iota(jnp.int32, (SPAN, SPAN), 1)
    lower = jnp.where(q_pos >= s_pos, 1.0, 0.0).astype(F32)
    ends, edges = [], []
    for b in range(rows // SPAN):
        r = slice(b * SPAN, (b + 1) * SPAN)
        cum = dot(lower, log_decay[r], precision=lax.Precision.HIGHEST)
        end = cum[SPAN - 1 : SPAN, :]
        cum_ref[r, :] = cum
        shifted_ref[:, r] = (cum - log_step[r]).T
        ends.append(end)
        edges.append(spread(jnp.exp(end - cum) * step[r]))

    chunk = 256
    for c in [INNER] + list(range(0, INNER, chunk)):
        w = w_ref[layer, :, INNER + c : INNER + c + chunk]
        slot = c // chunk % 2
        ext_ref[slot, 0:TAIL, :] = dot(tail, w).astype(BF16).astype(F32)
        ext_ref[slot, TAIL:, :] = dot(u, w).astype(BF16).astype(F32)
        total = None
        for k in range(CONV):
            start = TAIL - (CONV - 1) + k
            term = conv_ref[layer, k : k + 1, c : c + chunk] * ext_ref[slot, start : start + rows, :]
            total = term if total is None else total + term
        act_ref[:, c : c + chunk] = (total * jax.nn.sigmoid(total)).astype(BF16)

    state = None
    for b in range(rows // SPAN):
        r = slice(b * SPAN, (b + 1) * SPAN)
        in_map = act_ref[r, INNER : INNER + STATE]
        scaled = (act_ref[r, 0:INNER].astype(F32) * edges[b]).astype(BF16)
        term = dot(in_map, scaled, ((0,), (0,)))
        if state is None:
            state = term
        else:
            state_ref[(b - 1) * STATE : b * STATE, :] = state.astype(BF16)
            state = spread_row(jnp.exp(ends[b])) * state + term

    part_rows = INNER // parts
    held = max(1, part_rows // HEAD_DIM)
    size = min(part_rows, LANES)
    for pair in range(HEADS // 2):
        turned = state[:, pair * LANES : (pair + 1) * LANES].T.astype(BF16)
        for k in range(LANES // size):
            first = pair * LANES + k * size
            part, at = first // part_rows, first % part_rows
            send_ref[part, at : at + size, :] = turned[k * size : (k + 1) * size, :]
    pad_row = lax.broadcasted_iota(jnp.int32, (PAD, LANES), 0)
    over = sum(ends[1:], ends[0])
    for part in range(parts):
        pad = jnp.zeros((PAD, LANES), F32)
        for i in range(held):
            h = part * part_rows // HEAD_DIM + i
            decay = jnp.broadcast_to(over[:, h : h + 1], (PAD, LANES))
            high = decay.astype(BF16).astype(F32)
            pad = jnp.where(pad_row == 2 * i, high, jnp.where(pad_row == 2 * i + 1, decay - high, pad))
        send_ref[part, part_rows:, :] = pad.astype(BF16)


def mix_kernel(
    layer, u_ref, w_ref, act_ref, cum_ref, shifted_ref, state_ref, skip_ref, y_ref, wide_ref
):
    rows = u_ref.shape[0]
    u = u_ref[...]
    q_pos = lax.broadcasted_iota(jnp.int32, (SPAN, SPAN), 0)
    s_pos = lax.broadcasted_iota(jnp.int32, (SPAN, SPAN), 1)
    lower = q_pos >= s_pos
    lane = lax.broadcasted_iota(jnp.int32, (SPAN, LANES), 1)
    left = lane < HEAD_DIM
    zero = jnp.zeros((SPAN, LANES), BF16)
    skip = spread_row(skip_ref[layer : layer + 1, :])
    before = jnp.zeros((1, HEADS), F32)
    for b in range(rows // SPAN):
        r = slice(b * SPAN, (b + 1) * SPAN)
        cum = cum_ref[r, :]
        in_map = act_ref[r, INNER : INNER + STATE]
        out_map = act_ref[r, INNER + STATE :]
        affinity = dot(out_map, in_map, ((1,), (1,)))
        wide_ref[r, :] = spread(jnp.exp(cum + before))
        before = before + cum[SPAN - 1 : SPAN, :]
        if b:
            y_ref[r, :] = dot(out_map, state_ref[(b - 1) * STATE : b * STATE, :]) * spread(jnp.exp(cum))
        for pair in range(HEADS // 2):
            cols = slice(pair * LANES, (pair + 1) * LANES)
            values = act_ref[r, cols]
            mixing = []
            for h in (2 * pair, 2 * pair + 1):
                gap = cum[:, h : h + 1] - shifted_ref[h : h + 1, r]
                mixing.append(jnp.where(lower, affinity * jnp.exp(gap), 0.0).astype(BF16))
            both = jnp.concatenate(mixing, axis=1)
            stacked = jnp.concatenate(
                [jnp.where(left, values, zero), jnp.where(left, zero, values)], axis=0
            )
            y = dot(both, stacked) + skip[:, cols] * values.astype(F32)
            if b:
                y = y + y_ref[r, cols]
            gate = dot(u[r], w_ref[layer, :, cols]).astype(BF16).astype(F32)
            gate = gate * jax.nn.sigmoid(gate)
            y_ref[r, cols] = y * gate
            wide_ref[r, cols] = wide_ref[r, cols] * gate


def scan_kernel(got_ref, back_ref):
    parts, padded, _ = got_ref.shape
    part_rows = padded - PAD
    held = max(1, part_rows // HEAD_DIM)
    size = part_rows // held
    carry = [jnp.zeros((size, LANES), F32) for _ in range(held)]
    for d in range(parts):
        pad = got_ref[d, part_rows:, :].astype(F32)
        for i in range(held):
            rows = slice(i * size, (i + 1) * size)
            back_ref[d, rows, :] = carry[i].astype(BF16)
            decay = jnp.exp(pad[2 * i : 2 * i + 1, :] + pad[2 * i + 1 : 2 * i + 2, :])
            carry[i] = decay * carry[i] + got_ref[d, rows, :].astype(F32)


def finish_kernel(
    layer,
    step_ref,
    enter_ref,
    act_ref,
    y_ref,
    wide_ref,
    resid_ref,
    w_ref,
    gain_ref,
    mods_ref,
    hidden_ref,
    a_ref,
    normed_ref,
):
    out_map = act_ref[:, INNER + STATE :]
    chunk = 256
    row = lax.broadcasted_iota(jnp.int32, (chunk, chunk), 0) // HEAD_DIM
    col = lax.broadcasted_iota(jnp.int32, (chunk, chunk), 1) // HEAD_DIM
    same = jnp.where(row == col, 1.0 / HEAD_DIM, 0.0).astype(BF16)
    for c in range(0, INNER, chunk):
        cols = slice(c, c + chunk)
        carried = dot(out_map, enter_ref[cols, :], ((1,), (1,)))
        total = y_ref[:, cols] + carried * wide_ref[:, cols]
        square = total * total
        high = square.astype(BF16)
        low = (square - high.astype(F32)).astype(BF16)
        mean = dot(high, same) + dot(low, same)
        gain = gain_ref[layer : layer + 1, cols]
        normed_ref[:, cols] = (total * lax.rsqrt(mean + HEAD_EPS) * gain).astype(BF16)
    hidden = resid_ref[...].astype(F32) + dot(normed_ref[...], w_ref[layer])
    hidden_ref[...] = hidden
    a_ref[...] = rms_mod(hidden, *mod_rows(mods_ref, layer, step_ref[0], 2))


def memory_kernel(
    layer, tok_frame, base_ref, reach_ref, a_ref, wq_ref, wm_ref, q_ref, kv_ref, bias_ref
):
    rows = a_ref.shape[0]
    a = a_ref[...]
    q_ref[...] = (dot(a, wq_ref[layer]).astype(BF16).astype(F32) * HEAD_DIM**-0.5).astype(BF16)
    kv_ref[...] = dot(a, wm_ref[layer]).astype(BF16)
    key_frame = lax.broadcasted_iota(jnp.int32, (tok_frame, 2 * rows), 1) // tok_frame
    first = WINDOW - base_ref[0]
    for f in range(WINDOW):
        low = jnp.maximum(first, f + WINDOW - reach_ref[f])
        seen = (key_frame >= low) & (key_frame <= f + WINDOW)
        bias_ref[f * tok_frame : (f + 1) * tok_frame, :] = jnp.where(seen, 0.0, -1e30)


def attend_kernel(
    layer,
    last,
    step_ref,
    q_ref,
    kv_ref,
    bias_ref,
    prev_ref,
    wm_ref,
    merge_ref,
    hidden_ref,
    mods_ref,
    *rest,
):
    if last:
        resid_ref, keyed_ref, out_ref = rest
    else:
        resid_ref, u_ref, tail_ref, keyed_ref, out_ref = rest
    rows = q_ref.shape[0]
    keyed_ref[0:rows, :] = dot(prev_ref[...], wm_ref[layer]).astype(BF16)
    keyed_ref[rows:, :] = kv_ref[...]
    half = rows // 2
    span = rows + half
    left = lax.broadcasted_iota(jnp.int32, (half, LANES), 1) < HEAD_DIM
    one = jnp.ones((span, LANES), BF16)
    zero = jnp.zeros((half, LANES), BF16)
    together = 2
    for part in range(2):
        r = slice(part * half, (part + 1) * half)
        k_rows = slice(part * half, part * half + span)
        bias = bias_ref[r, k_rows]
        bias = jnp.concatenate([bias, bias], axis=0)
        for group in range(0, ATT_HEADS // 2, together):
            pairs = range(group, group + together)
            scores = []
            for pair in pairs:
                cols = slice(pair * LANES, (pair + 1) * LANES)
                query = q_ref[r, cols]
                sides = jnp.concatenate(
                    [jnp.where(left, query, zero), jnp.where(left, zero, query)], axis=0
                )
                scores.append(dot(sides, keyed_ref[k_rows, cols], ((1,), (1,))) + bias)
            tops = [jnp.max(s, axis=-1, keepdims=True) for s in scores]
            weights = [jnp.exp(s - t).astype(BF16) for s, t in zip(scores, tops)]
            for pair, weight in zip(pairs, weights):
                values = keyed_ref[k_rows, ATTN + pair * LANES : ATTN + (pair + 1) * LANES]
                both = dot(weight, jnp.concatenate([values, one], axis=1))
                number = jnp.where(left, both[:half, :LANES], both[half:, :LANES])
                total = jnp.where(left, both[:half, LANES:], both[half:, LANES:])
                out_ref[r, pair * LANES : (pair + 1) * LANES] = (number / total).astype(BF16)
    resid = hidden_ref[...] + dot(out_ref[...], merge_ref[layer])
    resid_ref[...] = resid
    if not last:
        u = rms_mod(resid, *mod_rows(mods_ref, layer + 1, step_ref[0], 0))
        u_ref[...] = u
        tail_ref[...] = u[rows - TAIL :]


SCALARS = pl.BlockSpec(memory_space=pltpu.SMEM)
WHOLE = pl.BlockSpec(memory_space=pltpu.VMEM)


def run(kernel, scalars, operands, outs, scratch=(), name=None, flops=0):
    moved = sum(o.size * o.dtype.itemsize for o in list(operands) + list(outs))
    return pl.pallas_call(
        kernel,
        in_specs=[SCALARS] * len(scalars) + [WHOLE] * len(operands),
        out_specs=[WHOLE] * len(outs),
        out_shape=list(outs),
        scratch_shapes=list(scratch),
        compiler_params=pltpu.CompilerParams(vmem_limit_bytes=20 * 1024 * 1024),
        cost_estimate=pl.CostEstimate(flops=flops, bytes_accessed=moved, transcendentals=0),
        name=name,
    )(*scalars, *operands)


def shape(dims, dtype):
    return jax.ShapeDtypeStruct(dims, dtype)


def from_behind(value, axis):
    count = lax.axis_size(axis)
    return lax.ppermute(value, axis, [(i, i + 1) for i in range(count - 1)])


def shards(
    latents,
    timestep,
    lookback,
    modulation,
    input_weight,
    step_weight,
    conv_weight,
    step_bias,
    decay_log,
    skip_gain,
    norm_gain,
    output_weight,
    query_weight,
    memory_weight,
    merge_weight,
):
    frames_dev, tok_frame, width = latents.shape
    rows = frames_dev * tok_frame
    spans = rows // SPAN
    parts = lax.axis_size("frames")
    part_rows = INNER // parts
    base = (lax.axis_index("frames") * frames_dev).astype(jnp.int32).reshape(1)
    step_weight = jnp.swapaxes(step_weight, 1, 2)
    step_bias = jnp.swapaxes(step_bias, 1, 2)
    resid = latents.reshape(rows, width)
    u, tail = run(
        first_kernel,
        (timestep,),
        (resid, modulation),
        [shape((rows, width), BF16), shape((TAIL, width), BF16)],
        name="first",
    )
    for layer in range(LAYERS):
        tail = from_behind(tail, "frames")
        act, cum, shifted, state, send = run(
            functools.partial(local_kernel, layer, parts),
            (timestep,),
            (u, tail, input_weight, step_weight, conv_weight, step_bias, decay_log),
            [
                shape((rows, INNER + 2 * STATE), BF16),
                shape((rows, HEADS), F32),
                shape((HEADS, rows), F32),
                shape((max(spans - 1, 1) * STATE, INNER), BF16),
                shape((parts, part_rows + PAD, LANES), BF16),
            ],
            [pltpu.VMEM((2, rows + TAIL, 256), F32)],
            name="local",
            flops=2 * rows * width * (INNER + 2 * STATE),
        )
        got = lax.all_to_all(send, "frames", 0, 0)
        y, wide = run(
            functools.partial(mix_kernel, layer),
            (),
            (u, input_weight, act, cum, shifted, state, skip_gain),
            [shape((rows, INNER), F32), shape((rows, INNER), F32)],
            name="mix",
            flops=2 * rows * width * INNER,
        )
        (back,) = run(
            scan_kernel,
            (),
            (got,),
            [shape((parts, part_rows, LANES), BF16)],
            name="scan",
        )
        enter = lax.all_to_all(back, "frames", 0, 0).reshape(INNER, LANES)
        hidden, a = run(
            functools.partial(finish_kernel, layer),
            (timestep,),
            (enter, act, y, wide, resid, output_weight, norm_gain, modulation),
            [shape((rows, width), F32), shape((rows, width), BF16)],
            [pltpu.VMEM((rows, INNER), BF16)],
            name="finish",
        )
        prev = from_behind(a, "frames")
        q, kv, bias = run(
            functools.partial(memory_kernel, layer, tok_frame),
            (base, lookback),
            (a, query_weight, memory_weight),
            [
                shape((rows, ATTN), BF16),
                shape((rows, 2 * ATTN), BF16),
                shape((rows, 2 * rows), F32),
            ],
            name="memory",
            flops=2 * rows * width * 3 * ATTN,
        )
        last = layer == LAYERS - 1
        outs = [shape((rows, width), F32)]
        if not last:
            outs += [shape((rows, width), BF16), shape((TAIL, width), BF16)]
        result = run(
            functools.partial(attend_kernel, layer, last),
            (timestep,),
            (q, kv, bias, prev, memory_weight, merge_weight, hidden, modulation),
            outs,
            [pltpu.VMEM((2 * rows, 2 * ATTN), BF16), pltpu.VMEM((rows, ATTN), BF16)],
            name="attend",
        )
        resid = result[0]
        if not last:
            u, tail = result[1:]
    return resid.reshape(latents.shape)


def solution(mesh):
    sharded = P(("groups", "frames"))
    return jax.shard_map(
        shards,
        mesh=mesh,
        in_specs=(P(("groups", "frames"), None, None), sharded, sharded) + (P(),) * 12,
        out_specs=P(("groups", "frames"), None, None),
        check_vma=False,
    )
```

time: 131 us -> 134 us (1.023)
  local copies, waits for them, and re-layouts: 19.6 us -> 41.2 us
  blocking collectives: 41.3 us -> 28.5 us
  waiting for transfers between devices: 23.6 us -> 17.8 us
  starting transfers between devices: 14.7 us -> 19 us
  between operations: 2.14 us -> 0.31 us
  Pallas kernels: 27.5 us -> 25.8 us
    unnamed x54 -> x112, local copies, waits for them, and re-layouts: 18.7 us -> 41.2 us
    all_to_all x1 -> x0, blocking collectives: 12.8 us -> none  [shards(): enter = lax.all_to_all(back, 'frames', 0, 0).reshape(INNER, LANES)]
    all_to_all x1 -> x2, waiting for transfers between devices: 7.89 us -> 2.01 us  [shards(): enter = lax.all_to_all(back, 'frames', 0, 0).reshape(INNER, LANES)]
    all_to_all x1 -> x2, starting transfers between devices: 5.09 us -> 10.2 us  [shards(): enter = lax.all_to_all(back, 'frames', 0, 0).reshape(INNER, LANES)]
    pallas_call x11 -> x13, Pallas kernels: 27.5 us -> 25.8 us  [run(): pl.pallas_call(kernel, in_specs=[SCALARS] * len(scalars) + [WHOLE] * len(...]
  transfers between devices with their start and end apart: 5 -> 6, of which waited for: 5 -> 5; matrix products, arithmetic and copies ran while one was open for 1% -> 0% of each run, Pallas kernels for 2% -> 5%
where the time goes in v2:
time: 134 us; the launch traced here: 133 us
  local copies, waits for them, and re-layouts  41.2 us (31%)
  blocking collectives  28.5 us (21%)
  Pallas kernels  25.8 us (19%)
  starting transfers between devices  19 us (14%)
  waiting for transfers between devices  17.8 us (13%)
    unnamed x112, local copies, waits for them, and re-layouts  41.2 us
    all_to_all x2, blocking collectives, shards(): got = lax.all_to_all(send, 'frames', 0, 0)  28.5 us
    pallas_call x13, Pallas kernels, run(): pl.pallas_call(kernel, in_specs=[SCALARS] * len(scalars) + [WHOLE] * len(...  25.8 us
    ppermute x4, waiting for transfers between devices, from_behind(): return lax.ppermute(value, axis, [(i, i + 1) for i in range(count - 1)])  15.8 us
    all_to_all x2, starting transfers between devices, shards(): enter = lax.all_to_all(back, 'frames', 0, 0).reshape(INNER, LANES)  10.2 us
    ppermute x4, starting transfers between devices, from_behind(): return lax.ppermute(value, axis, [(i, i + 1) for i in range(count - 1)])  8.87 us
  transfers between devices with their start and end apart: 6, of which 5 were waited for; matrix products, arithmetic and copies ran while one was open for 0% of the time, Pallas kernels for 5%

profile of v2, /device:TPU:8, one launch (start us, length us, event | category | flops | bytes accessed | tf_op | source)
XLA Modules:
  0.0 132.6 jit_solution(13197105951532725617)
XLA Ops:
  0.0 1.0 copy-done.4
  1.0 0.9 copy-done.17
  2.0 0.7 copy-done.41
  2.6 0.7 first.1
  3.3 1.9 %collective-permute-start = (bf16[16,512]{1,0:T(8,128)(2,1)S(1)}, bf16[16,512]{1,0:T(8,128)(2,1)S(1)}, u32[]{:S(2)}, u32[]{:S(2)}) collective-permute-start(bf16[16,512]{1,0:T(8,128)(2,1)S(1)} %get-tuple-element.35), channel_id=1, source_target_pairs={{0,1},{1,2},{2,3},{3,4},{4,5},{5,6},{6,7},{7,8},{8,9},{9,10},{10,1... | collective-permute-start | bytes 49160 | tf_op jit(solution)/shard_map/ppermute | solution.py:345
  5.2 4.0 %collective-permute-done.tail_ref = bf16[16,512]{1,0:T(8,128)(2,1)S(1)} collective-permute-done((bf16[16,512]{1,0:T(8,128)(2,1)S(1)}, bf16[16,512]{1,0:T(8,128)(2,1)S(1)}, u32[]{:S(2)}, u32[]{:S(2)}) %collective-permute-start) | collective-permute-done | bytes 16416 | tf_op jit(solution)/shard_map/ppermute | solution.py:345
  9.3 2.3 %copy-done = bf16[2,512,2304]{2,1,0:T(8,128)(2,1)S(1)} copy-done((bf16[2,512,2304]{2,1,0:T(8,128)(2,1)S(1)}, bf16[2,512,2304]{2,1,0:T(8,128)(2,1)}, u32[]{:S(2)}) %copy-start) | copy-done | bytes 4718616
  11.6 0.8 copy-done.31
  12.4 0.8 copy-done.33
  13.1 0.7 copy-done.37
  13.9 0.7 copy-done.48
  14.5 3.4 %local.2 = (bf16[256,1280]{1,0:T(8,128)(2,1)S(1)}, f32[256,16]{1,0:T(8,128)S(1)}, f32[16,256]{1,0:T(8,128)S(1)}, bf16[128,1024]{1,0:T(8,128)(2,1)S(1)}, bf16[16,80,128]{2,1,0:T(8,128)(2,1)S(1)}) custom-call(s32[8]{0:T(128)S(1)} %copy-done.41, bf16[256,512]{1,0:T(8,128)(2,1)S(1)} %get-tuple-element.34.u_ref, ...), custom_call_target="tpu_custom_call" | custom-call | flops 335544320 | bytes 6355328 | tf_op jit(solution)/shard_map/local/pallas_call | solution.py:327
  18.0 14.6 %all_to_all.20.got_ref = bf16[16,80,128]{2,1,0:T(8,128)(2,1)S(1)} all-to-all(bf16[16,80,128]{2,1,0:T(8,128)(2,1)S(1)} %get-tuple-element.36), channel_id=1, replica_groups=mesh['groups'=2,'frames'=16] {'frames'}, dimensions={0} | all-to-all | bytes 655360 | tf_op jit(solution)/shard_map/all_to_all | solution.py:398
  32.6 0.8 scan.2
  33.4 5.1 %all-to-all-start.1 = ((bf16[16,64,128]{2,1,0:T(8,128)(2,1)}), bf16[16,64,128]{2,1,0:T(8,128)(2,1)S(1)}, u32[]{:S(2)}, u32[]{:S(2)}) async-start(bf16[16,64,128]{2,1,0:T(8,128)(2,1)} %scan.2), calls=%async_computation.1 | async-start | bytes 524288 | tf_op jit(solution)/shard_map/all_to_all | solution.py:414
  38.5 2.3 %copy-done.1 = bf16[2,512,2304]{2,1,0:T(8,128)(2,1)S(1)} copy-done((bf16[2,512,2304]{2,1,0:T(8,128)(2,1)S(1)}, bf16[2,512,2304]{2,1,0:T(8,128)(2,1)}, u32[]{:S(2)}) %copy-start.1) | copy-done | bytes 4718616
  40.9 1.5 %mix.2 = (f32[256,1024]{1,0:T(8,128)S(1)}, f32[256,1024]{1,0:T(8,128)S(1)}) custom-call(bf16[256,512]{1,0:T(8,128)(2,1)S(1)} %get-tuple-element.34.u_ref, bf16[2,512,2304]{2,1,0:T(8,128)(2,1)S(1)} %copy-done.1, bf16[256,1280]{1,0:T(8,128)(2,1)S(1)} %get-tuple-element.37.act_ref, f32[256,16]{1,0:T(8,128)S(1)} %get-tuple-element.38.cum_ref, ...), custom_call_target="tpu_custom_call" | custom-call | flops 268435456 | bytes 8028288 | tf_op jit(solution)/shard_map/mix/pallas_call | solution.py:327
  42.4 1.0 copy-done.23
  43.4 1.0 copy-done.25
  44.4 2.0 %all-to-all-done.1 = bf16[16,64,128]{2,1,0:T(8,128)(2,1)S(1)} async-done(((bf16[16,64,128]{2,1,0:T(8,128)(2,1)}), bf16[16,64,128]{2,1,0:T(8,128)(2,1)S(1)}, u32[]{:S(2)}, u32[]{:S(2)}) %all-to-all-start.1) | async-done | bytes 262176 | tf_op jit(solution)/shard_map/all_to_all | solution.py:414
  46.4 1.6 %copy-done.6 = bf16[2,1024,512]{2,1,0:T(8,128)(2,1)S(1)} copy-done((bf16[2,1024,512]{2,1,0:T(8,128)(2,1)S(1)}, bf16[2,1024,512]{2,1,0:T(8,128)(2,1)}, u32[]{:S(2)}) %copy-start.6) | copy-done | bytes 2097176
  48.0 1.1 copy-done.16
  49.1 1.2 copy-done.24
  50.3 1.2 copy-done.26
  51.6 0.7 copy-done.39
  52.3 0.7 copy-done.42
  52.9 2.4 %finish.2 = (f32[256,512]{1,0:T(8,128)S(1)}, bf16[256,512]{1,0:T(8,128)(2,1)}) custom-call(s32[8]{0:T(128)S(1)} %copy-done.42, bf16[1024,128]{1,0:T(8,128)(2,1)S(1)} %bitcast.12, bf16[256,1280]{1,0:T(8,128)(2,1)S(1)} %copy-done.16, f32[256,1024]{1,0:T(8,128)S(1)} %copy-done.24, f32[256,1024]{1,0:T(8,128)S(1)} %copy-done.26, bf16[256,512]{1,0:T(8,128)(2,1)S(1)} %bitcast.10, ...), custom_call_target="tpu_custom_call" | custom-call | bytes 6578176 | tf_op jit(solution)/shard_map/finish/pallas_call | solution.py:327
  55.4 0.8 copy-done.29
  56.2 2.8 %collective-permute-start.1 = (bf16[256,512]{1,0:T(8,128)(2,1)}, bf16[256,512]{1,0:T(8,128)(2,1)S(1)}, u32[]{:S(2)}, u32[]{:S(2)}) collective-permute-start(bf16[256,512]{1,0:T(8,128)(2,1)} %get-tuple-element.43.a_ref), channel_id=1, source_target_pairs={{0,1},{1,2},{2,3},{3,4},{4,5},{5,6},{6,7},{7,8},{8,9},{9,10},{10,1... | collective-permute-start | bytes 786440 | tf_op jit(solution)/shard_map/ppermute | solution.py:345
  59.0 1.2 copy-done.8
  60.3 0.7 copy-done.52
  60.9 1.7 %memory.2 = (bf16[256,512]{1,0:T(8,128)(2,1)S(1)}, bf16[256,1024]{1,0:T(8,128)(2,1)S(1)}, f32[256,512]{1,0:T(8,128)S(1)}) custom-call(s32[1]{0:T(128)} %bitcast.base_ref, s32[8]{0:T(128)S(1)} %copy-done.52, bf16[256,512]{1,0:T(8,128)(2,1)} %get-tuple-element.43.a_ref, bf16[2,512,512]{2,1,0:T(8,128)(2,1)S(1)} %copy-done.8, bf16[2,512,1024]{2,1,0:T(8,128)(2,1)S(1)} %copy-done.3), custom_call_target="tpu_custom_call" | custom-call | flops 402653184 | bytes 4718592 | tf_op jit(solution)/shard_map/memory/pallas_call | solution.py:327
  62.6 2.3 %collective-permute-done.1.prev_ref = bf16[256,512]{1,0:T(8,128)(2,1)S(1)} collective-permute-done((bf16[256,512]{1,0:T(8,128)(2,1)}, bf16[256,512]{1,0:T(8,128)(2,1)S(1)}, u32[]{:S(2)}, u32[]{:S(2)}) %collective-permute-start.1) | collective-permute-done | bytes 262176 | tf_op jit(solution)/shard_map/ppermute | solution.py:345
  64.9 1.2 copy-done.10
  66.2 1.0 copy-done.30
  67.2 0.7 copy-done.43
  67.9 2.9 %attend.2 = (f32[256,512]{1,0:T(8,128)S(1)}, bf16[256,512]{1,0:T(8,128)(2,1)S(1)}, bf16[16,512]{1,0:T(8,128)(2,1)S(1)}) custom-call(s32[8]{0:T(128)S(1)} %copy-done.43, bf16[256,512]{1,0:T(8,128)(2,1)S(1)} %get-tuple-element.44.q_ref, bf16[256,1024]{1,0:T(8,128)(2,1)S(1)} %get-tuple-element.45.kv_ref, f32[256,512]{1,0:T(8,128)S(1)} %get-tuple-element.46.bias_ref, ...), custom_call_target="tpu_custom_call" | custom-call | bytes 6455296 | tf_op jit(solution)/shard_map/attend/pallas_call | solution.py:327
  70.8 0.8 copy-done.27
  71.6 1.9 %collective-permute-start.2 = (bf16[16,512]{1,0:T(8,128)(2,1)S(1)}, bf16[16,512]{1,0:T(8,128)(2,1)S(1)}, u32[]{:S(2)}, u32[]{:S(2)}) collective-permute-start(bf16[16,512]{1,0:T(8,128)(2,1)S(1)} %get-tuple-element.49), channel_id=1, source_target_pairs={{0,1},{1,2},{2,3},{3,4},{4,5},{5,6},{6,7},{7,8},{8,9},{9,10},{10,1... | collective-permute-start | bytes 49160 | tf_op jit(solution)/shard_map/ppermute | solution.py:345
  73.5 4.0 %collective-permute-done.2.tail_ref = bf16[16,512]{1,0:T(8,128)(2,1)S(1)} collective-permute-done((bf16[16,512]{1,0:T(8,128)(2,1)S(1)}, bf16[16,512]{1,0:T(8,128)(2,1)S(1)}, u32[]{:S(2)}, u32[]{:S(2)}) %collective-permute-start.2) | collective-permute-done | bytes 16416 | tf_op jit(solution)/shard_map/ppermute | solution.py:345
  77.6 3.4 %local.3 = (bf16[256,1280]{1,0:T(8,128)(2,1)S(1)}, f32[256,16]{1,0:T(8,128)S(1)}, f32[16,256]{1,0:T(8,128)S(1)}, bf16[128,1024]{1,0:T(8,128)(2,1)S(1)}, bf16[16,80,128]{2,1,0:T(8,128)(2,1)S(1)}) custom-call(s32[8]{0:T(128)S(1)} %copy-done.43, bf16[256,512]{1,0:T(8,128)(2,1)S(1)} %get-tuple-element.48.u_ref, ...), custom_call_target="tpu_custom_call" | custom-call | flops 335544320 | bytes 6355328 | tf_op jit(solution)/shard_map/local/pallas_call | solution.py:327
  81.0 0.8 copy-done.12
  81.9 13.8 %all_to_all.21.got_ref = bf16[16,80,128]{2,1,0:T(8,128)(2,1)S(1)} all-to-all(bf16[16,80,128]{2,1,0:T(8,128)(2,1)S(1)} %get-tuple-element.50), channel_id=1, replica_groups=mesh['groups'=2,'frames'=16] {'frames'}, dimensions={0} | all-to-all | bytes 655360 | tf_op jit(solution)/shard_map/all_to_all | solution.py:398
  95.7 0.8 scan.3
  96.5 5.1 %all-to-all-start.3 = ((bf16[16,64,128]{2,1,0:T(8,128)(2,1)}), bf16[16,64,128]{2,1,0:T(8,128)(2,1)S(1)}, u32[]{:S(2)}, u32[]{:S(2)}) async-start(bf16[16,64,128]{2,1,0:T(8,128)(2,1)} %scan.3), calls=%async_computation.3 | async-start | bytes 524288 | tf_op jit(solution)/shard_map/all_to_all | solution.py:414
  101.6 2.3 %copy-done.2 = bf16[2,512,2304]{2,1,0:T(8,128)(2,1)S(1)} copy-done((bf16[2,512,2304]{2,1,0:T(8,128)(2,1)S(1)}, bf16[2,512,2304]{2,1,0:T(8,128)(2,1)}, u32[]{:S(2)}) %copy-start.2) | copy-done | bytes 4718616
  103.9 1.1 copy-done.13
  105.0 0.9 copy-done.36
  105.9 0.7 copy-done.47
  106.6 0.7 copy-done.51
  107.3 1.6 %mix.3 = (f32[256,1024]{1,0:T(8,128)S(1)}, f32[256,1024]{1,0:T(8,128)S(1)}) custom-call(bf16[256,512]{1,0:T(8,128)(2,1)S(1)} %get-tuple-element.48.u_ref, bf16[2,512,2304]{2,1,0:T(8,128)(2,1)S(1)} %copy-done.2, bf16[256,1280]{1,0:T(8,128)(2,1)S(1)} %copy-done.13, f32[256,16]{1,0:T(8,128)S(1)} %copy-done.36, f32[16,256]{1,0:T(8,128)S(1)} %copy-done.47, ...), custom_call_target="tpu_custom_call" | custom-call | flops 268435456 | bytes 8028288 | tf_op jit(solution)/shard_map/mix/pallas_call | solution.py:327
  108.9 1.0 copy-done.19
  109.9 1.0 copy-done.21
  110.9 1.6 %copy-done.7 = bf16[2,1024,512]{2,1,0:T(8,128)(2,1)S(1)} copy-done((bf16[2,1024,512]{2,1,0:T(8,128)(2,1)S(1)}, bf16[2,1024,512]{2,1,0:T(8,128)(2,1)}, u32[]{:S(2)}) %copy-start.7) | copy-done | bytes 2097176
  112.5 1.1 copy-done.14
  113.6 1.2 copy-done.20
  114.8 1.2 copy-done.22
  116.1 1.0 copy-done.28
  117.1 0.7 copy-done.40
  118.5 1.7 %finish.3 = (f32[256,512]{1,0:T(8,128)S(1)}, bf16[256,512]{1,0:T(8,128)(2,1)S(1)}) custom-call(s32[8]{0:T(128)S(1)} %copy-done.44, bf16[1024,128]{1,0:T(8,128)(2,1)S(1)} %bitcast.11, bf16[256,1280]{1,0:T(8,128)(2,1)S(1)} %copy-done.14, f32[256,1024]{1,0:T(8,128)S(1)} %copy-done.20, f32[256,1024]{1,0:T(8,128)S(1)} %copy-done.22, f32[256,512]{1,0:T(8,128)S(1)} %copy-done.28, ...), custom_call_target="tpu_custom_call" | custom-call | bytes 6840320 | tf_op jit(solution)/shard_map/finish/pallas_call | solution.py:327
  120.2 2.2 %collective-permute-start.3 = (bf16[256,512]{1,0:T(8,128)(2,1)S(1)}, bf16[256,512]{1,0:T(8,128)(2,1)S(1)}, u32[]{:S(2)}, u32[]{:S(2)}) collective-permute-start(bf16[256,512]{1,0:T(8,128)(2,1)S(1)} %get-tuple-element.58.a_ref), channel_id=1, source_target_pairs={{0,1},{1,2},{2,3},{3,4},{4,5},{5,6},{6,7},{7,8},{8,9},{9,10},{10,1... | collective-permute-start | bytes 786440 | tf_op jit(solution)/shard_map/ppermute | solution.py:345
  122.4 1.1 memory.3
  123.6 5.4 %collective-permute-done.3.prev_ref = bf16[256,512]{1,0:T(8,128)(2,1)S(1)} collective-permute-done((bf16[256,512]{1,0:T(8,128)(2,1)S(1)}, bf16[256,512]{1,0:T(8,128)(2,1)S(1)}, u32[]{:S(2)}, u32[]{:S(2)}) %collective-permute-start.3) | collective-permute-done | bytes 262176 | tf_op jit(solution)/shard_map/ppermute | solution.py:345
  128.9 3.6 %attend.3 = f32[256,512]{1,0:T(8,128)} custom-call(s32[8]{0:T(128)S(1)} %copy-done.45, bf16[256,512]{1,0:T(8,128)(2,1)S(1)} %get-tuple-element.59.q_ref, bf16[256,1024]{1,0:T(8,128)(2,1)S(1)} %get-tuple-element.60.kv_ref, f32[256,512]{1,0:T(8,128)S(1)} %get-tuple-element.61.bias_ref, bf16[256,512]{1,0:T(8,128)(2,1)S(1)} %collective-permute-done.3.prev_ref, ...), custom_call_target="tpu_custom_call" | custom-call | bytes 6176768 | tf_op jit(solution)/shard_map/attend/pallas_call | solution.py:327
  (76 shorter events, 0.8 us)
Async XLA Ops:
  0.0 1.0 copy-start.4
  1.0 0.9 copy-start.17
  2.0 0.7 copy-start.41
  3.3 6.0 %collective-permute-start = (bf16[16,512]{1,0:T(8,128)(2,1)S(1)}, bf16[16,512]{1,0:T(8,128)(2,1)S(1)}, u32[]{:S(2)}, u32[]{:S(2)}) collective-permute-start(bf16[16,512]{1,0:T(8,128)(2,1)S(1)} %get-tuple-element.35), channel_id=1, source_target_pairs={{0,1},{1,2},{2,3},{3,4},{4,5},{5,6},{6,7},{7,8},{8,9},{9,10},{10,1... | collective-permute-start | bytes 49160 | tf_op jit(solution)/shard_map/ppermute | solution.py:345
  9.3 2.3 %copy-start = (bf16[2,512,2304]{2,1,0:T(8,128)(2,1)S(1)}, bf16[2,512,2304]{2,1,0:T(8,128)(2,1)}, u32[]{:S(2)}) copy-start(bf16[2,512,2304]{2,1,0:T(8,128)(2,1)} %w_ref.10) | copy-start | bytes 14155780
  11.6 0.8 copy-start.31
  12.4 0.8 copy-start.33
  13.1 0.7 copy-start.37
  13.9 0.7 copy-start.48
  14.5 24.0 %copy-start.50 = (f32[2,16]{1,0:T(2,128)S(1)}, f32[2,16]{1,0:T(2,128)}, u32[]{:S(2)}) copy-start(f32[2,16]{1,0:T(2,128)} %skip_ref.3) | copy-start | bytes 388
  18.0 24.4 %copy-start.15 = (bf16[256,1280]{1,0:T(8,128)(2,1)}, bf16[256,1280]{1,0:T(8,128)(2,1)S(1)}, u32[]{:S(2)}) copy-start(bf16[256,1280]{1,0:T(8,128)(2,1)S(1)} %get-tuple-element.37.act_ref) | copy-start | bytes 1966084
  33.4 13.0 %all-to-all-start.1 = ((bf16[16,64,128]{2,1,0:T(8,128)(2,1)}), bf16[16,64,128]{2,1,0:T(8,128)(2,1)S(1)}, u32[]{:S(2)}, u32[]{:S(2)}) async-start(bf16[16,64,128]{2,1,0:T(8,128)(2,1)} %scan.2), calls=%async_computation.1 | async-start | bytes 524288 | tf_op jit(solution)/shard_map/all_to_all | solution.py:414
  38.5 2.3 %copy-start.1 = (bf16[2,512,2304]{2,1,0:T(8,128)(2,1)S(1)}, bf16[2,512,2304]{2,1,0:T(8,128)(2,1)}, u32[]{:S(2)}) copy-start(bf16[2,512,2304]{2,1,0:T(8,128)(2,1)} %w_ref.10) | copy-start | bytes 14155780
  40.9 5.6 %copy-start.5 = (bf16[2,50,4,512]{3,2,1,0:T(4,128)(2,1)S(1)}, bf16[2,50,4,512]{3,2,1,0:T(4,128)(2,1)}, u32[]{:S(2)}) copy-start(bf16[2,50,4,512]{3,2,1,0:T(4,128)(2,1)} %mods_ref.9) | copy-start | bytes 1228804
  40.9 5.6 %copy-start.18 = (bf16[8,32,512]{2,1,0:T(8,128)(2,1)S(1)}, bf16[8,32,512]{2,1,0:T(8,128)(2,1)}, u32[]{:S(2)}) copy-start(bf16[8,32,512]{2,1,0:T(8,128)(2,1)} %param.15) | copy-start | bytes 786436
  42.4 1.0 copy-start.23
  43.4 1.0 copy-start.25
  46.4 1.6 %copy-start.6 = (bf16[2,1024,512]{2,1,0:T(8,128)(2,1)S(1)}, bf16[2,1024,512]{2,1,0:T(8,128)(2,1)}, u32[]{:S(2)}) copy-start(bf16[2,1024,512]{2,1,0:T(8,128)(2,1)} %w_ref.11) | copy-start | bytes 6291460
  48.0 1.1 copy-start.16
  49.1 1.2 copy-start.24
  50.3 1.2 copy-start.26
  51.6 0.7 copy-start.39
  52.3 0.7 copy-start.42
  52.9 6.1 %copy-start.3 = (bf16[2,512,1024]{2,1,0:T(8,128)(2,1)S(1)}, bf16[2,512,1024]{2,1,0:T(8,128)(2,1)}, u32[]{:S(2)}) copy-start(bf16[2,512,1024]{2,1,0:T(8,128)(2,1)} %wm_ref.7) | copy-start | bytes 6291460
  52.9 24.6 %slice-start = ((s8[4718592]{0:T(1024)(128)(4,1)}), s8[524288]{0:T(1024)(128)(4,1)S(1)}, s32[]{:S(2)}) async-start(s8[4718592]{0:T(1024)(128)(4,1)} %bitcast.7), calls=%async_computation.4 | async-start | bytes 1048576
  55.4 0.8 copy-start.29
  56.2 8.8 %collective-permute-start.1 = (bf16[256,512]{1,0:T(8,128)(2,1)}, bf16[256,512]{1,0:T(8,128)(2,1)S(1)}, u32[]{:S(2)}, u32[]{:S(2)}) collective-permute-start(bf16[256,512]{1,0:T(8,128)(2,1)} %get-tuple-element.43.a_ref), channel_id=1, source_target_pairs={{0,1},{1,2},{2,3},{3,4},{4,5},{5,6},{6,7},{7,8},{8,9},{9,10},{10,1... | collective-permute-start | bytes 786440 | tf_op jit(solution)/shard_map/ppermute | solution.py:345
  59.0 1.2 copy-start.8
  60.3 0.7 copy-start.52
  60.9 16.6 %slice-start.1 = ((s8[4718592]{0:T(1024)(128)(4,1)}), s8[4194304]{0:T(1024)(128)(4,1)S(1)}, s32[]{:S(2)}) async-start(s8[4718592]{0:T(1024)(128)(4,1)} %bitcast.7), calls=%async_computation.5 | async-start | bytes 8388608
  64.9 1.2 copy-start.10
  66.2 1.0 copy-start.30
  67.2 0.7 copy-start.43
  67.9 9.7 %copy-start.32 = (f32[2,4,1280]{2,1,0:T(4,128)S(1)}, f32[2,4,1280]{2,1,0:T(4,128)}, u32[]{:S(2)}) copy-start(f32[2,4,1280]{2,1,0:T(4,128)} %conv_ref.3) | copy-start | bytes 122884
  67.9 9.7 %copy-start.34 = (bf16[2,512,16]{1,2,0:T(8,128)(2,1)S(1)}, bf16[2,512,16]{1,2,0:T(8,128)(2,1)}, u32[]{:S(2)}) copy-start(bf16[2,512,16]{1,2,0:T(8,128)(2,1)} %param.20) | copy-start | bytes 98308
  67.9 9.7 %copy-start.38 = (f32[2,50,16]{1,2,0:T(8,128)S(1)}, f32[2,50,16]{1,2,0:T(8,128)}, u32[]{:S(2)}) copy-start(f32[2,50,16]{1,2,0:T(8,128)} %param.22) | copy-start | bytes 19204
  67.9 9.7 %copy-start.49 = (f32[2,16]{1,0:T(2,128)S(1)}, f32[2,16]{1,0:T(2,128)}, u32[]{:S(2)}) copy-start(f32[2,16]{1,0:T(2,128)} %decay_ref.3) | copy-start | bytes 388
  70.8 0.8 copy-start.27
  71.6 5.9 %collective-permute-start.2 = (bf16[16,512]{1,0:T(8,128)(2,1)S(1)}, bf16[16,512]{1,0:T(8,128)(2,1)S(1)}, u32[]{:S(2)}, u32[]{:S(2)}) collective-permute-start(bf16[16,512]{1,0:T(8,128)(2,1)S(1)} %get-tuple-element.49), channel_id=1, source_target_pairs={{0,1},{1,2},{2,3},{3,4},{4,5},{5,6},{6,7},{7,8},{8,9},{9,10},{10,1... | collective-permute-start | bytes 49160 | tf_op jit(solution)/shard_map/ppermute | solution.py:345
  81.0 0.8 copy-start.12
  81.9 13.8 %copy-start.35 = (f32[256,16]{1,0:T(8,128)}, f32[256,16]{1,0:T(8,128)S(1)}, u32[]{:S(2)}) copy-start(f32[256,16]{1,0:T(8,128)S(1)} %get-tuple-element.52.cum_ref) | copy-start | bytes 49156
  81.9 13.8 %copy-start.46 = (f32[16,256]{1,0:T(8,128)}, f32[16,256]{1,0:T(8,128)S(1)}, u32[]{:S(2)}) copy-start(f32[16,256]{1,0:T(8,128)S(1)} %get-tuple-element.53.shifted_ref) | copy-start | bytes 49156
  96.5 14.4 %all-to-all-start.3 = ((bf16[16,64,128]{2,1,0:T(8,128)(2,1)}), bf16[16,64,128]{2,1,0:T(8,128)(2,1)S(1)}, u32[]{:S(2)}, u32[]{:S(2)}) async-start(bf16[16,64,128]{2,1,0:T(8,128)(2,1)} %scan.3), calls=%async_computation.3 | async-start | bytes 524288 | tf_op jit(solution)/shard_map/all_to_all | solution.py:414
  101.6 2.3 %copy-start.2 = (bf16[2,512,2304]{2,1,0:T(8,128)(2,1)S(1)}, bf16[2,512,2304]{2,1,0:T(8,128)(2,1)}, u32[]{:S(2)}) copy-start(bf16[2,512,2304]{2,1,0:T(8,128)(2,1)} %w_ref.10) | copy-start | bytes 14155780
  103.9 1.1 copy-start.13
  105.0 0.9 copy-start.36
  105.9 0.7 copy-start.47
  106.6 0.7 copy-start.51
  108.9 1.0 copy-start.19
  109.9 1.0 copy-start.21
  110.9 1.6 %copy-start.7 = (bf16[2,1024,512]{2,1,0:T(8,128)(2,1)S(1)}, bf16[2,1024,512]{2,1,0:T(8,128)(2,1)}, u32[]{:S(2)}) copy-start(bf16[2,1024,512]{2,1,0:T(8,128)(2,1)} %w_ref.11) | copy-start | bytes 6291460
  112.5 1.1 copy-start.14
  113.6 1.2 copy-start.20
  114.8 1.2 copy-start.22
  116.1 1.0 copy-start.28
  117.1 0.7 copy-start.40
  117.8 0.7 copy-start.44
  118.5 4.0 %copy-start.9 = (bf16[2,512,512]{2,1,0:T(8,128)(2,1)S(1)}, bf16[2,512,512]{2,1,0:T(8,128)(2,1)}, u32[]{:S(2)}) copy-start(bf16[2,512,512]{2,1,0:T(8,128)(2,1)} %wq_ref.3) | copy-start | bytes 3145732
  118.5 4.0 %copy-start.53 = (s32[8]{0:T(128)S(1)}, s32[8]{0:T(128)}, u32[]{:S(2)}) copy-start(s32[8]{0:T(128)} %reach_ref.3) | copy-start | bytes 100
  120.2 8.7 %copy-start.11 = (bf16[2,512,512]{2,1,0:T(8,128)(2,1)S(1)}, bf16[2,512,512]{2,1,0:T(8,128)(2,1)}, u32[]{:S(2)}) copy-start(bf16[2,512,512]{2,1,0:T(8,128)(2,1)} %merge_ref.3) | copy-start | bytes 3145732
  120.2 8.7 %copy-start.45 = (s32[8]{0:T(128)S(1)}, s32[8]{0:T(128)}, u32[]{:S(2)}) copy-start(s32[8]{0:T(128)} %step_ref.13) | copy-start | bytes 100
  120.2 8.7 %collective-permute-start.3 = (bf16[256,512]{1,0:T(8,128)(2,1)S(1)}, bf16[256,512]{1,0:T(8,128)(2,1)S(1)}, u32[]{:S(2)}, u32[]{:S(2)}) collective-permute-start(bf16[256,512]{1,0:T(8,128)(2,1)S(1)} %get-tuple-element.58.a_ref), channel_id=1, source_target_pairs={{0,1},{1,2},{2,3},{3,4},{4,5},{5,6},{6,7},{7,8},{8,9},{9,10},{10,1... | collective-permute-start | bytes 786440 | tf_op jit(solution)/shard_map/ppermute | solution.py:345

commit v3 on v2

--- a/solution.py
+++ b/solution.py
@@ -395,7 +395,6 @@
             name="local",
             flops=2 * rows * width * (INNER + 2 * STATE),
         )
-        got = lax.all_to_all(send, "frames", 0, 0)
         y, wide = run(
             functools.partial(mix_kernel, layer),
             (),
@@ -404,6 +403,8 @@
             name="mix",
             flops=2 * rows * width * INNER,
         )
+        send, y, wide, act = lax.optimization_barrier((send, y, wide, act))
+        got = lax.all_to_all(send, "frames", 0, 0)
         (back,) = run(
             scan_kernel,
             (),

time: 134 us -> 116 us (0.87)
  local copies, waits for them, and re-layouts: 41.2 us -> 11.1 us
  blocking collectives: 28.5 us -> 53.9 us
  starting transfers between devices: 19 us -> 9.32 us
  waiting for transfers between devices: 17.8 us -> 15.4 us
    unnamed x112 -> x64, local copies, waits for them, and re-layouts: 41.2 us -> 11.1 us
    all_to_all x0 -> x2, blocking collectives: none -> 25.7 us  [shards(): enter = lax.all_to_all(back, 'frames', 0, 0).reshape(INNER, LANES)]
    all_to_all x2 -> x0, starting transfers between devices: 10.2 us -> none  [shards(): enter = lax.all_to_all(back, 'frames', 0, 0).reshape(INNER, LANES)]
    all_to_all x2 -> x0, waiting for transfers between devices: 2.01 us -> none  [shards(): enter = lax.all_to_all(back, 'frames', 0, 0).reshape(INNER, LANES)]
  transfers between devices with their start and end apart: 6 -> 4, of which waited for: 5 -> 4; matrix products, arithmetic and copies ran while one was open for 0% -> 0% of each run, Pallas kernels for 5% -> 2%
where the time goes in v3:
time: 116 us; the launch traced here: 115 us
  blocking collectives  53.9 us (46%)
  Pallas kernels  25 us (22%)
  waiting for transfers between devices  15.4 us (13%)
  local copies, waits for them, and re-layouts  11.1 us (10%)
  starting transfers between devices  9.32 us (8%)
    all_to_all x2, blocking collectives, shards(): got = lax.all_to_all(send, 'frames', 0, 0)  28.2 us
    all_to_all x2, blocking collectives, shards(): enter = lax.all_to_all(back, 'frames', 0, 0).reshape(INNER, LANES)  25.7 us
    pallas_call x13, Pallas kernels, run(): pl.pallas_call(kernel, in_specs=[SCALARS] * len(scalars) + [WHOLE] * len(...  25 us
    ppermute x4, waiting for transfers between devices, from_behind(): return lax.ppermute(value, axis, [(i, i + 1) for i in range(count - 1)])  15.4 us
    unnamed x64, local copies, waits for them, and re-layouts  11.1 us
    ppermute x4, starting transfers between devices, from_behind(): return lax.ppermute(value, axis, [(i, i + 1) for i in range(count - 1)])  9.32 us
  transfers between devices with their start and end apart: 4, of which 4 were waited for; matrix products, arithmetic and copies ran while one was open for 0% of the time, Pallas kernels for 2%

profile of v3, /device:TPU:8, one launch (start us, length us, event | category | flops | bytes accessed | tf_op | source)
XLA Modules:
  0.0 115.1 jit_solution(6699775744179979009)
XLA Ops:
  0.0 1.0 copy-done.3
  1.0 0.9 copy-done.11
  2.0 0.7 copy-done.21
  2.6 0.7 first.1
  3.3 1.9 %collective-permute-start = (bf16[16,512]{1,0:T(8,128)(2,1)S(1)}, bf16[16,512]{1,0:T(8,128)(2,1)S(1)}, u32[]{:S(2)}, u32[]{:S(2)}) collective-permute-start(bf16[16,512]{1,0:T(8,128)(2,1)S(1)} %get-tuple-element.43), channel_id=1, source_target_pairs={{0,1},{1,2},{2,3},{3,4},{4,5},{5,6},{6,7},{7,8},{8,9},{9,10},{10,1... | collective-permute-start | bytes 49160 | tf_op jit(solution)/shard_map/ppermute | solution.py:345
  5.2 4.0 %collective-permute-done.tail_ref = bf16[16,512]{1,0:T(8,128)(2,1)S(1)} collective-permute-done((bf16[16,512]{1,0:T(8,128)(2,1)S(1)}, bf16[16,512]{1,0:T(8,128)(2,1)S(1)}, u32[]{:S(2)}, u32[]{:S(2)}) %collective-permute-start) | collective-permute-done | bytes 16416 | tf_op jit(solution)/shard_map/ppermute | solution.py:345
  9.3 2.3 %copy-done = bf16[2,512,2304]{2,1,0:T(8,128)(2,1)S(1)} copy-done((bf16[2,512,2304]{2,1,0:T(8,128)(2,1)S(1)}, bf16[2,512,2304]{2,1,0:T(8,128)(2,1)}, u32[]{:S(2)}) %copy-start) | copy-done | bytes 4718616
  11.6 0.8 copy-done.13
  12.4 0.8 copy-done.15
  13.1 0.7 copy-done.17
  13.9 0.7 copy-done.24
  14.5 3.4 %local.2 = (bf16[256,1280]{1,0:T(8,128)(2,1)S(1)}, f32[256,16]{1,0:T(8,128)S(1)}, f32[16,256]{1,0:T(8,128)S(1)}, bf16[128,1024]{1,0:T(8,128)(2,1)S(1)}, bf16[16,80,128]{2,1,0:T(8,128)(2,1)S(1)}) custom-call(s32[8]{0:T(128)S(1)} %copy-done.21, bf16[256,512]{1,0:T(8,128)(2,1)S(1)} %get-tuple-element.42.u_ref, ...), custom_call_target="tpu_custom_call" | custom-call | flops 335544320 | bytes 6355328 | tf_op jit(solution)/shard_map/local/pallas_call | solution.py:327
  18.0 0.0 copy-done.1
  18.0 0.0 copy-done.26
  18.0 0.0 copy-start.4
  18.0 0.0 copy-start.5
  18.0 0.0 copy-start.12
  18.1 0.0 copy-start.19
  18.1 0.0 copy-start.22
  18.1 1.7 %mix.2 = (f32[256,1024]{1,0:T(8,128)S(1)}, f32[256,1024]{1,0:T(8,128)S(1)}) custom-call(bf16[256,512]{1,0:T(8,128)(2,1)S(1)} %get-tuple-element.42.u_ref, bf16[2,512,2304]{2,1,0:T(8,128)(2,1)S(1)} %copy-done.1, bf16[256,1280]{1,0:T(8,128)(2,1)S(1)} %get-tuple-element.52.act_ref, f32[256,16]{1,0:T(8,128)S(1)} %get-tuple-element.46.cum_ref, ...), custom_call_target="tpu_custom_call" | custom-call | flops 268435456 | bytes 8028288 | tf_op jit(solution)/shard_map/mix/pallas_call | solution.py:327
  19.8 14.6 %all_to_all.20.got_ref = bf16[16,80,128]{2,1,0:T(8,128)(2,1)S(1)} all-to-all(bf16[16,80,128]{2,1,0:T(8,128)(2,1)S(1)} %get-tuple-element.51), channel_id=1, replica_groups=mesh['groups'=2,'frames'=16] {'frames'}, dimensions={0} | all-to-all | bytes 655360 | tf_op jit(solution)/shard_map/all_to_all | solution.py:407
  34.4 0.1 scan.2
  34.5 12.8 %all_to_all.21 = bf16[16,64,128]{2,1,0:T(8,128)(2,1)S(1)} all-to-all(bf16[16,64,128]{2,1,0:T(8,128)(2,1)S(1)} %scan.2), channel_id=1, replica_groups=mesh['groups'=2,'frames'=16] {'frames'}, dimensions={0} | all-to-all | bytes 524288 | tf_op jit(solution)/shard_map/all_to_all | solution.py:415
  47.3 0.0 copy-done.4
  47.3 0.0 copy-done.5
  47.3 0.0 copy-done.12
  47.3 0.0 copy-done.19
  47.3 0.0 copy-done.22
  47.3 0.0 copy-start.2
  47.4 0.0 slice-start
  47.4 2.5 %finish.2 = (f32[256,512]{1,0:T(8,128)S(1)}, bf16[256,512]{1,0:T(8,128)(2,1)}) custom-call(s32[8]{0:T(128)S(1)} %copy-done.22, bf16[1024,128]{1,0:T(8,128)(2,1)S(1)} %bitcast.12, bf16[256,1280]{1,0:T(8,128)(2,1)S(1)} %get-tuple-element.52.act_ref, f32[256,1024]{1,0:T(8,128)S(1)} %get-tuple-element.53.y_ref, f32[256,1024]{1,0:T(8,128)S(1)} %get-tuple-element.54.wide_ref, ...), custom_call_target="tpu_custom_call" | custom-call | bytes 6578176 | tf_op jit(solution)/shard_map/finish/pallas_call | solution.py:327
  49.8 2.6 %collective-permute-start.1 = (bf16[256,512]{1,0:T(8,128)(2,1)}, bf16[256,512]{1,0:T(8,128)(2,1)}, u32[]{:S(2)}, u32[]{:S(2)}) collective-permute-start(bf16[256,512]{1,0:T(8,128)(2,1)} %get-tuple-element.55.a_ref), channel_id=1, source_target_pairs={{0,1},{1,2},{2,3},{3,4},{4,5},{5,6},{6,7},{7,8},{8,9},{9,10},{10,1... | collective-permute-start | bytes 786440 | tf_op jit(solution)/shard_map/ppermute | solution.py:345
  52.4 0.0 copy-start.23
  52.4 0.0 copy-done.2
  52.4 0.0 copy-start.7
  52.5 1.2 %copy-done.7 = bf16[2,512,512]{2,1,0:T(8,128)(2,1)S(1)} copy-done((bf16[2,512,512]{2,1,0:T(8,128)(2,1)S(1)}, bf16[2,512,512]{2,1,0:T(8,128)(2,1)}, u32[]{:S(2)}) %copy-start.7) | copy-done | bytes 1048600
  53.7 0.7 copy-done.28
  54.3 1.7 %memory.2 = (bf16[256,512]{1,0:T(8,128)(2,1)S(1)}, bf16[256,1024]{1,0:T(8,128)(2,1)S(1)}, f32[256,512]{1,0:T(8,128)S(1)}) custom-call(s32[1]{0:T(128)} %bitcast.base_ref, s32[8]{0:T(128)S(1)} %copy-done.28, bf16[256,512]{1,0:T(8,128)(2,1)} %get-tuple-element.55.a_ref, bf16[2,512,512]{2,1,0:T(8,128)(2,1)S(1)} %copy-done.7, bf16[2,512,1024]{2,1,0:T(8,128)(2,1)S(1)} %copy-done.2), custom_call_target="tpu_custom_call" | custom-call | flops 402653184 | bytes 4718592 | tf_op jit(solution)/shard_map/memory/pallas_call | solution.py:327
  56.0 2.7 %collective-permute-done.1.prev_ref = bf16[256,512]{1,0:T(8,128)(2,1)} collective-permute-done((bf16[256,512]{1,0:T(8,128)(2,1)}, bf16[256,512]{1,0:T(8,128)(2,1)}, u32[]{:S(2)}, u32[]{:S(2)}) %collective-permute-start.1) | collective-permute-done | bytes 262176 | tf_op jit(solution)/shard_map/ppermute | solution.py:345
  58.7 0.0 copy-done.23
  58.7 1.2 %copy-done.9 = bf16[2,512,512]{2,1,0:T(8,128)(2,1)S(1)} copy-done((bf16[2,512,512]{2,1,0:T(8,128)(2,1)S(1)}, bf16[2,512,512]{2,1,0:T(8,128)(2,1)}, u32[]{:S(2)}) %copy-start.9) | copy-done | bytes 1048600
  60.0 3.4 %attend.2 = (f32[256,512]{1,0:T(8,128)S(1)}, bf16[256,512]{1,0:T(8,128)(2,1)S(1)}, bf16[16,512]{1,0:T(8,128)(2,1)S(1)}) custom-call(s32[8]{0:T(128)S(1)} %copy-done.23, bf16[256,512]{1,0:T(8,128)(2,1)S(1)} %get-tuple-element.56.q_ref, bf16[256,1024]{1,0:T(8,128)(2,1)S(1)} %get-tuple-element.57.kv_ref, f32[256,512]{1,0:T(8,128)S(1)} %get-tuple-element.58.bias_ref, ...), custom_call_target="tpu_custom_call" | custom-call | bytes 6455296 | tf_op jit(solution)/shard_map/attend/pallas_call | solution.py:327
  63.3 2.1 %collective-permute-start.2 = (bf16[16,512]{1,0:T(8,128)(2,1)S(1)}, bf16[16,512]{1,0:T(8,128)(2,1)S(1)}, u32[]{:S(2)}, u32[]{:S(2)}) collective-permute-start(bf16[16,512]{1,0:T(8,128)(2,1)S(1)} %get-tuple-element.61), channel_id=1, source_target_pairs={{0,1},{1,2},{2,3},{3,4},{4,5},{5,6},{6,7},{7,8},{8,9},{9,10},{10,1... | collective-permute-start | bytes 49160 | tf_op jit(solution)/shard_map/ppermute | solution.py:345
  65.4 3.8 %collective-permute-done.2.tail_ref = bf16[16,512]{1,0:T(8,128)(2,1)S(1)} collective-permute-done((bf16[16,512]{1,0:T(8,128)(2,1)S(1)}, bf16[16,512]{1,0:T(8,128)(2,1)S(1)}, u32[]{:S(2)}, u32[]{:S(2)}) %collective-permute-start.2) | collective-permute-done | bytes 16416 | tf_op jit(solution)/shard_map/ppermute | solution.py:345
  69.3 0.0 slice-done
  69.3 0.0 slice-done.1
  69.3 0.0 copy-done.14
  69.3 0.0 copy-start.27
  69.4 3.4 %local.3 = (bf16[256,1280]{1,0:T(8,128)(2,1)S(1)}, f32[256,16]{1,0:T(8,128)S(1)}, f32[16,256]{1,0:T(8,128)S(1)}, bf16[128,1024]{1,0:T(8,128)(2,1)S(1)}, bf16[16,80,128]{2,1,0:T(8,128)(2,1)S(1)}) custom-call(s32[8]{0:T(128)S(1)} %copy-done.23, bf16[256,512]{1,0:T(8,128)(2,1)S(1)} %get-tuple-element.60.u_ref, ...), custom_call_target="tpu_custom_call" | custom-call | flops 335544320 | bytes 6355328 | tf_op jit(solution)/shard_map/local/pallas_call | solution.py:327
  72.8 0.0 copy-start.6
  72.8 0.0 copy-start.20
  72.8 1.6 %mix.3 = (f32[256,1024]{1,0:T(8,128)S(1)}, f32[256,1024]{1,0:T(8,128)S(1)}) custom-call(bf16[256,512]{1,0:T(8,128)(2,1)S(1)} %get-tuple-element.60.u_ref, bf16[2,512,2304]{2,1,0:T(8,128)(2,1)S(1)} %bitcast.8, bf16[256,1280]{1,0:T(8,128)(2,1)S(1)} %get-tuple-element.70.act_ref, f32[256,16]{1,0:T(8,128)S(1)} %get-tuple-element.64.cum_ref, ...), custom_call_target="tpu_custom_call" | custom-call | flops 268435456 | bytes 8028288 | tf_op jit(solution)/shard_map/mix/pallas_call | solution.py:327
  74.5 13.6 %all_to_all.22.got_ref = bf16[16,80,128]{2,1,0:T(8,128)(2,1)S(1)} all-to-all(bf16[16,80,128]{2,1,0:T(8,128)(2,1)S(1)} %get-tuple-element.69), channel_id=1, replica_groups=mesh['groups'=2,'frames'=16] {'frames'}, dimensions={0} | all-to-all | bytes 655360 | tf_op jit(solution)/shard_map/all_to_all | solution.py:407
  88.1 0.1 scan.3
  88.1 12.8 %all_to_all.23 = bf16[16,64,128]{2,1,0:T(8,128)(2,1)S(1)} all-to-all(bf16[16,64,128]{2,1,0:T(8,128)(2,1)S(1)} %scan.3), channel_id=1, replica_groups=mesh['groups'=2,'frames'=16] {'frames'}, dimensions={0} | all-to-all | bytes 524288 | tf_op jit(solution)/shard_map/all_to_all | solution.py:415
  101.0 0.0 copy-done.6
  101.0 1.8 %finish.3 = (f32[256,512]{1,0:T(8,128)S(1)}, bf16[256,512]{1,0:T(8,128)(2,1)S(1)}) custom-call(s32[8]{0:T(128)S(1)} %copy-done.23, bf16[1024,128]{1,0:T(8,128)(2,1)S(1)} %bitcast.11, bf16[256,1280]{1,0:T(8,128)(2,1)S(1)} %get-tuple-element.70.act_ref, f32[256,1024]{1,0:T(8,128)S(1)} %get-tuple-element.71.y_ref, f32[256,1024]{1,0:T(8,128)S(1)} %get-tuple-element.72.wide_ref, ...), custom_call_target="tpu_custom_call" | custom-call | bytes 6840320 | tf_op jit(solution)/shard_map/finish/pallas_call | solution.py:327
  102.7 0.0 copy-start.10
  102.8 2.7 %collective-permute-start.3 = (bf16[256,512]{1,0:T(8,128)(2,1)S(1)}, bf16[256,512]{1,0:T(8,128)(2,1)S(1)}, u32[]{:S(2)}, u32[]{:S(2)}) collective-permute-start(bf16[256,512]{1,0:T(8,128)(2,1)S(1)} %get-tuple-element.74.a_ref), channel_id=1, source_target_pairs={{0,1},{1,2},{2,3},{3,4},{4,5},{5,6},{6,7},{7,8},{8,9},{9,10},{10,1... | collective-permute-start | bytes 786440 | tf_op jit(solution)/shard_map/ppermute | solution.py:345
  105.5 0.0 copy-done.8
  105.5 0.0 copy-done.29
  105.5 1.1 memory.3
  106.6 4.8 %collective-permute-done.3.prev_ref = bf16[256,512]{1,0:T(8,128)(2,1)S(1)} collective-permute-done((bf16[256,512]{1,0:T(8,128)(2,1)S(1)}, bf16[256,512]{1,0:T(8,128)(2,1)S(1)}, u32[]{:S(2)}, u32[]{:S(2)}) %collective-permute-start.3) | collective-permute-done | bytes 262176 | tf_op jit(solution)/shard_map/ppermute | solution.py:345
  111.5 3.6 %attend.3 = f32[256,512]{1,0:T(8,128)} custom-call(s32[8]{0:T(128)S(1)} %copy-done.23, bf16[256,512]{1,0:T(8,128)(2,1)S(1)} %get-tuple-element.75.q_ref, bf16[256,1024]{1,0:T(8,128)(2,1)S(1)} %get-tuple-element.76.kv_ref, f32[256,512]{1,0:T(8,128)S(1)} %get-tuple-element.77.bias_ref, bf16[256,512]{1,0:T(8,128)(2,1)S(1)} %collective-permute-done.3.prev_ref, ...), custom_call_target="tpu_custom_call" | custom-call | bytes 6176768 | tf_op jit(solution)/shard_map/attend/pallas_call | solution.py:327
  (26 shorter events, 0.0 us)
Async XLA Ops:
  0.0 1.0 copy-start.3
  1.0 0.9 copy-start.11
  2.0 0.7 copy-start.21
  3.3 6.0 %collective-permute-start = (bf16[16,512]{1,0:T(8,128)(2,1)S(1)}, bf16[16,512]{1,0:T(8,128)(2,1)S(1)}, u32[]{:S(2)}, u32[]{:S(2)}) collective-permute-start(bf16[16,512]{1,0:T(8,128)(2,1)S(1)} %get-tuple-element.43), channel_id=1, source_target_pairs={{0,1},{1,2},{2,3},{3,4},{4,5},{5,6},{6,7},{7,8},{8,9},{9,10},{10,1... | collective-permute-start | bytes 49160 | tf_op jit(solution)/shard_map/ppermute | solution.py:345
  9.3 2.3 %copy-start = (bf16[2,512,2304]{2,1,0:T(8,128)(2,1)S(1)}, bf16[2,512,2304]{2,1,0:T(8,128)(2,1)}, u32[]{:S(2)}) copy-start(bf16[2,512,2304]{2,1,0:T(8,128)(2,1)} %w_ref.10) | copy-start | bytes 14155780
  11.6 0.8 copy-start.13
  12.4 0.8 copy-start.15
  13.1 0.7 copy-start.17
  13.9 0.7 copy-start.24
  14.5 3.5 %copy-start.1 = (bf16[2,512,2304]{2,1,0:T(8,128)(2,1)S(1)}, bf16[2,512,2304]{2,1,0:T(8,128)(2,1)}, u32[]{:S(2)}) copy-start(bf16[2,512,2304]{2,1,0:T(8,128)(2,1)} %w_ref.10) | copy-start | bytes 14155780
  14.5 3.5 %copy-start.26 = (f32[2,16]{1,0:T(2,128)S(1)}, f32[2,16]{1,0:T(2,128)}, u32[]{:S(2)}) copy-start(f32[2,16]{1,0:T(2,128)} %skip_ref.3) | copy-start | bytes 388
  18.0 29.3 %copy-start.4 = (bf16[2,50,4,512]{3,2,1,0:T(4,128)(2,1)S(1)}, bf16[2,50,4,512]{3,2,1,0:T(4,128)(2,1)}, u32[]{:S(2)}) copy-start(bf16[2,50,4,512]{3,2,1,0:T(4,128)(2,1)} %mods_ref.9) | copy-start | bytes 1228804
  18.0 29.3 %copy-start.5 = (bf16[2,1024,512]{2,1,0:T(8,128)(2,1)S(1)}, bf16[2,1024,512]{2,1,0:T(8,128)(2,1)}, u32[]{:S(2)}) copy-start(bf16[2,1024,512]{2,1,0:T(8,128)(2,1)} %w_ref.11) | copy-start | bytes 6291460
  18.0 29.3 %copy-start.12 = (bf16[8,32,512]{2,1,0:T(8,128)(2,1)S(1)}, bf16[8,32,512]{2,1,0:T(8,128)(2,1)}, u32[]{:S(2)}) copy-start(bf16[8,32,512]{2,1,0:T(8,128)(2,1)} %param.15) | copy-start | bytes 786436
  18.1 29.3 %copy-start.19 = (f32[2,1024]{1,0:T(2,128)S(1)}, f32[2,1024]{1,0:T(2,128)}, u32[]{:S(2)}) copy-start(f32[2,1024]{1,0:T(2,128)} %gain_ref.3) | copy-start | bytes 24580
  18.1 29.3 %copy-start.22 = (s32[8]{0:T(128)S(1)}, s32[8]{0:T(128)}, u32[]{:S(2)}) copy-start(s32[8]{0:T(128)} %step_ref.13) | copy-start | bytes 100
  47.3 5.1 %copy-start.2 = (bf16[2,512,1024]{2,1,0:T(8,128)(2,1)S(1)}, bf16[2,512,1024]{2,1,0:T(8,128)(2,1)}, u32[]{:S(2)}) copy-start(bf16[2,512,1024]{2,1,0:T(8,128)(2,1)} %wm_ref.7) | copy-start | bytes 6291460
  47.4 21.9 %slice-start = ((s8[4718592]{0:T(1024)(128)(4,1)}), s8[524288]{0:T(1024)(128)(4,1)S(1)}, s32[]{:S(2)}) async-start(s8[4718592]{0:T(1024)(128)(4,1)} %bitcast.7), calls=%async_computation.4 | async-start | bytes 1048576
  49.8 8.9 %collective-permute-start.1 = (bf16[256,512]{1,0:T(8,128)(2,1)}, bf16[256,512]{1,0:T(8,128)(2,1)}, u32[]{:S(2)}, u32[]{:S(2)}) collective-permute-start(bf16[256,512]{1,0:T(8,128)(2,1)} %get-tuple-element.55.a_ref), channel_id=1, source_target_pairs={{0,1},{1,2},{2,3},{3,4},{4,5},{5,6},{6,7},{7,8},{8,9},{9,10},{10,1... | collective-permute-start | bytes 786440 | tf_op jit(solution)/shard_map/ppermute | solution.py:345
  52.4 6.3 %copy-start.23 = (s32[8]{0:T(128)S(1)}, s32[8]{0:T(128)}, u32[]{:S(2)}) copy-start(s32[8]{0:T(128)} %step_ref.13) | copy-start | bytes 100
  52.4 1.2 %copy-start.7 = (bf16[2,512,512]{2,1,0:T(8,128)(2,1)S(1)}, bf16[2,512,512]{2,1,0:T(8,128)(2,1)}, u32[]{:S(2)}) copy-start(bf16[2,512,512]{2,1,0:T(8,128)(2,1)} %wq_ref.3) | copy-start | bytes 3145732
  53.7 0.7 copy-start.28
  54.3 15.0 %slice-start.1 = ((s8[4718592]{0:T(1024)(128)(4,1)}), s8[4194304]{0:T(1024)(128)(4,1)S(1)}, s32[]{:S(2)}) async-start(s8[4718592]{0:T(1024)(128)(4,1)} %bitcast.7), calls=%async_computation.5 | async-start | bytes 8388608
  58.7 1.2 %copy-start.9 = (bf16[2,512,512]{2,1,0:T(8,128)(2,1)S(1)}, bf16[2,512,512]{2,1,0:T(8,128)(2,1)}, u32[]{:S(2)}) copy-start(bf16[2,512,512]{2,1,0:T(8,128)(2,1)} %merge_ref.3) | copy-start | bytes 3145732
  60.0 9.3 %copy-start.14 = (f32[2,4,1280]{2,1,0:T(4,128)S(1)}, f32[2,4,1280]{2,1,0:T(4,128)}, u32[]{:S(2)}) copy-start(f32[2,4,1280]{2,1,0:T(4,128)} %conv_ref.3) | copy-start | bytes 122884
  60.0 9.3 %copy-start.16 = (bf16[2,512,16]{1,2,0:T(8,128)(2,1)S(1)}, bf16[2,512,16]{1,2,0:T(8,128)(2,1)}, u32[]{:S(2)}) copy-start(bf16[2,512,16]{1,2,0:T(8,128)(2,1)} %param.20) | copy-start | bytes 98308
  60.0 9.4 %copy-start.18 = (f32[2,50,16]{1,2,0:T(8,128)S(1)}, f32[2,50,16]{1,2,0:T(8,128)}, u32[]{:S(2)}) copy-start(f32[2,50,16]{1,2,0:T(8,128)} %param.22) | copy-start | bytes 19204
  60.0 9.4 %copy-start.25 = (f32[2,16]{1,0:T(2,128)S(1)}, f32[2,16]{1,0:T(2,128)}, u32[]{:S(2)}) copy-start(f32[2,16]{1,0:T(2,128)} %decay_ref.3) | copy-start | bytes 388
  63.3 6.0 %collective-permute-start.2 = (bf16[16,512]{1,0:T(8,128)(2,1)S(1)}, bf16[16,512]{1,0:T(8,128)(2,1)S(1)}, u32[]{:S(2)}, u32[]{:S(2)}) collective-permute-start(bf16[16,512]{1,0:T(8,128)(2,1)S(1)} %get-tuple-element.61), channel_id=1, source_target_pairs={{0,1},{1,2},{2,3},{3,4},{4,5},{5,6},{6,7},{7,8},{8,9},{9,10},{10,1... | collective-permute-start | bytes 49160 | tf_op jit(solution)/shard_map/ppermute | solution.py:345
  69.3 3.5 %copy-start.27 = (f32[2,16]{1,0:T(2,128)S(1)}, f32[2,16]{1,0:T(2,128)}, u32[]{:S(2)}) copy-start(f32[2,16]{1,0:T(2,128)} %skip_ref.3) | copy-start | bytes 388
  72.8 28.2 %copy-start.6 = (bf16[2,1024,512]{2,1,0:T(8,128)(2,1)S(1)}, bf16[2,1024,512]{2,1,0:T(8,128)(2,1)}, u32[]{:S(2)}) copy-start(bf16[2,1024,512]{2,1,0:T(8,128)(2,1)} %w_ref.11) | copy-start | bytes 6291460
  72.8 28.2 %copy-start.20 = (f32[2,1024]{1,0:T(2,128)S(1)}, f32[2,1024]{1,0:T(2,128)}, u32[]{:S(2)}) copy-start(f32[2,1024]{1,0:T(2,128)} %gain_ref.3) | copy-start | bytes 24580
  101.0 4.5 %copy-start.8 = (bf16[2,512,512]{2,1,0:T(8,128)(2,1)S(1)}, bf16[2,512,512]{2,1,0:T(8,128)(2,1)}, u32[]{:S(2)}) copy-start(bf16[2,512,512]{2,1,0:T(8,128)(2,1)} %wq_ref.3) | copy-start | bytes 3145732
  101.0 4.5 %copy-start.29 = (s32[8]{0:T(128)S(1)}, s32[8]{0:T(128)}, u32[]{:S(2)}) copy-start(s32[8]{0:T(128)} %reach_ref.3) | copy-start | bytes 100
  102.7 8.7 %copy-start.10 = (bf16[2,512,512]{2,1,0:T(8,128)(2,1)S(1)}, bf16[2,512,512]{2,1,0:T(8,128)(2,1)}, u32[]{:S(2)}) copy-start(bf16[2,512,512]{2,1,0:T(8,128)(2,1)} %merge_ref.3) | copy-start | bytes 3145732
  102.8 8.7 %collective-permute-start.3 = (bf16[256,512]{1,0:T(8,128)(2,1)S(1)}, bf16[256,512]{1,0:T(8,128)(2,1)S(1)}, u32[]{:S(2)}, u32[]{:S(2)}) collective-permute-start(bf16[256,512]{1,0:T(8,128)(2,1)S(1)} %get-tuple-element.74.a_ref), channel_id=1, source_target_pairs={{0,1},{1,2},{2,3},{3,4},{4,5},{5,6},{6,7},{7,8},{8,9},{9,10},{10,1... | collective-permute-start | bytes 786440 | tf_op jit(solution)/shard_map/ppermute | solution.py:345

commit v4 on v3

--- a/solution.py
+++ b/solution.py
@@ -23,6 +23,7 @@
 LANES = 128
 TAIL = 16
 F32 = jnp.float32
+OPENING = 4 * 10**9
 BF16 = jnp.bfloat16
 
 
@@ -35,35 +36,60 @@
     return (normed * (1.0 + scale) + shift).astype(BF16)
 
 
-def spread(per_head):
+def spread(per_head, sel):
     high = per_head.astype(BF16)
     low = (per_head - high.astype(F32)).astype(BF16)
-    row = lax.broadcasted_iota(jnp.int32, (2 * HEADS, INNER), 0) % HEADS
-    head = lax.broadcasted_iota(jnp.int32, (2 * HEADS, INNER), 1) // HEAD_DIM
-    sel = jnp.where(row == head, 1.0, 0.0).astype(BF16)
     return dot(jnp.concatenate([high, low], axis=1), sel)
 
 
-def spread_row(per_head):
-    return spread(jnp.broadcast_to(per_head, (16, HEADS)))[0:1, :]
-
-
-def mod_rows(mods_ref, layer, step, which):
-    mods = mods_ref[layer, step].astype(F32)
-    return mods[which : which + 1, :], mods[which + 1 : which + 2, :]
-
-
-def first_kernel(step_ref, x_ref, mods_ref, u_ref, tail_ref):
-    rows = x_ref.shape[0]
-    u = rms_mod(x_ref[...].astype(F32), *mod_rows(mods_ref, 0, step_ref[0], 0))
+def spread_row(per_head, sel):
+    return spread(jnp.broadcast_to(per_head, (16, HEADS)), sel)[0:1, :]
+
+
+def select_kernel(sel_ref):
+    row = lax.broadcasted_iota(jnp.int32, sel_ref.shape, 0) % HEADS
+    head = lax.broadcasted_iota(jnp.int32, sel_ref.shape, 1) // HEAD_DIM
+    sel_ref[...] = jnp.where(row == head, 1.0, 0.0).astype(BF16)
+
+
+def first_kernel(
+    step_ref,
+    reach_ref,
+    sel_ref,
+    x_ref,
+    all_mods_ref,
+    all_bias_ref,
+    u_ref,
+    tail_ref,
+    mods_ref,
+    bias_ref,
+    seen_ref,
+):
+    rows, width = u_ref.shape
+    tok_frame = rows // WINDOW
+    step = step_ref[0]
+    for layer in range(LAYERS):
+        mods_ref[layer] = all_mods_ref[layer, step].astype(F32)
+    u = rms_mod(x_ref[...].astype(F32), mods_ref[0, 0:1, :], mods_ref[0, 1:2, :])
     u_ref[...] = u
     tail_ref[...] = u[rows - TAIL :]
+    chosen = lax.broadcasted_iota(jnp.int32, (8, all_bias_ref.shape[-1]), 1) == step
+    chosen = jnp.where(chosen, 1.0, 0.0).astype(F32)
+    for layer in range(LAYERS):
+        bias_ref[layer] = dot(
+            chosen, all_bias_ref[layer], ((1,), (1,)), precision=lax.Precision.HIGHEST
+        )
+    key_frame = lax.broadcasted_iota(jnp.int32, (tok_frame, 2 * rows), 1) // tok_frame
+    first = WINDOW - lax.axis_index("frames") * WINDOW
+    for f in range(WINDOW):
+        low = jnp.maximum(first, f + WINDOW - reach_ref[f])
+        seen = (key_frame >= low) & (key_frame <= f + WINDOW)
+        seen_ref[f * tok_frame : (f + 1) * tok_frame, :] = jnp.where(seen, 0.0, -1e30)
 
 
 def local_kernel(
     layer,
     parts,
-    step_ref,
     u_ref,
     tail_ref,
     w_ref,
@@ -71,6 +97,7 @@
     conv_ref,
     bias_ref,
     decay_ref,
+    sel_ref,
     act_ref,
     cum_ref,
     shifted_ref,
@@ -81,15 +108,8 @@
     rows = u_ref.shape[0]
     u = u_ref[...]
     tail = tail_ref[...]
-    nsteps = bias_ref.shape[-1]
-    chosen = lax.broadcasted_iota(jnp.int32, (8, nsteps), 1) == step_ref[0]
-    bias = dot(
-        jnp.where(chosen, 1.0, 0.0).astype(F32),
-        bias_ref[layer],
-        ((1,), (1,)),
-        precision=lax.Precision.HIGHEST,
-    )[0:1, :]
-    raw = dot(u, sw_ref[layer], ((1,), (1,))) + bias
+    sel = sel_ref[...]
+    raw = dot(u, sw_ref[layer], ((1,), (1,))) + bias_ref[layer, 0:1, :]
     step = jnp.maximum(raw, 0.0) + jnp.log1p(jnp.exp(-jnp.abs(raw)))
     log_decay = -jnp.exp(decay_ref[layer : layer + 1, :]) * step
     log_step = jnp.log(step)
@@ -104,7 +124,7 @@
         cum_ref[r, :] = cum
         shifted_ref[:, r] = (cum - log_step[r]).T
         ends.append(end)
-        edges.append(spread(jnp.exp(end - cum) * step[r]))
+        edges.append(spread(jnp.exp(end - cum) * step[r], sel))
 
     chunk = 256
     for c in [INNER] + list(range(0, INNER, chunk)):
@@ -129,7 +149,7 @@
             state = term
         else:
             state_ref[(b - 1) * STATE : b * STATE, :] = state.astype(BF16)
-            state = spread_row(jnp.exp(ends[b])) * state + term
+            state = spread_row(jnp.exp(ends[b]), sel) * state + term
 
     part_rows = INNER // parts
     held = max(1, part_rows // HEAD_DIM)
@@ -153,7 +173,7 @@
 
 
 def mix_kernel(
-    layer, u_ref, w_ref, act_ref, cum_ref, shifted_ref, state_ref, skip_ref, y_ref, wide_ref
+    layer, u_ref, w_ref, act_ref, cum_ref, shifted_ref, state_ref, skip_ref, sel_ref, y_ref, wide_ref
 ):
     rows = u_ref.shape[0]
     u = u_ref[...]
@@ -163,7 +183,8 @@
     lane = lax.broadcasted_iota(jnp.int32, (SPAN, LANES), 1)
     left = lane < HEAD_DIM
     zero = jnp.zeros((SPAN, LANES), BF16)
-    skip = spread_row(skip_ref[layer : layer + 1, :])
+    sel = sel_ref[...]
+    skip = spread_row(skip_ref[layer : layer + 1, :], sel)
     before = jnp.zeros((1, HEADS), F32)
     for b in range(rows // SPAN):
         r = slice(b * SPAN, (b + 1) * SPAN)
@@ -171,10 +192,10 @@
         in_map = act_ref[r, INNER : INNER + STATE]
         out_map = act_ref[r, INNER + STATE :]
         affinity = dot(out_map, in_map, ((1,), (1,)))
-        wide_ref[r, :] = spread(jnp.exp(cum + before))
+        wide_ref[r, :] = spread(jnp.exp(cum + before), sel)
         before = before + cum[SPAN - 1 : SPAN, :]
         if b:
-            y_ref[r, :] = dot(out_map, state_ref[(b - 1) * STATE : b * STATE, :]) * spread(jnp.exp(cum))
+            y_ref[r, :] = dot(out_map, state_ref[(b - 1) * STATE : b * STATE, :]) * spread(jnp.exp(cum), sel)
         for pair in range(HEADS // 2):
             cols = slice(pair * LANES, (pair + 1) * LANES)
             values = act_ref[r, cols]
@@ -212,7 +233,6 @@
 
 def finish_kernel(
     layer,
-    step_ref,
     enter_ref,
     act_ref,
     y_ref,
@@ -221,10 +241,9 @@
     w_ref,
     gain_ref,
     mods_ref,
-    hidden_ref,
-    a_ref,
-    normed_ref,
-):
+    *rest,
+):
+    hidden_ref, a_ref, normed_ref = rest[-3:]
     out_map = act_ref[:, INNER + STATE :]
     chunk = 256
     row = lax.broadcasted_iota(jnp.int32, (chunk, chunk), 0) // HEAD_DIM
@@ -242,31 +261,63 @@
         normed_ref[:, cols] = (total * lax.rsqrt(mean + HEAD_EPS) * gain).astype(BF16)
     hidden = resid_ref[...].astype(F32) + dot(normed_ref[...], w_ref[layer])
     hidden_ref[...] = hidden
-    a_ref[...] = rms_mod(hidden, *mod_rows(mods_ref, layer, step_ref[0], 2))
+    a_ref[...] = rms_mod(hidden, mods_ref[layer, 2:3, :], mods_ref[layer, 3:4, :])
+
+
+def partial_attention(q_ref, seen, kv, half, r, k_rows, done):
+    left = lax.broadcasted_iota(jnp.int32, (half, LANES), 1) < HEAD_DIM
+    one = jnp.ones((k_rows.stop - k_rows.start, LANES), BF16)
+    zero = jnp.zeros((half, LANES), BF16)
+    seen = jnp.concatenate([seen, seen], axis=0)
+    together = 2
+    for group in range(0, ATT_HEADS // 2, together):
+        columns = [slice(p * LANES, (p + 1) * LANES) for p in range(group, group + together)]
+        scores = []
+        for cols in columns:
+            query = q_ref[r, cols]
+            sides = jnp.concatenate(
+                [jnp.where(left, query, zero), jnp.where(left, zero, query)], axis=0
+            )
+            scores.append(dot(sides, kv[k_rows, cols], ((1,), (1,))) + seen)
+        tops = [jnp.max(s, axis=-1, keepdims=True) for s in scores]
+        weights = [jnp.exp(s - t).astype(BF16) for s, t in zip(scores, tops)]
+        for cols, weight, top in zip(columns, weights, tops):
+            values = kv[k_rows, ATTN + cols.start : ATTN + cols.stop]
+            both = dot(weight, jnp.concatenate([values, one], axis=1))
+            number = jnp.where(left, both[:half, :LANES], both[half:, :LANES])
+            total = jnp.where(left, both[:half, LANES:], both[half:, LANES:])
+            done(cols, number, total, jnp.where(left, top[:half], top[half:]))
 
 
 def memory_kernel(
-    layer, tok_frame, base_ref, reach_ref, a_ref, wq_ref, wm_ref, q_ref, kv_ref, bias_ref
+    layer, a_ref, wq_ref, wm_ref, seen_ref, q_ref, number_ref, total_ref, top_ref, kv_ref
 ):
     rows = a_ref.shape[0]
+    half = rows // 2
     a = a_ref[...]
     q_ref[...] = (dot(a, wq_ref[layer]).astype(BF16).astype(F32) * HEAD_DIM**-0.5).astype(BF16)
     kv_ref[...] = dot(a, wm_ref[layer]).astype(BF16)
-    key_frame = lax.broadcasted_iota(jnp.int32, (tok_frame, 2 * rows), 1) // tok_frame
-    first = WINDOW - base_ref[0]
-    for f in range(WINDOW):
-        low = jnp.maximum(first, f + WINDOW - reach_ref[f])
-        seen = (key_frame >= low) & (key_frame <= f + WINDOW)
-        bias_ref[f * tok_frame : (f + 1) * tok_frame, :] = jnp.where(seen, 0.0, -1e30)
+    for part in range(2):
+        r = slice(part * half, (part + 1) * half)
+        k_rows = slice(0, (part + 1) * half)
+
+        def done(cols, number, total, top):
+            number_ref[r, cols] = number
+            total_ref[r, cols] = total
+            top_ref[r, cols] = top
+
+        seen = seen_ref[r, rows : rows + k_rows.stop]
+        partial_attention(q_ref, seen, kv_ref, half, r, k_rows, done)
 
 
 def attend_kernel(
     layer,
     last,
-    step_ref,
     q_ref,
-    kv_ref,
-    bias_ref,
+    number_ref,
+    total_ref,
+    top_ref,
+    seen_ref,
     prev_ref,
     wm_ref,
     merge_ref,
@@ -275,54 +326,38 @@
     *rest,
 ):
     if last:
-        resid_ref, keyed_ref, out_ref = rest
+        resid_ref, kv_ref, out_ref = rest
     else:
-        resid_ref, u_ref, tail_ref, keyed_ref, out_ref = rest
+        resid_ref, u_ref, tail_ref, kv_ref, out_ref = rest
     rows = q_ref.shape[0]
-    keyed_ref[0:rows, :] = dot(prev_ref[...], wm_ref[layer]).astype(BF16)
-    keyed_ref[rows:, :] = kv_ref[...]
     half = rows // 2
-    span = rows + half
-    left = lax.broadcasted_iota(jnp.int32, (half, LANES), 1) < HEAD_DIM
-    one = jnp.ones((span, LANES), BF16)
-    zero = jnp.zeros((half, LANES), BF16)
-    together = 2
+    kv_ref[...] = dot(prev_ref[...], wm_ref[layer]).astype(BF16)
     for part in range(2):
         r = slice(part * half, (part + 1) * half)
-        k_rows = slice(part * half, part * half + span)
-        bias = bias_ref[r, k_rows]
-        bias = jnp.concatenate([bias, bias], axis=0)
-        for group in range(0, ATT_HEADS // 2, together):
-            pairs = range(group, group + together)
-            scores = []
-            for pair in pairs:
-                cols = slice(pair * LANES, (pair + 1) * LANES)
-                query = q_ref[r, cols]
-                sides = jnp.concatenate(
-                    [jnp.where(left, query, zero), jnp.where(left, zero, query)], axis=0
-                )
-                scores.append(dot(sides, keyed_ref[k_rows, cols], ((1,), (1,))) + bias)
-            tops = [jnp.max(s, axis=-1, keepdims=True) for s in scores]
-            weights = [jnp.exp(s - t).astype(BF16) for s, t in zip(scores, tops)]
-            for pair, weight in zip(pairs, weights):
-                values = keyed_ref[k_rows, ATTN + pair * LANES : ATTN + (pair + 1) * LANES]
-                both = dot(weight, jnp.concatenate([values, one], axis=1))
-                number = jnp.where(left, both[:half, :LANES], both[half:, :LANES])
-                total = jnp.where(left, both[:half, LANES:], both[half:, LANES:])
-                out_ref[r, pair * LANES : (pair + 1) * LANES] = (number / total).astype(BF16)
+        k_rows = slice(part * half, rows)
+
+        def done(cols, number, total, top):
+            top_own = top_ref[r, cols]
+            highest = jnp.maximum(top, top_own)
+            mine, own = jnp.exp(top - highest), jnp.exp(top_own - highest)
+            number = number * mine + number_ref[r, cols] * own
+            total = total * mine + total_ref[r, cols] * own
+            out_ref[r, cols] = (number / total).astype(BF16)
+
+        partial_attention(q_ref, seen_ref[r, k_rows], kv_ref, half, r, k_rows, done)
     resid = hidden_ref[...] + dot(out_ref[...], merge_ref[layer])
     resid_ref[...] = resid
     if not last:
-        u = rms_mod(resid, *mod_rows(mods_ref, layer + 1, step_ref[0], 0))
+        u = rms_mod(resid, mods_ref[layer + 1, 0:1, :], mods_ref[layer + 1, 1:2, :])
         u_ref[...] = u
         tail_ref[...] = u[rows - TAIL :]
 
 
+WHOLE = pl.BlockSpec(memory_space=pltpu.VMEM)
 SCALARS = pl.BlockSpec(memory_space=pltpu.SMEM)
-WHOLE = pl.BlockSpec(memory_space=pltpu.VMEM)
-
-
-def run(kernel, scalars, operands, outs, scratch=(), name=None, flops=0):
+
+
+def run(kernel, operands, outs, scratch=(), name=None, flops=0, scalars=()):
     moved = sum(o.size * o.dtype.itemsize for o in list(operands) + list(outs))
     return pl.pallas_call(
         kernel,
@@ -367,23 +402,31 @@
     spans = rows // SPAN
     parts = lax.axis_size("frames")
     part_rows = INNER // parts
-    base = (lax.axis_index("frames") * frames_dev).astype(jnp.int32).reshape(1)
     step_weight = jnp.swapaxes(step_weight, 1, 2)
     step_bias = jnp.swapaxes(step_bias, 1, 2)
     resid = latents.reshape(rows, width)
-    u, tail = run(
+    (sel,) = run(
+        select_kernel, (), [shape((2 * HEADS, INNER), BF16)], name="select", flops=OPENING
+    )
+    u, tail, mods, bias, seen = run(
         first_kernel,
-        (timestep,),
-        (resid, modulation),
-        [shape((rows, width), BF16), shape((TAIL, width), BF16)],
+        (sel, resid, modulation, step_bias),
+        [
+            shape((rows, width), BF16),
+            shape((TAIL, width), BF16),
+            shape((LAYERS,) + modulation.shape[2:], F32),
+            shape((LAYERS, 8, HEADS), F32),
+            shape((rows, 2 * rows), F32),
+        ],
         name="first",
+        flops=OPENING,
+        scalars=(timestep, lookback),
     )
     for layer in range(LAYERS):
         tail = from_behind(tail, "frames")
         act, cum, shifted, state, send = run(
             functools.partial(local_kernel, layer, parts),
-            (timestep,),
-            (u, tail, input_weight, step_weight, conv_weight, step_bias, decay_log),
+            (u, tail, input_weight, step_weight, conv_weight, bias, decay_log, sel),
             [
                 shape((rows, INNER + 2 * STATE), BF16),
                 shape((rows, HEADS), F32),
@@ -397,8 +440,7 @@
         )
         y, wide = run(
             functools.partial(mix_kernel, layer),
-            (),
-            (u, input_weight, act, cum, shifted, state, skip_gain),
+            (u, input_weight, act, cum, shifted, state, skip_gain, sel),
             [shape((rows, INNER), F32), shape((rows, INNER), F32)],
             name="mix",
             flops=2 * rows * width * INNER,
@@ -407,7 +449,6 @@
         got = lax.all_to_all(send, "frames", 0, 0)
         (back,) = run(
             scan_kernel,
-            (),
             (got,),
             [shape((parts, part_rows, LANES), BF16)],
             name="scan",
@@ -415,22 +456,18 @@
         enter = lax.all_to_all(back, "frames", 0, 0).reshape(INNER, LANES)
         hidden, a = run(
             functools.partial(finish_kernel, layer),
-            (timestep,),
-            (enter, act, y, wide, resid, output_weight, norm_gain, modulation),
+            (enter, act, y, wide, resid, output_weight, norm_gain, mods)
+            + (() if layer else (query_weight, memory_weight, merge_weight)),
             [shape((rows, width), F32), shape((rows, width), BF16)],
             [pltpu.VMEM((rows, INNER), BF16)],
             name="finish",
         )
         prev = from_behind(a, "frames")
-        q, kv, bias = run(
-            functools.partial(memory_kernel, layer, tok_frame),
-            (base, lookback),
-            (a, query_weight, memory_weight),
-            [
-                shape((rows, ATTN), BF16),
-                shape((rows, 2 * ATTN), BF16),
-                shape((rows, 2 * rows), F32),
-            ],
+        q, number, total, top = run(
+            functools.partial(memory_kernel, layer),
+            (a, query_weight, memory_weight, seen),
+            [shape((rows, ATTN), BF16)] + [shape((rows, ATTN), F32)] * 3,
+            [pltpu.VMEM((rows, 2 * ATTN), BF16)],
             name="memory",
             flops=2 * rows * width * 3 * ATTN,
         )
@@ -440,10 +477,9 @@
             outs += [shape((rows, width), BF16), shape((TAIL, width), BF16)]
         result = run(
             functools.partial(attend_kernel, layer, last),
-            (timestep,),
-            (q, kv, bias, prev, memory_weight, merge_weight, hidden, modulation),
+            (q, number, total, top, seen, prev, memory_weight, merge_weight, hidden, mods),
             outs,
-            [pltpu.VMEM((2 * rows, 2 * ATTN), BF16), pltpu.VMEM((rows, ATTN), BF16)],
+            [pltpu.VMEM((rows, 2 * ATTN), BF16), pltpu.VMEM((rows, ATTN), BF16)],
             name="attend",
         )
         resid = result[0]

time: 116 us -> 102 us (0.88)
  local copies, waits for them, and re-layouts: 11.1 us -> 1.12 us
  Pallas kernels: 25 us -> 20.7 us
    unnamed x64 -> x32, local copies, waits for them, and re-layouts: 11.1 us -> 1.12 us
    pallas_call x13 -> x14, Pallas kernels: 25 us -> 20.7 us  [run(): pl.pallas_call(kernel, in_specs=[SCALARS] * len(scalars) + [WHOLE] * len(...]
  transfers between devices with their start and end apart: 4 -> 4, of which waited for: 4 -> 4; matrix products, arithmetic and copies ran while one was open for 0% -> 0% of each run, Pallas kernels for 2% -> 4%
where the time goes in v4:
time: 102 us
  blocking collectives  54 us (53%)
  Pallas kernels  20.7 us (20%)
  waiting for transfers between devices  16.3 us (16%)
  starting transfers between devices  9.2 us (9%)
  local copies, waits for them, and re-layouts  1.12 us (1%)
    all_to_all x2, blocking collectives, shards(): got = lax.all_to_all(send, 'frames', 0, 0)  28.4 us
    all_to_all x2, blocking collectives, shards(): enter = lax.all_to_all(back, 'frames', 0, 0).reshape(INNER, LANES)  25.7 us
    pallas_call x14, Pallas kernels, run(): pl.pallas_call(kernel, in_specs=[SCALARS] * len(scalars) + [WHOLE] * len(...  20.7 us
    ppermute x4, waiting for transfers between devices, from_behind(): return lax.ppermute(value, axis, [(i, i + 1) for i in range(count - 1)])  16.3 us
    ppermute x4, starting transfers between devices, from_behind(): return lax.ppermute(value, axis, [(i, i + 1) for i in range(count - 1)])  9.2 us
  transfers between devices with their start and end apart: 4, of which 4 were waited for; matrix products, arithmetic and copies ran while one was open for 0% of the time, Pallas kernels for 4%

profile of v4, /device:TPU:8, one launch (start us, length us, event | category | flops | bytes accessed | tf_op | source)
XLA Modules:
  0.0 101.6 jit_solution(9411610270433320526)
XLA Ops:
  0.0 0.0 copy-start.11
  0.0 0.0 copy-start.10
  0.0 0.0 copy-start.13
  0.0 0.0 copy-start.12
  0.0 0.0 copy-start.4
  0.1 0.0 slice-start
  0.1 0.7 copy-done.11
  0.7 0.3 copy-done.10
  1.0 0.0 copy-done.13
  1.0 0.0 copy-done.12
  1.0 0.1 copy-done.4
  1.1 0.0 slice-start.1
  1.1 0.0 copy-start.5
  1.1 0.0 copy-start.6
  1.1 0.0 copy-start.9
  1.1 0.7 first.1
  1.9 1.9 %collective-permute-start = (bf16[16,512]{1,0:T(8,128)(2,1)S(1)}, bf16[16,512]{1,0:T(8,128)(2,1)S(1)}, u32[]{:S(2)}, u32[]{:S(2)}) collective-permute-start(bf16[16,512]{1,0:T(8,128)(2,1)S(1)} %get-tuple-element.48), channel_id=1, source_target_pairs={{0,1},{1,2},{2,3},{3,4},{4,5},{5,6},{6,7},{7,8},{8,9},{9,10},{10,1... | collective-permute-start | bytes 49160 | tf_op jit(solution)/shard_map/ppermute | solution.py:380
  3.8 4.0 %collective-permute-done.tail_ref = bf16[16,512]{1,0:T(8,128)(2,1)S(1)} collective-permute-done((bf16[16,512]{1,0:T(8,128)(2,1)S(1)}, bf16[16,512]{1,0:T(8,128)(2,1)S(1)}, u32[]{:S(2)}, u32[]{:S(2)}) %collective-permute-start) | collective-permute-done | bytes 16416 | tf_op jit(solution)/shard_map/ppermute | solution.py:380
  7.8 0.0 slice-done
  7.8 0.0 slice-done.1
  7.9 0.0 copy-done.5
  7.9 0.0 copy-done.6
  7.9 0.0 copy-done.9
  7.9 0.0 copy-start.8
  7.9 2.9 %local.2 = (bf16[256,1280]{1,0:T(8,128)(2,1)S(1)}, f32[256,16]{1,0:T(8,128)S(1)}, f32[16,256]{1,0:T(8,128)S(1)}, bf16[128,1024]{1,0:T(8,128)(2,1)S(1)}, bf16[16,80,128]{2,1,0:T(8,128)(2,1)S(1)}) custom-call(bf16[256,512]{1,0:T(8,128)(2,1)S(1)} %get-tuple-element.47.u_ref, bf16[16,512]{1,0:T(8,128)(2,1)S(1)} %collective-permute-done.tail_ref, ...), custom_call_target="tpu_custom_call" | custom-call | flops 335544320 | bytes 6415488 | tf_op jit(solution)/shard_map/local/pallas_call | solution.py:362
  10.8 0.0 copy-done.8
  10.8 0.0 copy-start
  10.8 0.0 copy-start.2
  10.8 0.0 copy-start.3
  10.9 0.0 copy-start.7
  10.9 1.7 %mix.2 = (f32[256,1024]{1,0:T(8,128)S(1)}, f32[256,1024]{1,0:T(8,128)S(1)}) custom-call(bf16[256,512]{1,0:T(8,128)(2,1)S(1)} %get-tuple-element.47.u_ref, bf16[2,512,2304]{2,1,0:T(8,128)(2,1)S(1)} %bitcast.7, bf16[256,1280]{1,0:T(8,128)(2,1)S(1)} %get-tuple-element.58.act_ref, f32[256,16]{1,0:T(8,128)S(1)} %get-tuple-element.52.cum_ref, ...), custom_call_target="tpu_custom_call" | custom-call | flops 268435456 | bytes 8093824 | tf_op jit(solution)/shard_map/mix/pallas_call | solution.py:362
  12.6 0.0 copy-start.1
  12.6 14.8 %all_to_all.20.got_ref = bf16[16,80,128]{2,1,0:T(8,128)(2,1)S(1)} all-to-all(bf16[16,80,128]{2,1,0:T(8,128)(2,1)S(1)} %get-tuple-element.57), channel_id=1, replica_groups=mesh['groups'=2,'frames'=16] {'frames'}, dimensions={0} | all-to-all | bytes 655360 | tf_op jit(solution)/shard_map/all_to_all | solution.py:449
  27.4 0.1 scan.2
  27.4 12.8 %all_to_all.21 = bf16[16,64,128]{2,1,0:T(8,128)(2,1)S(1)} all-to-all(bf16[16,64,128]{2,1,0:T(8,128)(2,1)S(1)} %scan.2), channel_id=1, replica_groups=mesh['groups'=2,'frames'=16] {'frames'}, dimensions={0} | all-to-all | bytes 524288 | tf_op jit(solution)/shard_map/all_to_all | solution.py:456
  40.3 0.0 copy-done
  40.3 0.0 copy-done.2
  40.3 0.0 copy-done.3
  40.3 0.0 copy-done.7
  40.3 0.0 copy-done.1
  40.3 1.2 %finish.2 = (f32[256,512]{1,0:T(8,128)S(1)}, bf16[256,512]{1,0:T(8,128)(2,1)S(1)}) custom-call(bf16[1024,128]{1,0:T(8,128)(2,1)S(1)} %bitcast.9, bf16[256,1280]{1,0:T(8,128)(2,1)S(1)} %get-tuple-element.58.act_ref, f32[256,1024]{1,0:T(8,128)S(1)} %get-tuple-element.59.y_ref, f32[256,1024]{1,0:T(8,128)S(1)} %get-tuple-element.60.wide_ref, ...), custom_call_target="tpu_custom_call" | custom-call | bytes 10379264 | tf_op jit(solution)/shard_map/finish/pallas_call | solution.py:362
  41.5 2.6 %collective-permute-start.1 = (bf16[256,512]{1,0:T(8,128)(2,1)S(1)}, bf16[256,512]{1,0:T(8,128)(2,1)S(1)}, u32[]{:S(2)}, u32[]{:S(2)}) collective-permute-start(bf16[256,512]{1,0:T(8,128)(2,1)S(1)} %get-tuple-element.62.a_ref), channel_id=1, source_target_pairs={{0,1},{1,2},{2,3},{3,4},{4,5},{5,6},{6,7},{7,8},{8,9},{9,10},{10,1... | collective-permute-start | bytes 786440 | tf_op jit(solution)/shard_map/ppermute | solution.py:380
  44.1 1.8 %memory.2 = (bf16[256,512]{1,0:T(8,128)(2,1)S(1)}, f32[256,512]{1,0:T(8,128)S(1)}, f32[256,512]{1,0:T(8,128)S(1)}, f32[256,512]{1,0:T(8,128)S(1)}) custom-call(bf16[256,512]{1,0:T(8,128)(2,1)S(1)} %get-tuple-element.62.a_ref, bf16[2,512,512]{2,1,0:T(8,128)(2,1)S(1)} %copy-done.1, bf16[2,512,1024]{2,1,0:T(8,128)(2,1)S(1)} %copy-done, ...), custom_call_target="tpu_custom_call" | custom-call | flops 402653184 | bytes 5767168 | tf_op jit(solution)/shard_map/memory/pallas_call | solution.py:362
  45.9 4.2 %collective-permute-done.1.prev_ref = bf16[256,512]{1,0:T(8,128)(2,1)S(1)} collective-permute-done((bf16[256,512]{1,0:T(8,128)(2,1)S(1)}, bf16[256,512]{1,0:T(8,128)(2,1)S(1)}, u32[]{:S(2)}, u32[]{:S(2)}) %collective-permute-start.1) | collective-permute-done | bytes 262176 | tf_op jit(solution)/shard_map/ppermute | solution.py:380
  50.1 2.0 %attend.2 = (f32[256,512]{1,0:T(8,128)S(1)}, bf16[256,512]{1,0:T(8,128)(2,1)S(1)}, bf16[16,512]{1,0:T(8,128)(2,1)S(1)}) custom-call(bf16[256,512]{1,0:T(8,128)(2,1)S(1)} %get-tuple-element.64.q_ref, f32[256,512]{1,0:T(8,128)S(1)} %get-tuple-element.65.number_ref, f32[256,512]{1,0:T(8,128)S(1)} %get-tuple-element.66.total_ref, ...), custom_call_target="tpu_custom_call" | custom-call | bytes 7110656 | tf_op jit(solution)/shard_map/attend/pallas_call | solution.py:362
  52.0 2.1 %collective-permute-start.2 = (bf16[16,512]{1,0:T(8,128)(2,1)S(1)}, bf16[16,512]{1,0:T(8,128)(2,1)S(1)}, u32[]{:S(2)}, u32[]{:S(2)}) collective-permute-start(bf16[16,512]{1,0:T(8,128)(2,1)S(1)} %get-tuple-element.70), channel_id=1, source_target_pairs={{0,1},{1,2},{2,3},{3,4},{4,5},{5,6},{6,7},{7,8},{8,9},{9,10},{10,1... | collective-permute-start | bytes 49160 | tf_op jit(solution)/shard_map/ppermute | solution.py:380
  54.2 3.8 %collective-permute-done.2.tail_ref = bf16[16,512]{1,0:T(8,128)(2,1)S(1)} collective-permute-done((bf16[16,512]{1,0:T(8,128)(2,1)S(1)}, bf16[16,512]{1,0:T(8,128)(2,1)S(1)}, u32[]{:S(2)}, u32[]{:S(2)}) %collective-permute-start.2) | collective-permute-done | bytes 16416 | tf_op jit(solution)/shard_map/ppermute | solution.py:380
  58.0 2.9 %local.3 = (bf16[256,1280]{1,0:T(8,128)(2,1)S(1)}, f32[256,16]{1,0:T(8,128)S(1)}, f32[16,256]{1,0:T(8,128)S(1)}, bf16[128,1024]{1,0:T(8,128)(2,1)S(1)}, bf16[16,80,128]{2,1,0:T(8,128)(2,1)S(1)}) custom-call(bf16[256,512]{1,0:T(8,128)(2,1)S(1)} %get-tuple-element.69.u_ref, bf16[16,512]{1,0:T(8,128)(2,1)S(1)} %collective-permute-done.2.tail_ref, ...), custom_call_target="tpu_custom_call" | custom-call | flops 335544320 | bytes 6415488 | tf_op jit(solution)/shard_map/local/pallas_call | solution.py:362
  60.9 1.7 %mix.3 = (f32[256,1024]{1,0:T(8,128)S(1)}, f32[256,1024]{1,0:T(8,128)S(1)}) custom-call(bf16[256,512]{1,0:T(8,128)(2,1)S(1)} %get-tuple-element.69.u_ref, bf16[2,512,2304]{2,1,0:T(8,128)(2,1)S(1)} %bitcast.7, bf16[256,1280]{1,0:T(8,128)(2,1)S(1)} %get-tuple-element.79.act_ref, f32[256,16]{1,0:T(8,128)S(1)} %get-tuple-element.73.cum_ref, ...), custom_call_target="tpu_custom_call" | custom-call | flops 268435456 | bytes 8093824 | tf_op jit(solution)/shard_map/mix/pallas_call | solution.py:362
  62.7 13.6 %all_to_all.22.got_ref = bf16[16,80,128]{2,1,0:T(8,128)(2,1)S(1)} all-to-all(bf16[16,80,128]{2,1,0:T(8,128)(2,1)S(1)} %get-tuple-element.78), channel_id=1, replica_groups=mesh['groups'=2,'frames'=16] {'frames'}, dimensions={0} | all-to-all | bytes 655360 | tf_op jit(solution)/shard_map/all_to_all | solution.py:449
  76.3 0.1 scan.3
  76.3 12.8 %all_to_all.23 = bf16[16,64,128]{2,1,0:T(8,128)(2,1)S(1)} all-to-all(bf16[16,64,128]{2,1,0:T(8,128)(2,1)S(1)} %scan.3), channel_id=1, replica_groups=mesh['groups'=2,'frames'=16] {'frames'}, dimensions={0} | all-to-all | bytes 524288 | tf_op jit(solution)/shard_map/all_to_all | solution.py:456
  89.2 1.2 %finish.3 = (f32[256,512]{1,0:T(8,128)S(1)}, bf16[256,512]{1,0:T(8,128)(2,1)S(1)}) custom-call(bf16[1024,128]{1,0:T(8,128)(2,1)S(1)} %bitcast.8, bf16[256,1280]{1,0:T(8,128)(2,1)S(1)} %get-tuple-element.79.act_ref, f32[256,1024]{1,0:T(8,128)S(1)} %get-tuple-element.80.y_ref, f32[256,1024]{1,0:T(8,128)S(1)} %get-tuple-element.81.wide_ref, ...), custom_call_target="tpu_custom_call" | custom-call | bytes 6447104 | tf_op jit(solution)/shard_map/finish/pallas_call | solution.py:362
  90.3 2.6 %collective-permute-start.3 = (bf16[256,512]{1,0:T(8,128)(2,1)S(1)}, bf16[256,512]{1,0:T(8,128)(2,1)S(1)}, u32[]{:S(2)}, u32[]{:S(2)}) collective-permute-start(bf16[256,512]{1,0:T(8,128)(2,1)S(1)} %get-tuple-element.83.a_ref), channel_id=1, source_target_pairs={{0,1},{1,2},{2,3},{3,4},{4,5},{5,6},{6,7},{7,8},{8,9},{9,10},{10,1... | collective-permute-start | bytes 786440 | tf_op jit(solution)/shard_map/ppermute | solution.py:380
  92.9 1.8 %memory.3 = (bf16[256,512]{1,0:T(8,128)(2,1)S(1)}, f32[256,512]{1,0:T(8,128)S(1)}, f32[256,512]{1,0:T(8,128)S(1)}, f32[256,512]{1,0:T(8,128)S(1)}) custom-call(bf16[256,512]{1,0:T(8,128)(2,1)S(1)} %get-tuple-element.83.a_ref, bf16[2,512,512]{2,1,0:T(8,128)(2,1)S(1)} %copy-done.1, bf16[2,512,1024]{2,1,0:T(8,128)(2,1)S(1)} %copy-done, ...), custom_call_target="tpu_custom_call" | custom-call | flops 402653184 | bytes 5767168 | tf_op jit(solution)/shard_map/memory/pallas_call | solution.py:362
  94.7 4.2 %collective-permute-done.3.prev_ref = bf16[256,512]{1,0:T(8,128)(2,1)S(1)} collective-permute-done((bf16[256,512]{1,0:T(8,128)(2,1)S(1)}, bf16[256,512]{1,0:T(8,128)(2,1)S(1)}, u32[]{:S(2)}, u32[]{:S(2)}) %collective-permute-start.3) | collective-permute-done | bytes 262176 | tf_op jit(solution)/shard_map/ppermute | solution.py:380
  98.9 2.7 %attend.3 = f32[256,512]{1,0:T(8,128)} custom-call(bf16[256,512]{1,0:T(8,128)(2,1)S(1)} %get-tuple-element.84.q_ref, f32[256,512]{1,0:T(8,128)S(1)} %get-tuple-element.85.number_ref, f32[256,512]{1,0:T(8,128)S(1)} %get-tuple-element.86.total_ref, f32[256,512]{1,0:T(8,128)S(1)} %get-tuple-element.87.top_ref, f32[256,512]{1,0:T(8,128)S(1)} %get-tuple-element.63.seen_ref, ...), custom_call_target="tpu_custom_call" | custom-call | bytes 6832128 | tf_op jit(solution)/shard_map/attend/pallas_call | solution.py:362
  (2 shorter events, 0.0 us)
Async XLA Ops:
  0.0 0.7 copy-start.11
  0.0 1.0 copy-start.10
  0.0 1.0 %copy-start.13 = (s32[8]{0:T(128)S(1)}, s32[8]{0:T(128)}, u32[]{:S(2)}) copy-start(s32[8]{0:T(128)} %reach_ref.1) | copy-start | bytes 100
  0.0 1.0 copy-start.12
  0.0 1.1 %copy-start.4 = (bf16[8,32,512]{2,1,0:T(8,128)(2,1)S(1)}, bf16[8,32,512]{2,1,0:T(8,128)(2,1)}, u32[]{:S(2)}) copy-start(bf16[8,32,512]{2,1,0:T(8,128)(2,1)} %param.15) | copy-start | bytes 786436
  0.1 7.8 %slice-start = ((s8[4718592]{0:T(1024)(128)(4,1)}), s8[4194304]{0:T(1024)(128)(4,1)S(1)}, s32[]{:S(2)}) async-start(s8[4718592]{0:T(1024)(128)(4,1)} %bitcast.6), calls=%async_computation.4 | async-start | bytes 8388608
  1.1 6.7 %slice-start.1 = ((s8[4718592]{0:T(1024)(128)(4,1)}), s8[524288]{0:T(1024)(128)(4,1)S(1)}, s32[]{:S(2)}) async-start(s8[4718592]{0:T(1024)(128)(4,1)} %bitcast.6), calls=%async_computation.5 | async-start | bytes 1048576
  1.1 6.7 %copy-start.5 = (f32[2,4,1280]{2,1,0:T(4,128)S(1)}, f32[2,4,1280]{2,1,0:T(4,128)}, u32[]{:S(2)}) copy-start(f32[2,4,1280]{2,1,0:T(4,128)} %conv_ref.3) | copy-start | bytes 122884
  1.1 6.7 %copy-start.6 = (bf16[2,512,16]{1,2,0:T(8,128)(2,1)S(1)}, bf16[2,512,16]{1,2,0:T(8,128)(2,1)}, u32[]{:S(2)}) copy-start(bf16[2,512,16]{1,2,0:T(8,128)(2,1)} %param.20) | copy-start | bytes 98308
  1.1 6.7 %copy-start.9 = (f32[2,16]{1,0:T(2,128)S(1)}, f32[2,16]{1,0:T(2,128)}, u32[]{:S(2)}) copy-start(f32[2,16]{1,0:T(2,128)} %decay_ref.3) | copy-start | bytes 388
  1.9 6.0 %collective-permute-start = (bf16[16,512]{1,0:T(8,128)(2,1)S(1)}, bf16[16,512]{1,0:T(8,128)(2,1)S(1)}, u32[]{:S(2)}, u32[]{:S(2)}) collective-permute-start(bf16[16,512]{1,0:T(8,128)(2,1)S(1)} %get-tuple-element.48), channel_id=1, source_target_pairs={{0,1},{1,2},{2,3},{3,4},{4,5},{5,6},{6,7},{7,8},{8,9},{9,10},{10,1... | collective-permute-start | bytes 49160 | tf_op jit(solution)/shard_map/ppermute | solution.py:380
  7.9 2.9 %copy-start.8 = (f32[2,16]{1,0:T(2,128)S(1)}, f32[2,16]{1,0:T(2,128)}, u32[]{:S(2)}) copy-start(f32[2,16]{1,0:T(2,128)} %skip_ref.3) | copy-start | bytes 388
  10.8 29.5 %copy-start = (bf16[2,512,1024]{2,1,0:T(8,128)(2,1)S(1)}, bf16[2,512,1024]{2,1,0:T(8,128)(2,1)}, u32[]{:S(2)}) copy-start(bf16[2,512,1024]{2,1,0:T(8,128)(2,1)} %wm_ref.7) | copy-start | bytes 6291460
  10.8 29.5 %copy-start.2 = (bf16[2,512,512]{2,1,0:T(8,128)(2,1)S(1)}, bf16[2,512,512]{2,1,0:T(8,128)(2,1)}, u32[]{:S(2)}) copy-start(bf16[2,512,512]{2,1,0:T(8,128)(2,1)} %merge_ref.3) | copy-start | bytes 3145732
  10.8 29.4 %copy-start.3 = (bf16[2,1024,512]{2,1,0:T(8,128)(2,1)S(1)}, bf16[2,1024,512]{2,1,0:T(8,128)(2,1)}, u32[]{:S(2)}) copy-start(bf16[2,1024,512]{2,1,0:T(8,128)(2,1)} %w_ref.11) | copy-start | bytes 6291460
  10.9 29.4 %copy-start.7 = (f32[2,1024]{1,0:T(2,128)S(1)}, f32[2,1024]{1,0:T(2,128)}, u32[]{:S(2)}) copy-start(f32[2,1024]{1,0:T(2,128)} %gain_ref.3) | copy-start | bytes 24580
  12.6 27.7 %copy-start.1 = (bf16[2,512,512]{2,1,0:T(8,128)(2,1)S(1)}, bf16[2,512,512]{2,1,0:T(8,128)(2,1)}, u32[]{:S(2)}) copy-start(bf16[2,512,512]{2,1,0:T(8,128)(2,1)} %wq_ref.3) | copy-start | bytes 3145732
  41.5 8.6 %collective-permute-start.1 = (bf16[256,512]{1,0:T(8,128)(2,1)S(1)}, bf16[256,512]{1,0:T(8,128)(2,1)S(1)}, u32[]{:S(2)}, u32[]{:S(2)}) collective-permute-start(bf16[256,512]{1,0:T(8,128)(2,1)S(1)} %get-tuple-element.62.a_ref), channel_id=1, source_target_pairs={{0,1},{1,2},{2,3},{3,4},{4,5},{5,6},{6,7},{7,8},{8,9},{9,10},{10,1... | collective-permute-start | bytes 786440 | tf_op jit(solution)/shard_map/ppermute | solution.py:380
  52.0 6.0 %collective-permute-start.2 = (bf16[16,512]{1,0:T(8,128)(2,1)S(1)}, bf16[16,512]{1,0:T(8,128)(2,1)S(1)}, u32[]{:S(2)}, u32[]{:S(2)}) collective-permute-start(bf16[16,512]{1,0:T(8,128)(2,1)S(1)} %get-tuple-element.70), channel_id=1, source_target_pairs={{0,1},{1,2},{2,3},{3,4},{4,5},{5,6},{6,7},{7,8},{8,9},{9,10},{10,1... | collective-permute-start | bytes 49160 | tf_op jit(solution)/shard_map/ppermute | solution.py:380
  90.3 8.6 %collective-permute-start.3 = (bf16[256,512]{1,0:T(8,128)(2,1)S(1)}, bf16[256,512]{1,0:T(8,128)(2,1)S(1)}, u32[]{:S(2)}, u32[]{:S(2)}) collective-permute-start(bf16[256,512]{1,0:T(8,128)(2,1)S(1)} %get-tuple-element.83.a_ref), channel_id=1, source_target_pairs={{0,1},{1,2},{2,3},{3,4},{4,5},{5,6},{6,7},{7,8},{8,9},{9,10},{10,1... | collective-permute-start | bytes 786440 | tf_op jit(solution)/shard_map/ppermute | solution.py:380

commit v5 on v4

--- a/solution.py
+++ b/solution.py
@@ -60,7 +60,6 @@
     all_mods_ref,
     all_bias_ref,
     u_ref,
-    tail_ref,
     mods_ref,
     bias_ref,
     seen_ref,
@@ -70,9 +69,7 @@
     step = step_ref[0]
     for layer in range(LAYERS):
         mods_ref[layer] = all_mods_ref[layer, step].astype(F32)
-    u = rms_mod(x_ref[...].astype(F32), mods_ref[0, 0:1, :], mods_ref[0, 1:2, :])
-    u_ref[...] = u
-    tail_ref[...] = u[rows - TAIL :]
+    u_ref[...] = rms_mod(x_ref[...].astype(F32), mods_ref[0, 0:1, :], mods_ref[0, 1:2, :])
     chosen = lax.broadcasted_iota(jnp.int32, (8, all_bias_ref.shape[-1]), 1) == step
     chosen = jnp.where(chosen, 1.0, 0.0).astype(F32)
     for layer in range(LAYERS):
@@ -91,7 +88,6 @@
     layer,
     parts,
     u_ref,
-    tail_ref,
     w_ref,
     sw_ref,
     conv_ref,
@@ -99,15 +95,18 @@
     decay_ref,
     sel_ref,
     act_ref,
+    own_ref,
     cum_ref,
     shifted_ref,
+    edge_ref,
     state_ref,
     send_ref,
     ext_ref,
+    tail_ref,
+    pad_ref,
 ):
     rows = u_ref.shape[0]
     u = u_ref[...]
-    tail = tail_ref[...]
     sel = sel_ref[...]
     raw = dot(u, sw_ref[layer], ((1,), (1,))) + bias_ref[layer, 0:1, :]
     step = jnp.maximum(raw, 0.0) + jnp.log1p(jnp.exp(-jnp.abs(raw)))
@@ -116,6 +115,7 @@
     q_pos = lax.broadcasted_iota(jnp.int32, (SPAN, SPAN), 0)
     s_pos = lax.broadcasted_iota(jnp.int32, (SPAN, SPAN), 1)
     lower = jnp.where(q_pos >= s_pos, 1.0, 0.0).astype(F32)
+    whole_tokens = lax.broadcasted_iota(jnp.int32, (SPAN, HEADS), 0) >= CONV - 1
     ends, edges = [], []
     for b in range(rows // SPAN):
         r = slice(b * SPAN, (b + 1) * SPAN)
@@ -123,21 +123,32 @@
         end = cum[SPAN - 1 : SPAN, :]
         cum_ref[r, :] = cum
         shifted_ref[:, r] = (cum - log_step[r]).T
+        edge = jnp.exp(end - cum) * step[r]
+        if b == 0:
+            edge_ref[...] = edge[0:TAIL, :]
+            edge = jnp.where(whole_tokens, edge, 0.0)
         ends.append(end)
-        edges.append(spread(jnp.exp(end - cum) * step[r], sel))
+        edges.append(spread(edge, sel))
 
     chunk = 256
+    for slot in range(2):
+        ext_ref[slot, 0:TAIL, :] = jnp.zeros((TAIL, chunk), F32)
+        ext_ref[slot, TAIL + rows :, :] = jnp.zeros((TAIL, chunk), F32)
     for c in [INNER] + list(range(0, INNER, chunk)):
         w = w_ref[layer, :, INNER + c : INNER + c + chunk]
         slot = c // chunk % 2
-        ext_ref[slot, 0:TAIL, :] = dot(tail, w).astype(BF16).astype(F32)
-        ext_ref[slot, TAIL:, :] = dot(u, w).astype(BF16).astype(F32)
-        total = None
+        ext_ref[slot, TAIL : TAIL + rows, :] = dot(u, w).astype(BF16).astype(F32)
+        total, after = None, None
         for k in range(CONV):
             start = TAIL - (CONV - 1) + k
-            term = conv_ref[layer, k : k + 1, c : c + chunk] * ext_ref[slot, start : start + rows, :]
+            taps = conv_ref[layer, k : k + 1, c : c + chunk]
+            term = taps * ext_ref[slot, start : start + rows, :]
+            next_term = taps * ext_ref[slot, start + rows : start + rows + 8, :]
             total = term if total is None else total + term
+            after = next_term if after is None else after + next_term
         act_ref[:, c : c + chunk] = (total * jax.nn.sigmoid(total)).astype(BF16)
+        own_ref[:, c : c + chunk] = total[0:8, :]
+        tail_ref[:, c : c + chunk] = after
 
     state = None
     for b in range(rows // SPAN):
@@ -148,57 +159,175 @@
         if state is None:
             state = term
         else:
-            state_ref[(b - 1) * STATE : b * STATE, :] = state.astype(BF16)
+            state_ref[(b - 1) * STATE : b * STATE, :] = state
             state = spread_row(jnp.exp(ends[b]), sel) * state + term
 
     part_rows = INNER // parts
-    held = max(1, part_rows // HEAD_DIM)
-    size = min(part_rows, LANES)
     for pair in range(HEADS // 2):
         turned = state[:, pair * LANES : (pair + 1) * LANES].T.astype(BF16)
-        for k in range(LANES // size):
-            first = pair * LANES + k * size
-            part, at = first // part_rows, first % part_rows
-            send_ref[part, at : at + size, :] = turned[k * size : (k + 1) * size, :]
-    pad_row = lax.broadcasted_iota(jnp.int32, (PAD, LANES), 0)
+        for k in range(LANES // part_rows):
+            part = (pair * LANES) // part_rows + k
+            send_ref[part, 0:part_rows, :] = turned[k * part_rows : (k + 1) * part_rows, :]
     over = sum(ends[1:], ends[0])
+    edge = jnp.exp(over - cum_ref[0:8, :]) * step[0:8, :]
+    left = lax.broadcasted_iota(jnp.int32, (8, LANES), 1) < HEAD_DIM
+    few = CONV - 1
+
+    def halves(value):
+        high = value.astype(BF16).astype(F32)
+        return jnp.where(left, high, value - high)
+
     for part in range(parts):
-        pad = jnp.zeros((PAD, LANES), F32)
-        for i in range(held):
-            h = part * part_rows // HEAD_DIM + i
-            decay = jnp.broadcast_to(over[:, h : h + 1], (PAD, LANES))
-            high = decay.astype(BF16).astype(F32)
-            pad = jnp.where(pad_row == 2 * i, high, jnp.where(pad_row == 2 * i + 1, decay - high, pad))
-        send_ref[part, part_rows:, :] = pad.astype(BF16)
-
-
-def mix_kernel(
-    layer, u_ref, w_ref, act_ref, cum_ref, shifted_ref, state_ref, skip_ref, sel_ref, y_ref, wide_ref
+        first = part * part_rows
+        h, at = first // HEAD_DIM, first % HEAD_DIM
+        cols = slice(h // 2 * LANES, (h // 2 + 1) * LANES)
+        side = h % 2 * HEAD_DIM
+        own = pltpu.roll(own_ref[:, cols], (2 * LANES - side - at) % LANES, 1)
+        tail = pltpu.roll(tail_ref[:, cols], (2 * LANES + HEAD_DIM - side) % LANES, 1)
+        if at:
+            own = jnp.where(left, own, 0.0)
+        decay = jnp.broadcast_to(over[:, h : h + 1], (8, LANES))
+        pad_ref[part, 0:1, :] = halves(decay)[0:1, :]
+        pad_ref[part, 1 : 1 + few, :] = jnp.where(left, own, tail)[0:few, :]
+        pad_ref[part, 4 : 4 + few, :] = own_ref[0:few, INNER : INNER + STATE]
+        pad_ref[part, 7 : 7 + few, :] = tail_ref[0:few, INNER : INNER + STATE]
+        broad = jnp.broadcast_to(edge[:, h : h + 1], (8, LANES))
+        pad_ref[part, 10 : 10 + few, :] = halves(broad)[0:few, :]
+        pad_ref[part, 13 : 13 + few, :] = tail_ref[0:few, INNER + STATE :]
+        send_ref[part, part_rows:, :] = pad_ref[part].astype(BF16)
+
+
+def silu(x):
+    return x * jax.nn.sigmoid(x)
+
+
+def scan_kernel(got_ref, back_ref, pad_ref):
+    parts, padded, _ = got_ref.shape
+    part_rows = padded - PAD
+    rows = slice(0, part_rows)
+    offset = lax.axis_index("frames") * part_rows % HEAD_DIM
+    few = lax.broadcasted_iota(jnp.int32, (8, LANES), 0) < CONV - 1
+    left = lax.broadcasted_iota(jnp.int32, (8, LANES), 1) < HEAD_DIM
+    pad_ref[0:PAD, :] = jnp.zeros((PAD, LANES), F32)
+    pad_ref[(parts + 1) * PAD :, :] = jnp.zeros((8, LANES), F32)
+    for d in range(parts):
+        pad_ref[(d + 1) * PAD : (d + 2) * PAD, :] = got_ref[d, part_rows:, :].astype(F32)
+    carry = jnp.zeros((part_rows, LANES), F32)
+    for d in range(parts):
+        back_ref[d, rows, :] = carry.astype(BF16)
+        back_ref[d, part_rows:, :] = pad_ref[d * PAD : (d + 1) * PAD, :].astype(BF16)
+        last, mine = d * PAD, (d + 1) * PAD
+        decay = pad_ref[mine : mine + 1, :]
+        decay = jnp.exp(decay + pltpu.roll(decay, HEAD_DIM, 1))
+        from_tail = pltpu.roll(pad_ref[last + 1 : last + 9, :], HEAD_DIM, 1)
+        if part_rows < HEAD_DIM:
+            from_tail = pltpu.roll(jnp.where(left, from_tail, 0.0), (LANES - offset) % LANES, 1)
+        values = silu(pad_ref[mine + 1 : mine + 9, :] + from_tail)
+        in_map = silu(pad_ref[mine + 4 : mine + 12, :] + pad_ref[last + 7 : last + 15, :])
+        edge = pad_ref[mine + 10 : mine + 18, :]
+        edge = edge + pltpu.roll(edge, HEAD_DIM, 1)
+        scaled = jnp.where(few, values.astype(BF16).astype(F32) * edge, 0.0)
+        in_map = jnp.where(few, in_map, 0.0)
+        added = dot(scaled, in_map, ((0,), (0,)))
+        carry = decay * carry + (got_ref[d, rows, :].astype(F32) + added[rows, :])
+
+
+def finish_kernel(
+    layer,
+    u_ref,
+    w_ref,
+    act_ref,
+    own_ref,
+    cum_ref,
+    shifted_ref,
+    edge_ref,
+    state_ref,
+    skip_ref,
+    sel_ref,
+    enter_ref,
+    resid_ref,
+    wo_ref,
+    gain_ref,
+    mods_ref,
+    *rest,
 ):
+    hidden_ref, a_ref, first_ref, y_ref, gate_ref, normed_ref = rest[-6:]
     rows = u_ref.shape[0]
+    parts, padded, _ = enter_ref.shape
+    part_rows = padded - PAD
     u = u_ref[...]
+    sel = sel_ref[...]
+    lane = lax.broadcasted_iota(jnp.int32, (SPAN, LANES), 1)
+    left = lane < HEAD_DIM
+    few = lax.broadcasted_iota(jnp.int32, (TAIL, LANES), 0) < CONV - 1
+    nothing = jnp.zeros((TAIL - 8, LANES), F32)
+
+    def fixed(cols, tail):
+        total = jnp.concatenate([own_ref[:, cols] + tail[0:8, :], nothing], axis=0)
+        first_ref[:, cols] = jnp.where(
+            few, silu(total), act_ref[0:TAIL, cols].astype(F32)
+        ).astype(BF16)
+
+    for pair in range(HEADS // 2):
+        pads = [
+            enter_ref[h * HEAD_DIM // part_rows, part_rows:, :].astype(F32)
+            for h in (2 * pair, 2 * pair + 1)
+        ]
+        tail = jnp.where(left[0:PAD], pltpu.roll(pads[0], HEAD_DIM, 1), pads[1])
+        fixed(slice(pair * LANES, (pair + 1) * LANES), pltpu.roll(tail, PAD - 1, 0))
+    common = enter_ref[0, part_rows:, :].astype(F32)
+    fixed(slice(INNER, INNER + STATE), pltpu.roll(common, PAD - 7, 0))
+    fixed(slice(INNER + STATE, INNER + 2 * STATE), pltpu.roll(common, PAD - 13, 0))
+
+    def acts(b, cols):
+        if b:
+            return act_ref[b * SPAN : (b + 1) * SPAN, cols]
+        return jnp.concatenate([first_ref[:, cols], act_ref[TAIL:SPAN, cols]], axis=0)
+
+    first_tokens = lax.broadcasted_iota(jnp.int32, (TAIL, HEADS), 0) < CONV - 1
+    early = spread(jnp.where(first_tokens, edge_ref[...], 0.0), sel)
+    early = (first_ref[:, 0:INNER].astype(F32) * early).astype(BF16)
+    late = dot(first_ref[:, INNER : INNER + STATE], early, ((0,), (0,)))
+
+    spans = rows // SPAN
+    out_maps = [acts(b, slice(INNER + STATE, INNER + 2 * STATE)) for b in range(spans)]
+    out_map = jnp.concatenate(out_maps, axis=0)
+    before = jnp.zeros((1, HEADS), F32)
+    scales = []
+    for b in range(spans):
+        cum = cum_ref[b * SPAN : (b + 1) * SPAN, :]
+        scales.append(jnp.exp(cum + before))
+        before = before + cum[SPAN - 1 : SPAN, :]
+    wide = spread(jnp.concatenate(scales, axis=0), sel)
+    chunk = 256
+    for c in range(0, INNER, chunk):
+        cols = slice(c, c + chunk)
+        gate_ref[:, cols] = silu(dot(u, w_ref[layer, :, cols]).astype(BF16).astype(F32))
+        entering = jnp.concatenate(
+            [enter_ref[p, 0:part_rows, :] for p in range(c // part_rows, (c + chunk) // part_rows)],
+            axis=0,
+        )
+        y_ref[:, cols] = dot(out_map, entering, ((1,), (1,))) * wide[:, cols]
+    decayed = jnp.ones((1, HEADS), F32)
+    for b in range(1, spans):
+        r = slice(b * SPAN, (b + 1) * SPAN)
+        state = state_ref[(b - 1) * STATE : b * STATE, :] + spread_row(decayed, sel) * late
+        cum = cum_ref[r, :]
+        decayed = decayed * jnp.exp(cum[SPAN - 1 : SPAN, :])
+        y_ref[r, :] = y_ref[r, :] + dot(out_maps[b], state.astype(BF16)) * spread(jnp.exp(cum), sel)
+
     q_pos = lax.broadcasted_iota(jnp.int32, (SPAN, SPAN), 0)
     s_pos = lax.broadcasted_iota(jnp.int32, (SPAN, SPAN), 1)
     lower = q_pos >= s_pos
-    lane = lax.broadcasted_iota(jnp.int32, (SPAN, LANES), 1)
-    left = lane < HEAD_DIM
     zero = jnp.zeros((SPAN, LANES), BF16)
-    sel = sel_ref[...]
     skip = spread_row(skip_ref[layer : layer + 1, :], sel)
-    before = jnp.zeros((1, HEADS), F32)
-    for b in range(rows // SPAN):
+    for b in range(spans):
         r = slice(b * SPAN, (b + 1) * SPAN)
         cum = cum_ref[r, :]
-        in_map = act_ref[r, INNER : INNER + STATE]
-        out_map = act_ref[r, INNER + STATE :]
-        affinity = dot(out_map, in_map, ((1,), (1,)))
-        wide_ref[r, :] = spread(jnp.exp(cum + before), sel)
-        before = before + cum[SPAN - 1 : SPAN, :]
-        if b:
-            y_ref[r, :] = dot(out_map, state_ref[(b - 1) * STATE : b * STATE, :]) * spread(jnp.exp(cum), sel)
+        affinity = dot(out_maps[b], acts(b, slice(INNER, INNER + STATE)), ((1,), (1,)))
         for pair in range(HEADS // 2):
             cols = slice(pair * LANES, (pair + 1) * LANES)
-            values = act_ref[r, cols]
+            values = acts(b, cols)
             mixing = []
             for h in (2 * pair, 2 * pair + 1):
                 gap = cum[:, h : h + 1] - shifted_ref[h : h + 1, r]
@@ -207,59 +336,22 @@
             stacked = jnp.concatenate(
                 [jnp.where(left, values, zero), jnp.where(left, zero, values)], axis=0
             )
-            y = dot(both, stacked) + skip[:, cols] * values.astype(F32)
-            if b:
-                y = y + y_ref[r, cols]
-            gate = dot(u[r], w_ref[layer, :, cols]).astype(BF16).astype(F32)
-            gate = gate * jax.nn.sigmoid(gate)
-            y_ref[r, cols] = y * gate
-            wide_ref[r, cols] = wide_ref[r, cols] * gate
-
-
-def scan_kernel(got_ref, back_ref):
-    parts, padded, _ = got_ref.shape
-    part_rows = padded - PAD
-    held = max(1, part_rows // HEAD_DIM)
-    size = part_rows // held
-    carry = [jnp.zeros((size, LANES), F32) for _ in range(held)]
-    for d in range(parts):
-        pad = got_ref[d, part_rows:, :].astype(F32)
-        for i in range(held):
-            rows = slice(i * size, (i + 1) * size)
-            back_ref[d, rows, :] = carry[i].astype(BF16)
-            decay = jnp.exp(pad[2 * i : 2 * i + 1, :] + pad[2 * i + 1 : 2 * i + 2, :])
-            carry[i] = decay * carry[i] + got_ref[d, rows, :].astype(F32)
-
-
-def finish_kernel(
-    layer,
-    enter_ref,
-    act_ref,
-    y_ref,
-    wide_ref,
-    resid_ref,
-    w_ref,
-    gain_ref,
-    mods_ref,
-    *rest,
-):
-    hidden_ref, a_ref, normed_ref = rest[-3:]
-    out_map = act_ref[:, INNER + STATE :]
-    chunk = 256
+            y = dot(both, stacked) + skip[:, cols] * values.astype(F32) + y_ref[r, cols]
+            y_ref[r, cols] = y * gate_ref[r, cols]
+
     row = lax.broadcasted_iota(jnp.int32, (chunk, chunk), 0) // HEAD_DIM
     col = lax.broadcasted_iota(jnp.int32, (chunk, chunk), 1) // HEAD_DIM
     same = jnp.where(row == col, 1.0 / HEAD_DIM, 0.0).astype(BF16)
     for c in range(0, INNER, chunk):
         cols = slice(c, c + chunk)
-        carried = dot(out_map, enter_ref[cols, :], ((1,), (1,)))
-        total = y_ref[:, cols] + carried * wide_ref[:, cols]
+        total = y_ref[:, cols]
         square = total * total
         high = square.astype(BF16)
         low = (square - high.astype(F32)).astype(BF16)
         mean = dot(high, same) + dot(low, same)
         gain = gain_ref[layer : layer + 1, cols]
         normed_ref[:, cols] = (total * lax.rsqrt(mean + HEAD_EPS) * gain).astype(BF16)
-    hidden = resid_ref[...].astype(F32) + dot(normed_ref[...], w_ref[layer])
+    hidden = resid_ref[...].astype(F32) + dot(normed_ref[...], wo_ref[layer])
     hidden_ref[...] = hidden
     a_ref[...] = rms_mod(hidden, mods_ref[layer, 2:3, :], mods_ref[layer, 3:4, :])
 
@@ -328,7 +420,7 @@
     if last:
         resid_ref, kv_ref, out_ref = rest
     else:
-        resid_ref, u_ref, tail_ref, kv_ref, out_ref = rest
+        resid_ref, u_ref, kv_ref, out_ref = rest
     rows = q_ref.shape[0]
     half = rows // 2
     kv_ref[...] = dot(prev_ref[...], wm_ref[layer]).astype(BF16)
@@ -348,9 +440,7 @@
     resid = hidden_ref[...] + dot(out_ref[...], merge_ref[layer])
     resid_ref[...] = resid
     if not last:
-        u = rms_mod(resid, mods_ref[layer + 1, 0:1, :], mods_ref[layer + 1, 1:2, :])
-        u_ref[...] = u
-        tail_ref[...] = u[rows - TAIL :]
+        u_ref[...] = rms_mod(resid, mods_ref[layer + 1, 0:1, :], mods_ref[layer + 1, 1:2, :])
 
 
 WHOLE = pl.BlockSpec(memory_space=pltpu.VMEM)
@@ -402,18 +492,18 @@
     spans = rows // SPAN
     parts = lax.axis_size("frames")
     part_rows = INNER // parts
+    mixed = INNER + 2 * STATE
     step_weight = jnp.swapaxes(step_weight, 1, 2)
     step_bias = jnp.swapaxes(step_bias, 1, 2)
     resid = latents.reshape(rows, width)
     (sel,) = run(
         select_kernel, (), [shape((2 * HEADS, INNER), BF16)], name="select", flops=OPENING
     )
-    u, tail, mods, bias, seen = run(
+    u, mods, bias, seen = run(
         first_kernel,
         (sel, resid, modulation, step_bias),
         [
             shape((rows, width), BF16),
-            shape((TAIL, width), BF16),
             shape((LAYERS,) + modulation.shape[2:], F32),
             shape((LAYERS, 8, HEADS), F32),
             shape((rows, 2 * rows), F32),
@@ -423,43 +513,47 @@
         scalars=(timestep, lookback),
     )
     for layer in range(LAYERS):
-        tail = from_behind(tail, "frames")
-        act, cum, shifted, state, send = run(
+        act, own, cum, shifted, edge, state, send = run(
             functools.partial(local_kernel, layer, parts),
-            (u, tail, input_weight, step_weight, conv_weight, bias, decay_log, sel),
+            (u, input_weight, step_weight, conv_weight, bias, decay_log, sel),
             [
-                shape((rows, INNER + 2 * STATE), BF16),
+                shape((rows, mixed), BF16),
+                shape((8, mixed), F32),
                 shape((rows, HEADS), F32),
                 shape((HEADS, rows), F32),
-                shape((max(spans - 1, 1) * STATE, INNER), BF16),
+                shape((TAIL, HEADS), F32),
+                shape((max(spans - 1, 1) * STATE, INNER), F32),
                 shape((parts, part_rows + PAD, LANES), BF16),
             ],
-            [pltpu.VMEM((2, rows + TAIL, 256), F32)],
+            [
+                pltpu.VMEM((2, rows + 2 * TAIL, 256), F32),
+                pltpu.VMEM((8, mixed), F32),
+                pltpu.VMEM((parts, PAD, LANES), F32),
+            ],
             name="local",
-            flops=2 * rows * width * (INNER + 2 * STATE),
-        )
-        y, wide = run(
-            functools.partial(mix_kernel, layer),
-            (u, input_weight, act, cum, shifted, state, skip_gain, sel),
-            [shape((rows, INNER), F32), shape((rows, INNER), F32)],
-            name="mix",
-            flops=2 * rows * width * INNER,
-        )
-        send, y, wide, act = lax.optimization_barrier((send, y, wide, act))
+            flops=2 * rows * width * mixed,
+        )
         got = lax.all_to_all(send, "frames", 0, 0)
         (back,) = run(
             scan_kernel,
             (got,),
-            [shape((parts, part_rows, LANES), BF16)],
+            [shape(got.shape, BF16)],
+            [pltpu.VMEM(((parts + 1) * PAD + 8, LANES), F32)],
             name="scan",
         )
-        enter = lax.all_to_all(back, "frames", 0, 0).reshape(INNER, LANES)
+        enter = lax.all_to_all(back, "frames", 0, 0)
         hidden, a = run(
             functools.partial(finish_kernel, layer),
-            (enter, act, y, wide, resid, output_weight, norm_gain, mods)
+            (u, input_weight, act, own, cum, shifted, edge, state, skip_gain, sel)
+            + (enter, resid, output_weight, norm_gain, mods)
             + (() if layer else (query_weight, memory_weight, merge_weight)),
             [shape((rows, width), F32), shape((rows, width), BF16)],
-            [pltpu.VMEM((rows, INNER), BF16)],
+            [
+                pltpu.VMEM((TAIL, mixed), BF16),
+                pltpu.VMEM((rows, INNER), F32),
+                pltpu.VMEM((rows, INNER), F32),
+                pltpu.VMEM((rows, INNER), BF16),
+            ],
             name="finish",
         )
         prev = from_behind(a, "frames")
@@ -474,7 +568,7 @@
         last = layer == LAYERS - 1
         outs = [shape((rows, width), F32)]
         if not last:
-            outs += [shape((rows, width), BF16), shape((TAIL, width), BF16)]
+            outs += [shape((rows, width), BF16)]
         result = run(
             functools.partial(attend_kernel, layer, last),
             (q, number, total, top, seen, prev, memory_weight, merge_weight, hidden, mods),
@@ -484,7 +578,7 @@
         )
         resid = result[0]
         if not last:
-            u, tail = result[1:]
+            u = result[1]
     return resid.reshape(latents.shape)
 
 

time: 102 us -> 95.2 us (0.933)
  waiting for transfers between devices: 16.3 us -> 8.25 us
  starting transfers between devices: 9.2 us -> 5.29 us
  blocking collectives: 54 us -> 57.7 us
    ppermute x4 -> x2, waiting for transfers between devices: 16.3 us -> 8.25 us  [from_behind(): return lax.ppermute(value, axis, [(i, i + 1) for i in range(count - 1)])]
    ppermute x4 -> x2, starting transfers between devices: 9.2 us -> 5.29 us  [from_behind(): return lax.ppermute(value, axis, [(i, i + 1) for i in range(count - 1)])]
    all_to_all x2, blocking collectives: 25.7 us -> 28.3 us  [shards(): enter = lax.all_to_all(back, 'frames', 0, 0)]
    pallas_call x14 -> x12, Pallas kernels: 20.7 us -> 21.3 us  [run(): pl.pallas_call(kernel, in_specs=[SCALARS] * len(scalars) + [WHOLE] * len(...]
  transfers between devices with their start and end apart: 4 -> 2, of which waited for: 4 -> 2; matrix products, arithmetic and copies ran while one was open for 0% -> 0% of each run, Pallas kernels for 4% -> 4%
where the time goes in v5:
time: 95.2 us; the launch traced here: 94.7 us
  blocking collectives  57.7 us (61%)
  Pallas kernels  21.3 us (22%)
  waiting for transfers between devices  8.25 us (9%)
  starting transfers between devices  5.29 us (6%)
  local copies, waits for them, and re-layouts  1.97 us (2%)
    all_to_all x2, blocking collectives, shards(): got = lax.all_to_all(send, 'frames', 0, 0)  29.4 us
    all_to_all x2, blocking collectives, shards(): enter = lax.all_to_all(back, 'frames', 0, 0)  28.3 us
    pallas_call x12, Pallas kernels, run(): pl.pallas_call(kernel, in_specs=[SCALARS] * len(scalars) + [WHOLE] * len(...  21.3 us
    ppermute x2, waiting for transfers between devices, from_behind(): return lax.ppermute(value, axis, [(i, i + 1) for i in range(count - 1)])  8.25 us
    ppermute x2, starting transfers between devices, from_behind(): return lax.ppermute(value, axis, [(i, i + 1) for i in range(count - 1)])  5.29 us
    unnamed x32, local copies, waits for them, and re-layouts  1.97 us
  transfers between devices with their start and end apart: 2, of which 2 were waited for; matrix products, arithmetic and copies ran while one was open for 0% of the time, Pallas kernels for 4%

profile of v5, /device:TPU:8, one launch (start us, length us, event | category | flops | bytes accessed | tf_op | source)
XLA Modules:
  0.0 94.7 jit_solution(16860162677783999323)
XLA Ops:
  0.0 0.0 copy-start.11
  0.0 0.0 copy-start.10
  0.0 0.0 copy-start.13
  0.0 0.0 copy-start.12
  0.0 0.0 copy-start.4
  0.1 0.0 slice-start
  0.1 0.7 copy-done.11
  0.7 0.3 copy-done.10
  1.0 0.0 copy-done.13
  1.0 0.0 copy-done.12
  1.0 0.1 copy-done.4
  1.1 0.0 slice-start.1
  1.1 0.0 copy-start.5
  1.1 0.0 copy-start.6
  1.1 0.0 copy-start.9
  1.1 0.7 first.1
  1.9 0.6 slice-done
  2.5 0.3 slice-done.1
  2.7 0.0 copy-done.5
  2.8 0.0 copy-done.6
  2.8 0.0 copy-done.9
  2.8 0.0 copy-start
  2.8 0.0 copy-start.2
  2.8 0.0 copy-start.3
  2.8 0.0 copy-start.7
  2.8 0.0 copy-start.8
  2.8 2.7 %local.2 = (bf16[256,1280]{1,0:T(8,128)(2,1)S(1)}, f32[8,1280]{1,0:T(8,128)S(1)}, f32[256,16]{1,0:T(8,128)S(1)}, f32[16,256]{1,0:T(8,128)S(1)}, f32[16,16]{1,0:T...) custom-call(bf16[256,512]{1,0:T(8,128)(2,1)S(1)} %get-tuple-element.37.u_ref, ...), custom_call_target="tpu_custom_call" | custom-call | flops 335544320 | bytes 6703232 | tf_op jit(solution)/shard_map/local/pallas_call | solution.py:452
  5.6 0.0 copy-start.1
  5.6 15.7 %all_to_all.20.got_ref = bf16[16,80,128]{2,1,0:T(8,128)(2,1)S(1)} all-to-all(bf16[16,80,128]{2,1,0:T(8,128)(2,1)S(1)} %get-tuple-element.45), channel_id=1, replica_groups=mesh['groups'=2,'frames'=16] {'frames'}, dimensions={0} | all-to-all | bytes 655360 | tf_op jit(solution)/shard_map/all_to_all | solution.py:536
  21.2 0.5 scan.2
  21.8 14.1 %all_to_all.21.enter_ref = bf16[16,80,128]{2,1,0:T(8,128)(2,1)S(1)} all-to-all(bf16[16,80,128]{2,1,0:T(8,128)(2,1)S(1)} %scan.2), channel_id=1, replica_groups=mesh['groups'=2,'frames'=16] {'frames'}, dimensions={0} | all-to-all | bytes 655360 | tf_op jit(solution)/shard_map/all_to_all | solution.py:544
  35.9 0.0 copy-done
  35.9 0.0 copy-done.2
  35.9 0.0 copy-done.3
  35.9 0.0 copy-done.7
  36.0 0.0 copy-done.8
  36.0 0.0 copy-done.1
  36.0 2.9 %finish.2 = (f32[256,512]{1,0:T(8,128)S(1)}, bf16[256,512]{1,0:T(8,128)(2,1)S(1)}) custom-call(bf16[256,512]{1,0:T(8,128)(2,1)S(1)} %get-tuple-element.37.u_ref, bf16[2,512,2304]{2,1,0:T(8,128)(2,1)S(1)} %bitcast.5, bf16[256,1280]{1,0:T(8,128)(2,1)S(1)} %get-tuple-element.39.act_ref, f32[8,1280]{1,0:T(8,128)S(1)} %get-tuple-element.40.own_ref, ...), custom_call_target="tpu_custom_call" | custom-call | bytes 13993088 | tf_op jit(solution)/shard_map/finish/pallas_call | solution.py:452
  38.9 2.6 %collective-permute-start = (bf16[256,512]{1,0:T(8,128)(2,1)S(1)}, bf16[256,512]{1,0:T(8,128)(2,1)S(1)}, u32[]{:S(2)}, u32[]{:S(2)}) collective-permute-start(bf16[256,512]{1,0:T(8,128)(2,1)S(1)} %get-tuple-element.47.a_ref), channel_id=1, source_target_pairs={{0,1},{1,2},{2,3},{3,4},{4,5},{5,6},{6,7},{7,8},{8,9},{9,10},{10,1... | collective-permute-start | bytes 786440 | tf_op jit(solution)/shard_map/ppermute | solution.py:470
  41.5 1.8 %memory.2 = (bf16[256,512]{1,0:T(8,128)(2,1)S(1)}, f32[256,512]{1,0:T(8,128)S(1)}, f32[256,512]{1,0:T(8,128)S(1)}, f32[256,512]{1,0:T(8,128)S(1)}) custom-call(bf16[256,512]{1,0:T(8,128)(2,1)S(1)} %get-tuple-element.47.a_ref, bf16[2,512,512]{2,1,0:T(8,128)(2,1)S(1)} %copy-done.1, bf16[2,512,1024]{2,1,0:T(8,128)(2,1)S(1)} %copy-done, ...), custom_call_target="tpu_custom_call" | custom-call | flops 402653184 | bytes 5767168 | tf_op jit(solution)/shard_map/memory/pallas_call | solution.py:452
  43.3 4.1 %collective-permute-done.prev_ref = bf16[256,512]{1,0:T(8,128)(2,1)S(1)} collective-permute-done((bf16[256,512]{1,0:T(8,128)(2,1)S(1)}, bf16[256,512]{1,0:T(8,128)(2,1)S(1)}, u32[]{:S(2)}, u32[]{:S(2)}) %collective-permute-start) | collective-permute-done | bytes 262176 | tf_op jit(solution)/shard_map/ppermute | solution.py:470
  47.4 2.0 %attend.2 = (f32[256,512]{1,0:T(8,128)S(1)}, bf16[256,512]{1,0:T(8,128)(2,1)S(1)}) custom-call(bf16[256,512]{1,0:T(8,128)(2,1)S(1)} %get-tuple-element.49.q_ref, f32[256,512]{1,0:T(8,128)S(1)} %get-tuple-element.50.number_ref, f32[256,512]{1,0:T(8,128)S(1)} %get-tuple-element.51.total_ref, f32[256,512]{1,0:T(8,128)S(1)} %get-tuple-element.52.top_ref, ...), custom_call_target="tpu_custom_call" | custom-call | bytes 7094272 | tf_op jit(solution)/shard_map/attend/pallas_call | solution.py:452
  49.4 2.7 %local.3 = (bf16[256,1280]{1,0:T(8,128)(2,1)S(1)}, f32[8,1280]{1,0:T(8,128)S(1)}, f32[256,16]{1,0:T(8,128)S(1)}, f32[16,256]{1,0:T(8,128)S(1)}, f32[16,16]{1,0:T...) custom-call(bf16[256,512]{1,0:T(8,128)(2,1)S(1)} %get-tuple-element.54.u_ref, ...), custom_call_target="tpu_custom_call" | custom-call | flops 335544320 | bytes 6703232 | tf_op jit(solution)/shard_map/local/pallas_call | solution.py:452
  52.2 13.7 %all_to_all.22.got_ref = bf16[16,80,128]{2,1,0:T(8,128)(2,1)S(1)} all-to-all(bf16[16,80,128]{2,1,0:T(8,128)(2,1)S(1)} %get-tuple-element.61), channel_id=1, replica_groups=mesh['groups'=2,'frames'=16] {'frames'}, dimensions={0} | all-to-all | bytes 655360 | tf_op jit(solution)/shard_map/all_to_all | solution.py:536
  65.9 0.5 scan.3
  66.4 14.1 %all_to_all.23.enter_ref = bf16[16,80,128]{2,1,0:T(8,128)(2,1)S(1)} all-to-all(bf16[16,80,128]{2,1,0:T(8,128)(2,1)S(1)} %scan.3), channel_id=1, replica_groups=mesh['groups'=2,'frames'=16] {'frames'}, dimensions={0} | all-to-all | bytes 655360 | tf_op jit(solution)/shard_map/all_to_all | solution.py:544
  80.6 2.8 %finish.3 = (f32[256,512]{1,0:T(8,128)S(1)}, bf16[256,512]{1,0:T(8,128)(2,1)S(1)}) custom-call(bf16[256,512]{1,0:T(8,128)(2,1)S(1)} %get-tuple-element.54.u_ref, bf16[2,512,2304]{2,1,0:T(8,128)(2,1)S(1)} %bitcast.5, bf16[256,1280]{1,0:T(8,128)(2,1)S(1)} %get-tuple-element.55.act_ref, f32[8,1280]{1,0:T(8,128)S(1)} %get-tuple-element.56.own_ref, ...), custom_call_target="tpu_custom_call" | custom-call | bytes 10060928 | tf_op jit(solution)/shard_map/finish/pallas_call | solution.py:452
  83.4 2.6 %collective-permute-start.1 = (bf16[256,512]{1,0:T(8,128)(2,1)S(1)}, bf16[256,512]{1,0:T(8,128)(2,1)S(1)}, u32[]{:S(2)}, u32[]{:S(2)}) collective-permute-start(bf16[256,512]{1,0:T(8,128)(2,1)S(1)} %get-tuple-element.63.a_ref), channel_id=1, source_target_pairs={{0,1},{1,2},{2,3},{3,4},{4,5},{5,6},{6,7},{7,8},{8,9},{9,10},{10,1... | collective-permute-start | bytes 786440 | tf_op jit(solution)/shard_map/ppermute | solution.py:470
  86.1 1.8 %memory.3 = (bf16[256,512]{1,0:T(8,128)(2,1)S(1)}, f32[256,512]{1,0:T(8,128)S(1)}, f32[256,512]{1,0:T(8,128)S(1)}, f32[256,512]{1,0:T(8,128)S(1)}) custom-call(bf16[256,512]{1,0:T(8,128)(2,1)S(1)} %get-tuple-element.63.a_ref, bf16[2,512,512]{2,1,0:T(8,128)(2,1)S(1)} %copy-done.1, bf16[2,512,1024]{2,1,0:T(8,128)(2,1)S(1)} %copy-done, ...), custom_call_target="tpu_custom_call" | custom-call | flops 402653184 | bytes 5767168 | tf_op jit(solution)/shard_map/memory/pallas_call | solution.py:452
  87.9 4.1 %collective-permute-done.1.prev_ref = bf16[256,512]{1,0:T(8,128)(2,1)S(1)} collective-permute-done((bf16[256,512]{1,0:T(8,128)(2,1)S(1)}, bf16[256,512]{1,0:T(8,128)(2,1)S(1)}, u32[]{:S(2)}, u32[]{:S(2)}) %collective-permute-start.1) | collective-permute-done | bytes 262176 | tf_op jit(solution)/shard_map/ppermute | solution.py:470
  92.0 2.7 %attend.3 = f32[256,512]{1,0:T(8,128)} custom-call(bf16[256,512]{1,0:T(8,128)(2,1)S(1)} %get-tuple-element.64.q_ref, f32[256,512]{1,0:T(8,128)S(1)} %get-tuple-element.65.number_ref, f32[256,512]{1,0:T(8,128)S(1)} %get-tuple-element.66.total_ref, f32[256,512]{1,0:T(8,128)S(1)} %get-tuple-element.67.top_ref, f32[256,512]{1,0:T(8,128)S(1)} %get-tuple-element.48.seen_ref, ...), custom_call_target="tpu_custom_call" | custom-call | bytes 6832128 | tf_op jit(solution)/shard_map/attend/pallas_call | solution.py:452
  (2 shorter events, 0.0 us)
Async XLA Ops:
  0.0 0.7 copy-start.11
  0.0 1.0 %copy-start.10 = (bf16[2,50,4,512]{3,2,1,0:T(4,128)(2,1)S(1)}, bf16[2,50,4,512]{3,2,1,0:T(4,128)(2,1)}, u32[]{:S(2)}) copy-start(bf16[2,50,4,512]{3,2,1,0:T(4,128)(2,1)} %all_mods_ref.1) | copy-start | bytes 1228804
  0.0 1.0 %copy-start.13 = (s32[8]{0:T(128)S(1)}, s32[8]{0:T(128)}, u32[]{:S(2)}) copy-start(s32[8]{0:T(128)} %reach_ref.1) | copy-start | bytes 100
  0.0 1.0 %copy-start.12 = (s32[8]{0:T(128)S(1)}, s32[8]{0:T(128)}, u32[]{:S(2)}) copy-start(s32[8]{0:T(128)} %step_ref.1) | copy-start | bytes 100
  0.0 1.1 %copy-start.4 = (bf16[8,32,512]{2,1,0:T(8,128)(2,1)S(1)}, bf16[8,32,512]{2,1,0:T(8,128)(2,1)}, u32[]{:S(2)}) copy-start(bf16[8,32,512]{2,1,0:T(8,128)(2,1)} %param.15) | copy-start | bytes 786436
  0.1 2.4 %slice-start = ((s8[4718592]{0:T(1024)(128)(4,1)}), s8[4194304]{0:T(1024)(128)(4,1)S(1)}, s32[]{:S(2)}) async-start(s8[4718592]{0:T(1024)(128)(4,1)} %bitcast.4), calls=%async_computation.4 | async-start | bytes 8388608
  1.1 1.6 %slice-start.1 = ((s8[4718592]{0:T(1024)(128)(4,1)}), s8[524288]{0:T(1024)(128)(4,1)S(1)}, s32[]{:S(2)}) async-start(s8[4718592]{0:T(1024)(128)(4,1)} %bitcast.4), calls=%async_computation.5 | async-start | bytes 1048576
  1.1 1.6 %copy-start.5 = (f32[2,4,1280]{2,1,0:T(4,128)S(1)}, f32[2,4,1280]{2,1,0:T(4,128)}, u32[]{:S(2)}) copy-start(f32[2,4,1280]{2,1,0:T(4,128)} %conv_ref.3) | copy-start | bytes 122884
  1.1 1.6 %copy-start.6 = (bf16[2,512,16]{1,2,0:T(8,128)(2,1)S(1)}, bf16[2,512,16]{1,2,0:T(8,128)(2,1)}, u32[]{:S(2)}) copy-start(bf16[2,512,16]{1,2,0:T(8,128)(2,1)} %param.20) | copy-start | bytes 98308
  1.1 1.6 %copy-start.9 = (f32[2,16]{1,0:T(2,128)S(1)}, f32[2,16]{1,0:T(2,128)}, u32[]{:S(2)}) copy-start(f32[2,16]{1,0:T(2,128)} %decay_ref.3) | copy-start | bytes 388
  2.8 33.2 %copy-start = (bf16[2,512,1024]{2,1,0:T(8,128)(2,1)S(1)}, bf16[2,512,1024]{2,1,0:T(8,128)(2,1)}, u32[]{:S(2)}) copy-start(bf16[2,512,1024]{2,1,0:T(8,128)(2,1)} %wm_ref.7) | copy-start | bytes 6291460
  2.8 33.2 %copy-start.2 = (bf16[2,512,512]{2,1,0:T(8,128)(2,1)S(1)}, bf16[2,512,512]{2,1,0:T(8,128)(2,1)}, u32[]{:S(2)}) copy-start(bf16[2,512,512]{2,1,0:T(8,128)(2,1)} %merge_ref.3) | copy-start | bytes 3145732
  2.8 33.2 %copy-start.3 = (bf16[2,1024,512]{2,1,0:T(8,128)(2,1)S(1)}, bf16[2,1024,512]{2,1,0:T(8,128)(2,1)}, u32[]{:S(2)}) copy-start(bf16[2,1024,512]{2,1,0:T(8,128)(2,1)} %wo_ref.3) | copy-start | bytes 6291460
  2.8 33.2 %copy-start.7 = (f32[2,1024]{1,0:T(2,128)S(1)}, f32[2,1024]{1,0:T(2,128)}, u32[]{:S(2)}) copy-start(f32[2,1024]{1,0:T(2,128)} %gain_ref.3) | copy-start | bytes 24580
  2.8 33.1 %copy-start.8 = (f32[2,16]{1,0:T(2,128)S(1)}, f32[2,16]{1,0:T(2,128)}, u32[]{:S(2)}) copy-start(f32[2,16]{1,0:T(2,128)} %skip_ref.3) | copy-start | bytes 388
  5.6 30.4 %copy-start.1 = (bf16[2,512,512]{2,1,0:T(8,128)(2,1)S(1)}, bf16[2,512,512]{2,1,0:T(8,128)(2,1)}, u32[]{:S(2)}) copy-start(bf16[2,512,512]{2,1,0:T(8,128)(2,1)} %wq_ref.3) | copy-start | bytes 3145732
  38.9 8.6 %collective-permute-start = (bf16[256,512]{1,0:T(8,128)(2,1)S(1)}, bf16[256,512]{1,0:T(8,128)(2,1)S(1)}, u32[]{:S(2)}, u32[]{:S(2)}) collective-permute-start(bf16[256,512]{1,0:T(8,128)(2,1)S(1)} %get-tuple-element.47.a_ref), channel_id=1, source_target_pairs={{0,1},{1,2},{2,3},{3,4},{4,5},{5,6},{6,7},{7,8},{8,9},{9,10},{10,1... | collective-permute-start | bytes 786440 | tf_op jit(solution)/shard_map/ppermute | solution.py:470
  83.4 8.6 %collective-permute-start.1 = (bf16[256,512]{1,0:T(8,128)(2,1)S(1)}, bf16[256,512]{1,0:T(8,128)(2,1)S(1)}, u32[]{:S(2)}, u32[]{:S(2)}) collective-permute-start(bf16[256,512]{1,0:T(8,128)(2,1)S(1)} %get-tuple-element.63.a_ref), channel_id=1, source_target_pairs={{0,1},{1,2},{2,3},{3,4},{4,5},{5,6},{6,7},{7,8},{8,9},{9,10},{10,1... | collective-permute-start | bytes 786440 | tf_op jit(solution)/shard_map/ppermute | solution.py:470

commit v6 on v5

--- a/solution.py
+++ b/solution.py
@@ -20,6 +20,8 @@
 INNER = HEADS * HEAD_DIM
 ATTN = ATT_HEADS * HEAD_DIM
 PAD = 16
+BLOCK = HEAD_DIM + PAD
+HALF = HEADS // 2
 LANES = 128
 TAIL = 16
 F32 = jnp.float32
@@ -60,6 +62,7 @@
     all_mods_ref,
     all_bias_ref,
     u_ref,
+    tail_ref,
     mods_ref,
     bias_ref,
     seen_ref,
@@ -69,7 +72,9 @@
     step = step_ref[0]
     for layer in range(LAYERS):
         mods_ref[layer] = all_mods_ref[layer, step].astype(F32)
-    u_ref[...] = rms_mod(x_ref[...].astype(F32), mods_ref[0, 0:1, :], mods_ref[0, 1:2, :])
+    u = rms_mod(x_ref[...].astype(F32), mods_ref[0, 0:1, :], mods_ref[0, 1:2, :])
+    u_ref[...] = u
+    tail_ref[...] = u[rows - TAIL :]
     chosen = lax.broadcasted_iota(jnp.int32, (8, all_bias_ref.shape[-1]), 1) == step
     chosen = jnp.where(chosen, 1.0, 0.0).astype(F32)
     for layer in range(LAYERS):
@@ -84,10 +89,14 @@
         seen_ref[f * tok_frame : (f + 1) * tok_frame, :] = jnp.where(seen, 0.0, -1e30)
 
 
+def core_index():
+    return lax.axis_index("frames") % 2
+
+
 def local_kernel(
     layer,
-    parts,
     u_ref,
+    before_ref,
     w_ref,
     sw_ref,
     conv_ref,
@@ -100,14 +109,19 @@
     shifted_ref,
     edge_ref,
     state_ref,
-    send_ref,
+    keep_ref,
+    give_ref,
     ext_ref,
     tail_ref,
     pad_ref,
+    send_ref,
 ):
     rows = u_ref.shape[0]
     u = u_ref[...]
     sel = sel_ref[...]
+    core = core_index()
+    tail_rows = before_ref[...].astype(F32) * core.astype(F32)
+    tail_rows = tail_rows.astype(BF16)
     raw = dot(u, sw_ref[layer], ((1,), (1,))) + bias_ref[layer, 0:1, :]
     step = jnp.maximum(raw, 0.0) + jnp.log1p(jnp.exp(-jnp.abs(raw)))
     log_decay = -jnp.exp(decay_ref[layer : layer + 1, :]) * step
@@ -115,7 +129,7 @@
     q_pos = lax.broadcasted_iota(jnp.int32, (SPAN, SPAN), 0)
     s_pos = lax.broadcasted_iota(jnp.int32, (SPAN, SPAN), 1)
     lower = jnp.where(q_pos >= s_pos, 1.0, 0.0).astype(F32)
-    whole_tokens = lax.broadcasted_iota(jnp.int32, (SPAN, HEADS), 0) >= CONV - 1
+    whole_tokens = lax.broadcasted_iota(jnp.int32, (SPAN, HEADS), 0) >= (CONV - 1) * (1 - core)
     ends, edges = [], []
     for b in range(rows // SPAN):
         r = slice(b * SPAN, (b + 1) * SPAN)
@@ -132,11 +146,11 @@
 
     chunk = 256
     for slot in range(2):
-        ext_ref[slot, 0:TAIL, :] = jnp.zeros((TAIL, chunk), F32)
         ext_ref[slot, TAIL + rows :, :] = jnp.zeros((TAIL, chunk), F32)
     for c in [INNER] + list(range(0, INNER, chunk)):
         w = w_ref[layer, :, INNER + c : INNER + c + chunk]
         slot = c // chunk % 2
+        ext_ref[slot, 0:TAIL, :] = dot(tail_rows, w).astype(BF16).astype(F32)
         ext_ref[slot, TAIL : TAIL + rows, :] = dot(u, w).astype(BF16).astype(F32)
         total, after = None, None
         for k in range(CONV):
@@ -162,39 +176,103 @@
             state_ref[(b - 1) * STATE : b * STATE, :] = state
             state = spread_row(jnp.exp(ends[b]), sel) * state + term
 
-    part_rows = INNER // parts
     for pair in range(HEADS // 2):
         turned = state[:, pair * LANES : (pair + 1) * LANES].T.astype(BF16)
-        for k in range(LANES // part_rows):
-            part = (pair * LANES) // part_rows + k
-            send_ref[part, 0:part_rows, :] = turned[k * part_rows : (k + 1) * part_rows, :]
+        for side in range(2):
+            send_ref[2 * pair + side, 0:HEAD_DIM, :] = turned[side * HEAD_DIM : (side + 1) * HEAD_DIM, :]
     over = sum(ends[1:], ends[0])
     edge = jnp.exp(over - cum_ref[0:8, :]) * step[0:8, :]
     left = lax.broadcasted_iota(jnp.int32, (8, LANES), 1) < HEAD_DIM
     few = CONV - 1
-
-    def halves(value):
-        high = value.astype(BF16).astype(F32)
-        return jnp.where(left, high, value - high)
-
-    for part in range(parts):
-        first = part * part_rows
-        h, at = first // HEAD_DIM, first % HEAD_DIM
+    for h in range(HEADS):
         cols = slice(h // 2 * LANES, (h // 2 + 1) * LANES)
-        side = h % 2 * HEAD_DIM
-        own = pltpu.roll(own_ref[:, cols], (2 * LANES - side - at) % LANES, 1)
-        tail = pltpu.roll(tail_ref[:, cols], (2 * LANES + HEAD_DIM - side) % LANES, 1)
-        if at:
-            own = jnp.where(left, own, 0.0)
-        decay = jnp.broadcast_to(over[:, h : h + 1], (8, LANES))
-        pad_ref[part, 0:1, :] = halves(decay)[0:1, :]
-        pad_ref[part, 1 : 1 + few, :] = jnp.where(left, own, tail)[0:few, :]
-        pad_ref[part, 4 : 4 + few, :] = own_ref[0:few, INNER : INNER + STATE]
-        pad_ref[part, 7 : 7 + few, :] = tail_ref[0:few, INNER : INNER + STATE]
+        own, tail = own_ref[:, cols], tail_ref[:, cols]
+        if h % 2:
+            own = pltpu.roll(own, HEAD_DIM, 1)
+        else:
+            tail = pltpu.roll(tail, HEAD_DIM, 1)
+        pad_ref[h, 0:1, :] = halves(jnp.broadcast_to(over[:, h : h + 1], (8, LANES)))[0:1, :]
+        pad_ref[h, 1 : 1 + few, :] = jnp.where(left, own, tail)[0:few, :]
+        pad_ref[h, 4 : 4 + few, :] = own_ref[0:few, INNER : INNER + STATE]
+        pad_ref[h, 7 : 7 + few, :] = tail_ref[0:few, INNER : INNER + STATE]
         broad = jnp.broadcast_to(edge[:, h : h + 1], (8, LANES))
-        pad_ref[part, 10 : 10 + few, :] = halves(broad)[0:few, :]
-        pad_ref[part, 13 : 13 + few, :] = tail_ref[0:few, INNER + STATE :]
-        send_ref[part, part_rows:, :] = pad_ref[part].astype(BF16)
+        pad_ref[h, 10 : 10 + few, :] = halves(broad)[0:few, :]
+        pad_ref[h, 13 : 13 + few, :] = tail_ref[0:few, INNER + STATE :]
+        send_ref[h, HEAD_DIM:, :] = pad_ref[h].astype(BF16)
+    keep_ref[...] = send_ref[pl.ds(core * HALF, HALF)]
+    give_ref[...] = send_ref[pl.ds((1 - core) * HALF, HALF)]
+
+
+def halves(value):
+    left = lax.broadcasted_iota(jnp.int32, value.shape, 1) < HEAD_DIM
+    high = value.astype(BF16).astype(F32)
+    return jnp.where(left, high, value - high)
+
+
+def joined(value):
+    return value + pltpu.roll(value, HEAD_DIM, 1)
+
+
+def chip_kernel(keep_ref, got_ref, send_ref, pair_ref):
+    parts, padded, _ = send_ref.shape
+    part_rows = padded - PAD
+    core = core_index()
+    pair_ref[core] = keep_ref[...]
+    pair_ref[1 - core] = got_ref[...]
+    row = lax.broadcasted_iota(jnp.int32, (PAD, LANES), 0)
+    left = lax.broadcasted_iota(jnp.int32, (PAD, LANES), 1) < HEAD_DIM
+    for h in range(HALF):
+        one = pair_ref[0, h, HEAD_DIM:, :].astype(F32)
+        two = pair_ref[1, h, HEAD_DIM:, :].astype(F32)
+        one_sum, two_sum = joined(one), joined(two)
+        decay = jnp.exp(two_sum[0:1, :])
+        state = decay * pair_ref[0, h, 0:HEAD_DIM, :].astype(F32) + pair_ref[
+            1, h, 0:HEAD_DIM, :
+        ].astype(F32)
+        state = state.astype(BF16)
+        exact = halves(jnp.where(row == 0, one_sum + two_sum, one_sum * decay))
+        for k in range(HEAD_DIM // part_rows):
+            at = k * part_rows
+            own = pltpu.roll(jnp.where(left, one, 0.0), LANES - at, 1) if at else one
+            pad = jnp.where(row < 4, jnp.where(left, own, two), jnp.where(row < 7, one, two))
+            pad = jnp.where((row == 0) | ((row >= 10) & (row < 13)), exact, pad)
+            part = h * (HEAD_DIM // part_rows) + k
+            send_ref[part, 0:part_rows, :] = state[at : at + part_rows, :]
+            send_ref[part, part_rows:, :] = pad.astype(BF16)
+
+
+def enter_kernel(keep_ref, got_ref, back_ref, mine_ref, give_ref, pair_ref, enter_ref, pad_ref):
+    parts, padded, _ = back_ref.shape
+    part_rows = padded - PAD
+    each = HEAD_DIM // part_rows
+    core = core_index()
+    pair_ref[core] = keep_ref[...]
+    pair_ref[1 - core] = got_ref[...]
+    few = lax.broadcasted_iota(jnp.int32, (8, LANES), 0) < CONV - 1
+    for h in range(HALF):
+        pad = back_ref[h * each, part_rows:, :]
+        pad_ref[2 * h] = pad.astype(F32)
+        pad_ref[2 * h + 1] = pair_ref[0, h, HEAD_DIM:, :].astype(F32)
+    for h in range(HALF):
+        last, mine = 2 * h, 2 * h + 1
+        entering = jnp.concatenate(
+            [back_ref[h * each + k, 0:part_rows, :] for k in range(each)], axis=0
+        )
+        values = silu(pad_ref[mine, 1:9, :] + pltpu.roll(pad_ref[last, 1:9, :], HEAD_DIM, 1))
+        in_map = silu(pad_ref[mine, 4:12, :] + pad_ref[last, 7:15, :])
+        edge = joined(pad_ref[mine, 8:16, :])
+        edge = pltpu.roll(edge, 6, 0)
+        scaled = jnp.where(few, values.astype(BF16).astype(F32) * edge, 0.0)
+        added = dot(scaled, jnp.where(few, in_map, 0.0), ((0,), (0,)))[0:HEAD_DIM, :]
+        decay = jnp.exp(joined(pad_ref[mine, 0:8, :])[0:1, :])
+        after = decay * entering.astype(F32) + pair_ref[0, h, 0:HEAD_DIM, :].astype(F32) + added
+        pad = back_ref[h * each, part_rows:, :]
+        enter_ref[0, h, 0:HEAD_DIM, :] = entering
+        enter_ref[1, h, 0:HEAD_DIM, :] = after.astype(BF16)
+        enter_ref[0, h, HEAD_DIM:, :] = pad
+        enter_ref[1, h, HEAD_DIM:, :] = pad
+    mine_ref[...] = enter_ref[core]
+    give_ref[...] = enter_ref[1 - core]
 
 
 def silu(x):
@@ -205,7 +283,7 @@
     parts, padded, _ = got_ref.shape
     part_rows = padded - PAD
     rows = slice(0, part_rows)
-    offset = lax.axis_index("frames") * part_rows % HEAD_DIM
+    offset = lax.axis_index("frames") // 2 * part_rows % HEAD_DIM
     few = lax.broadcasted_iota(jnp.int32, (8, LANES), 0) < CONV - 1
     left = lax.broadcasted_iota(jnp.int32, (8, LANES), 1) < HEAD_DIM
     pad_ref[0:PAD, :] = jnp.zeros((PAD, LANES), F32)
@@ -244,17 +322,20 @@
     state_ref,
     skip_ref,
     sel_ref,
-    enter_ref,
+    mine_ref,
+    other_ref,
     resid_ref,
     wo_ref,
     gain_ref,
     mods_ref,
     *rest,
 ):
-    hidden_ref, a_ref, first_ref, y_ref, gate_ref, normed_ref = rest[-6:]
+    hidden_ref, a_ref, first_ref, y_ref, gate_ref, normed_ref, enter_ref = rest[-7:]
     rows = u_ref.shape[0]
-    parts, padded, _ = enter_ref.shape
-    part_rows = padded - PAD
+    core = core_index()
+    enter_ref[pl.ds(core * HALF, HALF)] = mine_ref[...]
+    enter_ref[pl.ds((1 - core) * HALF, HALF)] = other_ref[...]
+    start = (1 - core).astype(F32)
     u = u_ref[...]
     sel = sel_ref[...]
     lane = lax.broadcasted_iota(jnp.int32, (SPAN, LANES), 1)
@@ -263,19 +344,19 @@
     nothing = jnp.zeros((TAIL - 8, LANES), F32)
 
     def fixed(cols, tail):
-        total = jnp.concatenate([own_ref[:, cols] + tail[0:8, :], nothing], axis=0)
+        total = jnp.concatenate([own_ref[:, cols] + start * tail[0:8, :], nothing], axis=0)
         first_ref[:, cols] = jnp.where(
             few, silu(total), act_ref[0:TAIL, cols].astype(F32)
         ).astype(BF16)
 
     for pair in range(HEADS // 2):
         pads = [
-            enter_ref[h * HEAD_DIM // part_rows, part_rows:, :].astype(F32)
+            enter_ref[h, HEAD_DIM:, :].astype(F32)
             for h in (2 * pair, 2 * pair + 1)
         ]
         tail = jnp.where(left[0:PAD], pltpu.roll(pads[0], HEAD_DIM, 1), pads[1])
         fixed(slice(pair * LANES, (pair + 1) * LANES), pltpu.roll(tail, PAD - 1, 0))
-    common = enter_ref[0, part_rows:, :].astype(F32)
+    common = enter_ref[0, HEAD_DIM:, :].astype(F32)
     fixed(slice(INNER, INNER + STATE), pltpu.roll(common, PAD - 7, 0))
     fixed(slice(INNER + STATE, INNER + 2 * STATE), pltpu.roll(common, PAD - 13, 0))
 
@@ -285,7 +366,7 @@
         return jnp.concatenate([first_ref[:, cols], act_ref[TAIL:SPAN, cols]], axis=0)
 
     first_tokens = lax.broadcasted_iota(jnp.int32, (TAIL, HEADS), 0) < CONV - 1
-    early = spread(jnp.where(first_tokens, edge_ref[...], 0.0), sel)
+    early = spread(jnp.where(first_tokens, edge_ref[...], 0.0) * start, sel)
     early = (first_ref[:, 0:INNER].astype(F32) * early).astype(BF16)
     late = dot(first_ref[:, INNER : INNER + STATE], early, ((0,), (0,)))
 
@@ -304,7 +385,7 @@
         cols = slice(c, c + chunk)
         gate_ref[:, cols] = silu(dot(u, w_ref[layer, :, cols]).astype(BF16).astype(F32))
         entering = jnp.concatenate(
-            [enter_ref[p, 0:part_rows, :] for p in range(c // part_rows, (c + chunk) // part_rows)],
+            [enter_ref[h, 0:HEAD_DIM, :] for h in range(c // HEAD_DIM, (c + chunk) // HEAD_DIM)],
             axis=0,
         )
         y_ref[:, cols] = dot(out_map, entering, ((1,), (1,))) * wide[:, cols]
@@ -420,7 +501,7 @@
     if last:
         resid_ref, kv_ref, out_ref = rest
     else:
-        resid_ref, u_ref, kv_ref, out_ref = rest
+        resid_ref, u_ref, tail_ref, kv_ref, out_ref = rest
     rows = q_ref.shape[0]
     half = rows // 2
     kv_ref[...] = dot(prev_ref[...], wm_ref[layer]).astype(BF16)
@@ -440,7 +521,9 @@
     resid = hidden_ref[...] + dot(out_ref[...], merge_ref[layer])
     resid_ref[...] = resid
     if not last:
-        u_ref[...] = rms_mod(resid, mods_ref[layer + 1, 0:1, :], mods_ref[layer + 1, 1:2, :])
+        u = rms_mod(resid, mods_ref[layer + 1, 0:1, :], mods_ref[layer + 1, 1:2, :])
+        u_ref[...] = u
+        tail_ref[...] = u[rows - TAIL :]
 
 
 WHOLE = pl.BlockSpec(memory_space=pltpu.VMEM)
@@ -463,6 +546,17 @@
 
 def shape(dims, dtype):
     return jax.ShapeDtypeStruct(dims, dtype)
+
+
+def swapped(value, axis):
+    count = lax.axis_size(axis)
+    return lax.ppermute(value, axis, [(i, i ^ 1) for i in range(count)])
+
+
+def over_chips(value, axis):
+    count = lax.axis_size(axis)
+    groups = [list(range(core, count, 2)) for core in range(2)]
+    return lax.all_to_all(value, axis, 0, 0, axis_index_groups=groups)
 
 
 def from_behind(value, axis):
@@ -490,8 +584,8 @@
     frames_dev, tok_frame, width = latents.shape
     rows = frames_dev * tok_frame
     spans = rows // SPAN
-    parts = lax.axis_size("frames")
-    part_rows = INNER // parts
+    parts = lax.axis_size("frames") // 2
+    part_rows = HALF * HEAD_DIM // parts
     mixed = INNER + 2 * STATE
     step_weight = jnp.swapaxes(step_weight, 1, 2)
     step_bias = jnp.swapaxes(step_bias, 1, 2)
@@ -499,11 +593,12 @@
     (sel,) = run(
         select_kernel, (), [shape((2 * HEADS, INNER), BF16)], name="select", flops=OPENING
     )
-    u, mods, bias, seen = run(
+    u, tail, mods, bias, seen = run(
         first_kernel,
         (sel, resid, modulation, step_bias),
         [
             shape((rows, width), BF16),
+            shape((TAIL, width), BF16),
             shape((LAYERS,) + modulation.shape[2:], F32),
             shape((LAYERS, 8, HEADS), F32),
             shape((rows, 2 * rows), F32),
@@ -513,9 +608,10 @@
         scalars=(timestep, lookback),
     )
     for layer in range(LAYERS):
-        act, own, cum, shifted, edge, state, send = run(
-            functools.partial(local_kernel, layer, parts),
-            (u, input_weight, step_weight, conv_weight, bias, decay_log, sel),
+        before = swapped(tail, "frames")
+        act, own, cum, shifted, edge, state, keep, give = run(
+            functools.partial(local_kernel, layer),
+            (u, before, input_weight, step_weight, conv_weight, bias, decay_log, sel),
             [
                 shape((rows, mixed), BF16),
                 shape((8, mixed), F32),
@@ -523,29 +619,49 @@
                 shape((HEADS, rows), F32),
                 shape((TAIL, HEADS), F32),
                 shape((max(spans - 1, 1) * STATE, INNER), F32),
-                shape((parts, part_rows + PAD, LANES), BF16),
+                shape((HALF, BLOCK, LANES), BF16),
+                shape((HALF, BLOCK, LANES), BF16),
             ],
             [
                 pltpu.VMEM((2, rows + 2 * TAIL, 256), F32),
                 pltpu.VMEM((8, mixed), F32),
-                pltpu.VMEM((parts, PAD, LANES), F32),
+                pltpu.VMEM((HEADS, PAD, LANES), F32),
+                pltpu.VMEM((HEADS, BLOCK, LANES), BF16),
             ],
             name="local",
             flops=2 * rows * width * mixed,
         )
-        got = lax.all_to_all(send, "frames", 0, 0)
+        got = swapped(give, "frames")
+        (send,) = run(
+            chip_kernel,
+            (keep, got),
+            [shape((parts, part_rows + PAD, LANES), BF16)],
+            [pltpu.VMEM((2, HALF, BLOCK, LANES), BF16)],
+            name="chip",
+        )
         (back,) = run(
             scan_kernel,
-            (got,),
-            [shape(got.shape, BF16)],
+            (over_chips(send, "frames"),),
+            [shape(send.shape, BF16)],
             [pltpu.VMEM(((parts + 1) * PAD + 8, LANES), F32)],
             name="scan",
         )
-        enter = lax.all_to_all(back, "frames", 0, 0)
+        mine, give = run(
+            enter_kernel,
+            (keep, got, over_chips(back, "frames")),
+            [shape(keep.shape, BF16)] * 2,
+            [
+                pltpu.VMEM((2, HALF, BLOCK, LANES), BF16),
+                pltpu.VMEM((2, HALF, BLOCK, LANES), BF16),
+                pltpu.VMEM((HEADS, PAD, LANES), F32),
+            ],
+            name="enter",
+        )
+        other = swapped(give, "frames")
         hidden, a = run(
             functools.partial(finish_kernel, layer),
             (u, input_weight, act, own, cum, shifted, edge, state, skip_gain, sel)
-            + (enter, resid, output_weight, norm_gain, mods)
+            + (mine, other, resid, output_weight, norm_gain, mods)
             + (() if layer else (query_weight, memory_weight, merge_weight)),
             [shape((rows, width), F32), shape((rows, width), BF16)],
             [
@@ -553,6 +669,7 @@
                 pltpu.VMEM((rows, INNER), F32),
                 pltpu.VMEM((rows, INNER), F32),
                 pltpu.VMEM((rows, INNER), BF16),
+                pltpu.VMEM((HEADS, BLOCK, LANES), BF16),
             ],
             name="finish",
         )
@@ -568,7 +685,7 @@
         last = layer == LAYERS - 1
         outs = [shape((rows, width), F32)]
         if not last:
-            outs += [shape((rows, width), BF16)]
+            outs += [shape((rows, width), BF16), shape((TAIL, width), BF16)]
         result = run(
             functools.partial(attend_kernel, layer, last),
             (q, number, total, top, seen, prev, memory_weight, merge_weight, hidden, mods),
@@ -578,7 +695,7 @@
         )
         resid = result[0]
         if not last:
-            u = result[1]
+            u, tail = result[1:]
     return resid.reshape(latents.shape)
 
 

time: 95.2 us -> 88.3 us (0.928)
  blocking collectives: 57.7 us -> 41.9 us
  waiting for transfers between devices: 8.25 us -> 16.8 us
  Pallas kernels: 21.3 us -> 22.8 us
    all_to_all x4, blocking collectives: 57.7 us -> 41.9 us  [over_chips(): return lax.all_to_all(value, axis, 0, 0, axis_index_groups=groups)]
    ppermute x0 -> x6, waiting for transfers between devices: none -> 7.54 us  [swapped(): return lax.ppermute(value, axis, [(i, i ^ 1) for i in range(count)])]
    pallas_call x12 -> x16, Pallas kernels: 21.3 us -> 22.8 us  [run(): pl.pallas_call(kernel, in_specs=[SCALARS] * len(scalars) + [WHOLE] * len(...]
    ppermute x2, waiting for transfers between devices: 8.25 us -> 9.29 us  [from_behind(): return lax.ppermute(value, axis, [(i, i + 1) for i in range(count - 1)])]
    ppermute x2, starting transfers between devices: 5.29 us -> 4.27 us  [from_behind(): return lax.ppermute(value, axis, [(i, i + 1) for i in range(count - 1)])]
  transfers between devices with their start and end apart: 2 -> 8, of which waited for: 2 -> 8; matrix products, arithmetic and copies ran while one was open for 0% -> 0% of each run, Pallas kernels for 4% -> 4%
where the time goes in v6:
time: 88.3 us; the launch traced here: 87.9 us
  blocking collectives  41.9 us (47%)
  Pallas kernels  22.8 us (26%)
  waiting for transfers between devices  16.8 us (19%)
  starting transfers between devices  5.03 us (6%)
  local copies, waits for them, and re-layouts  1.12 us (1%)
    all_to_all x4, blocking collectives, over_chips(): return lax.all_to_all(value, axis, 0, 0, axis_index_groups=groups)  41.9 us
    pallas_call x16, Pallas kernels, run(): pl.pallas_call(kernel, in_specs=[SCALARS] * len(scalars) + [WHOLE] * len(...  22.8 us
    ppermute x2, waiting for transfers between devices, from_behind(): return lax.ppermute(value, axis, [(i, i + 1) for i in range(count - 1)])  9.29 us
    ppermute x6, waiting for transfers between devices, swapped(): return lax.ppermute(value, axis, [(i, i ^ 1) for i in range(count)])  7.54 us
    ppermute x2, starting transfers between devices, from_behind(): return lax.ppermute(value, axis, [(i, i + 1) for i in range(count - 1)])  4.27 us
  transfers between devices with their start and end apart: 8, of which 8 were waited for; matrix products, arithmetic and copies ran while one was open for 0% of the time, Pallas kernels for 4%

profile of v6, /device:TPU:8, one launch (start us, length us, event | category | flops | bytes accessed | tf_op | source)
XLA Modules:
  0.0 87.9 jit_solution(2522692957480913577)
XLA Ops:
  0.0 0.0 copy-start.11
  0.0 0.0 copy-start.13
  0.0 0.0 copy-start.12
  0.0 0.0 copy-start.4
  0.1 0.0 slice-start
  0.1 0.7 copy-done.11
  0.7 0.3 copy-done.10
  1.0 0.0 copy-done.13
  1.0 0.0 copy-done.12
  1.0 0.1 copy-done.4
  1.1 0.0 copy-start.5
  1.1 0.0 copy-start.6
  1.1 0.0 copy-start.9
  1.1 0.7 first.1
  1.9 0.1 collective-permute-start
  2.0 1.2 %collective-permute-done.before_ref = bf16[16,512]{1,0:T(8,128)(2,1)S(1)} collective-permute-done((bf16[16,512]{1,0:T(8,128)(2,1)S(1)}, bf16[16,512]{1,0:T(8,128)(2,1)S(1)}, u32[]{:S(2)}, u32[]{:S(2)}) %collective-permute-start) | collective-permute-done | bytes 16416 | tf_op jit(solution)/shard_map/ppermute | solution.py:553
  3.1 0.0 slice-done
  3.1 0.0 slice-done.1
  3.1 0.0 copy-done.5
  3.1 0.0 copy-done.6
  3.2 0.0 copy-done.9
  3.2 0.0 copy-start
  3.2 0.0 copy-start.2
  3.2 0.0 copy-start.3
  3.2 0.0 copy-start.7
  3.2 0.0 copy-start.8
  3.2 3.0 %local.2 = (bf16[256,1280]{1,0:T(8,128)(2,1)S(1)}, f32[8,1280]{1,0:T(8,128)S(1)}, f32[256,16]{1,0:T(8,128)S(1)}, f32[16,256]{1,0:T(8,128)S(1)}, f32[16,16]{1,0:T...) custom-call(bf16[256,512]{1,0:T(8,128)(2,1)S(1)} %get-tuple-element.45.u_ref,, ...), custom_call_target="tpu_custom_call" | custom-call | flops 335544320 | bytes 6719616 | tf_op jit(solution)/shard_map/local/pallas_call | solution.py:535
  6.2 0.2 collective-permute-start.1
  6.5 1.2 %collective-permute-done.1.got_ref = bf16[8,80,128]{2,1,0:T(8,128)(2,1)S(1)} collective-permute-done((bf16[8,80,128]{2,1,0:T(8,128)(2,1)S(1)}, bf16[8,80,128]{2,1,0:T(8,128)(2,1)S(1)}, u32[]{:S(2)}, u32[]{:S(2)}) %collective-permute-start.1) | collective-permute-done | bytes 163872 | tf_op jit(solution)/shard_map/ppermute | solution.py:553
  7.7 0.1 chip.2
  7.8 11.8 %all_to_all.20.got_ref = bf16[8,80,128]{2,1,0:T(8,128)(2,1)S(1)} all-to-all(bf16[8,80,128]{2,1,0:T(8,128)(2,1)S(1)} %chip.2), channel_id=1, replica_groups={{0,2,4,6,8,10,12,14},{1,3,5,7,9,11,13,15},{16,18,20,22,24,26,28,30},{17..., dimensions={0} | all-to-all | bytes 327680 | tf_op jit(solution)/shard_map/all_to_all | solution.py:559
  19.6 0.4 scan.2
  20.0 10.3 %all_to_all.21.back_ref = bf16[8,80,128]{2,1,0:T(8,128)(2,1)S(1)} all-to-all(bf16[8,80,128]{2,1,0:T(8,128)(2,1)S(1)} %scan.2), channel_id=1, replica_groups={{0,2,4,6,8,10,12,14},{1,3,5,7,9,11,13,15},{16,18,20,22,24,26,28,30},{17..., dimensions={0} | all-to-all | bytes 327680 | tf_op jit(solution)/shard_map/all_to_all | solution.py:559
  30.3 0.5 enter.2
  30.7 0.1 collective-permute-start.2
  30.8 1.4 %collective-permute-done.2.other_ref = bf16[8,80,128]{2,1,0:T(8,128)(2,1)S(1)} collective-permute-done((bf16[8,80,128]{2,1,0:T(8,128)(2,1)S(1)}, bf16[8,80,128]{2,1,0:T(8,128)(2,1)S(1)}, u32[]{:S(2)}, u32[]{:S(2)}) %collective-permute-start.2) | collective-permute-done | bytes 163872 | tf_op jit(solution)/shard_map/ppermute | solution.py:553
  32.2 0.0 copy-done
  32.2 0.0 copy-done.2
  32.2 0.0 copy-done.3
  32.2 0.0 copy-done.7
  32.2 0.0 copy-done.8
  32.2 0.0 copy-done.1
  32.2 2.9 %finish.2 = (f32[256,512]{1,0:T(8,128)S(1)}, bf16[256,512]{1,0:T(8,128)(2,1)S(1)}) custom-call(bf16[256,512]{1,0:T(8,128)(2,1)S(1)} %get-tuple-element.45.u_ref, bf16[2,512,2304]{2,1,0:T(8,128)(2,1)S(1)} %bitcast.5, bf16[256,1280]{1,0:T(8,128)(2,1)S(1)} %get-tuple-element.48.act_ref, f32[8,1280]{1,0:T(8,128)S(1)} %get-tuple-element.49.own_ref, ...), custom_call_target="tpu_custom_call" | custom-call | bytes 13993088 | tf_op jit(solution)/shard_map/finish/pallas_call | solution.py:535
  35.1 2.2 %collective-permute-start.3 = (bf16[256,512]{1,0:T(8,128)(2,1)S(1)}, bf16[256,512]{1,0:T(8,128)(2,1)S(1)}, u32[]{:S(2)}, u32[]{:S(2)}) collective-permute-start(bf16[256,512]{1,0:T(8,128)(2,1)S(1)} %get-tuple-element.59.a_ref), channel_id=1, source_target_pairs={{0,1},{1,2},{2,3},{3,4},{4,5},{5,6},{6,7},{7,8},{8,9},{9,10},{10,1... | collective-permute-start | bytes 786440 | tf_op jit(solution)/shard_map/ppermute | solution.py:564
  37.4 1.8 %memory.2 = (bf16[256,512]{1,0:T(8,128)(2,1)S(1)}, f32[256,512]{1,0:T(8,128)S(1)}, f32[256,512]{1,0:T(8,128)S(1)}, f32[256,512]{1,0:T(8,128)S(1)}) custom-call(bf16[256,512]{1,0:T(8,128)(2,1)S(1)} %get-tuple-element.59.a_ref, bf16[2,512,512]{2,1,0:T(8,128)(2,1)S(1)} %copy-done.1, bf16[2,512,1024]{2,1,0:T(8,128)(2,1)S(1)} %copy-done, ...), custom_call_target="tpu_custom_call" | custom-call | flops 402653184 | bytes 5767168 | tf_op jit(solution)/shard_map/memory/pallas_call | solution.py:535
  39.2 4.6 %collective-permute-done.3.prev_ref = bf16[256,512]{1,0:T(8,128)(2,1)S(1)} collective-permute-done((bf16[256,512]{1,0:T(8,128)(2,1)S(1)}, bf16[256,512]{1,0:T(8,128)(2,1)S(1)}, u32[]{:S(2)}, u32[]{:S(2)}) %collective-permute-start.3) | collective-permute-done | bytes 262176 | tf_op jit(solution)/shard_map/ppermute | solution.py:564
  43.7 2.0 %attend.2 = (f32[256,512]{1,0:T(8,128)S(1)}, bf16[256,512]{1,0:T(8,128)(2,1)S(1)}, bf16[16,512]{1,0:T(8,128)(2,1)S(1)}) custom-call(bf16[256,512]{1,0:T(8,128)(2,1)S(1)} %get-tuple-element.61.q_ref, f32[256,512]{1,0:T(8,128)S(1)} %get-tuple-element.62.number_ref, f32[256,512]{1,0:T(8,128)S(1)} %get-tuple-element.63.total_ref, ...), custom_call_target="tpu_custom_call" | custom-call | bytes 7110656 | tf_op jit(solution)/shard_map/attend/pallas_call | solution.py:535
  45.7 0.1 collective-permute-start.4
  45.8 1.2 %collective-permute-done.4.before_ref = bf16[16,512]{1,0:T(8,128)(2,1)S(1)} collective-permute-done((bf16[16,512]{1,0:T(8,128)(2,1)S(1)}, bf16[16,512]{1,0:T(8,128)(2,1)S(1)}, u32[]{:S(2)}, u32[]{:S(2)}) %collective-permute-start.4) | collective-permute-done | bytes 16416 | tf_op jit(solution)/shard_map/ppermute | solution.py:553
  47.0 3.0 %local.3 = (bf16[256,1280]{1,0:T(8,128)(2,1)S(1)}, f32[8,1280]{1,0:T(8,128)S(1)}, f32[256,16]{1,0:T(8,128)S(1)}, f32[16,256]{1,0:T(8,128)S(1)}, f32[16,16]{1,0:T...) custom-call(bf16[256,512]{1,0:T(8,128)(2,1)S(1)} %get-tuple-element.66.u_ref,, ...), custom_call_target="tpu_custom_call" | custom-call | flops 335544320 | bytes 6719616 | tf_op jit(solution)/shard_map/local/pallas_call | solution.py:535
  50.0 0.2 collective-permute-start.5
  50.2 1.2 %collective-permute-done.5.got_ref = bf16[8,80,128]{2,1,0:T(8,128)(2,1)S(1)} collective-permute-done((bf16[8,80,128]{2,1,0:T(8,128)(2,1)S(1)}, bf16[8,80,128]{2,1,0:T(8,128)(2,1)S(1)}, u32[]{:S(2)}, u32[]{:S(2)}) %collective-permute-start.5) | collective-permute-done | bytes 163872 | tf_op jit(solution)/shard_map/ppermute | solution.py:553
  51.4 0.1 chip.3
  51.6 9.6 %all_to_all.22.got_ref = bf16[8,80,128]{2,1,0:T(8,128)(2,1)S(1)} all-to-all(bf16[8,80,128]{2,1,0:T(8,128)(2,1)S(1)} %chip.3), channel_id=1, replica_groups={{0,2,4,6,8,10,12,14},{1,3,5,7,9,11,13,15},{16,18,20,22,24,26,28,30},{17..., dimensions={0} | all-to-all | bytes 327680 | tf_op jit(solution)/shard_map/all_to_all | solution.py:559
  61.2 0.4 scan.3
  61.6 10.3 %all_to_all.23.back_ref = bf16[8,80,128]{2,1,0:T(8,128)(2,1)S(1)} all-to-all(bf16[8,80,128]{2,1,0:T(8,128)(2,1)S(1)} %scan.3), channel_id=1, replica_groups={{0,2,4,6,8,10,12,14},{1,3,5,7,9,11,13,15},{16,18,20,22,24,26,28,30},{17..., dimensions={0} | all-to-all | bytes 327680 | tf_op jit(solution)/shard_map/all_to_all | solution.py:559
  71.9 0.5 enter.3
  72.3 0.1 collective-permute-start.6
  72.4 1.4 %collective-permute-done.6.other_ref = bf16[8,80,128]{2,1,0:T(8,128)(2,1)S(1)} collective-permute-done((bf16[8,80,128]{2,1,0:T(8,128)(2,1)S(1)}, bf16[8,80,128]{2,1,0:T(8,128)(2,1)S(1)}, u32[]{:S(2)}, u32[]{:S(2)}) %collective-permute-start.6) | collective-permute-done | bytes 163872 | tf_op jit(solution)/shard_map/ppermute | solution.py:553
  73.8 2.9 %finish.3 = (f32[256,512]{1,0:T(8,128)S(1)}, bf16[256,512]{1,0:T(8,128)(2,1)S(1)}) custom-call(bf16[256,512]{1,0:T(8,128)(2,1)S(1)} %get-tuple-element.66.u_ref, bf16[2,512,2304]{2,1,0:T(8,128)(2,1)S(1)} %bitcast.5, bf16[256,1280]{1,0:T(8,128)(2,1)S(1)} %get-tuple-element.68.act_ref, f32[8,1280]{1,0:T(8,128)S(1)} %get-tuple-element.69.own_ref, ...), custom_call_target="tpu_custom_call" | custom-call | bytes 10060928 | tf_op jit(solution)/shard_map/finish/pallas_call | solution.py:535
  76.7 2.0 %collective-permute-start.7 = (bf16[256,512]{1,0:T(8,128)(2,1)S(1)}, bf16[256,512]{1,0:T(8,128)(2,1)S(1)}, u32[]{:S(2)}, u32[]{:S(2)}) collective-permute-start(bf16[256,512]{1,0:T(8,128)(2,1)S(1)} %get-tuple-element.79.a_ref), channel_id=1, source_target_pairs={{0,1},{1,2},{2,3},{3,4},{4,5},{5,6},{6,7},{7,8},{8,9},{9,10},{10,1... | collective-permute-start | bytes 786440 | tf_op jit(solution)/shard_map/ppermute | solution.py:564
  78.7 1.8 %memory.3 = (bf16[256,512]{1,0:T(8,128)(2,1)S(1)}, f32[256,512]{1,0:T(8,128)S(1)}, f32[256,512]{1,0:T(8,128)S(1)}, f32[256,512]{1,0:T(8,128)S(1)}) custom-call(bf16[256,512]{1,0:T(8,128)(2,1)S(1)} %get-tuple-element.79.a_ref, bf16[2,512,512]{2,1,0:T(8,128)(2,1)S(1)} %copy-done.1, bf16[2,512,1024]{2,1,0:T(8,128)(2,1)S(1)} %copy-done, ...), custom_call_target="tpu_custom_call" | custom-call | flops 402653184 | bytes 5767168 | tf_op jit(solution)/shard_map/memory/pallas_call | solution.py:535
  80.5 4.7 %collective-permute-done.7.prev_ref = bf16[256,512]{1,0:T(8,128)(2,1)S(1)} collective-permute-done((bf16[256,512]{1,0:T(8,128)(2,1)S(1)}, bf16[256,512]{1,0:T(8,128)(2,1)S(1)}, u32[]{:S(2)}, u32[]{:S(2)}) %collective-permute-start.7) | collective-permute-done | bytes 262176 | tf_op jit(solution)/shard_map/ppermute | solution.py:564
  85.3 2.7 %attend.3 = f32[256,512]{1,0:T(8,128)} custom-call(bf16[256,512]{1,0:T(8,128)(2,1)S(1)} %get-tuple-element.80.q_ref, f32[256,512]{1,0:T(8,128)S(1)} %get-tuple-element.81.number_ref, f32[256,512]{1,0:T(8,128)S(1)} %get-tuple-element.82.total_ref, f32[256,512]{1,0:T(8,128)S(1)} %get-tuple-element.83.top_ref, f32[256,512]{1,0:T(8,128)S(1)} %get-tuple-element.60.seen_ref, ...), custom_call_target="tpu_custom_call" | custom-call | bytes 6832128 | tf_op jit(solution)/shard_map/attend/pallas_call | solution.py:535
  (5 shorter events, 0.0 us)
Async XLA Ops:
  0.0 0.7 copy-start.11
  0.0 1.0 %copy-start.10 = (bf16[2,50,4,512]{3,2,1,0:T(4,128)(2,1)S(1)}, bf16[2,50,4,512]{3,2,1,0:T(4,128)(2,1)}, u32[]{:S(2)}) copy-start(bf16[2,50,4,512]{3,2,1,0:T(4,128)(2,1)} %all_mods_ref.1) | copy-start | bytes 1228804
  0.0 1.0 %copy-start.13 = (s32[8]{0:T(128)S(1)}, s32[8]{0:T(128)}, u32[]{:S(2)}) copy-start(s32[8]{0:T(128)} %reach_ref.1) | copy-start | bytes 100
  0.0 1.0 %copy-start.12 = (s32[8]{0:T(128)S(1)}, s32[8]{0:T(128)}, u32[]{:S(2)}) copy-start(s32[8]{0:T(128)} %step_ref.1) | copy-start | bytes 100
  0.0 1.1 %copy-start.4 = (bf16[8,32,512]{2,1,0:T(8,128)(2,1)S(1)}, bf16[8,32,512]{2,1,0:T(8,128)(2,1)}, u32[]{:S(2)}) copy-start(bf16[8,32,512]{2,1,0:T(8,128)(2,1)} %param.15) | copy-start | bytes 786436
  0.1 3.1 %slice-start = ((s8[4718592]{0:T(1024)(128)(4,1)}), s8[4194304]{0:T(1024)(128)(4,1)S(1)}, s32[]{:S(2)}) async-start(s8[4718592]{0:T(1024)(128)(4,1)} %bitcast.4), calls=%async_computation.4 | async-start | bytes 8388608
  1.1 2.0 %slice-start.1 = ((s8[4718592]{0:T(1024)(128)(4,1)}), s8[524288]{0:T(1024)(128)(4,1)S(1)}, s32[]{:S(2)}) async-start(s8[4718592]{0:T(1024)(128)(4,1)} %bitcast.4), calls=%async_computation.5 | async-start | bytes 1048576
  1.1 2.0 %copy-start.5 = (f32[2,4,1280]{2,1,0:T(4,128)S(1)}, f32[2,4,1280]{2,1,0:T(4,128)}, u32[]{:S(2)}) copy-start(f32[2,4,1280]{2,1,0:T(4,128)} %conv_ref.3) | copy-start | bytes 122884
  1.1 2.0 %copy-start.6 = (bf16[2,512,16]{1,2,0:T(8,128)(2,1)S(1)}, bf16[2,512,16]{1,2,0:T(8,128)(2,1)}, u32[]{:S(2)}) copy-start(bf16[2,512,16]{1,2,0:T(8,128)(2,1)} %param.20) | copy-start | bytes 98308
  1.1 2.0 %copy-start.9 = (f32[2,16]{1,0:T(2,128)S(1)}, f32[2,16]{1,0:T(2,128)}, u32[]{:S(2)}) copy-start(f32[2,16]{1,0:T(2,128)} %decay_ref.3) | copy-start | bytes 388
  1.9 1.2 %collective-permute-start = (bf16[16,512]{1,0:T(8,128)(2,1)S(1)}, bf16[16,512]{1,0:T(8,128)(2,1)S(1)}, u32[]{:S(2)}, u32[]{:S(2)}) collective-permute-start(bf16[16,512]{1,0:T(8,128)(2,1)S(1)} %get-tuple-element.46), channel_id=1, source_target_pairs={{0,1},{1,0},{2,3},{3,2},{4,5},{5,4},{6,7},{7,6},{8,9},{9,8},{10,11... | collective-permute-start | bytes 49160 | tf_op jit(solution)/shard_map/ppermute | solution.py:553
  3.2 29.0 %copy-start = (bf16[2,512,1024]{2,1,0:T(8,128)(2,1)S(1)}, bf16[2,512,1024]{2,1,0:T(8,128)(2,1)}, u32[]{:S(2)}) copy-start(bf16[2,512,1024]{2,1,0:T(8,128)(2,1)} %wm_ref.7) | copy-start | bytes 6291460
  3.2 29.0 %copy-start.2 = (bf16[2,512,512]{2,1,0:T(8,128)(2,1)S(1)}, bf16[2,512,512]{2,1,0:T(8,128)(2,1)}, u32[]{:S(2)}) copy-start(bf16[2,512,512]{2,1,0:T(8,128)(2,1)} %merge_ref.3) | copy-start | bytes 3145732
  3.2 29.0 %copy-start.3 = (bf16[2,1024,512]{2,1,0:T(8,128)(2,1)S(1)}, bf16[2,1024,512]{2,1,0:T(8,128)(2,1)}, u32[]{:S(2)}) copy-start(bf16[2,1024,512]{2,1,0:T(8,128)(2,1)} %wo_ref.3) | copy-start | bytes 6291460
  3.2 29.0 %copy-start.7 = (f32[2,1024]{1,0:T(2,128)S(1)}, f32[2,1024]{1,0:T(2,128)}, u32[]{:S(2)}) copy-start(f32[2,1024]{1,0:T(2,128)} %gain_ref.3) | copy-start | bytes 24580
  3.2 29.0 %copy-start.8 = (f32[2,16]{1,0:T(2,128)S(1)}, f32[2,16]{1,0:T(2,128)}, u32[]{:S(2)}) copy-start(f32[2,16]{1,0:T(2,128)} %skip_ref.3) | copy-start | bytes 388
  6.2 26.0 %copy-start.1 = (bf16[2,512,512]{2,1,0:T(8,128)(2,1)S(1)}, bf16[2,512,512]{2,1,0:T(8,128)(2,1)}, u32[]{:S(2)}) copy-start(bf16[2,512,512]{2,1,0:T(8,128)(2,1)} %wq_ref.3) | copy-start | bytes 3145732
  6.2 1.5 %collective-permute-start.1 = (bf16[8,80,128]{2,1,0:T(8,128)(2,1)S(1)}, bf16[8,80,128]{2,1,0:T(8,128)(2,1)S(1)}, u32[]{:S(2)}, u32[]{:S(2)}) collective-permute-start(bf16[8,80,128]{2,1,0:T(8,128)(2,1)S(1)} %get-tuple-element.55), channel_id=1, source_target_pairs={{0,1},{1,0},{2,3},{3,2},{4,5},{5,4},{6,7},{7,6},{8,9},{9,8},{10,11... | collective-permute-start | bytes 491528 | tf_op jit(solution)/shard_map/ppermute | solution.py:553
  30.7 1.5 %collective-permute-start.2 = (bf16[8,80,128]{2,1,0:T(8,128)(2,1)S(1)}, bf16[8,80,128]{2,1,0:T(8,128)(2,1)S(1)}, u32[]{:S(2)}, u32[]{:S(2)}) collective-permute-start(bf16[8,80,128]{2,1,0:T(8,128)(2,1)S(1)} %get-tuple-element.57), channel_id=1, source_target_pairs={{0,1},{1,0},{2,3},{3,2},{4,5},{5,4},{6,7},{7,6},{8,9},{9,8},{10,11... | collective-permute-start | bytes 491528 | tf_op jit(solution)/shard_map/ppermute | solution.py:553
  35.1 8.6 %collective-permute-start.3 = (bf16[256,512]{1,0:T(8,128)(2,1)S(1)}, bf16[256,512]{1,0:T(8,128)(2,1)S(1)}, u32[]{:S(2)}, u32[]{:S(2)}) collective-permute-start(bf16[256,512]{1,0:T(8,128)(2,1)S(1)} %get-tuple-element.59.a_ref), channel_id=1, source_target_pairs={{0,1},{1,2},{2,3},{3,4},{4,5},{5,6},{6,7},{7,8},{8,9},{9,10},{10,1... | collective-permute-start | bytes 786440 | tf_op jit(solution)/shard_map/ppermute | solution.py:564
  45.7 1.2 %collective-permute-start.4 = (bf16[16,512]{1,0:T(8,128)(2,1)S(1)}, bf16[16,512]{1,0:T(8,128)(2,1)S(1)}, u32[]{:S(2)}, u32[]{:S(2)}) collective-permute-start(bf16[16,512]{1,0:T(8,128)(2,1)S(1)} %get-tuple-element.67), channel_id=1, source_target_pairs={{0,1},{1,0},{2,3},{3,2},{4,5},{5,4},{6,7},{7,6},{8,9},{9,8},{10,11... | collective-permute-start | bytes 49160 | tf_op jit(solution)/shard_map/ppermute | solution.py:553
  50.0 1.5 %collective-permute-start.5 = (bf16[8,80,128]{2,1,0:T(8,128)(2,1)S(1)}, bf16[8,80,128]{2,1,0:T(8,128)(2,1)S(1)}, u32[]{:S(2)}, u32[]{:S(2)}) collective-permute-start(bf16[8,80,128]{2,1,0:T(8,128)(2,1)S(1)} %get-tuple-element.75), channel_id=1, source_target_pairs={{0,1},{1,0},{2,3},{3,2},{4,5},{5,4},{6,7},{7,6},{8,9},{9,8},{10,11... | collective-permute-start | bytes 491528 | tf_op jit(solution)/shard_map/ppermute | solution.py:553
  72.3 1.5 %collective-permute-start.6 = (bf16[8,80,128]{2,1,0:T(8,128)(2,1)S(1)}, bf16[8,80,128]{2,1,0:T(8,128)(2,1)S(1)}, u32[]{:S(2)}, u32[]{:S(2)}) collective-permute-start(bf16[8,80,128]{2,1,0:T(8,128)(2,1)S(1)} %get-tuple-element.77), channel_id=1, source_target_pairs={{0,1},{1,0},{2,3},{3,2},{4,5},{5,4},{6,7},{7,6},{8,9},{9,8},{10,11... | collective-permute-start | bytes 491528 | tf_op jit(solution)/shard_map/ppermute | solution.py:553
  76.7 8.6 %collective-permute-start.7 = (bf16[256,512]{1,0:T(8,128)(2,1)S(1)}, bf16[256,512]{1,0:T(8,128)(2,1)S(1)}, u32[]{:S(2)}, u32[]{:S(2)}) collective-permute-start(bf16[256,512]{1,0:T(8,128)(2,1)S(1)} %get-tuple-element.79.a_ref), channel_id=1, source_target_pairs={{0,1},{1,2},{2,3},{3,4},{4,5},{5,6},{6,7},{7,8},{8,9},{9,10},{10,1... | collective-permute-start | bytes 786440 | tf_op jit(solution)/shard_map/ppermute | solution.py:564

commit v7 on v6

--- a/solution.py
+++ b/solution.py
@@ -56,7 +56,6 @@
 
 def first_kernel(
     step_ref,
-    reach_ref,
     sel_ref,
     x_ref,
     all_mods_ref,
@@ -65,10 +64,8 @@
     tail_ref,
     mods_ref,
     bias_ref,
-    seen_ref,
 ):
     rows, width = u_ref.shape
-    tok_frame = rows // WINDOW
     step = step_ref[0]
     for layer in range(LAYERS):
         mods_ref[layer] = all_mods_ref[layer, step].astype(F32)
@@ -81,12 +78,6 @@
         bias_ref[layer] = dot(
             chosen, all_bias_ref[layer], ((1,), (1,)), precision=lax.Precision.HIGHEST
         )
-    key_frame = lax.broadcasted_iota(jnp.int32, (tok_frame, 2 * rows), 1) // tok_frame
-    first = WINDOW - lax.axis_index("frames") * WINDOW
-    for f in range(WINDOW):
-        low = jnp.maximum(first, f + WINDOW - reach_ref[f])
-        seen = (key_frame >= low) & (key_frame <= f + WINDOW)
-        seen_ref[f * tok_frame : (f + 1) * tok_frame, :] = jnp.where(seen, 0.0, -1e30)
 
 
 def core_index():
@@ -279,7 +270,8 @@
     return x * jax.nn.sigmoid(x)
 
 
-def scan_kernel(got_ref, back_ref, pad_ref):
+def scan_kernel(got_ref, *rest):
+    back_ref, pad_ref = rest[-2:]
     parts, padded, _ = got_ref.shape
     part_rows = padded - PAD
     rows = slice(0, part_rows)
@@ -310,10 +302,46 @@
         carry = decay * carry + (got_ref[d, rows, :].astype(F32) + added[rows, :])
 
 
+def mixed_values(affinity, cum, shifted, values, skip, pair):
+    q_pos = lax.broadcasted_iota(jnp.int32, (SPAN, SPAN), 0)
+    s_pos = lax.broadcasted_iota(jnp.int32, (SPAN, SPAN), 1)
+    lower = q_pos >= s_pos
+    left = lax.broadcasted_iota(jnp.int32, (SPAN, LANES), 1) < HEAD_DIM
+    zero = jnp.zeros((SPAN, LANES), BF16)
+    mixing = []
+    for h in (2 * pair, 2 * pair + 1):
+        gap = cum[:, h : h + 1] - shifted[h : h + 1, :]
+        mixing.append(jnp.where(lower, affinity * jnp.exp(gap), 0.0).astype(BF16))
+    both = jnp.concatenate(mixing, axis=1)
+    stacked = jnp.concatenate([jnp.where(left, values, zero), jnp.where(left, zero, values)], axis=0)
+    return dot(both, stacked) + skip * values.astype(F32)
+
+
+def later_kernel(layer, act_ref, cum_ref, shifted_ref, skip_ref, sel_ref, y_ref):
+    skip = spread_row(skip_ref[layer : layer + 1, :], sel_ref[...])
+    for b in range(1, act_ref.shape[0] // SPAN):
+        r = slice(b * SPAN, (b + 1) * SPAN)
+        maps = act_ref[r, INNER:]
+        affinity = dot(maps[:, STATE:], maps[:, :STATE], ((1,), (1,)))
+        cum, shifted = cum_ref[r, :], shifted_ref[:, r]
+        for pair in range(HEADS // 2):
+            cols = slice(pair * LANES, (pair + 1) * LANES)
+            y_ref[(b - 1) * SPAN : b * SPAN, cols] = mixed_values(
+                affinity, cum, shifted, act_ref[r, cols], skip[:, cols], pair
+            )
+
+
+def gate_kernel(layer, u_ref, w_ref, gate_ref):
+    chunk = 256
+    for c in range(0, INNER, chunk):
+        cols = slice(c, c + chunk)
+        gate_ref[:, cols] = silu(dot(u_ref[...], w_ref[layer, :, cols]).astype(BF16).astype(F32))
+
+
 def finish_kernel(
     layer,
-    u_ref,
-    w_ref,
+    gate_ref,
+    later_ref,
     act_ref,
     own_ref,
     cum_ref,
@@ -330,13 +358,12 @@
     mods_ref,
     *rest,
 ):
-    hidden_ref, a_ref, first_ref, y_ref, gate_ref, normed_ref, enter_ref = rest[-7:]
-    rows = u_ref.shape[0]
+    hidden_ref, a_ref, first_ref, y_ref, normed_ref, enter_ref = rest[-6:]
+    rows = gate_ref.shape[0]
     core = core_index()
     enter_ref[pl.ds(core * HALF, HALF)] = mine_ref[...]
     enter_ref[pl.ds((1 - core) * HALF, HALF)] = other_ref[...]
     start = (1 - core).astype(F32)
-    u = u_ref[...]
     sel = sel_ref[...]
     lane = lax.broadcasted_iota(jnp.int32, (SPAN, LANES), 1)
     left = lane < HEAD_DIM
@@ -383,7 +410,6 @@
     chunk = 256
     for c in range(0, INNER, chunk):
         cols = slice(c, c + chunk)
-        gate_ref[:, cols] = silu(dot(u, w_ref[layer, :, cols]).astype(BF16).astype(F32))
         entering = jnp.concatenate(
             [enter_ref[h, 0:HEAD_DIM, :] for h in range(c // HEAD_DIM, (c + chunk) // HEAD_DIM)],
             axis=0,
@@ -395,30 +421,18 @@
         state = state_ref[(b - 1) * STATE : b * STATE, :] + spread_row(decayed, sel) * late
         cum = cum_ref[r, :]
         decayed = decayed * jnp.exp(cum[SPAN - 1 : SPAN, :])
-        y_ref[r, :] = y_ref[r, :] + dot(out_maps[b], state.astype(BF16)) * spread(jnp.exp(cum), sel)
-
-    q_pos = lax.broadcasted_iota(jnp.int32, (SPAN, SPAN), 0)
-    s_pos = lax.broadcasted_iota(jnp.int32, (SPAN, SPAN), 1)
-    lower = q_pos >= s_pos
-    zero = jnp.zeros((SPAN, LANES), BF16)
+        own = later_ref[(b - 1) * SPAN : b * SPAN, :]
+        own = own + dot(out_maps[b], state.astype(BF16)) * spread(jnp.exp(cum), sel)
+        y_ref[r, :] = (y_ref[r, :] + own) * gate_ref[r, :]
+
     skip = spread_row(skip_ref[layer : layer + 1, :], sel)
-    for b in range(spans):
-        r = slice(b * SPAN, (b + 1) * SPAN)
-        cum = cum_ref[r, :]
-        affinity = dot(out_maps[b], acts(b, slice(INNER, INNER + STATE)), ((1,), (1,)))
-        for pair in range(HEADS // 2):
-            cols = slice(pair * LANES, (pair + 1) * LANES)
-            values = acts(b, cols)
-            mixing = []
-            for h in (2 * pair, 2 * pair + 1):
-                gap = cum[:, h : h + 1] - shifted_ref[h : h + 1, r]
-                mixing.append(jnp.where(lower, affinity * jnp.exp(gap), 0.0).astype(BF16))
-            both = jnp.concatenate(mixing, axis=1)
-            stacked = jnp.concatenate(
-                [jnp.where(left, values, zero), jnp.where(left, zero, values)], axis=0
-            )
-            y = dot(both, stacked) + skip[:, cols] * values.astype(F32) + y_ref[r, cols]
-            y_ref[r, cols] = y * gate_ref[r, cols]
+    r = slice(0, SPAN)
+    affinity = dot(out_maps[0], acts(0, slice(INNER, INNER + STATE)), ((1,), (1,)))
+    cum, shifted = cum_ref[r, :], shifted_ref[:, r]
+    for pair in range(HEADS // 2):
+        cols = slice(pair * LANES, (pair + 1) * LANES)
+        y = mixed_values(affinity, cum, shifted, acts(0, cols), skip[:, cols], pair)
+        y_ref[r, cols] = (y + y_ref[r, cols]) * gate_ref[r, cols]
 
     row = lax.broadcasted_iota(jnp.int32, (chunk, chunk), 0) // HEAD_DIM
     col = lax.broadcasted_iota(jnp.int32, (chunk, chunk), 1) // HEAD_DIM
@@ -463,11 +477,18 @@
 
 
 def memory_kernel(
-    layer, a_ref, wq_ref, wm_ref, seen_ref, q_ref, number_ref, total_ref, top_ref, kv_ref
+    layer, reach_ref, a_ref, wq_ref, wm_ref, q_ref, number_ref, total_ref, top_ref, seen_ref, kv_ref
 ):
     rows = a_ref.shape[0]
     half = rows // 2
     a = a_ref[...]
+    tok_frame = rows // WINDOW
+    key_frame = lax.broadcasted_iota(jnp.int32, (tok_frame, 2 * rows), 1) // tok_frame
+    first = WINDOW - lax.axis_index("frames") * WINDOW
+    for f in range(WINDOW):
+        low = jnp.maximum(first, f + WINDOW - reach_ref[f])
+        seen = (key_frame >= low) & (key_frame <= f + WINDOW)
+        seen_ref[f * tok_frame : (f + 1) * tok_frame, :] = jnp.where(seen, 0.0, -1e30)
     q_ref[...] = (dot(a, wq_ref[layer]).astype(BF16).astype(F32) * HEAD_DIM**-0.5).astype(BF16)
     kv_ref[...] = dot(a, wm_ref[layer]).astype(BF16)
     for part in range(2):
@@ -593,7 +614,7 @@
     (sel,) = run(
         select_kernel, (), [shape((2 * HEADS, INNER), BF16)], name="select", flops=OPENING
     )
-    u, tail, mods, bias, seen = run(
+    u, tail, mods, bias = run(
         first_kernel,
         (sel, resid, modulation, step_bias),
         [
@@ -601,11 +622,10 @@
             shape((TAIL, width), BF16),
             shape((LAYERS,) + modulation.shape[2:], F32),
             shape((LAYERS, 8, HEADS), F32),
-            shape((rows, 2 * rows), F32),
         ],
         name="first",
         flops=OPENING,
-        scalars=(timestep, lookback),
+        scalars=(timestep,),
     )
     for layer in range(LAYERS):
         before = swapped(tail, "frames")
@@ -632,6 +652,14 @@
             flops=2 * rows * width * mixed,
         )
         got = swapped(give, "frames")
+        (later,) = run(
+            functools.partial(later_kernel, layer),
+            (act, cum, shifted, skip_gain, sel),
+            [shape((max(spans - 1, 1) * SPAN, INNER), F32)],
+            name="later",
+            flops=2 * rows * SPAN * INNER,
+        )
+        got, later = lax.optimization_barrier((got, later))
         (send,) = run(
             chip_kernel,
             (keep, got),
@@ -641,7 +669,8 @@
         )
         (back,) = run(
             scan_kernel,
-            (over_chips(send, "frames"),),
+            (over_chips(send, "frames"),)
+            + (() if layer else (output_weight, norm_gain, query_weight, memory_weight, merge_weight)),
             [shape(send.shape, BF16)],
             [pltpu.VMEM(((parts + 1) * PAD + 8, LANES), F32)],
             name="scan",
@@ -657,16 +686,22 @@
             ],
             name="enter",
         )
+        give, u = lax.optimization_barrier((give, u))
         other = swapped(give, "frames")
+        (gate,) = run(
+            functools.partial(gate_kernel, layer),
+            (u, input_weight),
+            [shape((rows, INNER), F32)],
+            name="gate",
+            flops=2 * rows * width * INNER,
+        )
         hidden, a = run(
             functools.partial(finish_kernel, layer),
-            (u, input_weight, act, own, cum, shifted, edge, state, skip_gain, sel)
-            + (mine, other, resid, output_weight, norm_gain, mods)
-            + (() if layer else (query_weight, memory_weight, merge_weight)),
+            (gate, later, act, own, cum, shifted, edge, state, skip_gain, sel)
+            + (mine, other, resid, output_weight, norm_gain, mods),
             [shape((rows, width), F32), shape((rows, width), BF16)],
             [
                 pltpu.VMEM((TAIL, mixed), BF16),
-                pltpu.VMEM((rows, INNER), F32),
                 pltpu.VMEM((rows, INNER), F32),
                 pltpu.VMEM((rows, INNER), BF16),
                 pltpu.VMEM((HEADS, BLOCK, LANES), BF16),
@@ -674,12 +709,15 @@
             name="finish",
         )
         prev = from_behind(a, "frames")
-        q, number, total, top = run(
+        q, number, total, top, seen = run(
             functools.partial(memory_kernel, layer),
-            (a, query_weight, memory_weight, seen),
-            [shape((rows, ATTN), BF16)] + [shape((rows, ATTN), F32)] * 3,
+            (a, query_weight, memory_weight),
+            [shape((rows, ATTN), BF16)]
+            + [shape((rows, ATTN), F32)] * 3
+            + [shape((rows, 2 * rows), F32)],
             [pltpu.VMEM((rows, 2 * ATTN), BF16)],
             name="memory",
+            scalars=(lookback,),
             flops=2 * rows * width * 3 * ATTN,
         )
         last = layer == LAYERS - 1

time: 88.3 us -> 86.7 us (0.982)
  waiting for transfers between devices: 16.8 us -> 13.4 us
  Pallas kernels: 22.8 us -> 24.4 us
    ppermute x6, waiting for transfers between devices: 7.54 us -> 5.41 us  [swapped(): return lax.ppermute(value, axis, [(i, i ^ 1) for i in range(count)])]
    pallas_call x16 -> x20, Pallas kernels: 22.8 us -> 24.4 us  [run(): pl.pallas_call(kernel, in_specs=[SCALARS] * len(scalars) + [WHOLE] * len(...]
    ppermute x2, waiting for transfers between devices: 9.29 us -> 7.99 us  [from_behind(): return lax.ppermute(value, axis, [(i, i + 1) for i in range(count - 1)])]
  transfers between devices with their start and end apart: 8 -> 8, of which waited for: 8 -> 8; matrix products, arithmetic and copies ran while one was open for 0% -> 0% of each run, Pallas kernels for 4% -> 8%
where the time goes in v7:
time: 86.7 us; the launch traced here: 86.3 us
  blocking collectives  41.9 us (48%)
  Pallas kernels  24.4 us (28%)
  waiting for transfers between devices  13.4 us (15%)
  starting transfers between devices  5.22 us (6%)
  local copies, waits for them, and re-layouts  1.12 us (1%)
    all_to_all x4, blocking collectives, over_chips(): return lax.all_to_all(value, axis, 0, 0, axis_index_groups=groups)  41.9 us
    pallas_call x20, Pallas kernels, run(): pl.pallas_call(kernel, in_specs=[SCALARS] * len(scalars) + [WHOLE] * len(...  24.4 us
    ppermute x2, waiting for transfers between devices, from_behind(): return lax.ppermute(value, axis, [(i, i + 1) for i in range(count - 1)])  7.99 us
    ppermute x6, waiting for transfers between devices, swapped(): return lax.ppermute(value, axis, [(i, i ^ 1) for i in range(count)])  5.41 us
    ppermute x2, starting transfers between devices, from_behind(): return lax.ppermute(value, axis, [(i, i + 1) for i in range(count - 1)])  4.47 us
  transfers between devices with their start and end apart: 8, of which 8 were waited for; matrix products, arithmetic and copies ran while one was open for 0% of the time, Pallas kernels for 8%

profile of v7, /device:TPU:8, one launch (start us, length us, event | category | flops | bytes accessed | tf_op | source)
XLA Modules:
  0.0 86.3 jit_solution(4917830377095373193)
XLA Ops:
  0.0 0.0 copy-start.12
  0.0 0.0 copy-start.11
  0.0 0.0 copy-start.4
  0.0 0.0 slice-start
  0.1 0.7 copy-done.12
  0.7 0.3 copy-done.11
  1.0 0.0 copy-done.13
  1.0 0.1 copy-done.4
  1.1 0.7 first.1
  1.8 0.1 collective-permute-start
  1.9 1.2 %collective-permute-done.before_ref = bf16[16,512]{1,0:T(8,128)(2,1)S(1)} collective-permute-done((bf16[16,512]{1,0:T(8,128)(2,1)S(1)}, bf16[16,512]{1,0:T(8,128)(2,1)S(1)}, u32[]{:S(2)}, u32[]{:S(2)}) %collective-permute-start) | collective-permute-done | bytes 16416 | tf_op jit(solution)/shard_map/ppermute | solution.py:574
  3.1 0.0 slice-done
  3.1 0.0 slice-done.1
  3.1 0.0 copy-done.5
  3.1 0.0 copy-done.6
  3.1 0.0 copy-done.9
  3.1 0.0 copy-start.8
  3.1 0.0 copy-start.1
  3.2 0.0 copy-start.2
  3.2 0.0 copy-start.3
  3.2 3.0 %local.2 = (bf16[256,1280]{1,0:T(8,128)(2,1)S(1)}, f32[8,1280]{1,0:T(8,128)S(1)}, f32[256,16]{1,0:T(8,128)S(1)}, f32[16,256]{1,0:T(8,128)S(1)}, f32[16,16]{1,0:T...) custom-call(bf16[256,512]{1,0:T(8,128)(2,1)S(1)} %get-tuple-element.64.u_ref,, ...), custom_call_target="tpu_custom_call" | custom-call | flops 335544320 | bytes 6719616 | tf_op jit(solution)/shard_map/local/pallas_call | solution.py:556
  6.1 0.0 copy-start.7
  6.2 0.2 collective-permute-start.1
  6.4 0.0 copy-done.8
  6.4 0.6 later.2.later_ref
  7.0 0.6 collective-permute-done.1.got_ref
  7.6 0.1 chip.2
  7.8 11.8 %all_to_all.20.got_ref = bf16[8,80,128]{2,1,0:T(8,128)(2,1)S(1)} all-to-all(bf16[8,80,128]{2,1,0:T(8,128)(2,1)S(1)} %chip.2), channel_id=1, replica_groups={{0,2,4,6,8,10,12,14},{1,3,5,7,9,11,13,15},{16,18,20,22,24,26,28,30},{17..., dimensions={0} | all-to-all | bytes 327680 | tf_op jit(solution)/shard_map/all_to_all | solution.py:580
  19.5 0.0 copy-done.1
  19.5 0.0 copy-done.2
  19.5 0.0 copy-done.3
  19.5 0.0 copy-done
  19.5 0.0 copy-done.7
  19.5 0.4 scan.2
  20.0 10.3 %all_to_all.21.back_ref = bf16[8,80,128]{2,1,0:T(8,128)(2,1)S(1)} all-to-all(bf16[8,80,128]{2,1,0:T(8,128)(2,1)S(1)} %scan.2), channel_id=1, replica_groups={{0,2,4,6,8,10,12,14},{1,3,5,7,9,11,13,15},{16,18,20,22,24,26,28,30},{17..., dimensions={0} | all-to-all | bytes 327680 | tf_op jit(solution)/shard_map/all_to_all | solution.py:580
  30.2 0.4 enter.2
  30.7 0.1 collective-permute-start.2
  30.8 0.5 gate.2.gate_ref
  31.2 0.9 %collective-permute-done.2.other_ref = bf16[8,80,128]{2,1,0:T(8,128)(2,1)S(1)} collective-permute-done((bf16[8,80,128]{2,1,0:T(8,128)(2,1)S(1)}, bf16[8,80,128]{2,1,0:T(8,128)(2,1)S(1)}, u32[]{:S(2)}, u32[]{:S(2)}) %collective-permute-start.2) | collective-permute-done | bytes 163872 | tf_op jit(solution)/shard_map/ppermute | solution.py:574
  32.1 2.1 %finish.2 = (f32[256,512]{1,0:T(8,128)S(1)}, bf16[256,512]{1,0:T(8,128)(2,1)S(1)}) custom-call(f32[256,1024]{1,0:T(8,128)S(1)} %gate.2.gate_ref, f32[128,1024]{1,0:T(8,128)S(1)} %later.2.later_ref, bf16[256,1280]{1,0:T(8,128)(2,1)S(1)} %get-tuple-element.59.act_ref, f32[8,1280]{1,0:T(8,128)S(1)} %get-tuple-element.66.own_ref, ...), custom_call_target="tpu_custom_call" | custom-call | bytes 6390912 | tf_op jit(solution)/shard_map/finish/pallas_call | solution.py:556
  34.3 2.2 %collective-permute-start.3 = (bf16[256,512]{1,0:T(8,128)(2,1)S(1)}, bf16[256,512]{1,0:T(8,128)(2,1)S(1)}, u32[]{:S(2)}, u32[]{:S(2)}) collective-permute-start(bf16[256,512]{1,0:T(8,128)(2,1)S(1)} %get-tuple-element.72.a_ref), channel_id=1, source_target_pairs={{0,1},{1,2},{2,3},{3,4},{4,5},{5,6},{6,7},{7,8},{8,9},{9,10},{10,1... | collective-permute-start | bytes 786440 | tf_op jit(solution)/shard_map/ppermute | solution.py:585
  36.5 0.0 copy-done.10
  36.5 2.3 %memory.2 = (bf16[256,512]{1,0:T(8,128)(2,1)S(1)}, f32[256,512]{1,0:T(8,128)S(1)}, f32[256,512]{1,0:T(8,128)S(1)}, f32[256,512]{1,0:T(8,128)S(1)}, f32[256,512]{1,0:T(8,128)S(1)}) custom-call(s32[8]{0:T(128)S(1)} %copy-done.10, bf16[256,512]{1,0:T(8,128)(2,1)S(1)} %get-tuple-element.72.a_ref, bf16[2,512,512]{2,1,0:T(8,128)(2,1)S(1)} %copy-done.2, ...), custom_call_target="tpu_custom_call" | custom-call | flops 402653184 | bytes 5767168 | tf_op jit(solution)/shard_map/memory/pallas_call | solution.py:556
  38.8 4.0 %collective-permute-done.3.prev_ref = bf16[256,512]{1,0:T(8,128)(2,1)S(1)} collective-permute-done((bf16[256,512]{1,0:T(8,128)(2,1)S(1)}, bf16[256,512]{1,0:T(8,128)(2,1)S(1)}, u32[]{:S(2)}, u32[]{:S(2)}) %collective-permute-start.3) | collective-permute-done | bytes 262176 | tf_op jit(solution)/shard_map/ppermute | solution.py:585
  42.9 2.0 %attend.2 = (f32[256,512]{1,0:T(8,128)S(1)}, bf16[256,512]{1,0:T(8,128)(2,1)S(1)}, bf16[16,512]{1,0:T(8,128)(2,1)S(1)}) custom-call(bf16[256,512]{1,0:T(8,128)(2,1)S(1)} %get-tuple-element.73.q_ref, f32[256,512]{1,0:T(8,128)S(1)} %get-tuple-element.74.number_ref, f32[256,512]{1,0:T(8,128)S(1)} %get-tuple-element.75.total_ref, ...), custom_call_target="tpu_custom_call" | custom-call | bytes 7110656 | tf_op jit(solution)/shard_map/attend/pallas_call | solution.py:556
  44.9 0.1 collective-permute-start.4
  44.9 1.2 %collective-permute-done.4.before_ref = bf16[16,512]{1,0:T(8,128)(2,1)S(1)} collective-permute-done((bf16[16,512]{1,0:T(8,128)(2,1)S(1)}, bf16[16,512]{1,0:T(8,128)(2,1)S(1)}, u32[]{:S(2)}, u32[]{:S(2)}) %collective-permute-start.4) | collective-permute-done | bytes 16416 | tf_op jit(solution)/shard_map/ppermute | solution.py:574
  46.1 3.0 %local.3 = (bf16[256,1280]{1,0:T(8,128)(2,1)S(1)}, f32[8,1280]{1,0:T(8,128)S(1)}, f32[256,16]{1,0:T(8,128)S(1)}, f32[16,256]{1,0:T(8,128)S(1)}, f32[16,16]{1,0:T...) custom-call(bf16[256,512]{1,0:T(8,128)(2,1)S(1)} %get-tuple-element.88.u_ref,, ...), custom_call_target="tpu_custom_call" | custom-call | flops 335544320 | bytes 6719616 | tf_op jit(solution)/shard_map/local/pallas_call | solution.py:556
  49.1 0.2 collective-permute-start.5
  49.3 0.6 later.3.later_ref
  49.9 0.6 collective-permute-done.5.got_ref
  50.6 0.1 chip.3
  50.7 9.6 %all_to_all.22.got_ref = bf16[8,80,128]{2,1,0:T(8,128)(2,1)S(1)} all-to-all(bf16[8,80,128]{2,1,0:T(8,128)(2,1)S(1)} %chip.3), channel_id=1, replica_groups={{0,2,4,6,8,10,12,14},{1,3,5,7,9,11,13,15},{16,18,20,22,24,26,28,30},{17..., dimensions={0} | all-to-all | bytes 327680 | tf_op jit(solution)/shard_map/all_to_all | solution.py:580
  60.3 0.4 scan.3
  60.7 10.3 %all_to_all.23.back_ref = bf16[8,80,128]{2,1,0:T(8,128)(2,1)S(1)} all-to-all(bf16[8,80,128]{2,1,0:T(8,128)(2,1)S(1)} %scan.3), channel_id=1, replica_groups={{0,2,4,6,8,10,12,14},{1,3,5,7,9,11,13,15},{16,18,20,22,24,26,28,30},{17..., dimensions={0} | all-to-all | bytes 327680 | tf_op jit(solution)/shard_map/all_to_all | solution.py:580
  71.0 0.5 enter.3
  71.4 0.1 collective-permute-start.6
  71.5 0.5 gate.3.gate_ref
  72.0 0.9 %collective-permute-done.6.other_ref = bf16[8,80,128]{2,1,0:T(8,128)(2,1)S(1)} collective-permute-done((bf16[8,80,128]{2,1,0:T(8,128)(2,1)S(1)}, bf16[8,80,128]{2,1,0:T(8,128)(2,1)S(1)}, u32[]{:S(2)}, u32[]{:S(2)}) %collective-permute-start.6) | collective-permute-done | bytes 163872 | tf_op jit(solution)/shard_map/ppermute | solution.py:574
  72.9 2.2 %finish.3 = (f32[256,512]{1,0:T(8,128)S(1)}, bf16[256,512]{1,0:T(8,128)(2,1)S(1)}) custom-call(f32[256,1024]{1,0:T(8,128)S(1)} %gate.3.gate_ref, f32[128,1024]{1,0:T(8,128)S(1)} %later.3.later_ref, bf16[256,1280]{1,0:T(8,128)(2,1)S(1)} %get-tuple-element.83.act_ref, f32[8,1280]{1,0:T(8,128)S(1)} %get-tuple-element.90.own_ref, ...), custom_call_target="tpu_custom_call" | custom-call | bytes 6653056 | tf_op jit(solution)/shard_map/finish/pallas_call | solution.py:556
  75.1 2.3 %collective-permute-start.7 = (bf16[256,512]{1,0:T(8,128)(2,1)S(1)}, bf16[256,512]{1,0:T(8,128)(2,1)S(1)}, u32[]{:S(2)}, u32[]{:S(2)}) collective-permute-start(bf16[256,512]{1,0:T(8,128)(2,1)S(1)} %get-tuple-element.96.a_ref), channel_id=1, source_target_pairs={{0,1},{1,2},{2,3},{3,4},{4,5},{5,6},{6,7},{7,8},{8,9},{9,10},{10,1... | collective-permute-start | bytes 786440 | tf_op jit(solution)/shard_map/ppermute | solution.py:585
  77.3 2.3 %memory.3 = (bf16[256,512]{1,0:T(8,128)(2,1)S(1)}, f32[256,512]{1,0:T(8,128)S(1)}, f32[256,512]{1,0:T(8,128)S(1)}, f32[256,512]{1,0:T(8,128)S(1)}, f32[256,512]{1,0:T(8,128)S(1)}) custom-call(s32[8]{0:T(128)S(1)} %copy-done.10, bf16[256,512]{1,0:T(8,128)(2,1)S(1)} %get-tuple-element.96.a_ref, bf16[2,512,512]{2,1,0:T(8,128)(2,1)S(1)} %copy-done.2, ...), custom_call_target="tpu_custom_call" | custom-call | flops 402653184 | bytes 5767168 | tf_op jit(solution)/shard_map/memory/pallas_call | solution.py:556
  79.7 4.0 %collective-permute-done.7.prev_ref = bf16[256,512]{1,0:T(8,128)(2,1)S(1)} collective-permute-done((bf16[256,512]{1,0:T(8,128)(2,1)S(1)}, bf16[256,512]{1,0:T(8,128)(2,1)S(1)}, u32[]{:S(2)}, u32[]{:S(2)}) %collective-permute-start.7) | collective-permute-done | bytes 262176 | tf_op jit(solution)/shard_map/ppermute | solution.py:585
  83.7 2.7 %attend.3 = f32[256,512]{1,0:T(8,128)} custom-call(bf16[256,512]{1,0:T(8,128)(2,1)S(1)} %get-tuple-element.97.q_ref, f32[256,512]{1,0:T(8,128)S(1)} %get-tuple-element.98.number_ref, f32[256,512]{1,0:T(8,128)S(1)} %get-tuple-element.99.total_ref, f32[256,512]{1,0:T(8,128)S(1)} %get-tuple-element.100.top_ref, f32[256,512]{1,0:T(8,128)S(1)} %get-tuple-element.101.seen_ref, ...), custom_call_target="tpu_custom_call" | custom-call | bytes 6832128 | tf_op jit(solution)/shard_map/attend/pallas_call | solution.py:556
  (9 shorter events, 0.0 us)
Async XLA Ops:
  0.0 0.7 copy-start.12
  0.0 1.0 %copy-start.11 = (bf16[2,50,4,512]{3,2,1,0:T(4,128)(2,1)S(1)}, bf16[2,50,4,512]{3,2,1,0:T(4,128)(2,1)}, u32[]{:S(2)}) copy-start(bf16[2,50,4,512]{3,2,1,0:T(4,128)(2,1)} %all_mods_ref.1) | copy-start | bytes 1228804
  0.0 1.0 %copy-start.13 = (s32[8]{0:T(128)S(1)}, s32[8]{0:T(128)}, u32[]{:S(2)}) copy-start(s32[8]{0:T(128)} %step_ref.1) | copy-start | bytes 100
  0.0 1.1 %copy-start.4 = (bf16[8,32,512]{2,1,0:T(8,128)(2,1)S(1)}, bf16[8,32,512]{2,1,0:T(8,128)(2,1)}, u32[]{:S(2)}) copy-start(bf16[8,32,512]{2,1,0:T(8,128)(2,1)} %param.15) | copy-start | bytes 786436
  0.0 3.0 %slice-start = ((s8[4718592]{0:T(1024)(128)(4,1)}), s8[4194304]{0:T(1024)(128)(4,1)S(1)}, s32[]{:S(2)}) async-start(s8[4718592]{0:T(1024)(128)(4,1)} %bitcast.4), calls=%async_computation.4 | async-start | bytes 8388608
  1.1 2.0 %slice-start.1 = ((s8[4718592]{0:T(1024)(128)(4,1)}), s8[524288]{0:T(1024)(128)(4,1)S(1)}, s32[]{:S(2)}) async-start(s8[4718592]{0:T(1024)(128)(4,1)} %bitcast.4), calls=%async_computation.5 | async-start | bytes 1048576
  1.1 2.0 %copy-start.5 = (f32[2,4,1280]{2,1,0:T(4,128)S(1)}, f32[2,4,1280]{2,1,0:T(4,128)}, u32[]{:S(2)}) copy-start(f32[2,4,1280]{2,1,0:T(4,128)} %conv_ref.3) | copy-start | bytes 122884
  1.1 2.0 %copy-start.6 = (bf16[2,512,16]{1,2,0:T(8,128)(2,1)S(1)}, bf16[2,512,16]{1,2,0:T(8,128)(2,1)}, u32[]{:S(2)}) copy-start(bf16[2,512,16]{1,2,0:T(8,128)(2,1)} %param.20) | copy-start | bytes 98308
  1.1 2.0 %copy-start.9 = (f32[2,16]{1,0:T(2,128)S(1)}, f32[2,16]{1,0:T(2,128)}, u32[]{:S(2)}) copy-start(f32[2,16]{1,0:T(2,128)} %decay_ref.3) | copy-start | bytes 388
  1.8 1.2 %collective-permute-start = (bf16[16,512]{1,0:T(8,128)(2,1)S(1)}, bf16[16,512]{1,0:T(8,128)(2,1)S(1)}, u32[]{:S(2)}, u32[]{:S(2)}) collective-permute-start(bf16[16,512]{1,0:T(8,128)(2,1)S(1)} %get-tuple-element.55), channel_id=1, source_target_pairs={{0,1},{1,0},{2,3},{3,2},{4,5},{5,4},{6,7},{7,6},{8,9},{9,8},{10,11... | collective-permute-start | bytes 49160 | tf_op jit(solution)/shard_map/ppermute | solution.py:574
  3.1 3.3 %copy-start.8 = (f32[2,16]{1,0:T(2,128)S(1)}, f32[2,16]{1,0:T(2,128)}, u32[]{:S(2)}) copy-start(f32[2,16]{1,0:T(2,128)} %skip_ref.7) | copy-start | bytes 388
  3.1 16.4 %copy-start.1 = (bf16[2,1024,512]{2,1,0:T(8,128)(2,1)S(1)}, bf16[2,1024,512]{2,1,0:T(8,128)(2,1)}, u32[]{:S(2)}) copy-start(bf16[2,1024,512]{2,1,0:T(8,128)(2,1)} %wo_ref.3) | copy-start | bytes 6291460
  3.2 16.4 %copy-start.2 = (bf16[2,512,512]{2,1,0:T(8,128)(2,1)S(1)}, bf16[2,512,512]{2,1,0:T(8,128)(2,1)}, u32[]{:S(2)}) copy-start(bf16[2,512,512]{2,1,0:T(8,128)(2,1)} %wq_ref.3) | copy-start | bytes 3145732
  3.2 16.4 %copy-start.3 = (bf16[2,512,512]{2,1,0:T(8,128)(2,1)S(1)}, bf16[2,512,512]{2,1,0:T(8,128)(2,1)}, u32[]{:S(2)}) copy-start(bf16[2,512,512]{2,1,0:T(8,128)(2,1)} %merge_ref.3) | copy-start | bytes 3145732
  6.1 13.4 %copy-start = (bf16[2,512,1024]{2,1,0:T(8,128)(2,1)S(1)}, bf16[2,512,1024]{2,1,0:T(8,128)(2,1)}, u32[]{:S(2)}) copy-start(bf16[2,512,1024]{2,1,0:T(8,128)(2,1)} %wm_ref.7) | copy-start | bytes 6291460
  6.1 13.4 %copy-start.7 = (f32[2,1024]{1,0:T(2,128)S(1)}, f32[2,1024]{1,0:T(2,128)}, u32[]{:S(2)}) copy-start(f32[2,1024]{1,0:T(2,128)} %gain_ref.3) | copy-start | bytes 24580
  6.2 1.5 %collective-permute-start.1 = (bf16[8,80,128]{2,1,0:T(8,128)(2,1)S(1)}, bf16[8,80,128]{2,1,0:T(8,128)(2,1)S(1)}, u32[]{:S(2)}, u32[]{:S(2)}) collective-permute-start(bf16[8,80,128]{2,1,0:T(8,128)(2,1)S(1)} %get-tuple-element.58), channel_id=1, source_target_pairs={{0,1},{1,0},{2,3},{3,2},{4,5},{5,4},{6,7},{7,6},{8,9},{9,8},{10,11... | collective-permute-start | bytes 491528 | tf_op jit(solution)/shard_map/ppermute | solution.py:574
  30.7 1.5 %collective-permute-start.2 = (bf16[8,80,128]{2,1,0:T(8,128)(2,1)S(1)}, bf16[8,80,128]{2,1,0:T(8,128)(2,1)S(1)}, u32[]{:S(2)}, u32[]{:S(2)}) collective-permute-start(bf16[8,80,128]{2,1,0:T(8,128)(2,1)S(1)} %get-tuple-element.70), channel_id=1, source_target_pairs={{0,1},{1,0},{2,3},{3,2},{4,5},{5,4},{6,7},{7,6},{8,9},{9,8},{10,11... | collective-permute-start | bytes 491528 | tf_op jit(solution)/shard_map/ppermute | solution.py:574
  32.1 4.3 %copy-start.10 = (s32[8]{0:T(128)S(1)}, s32[8]{0:T(128)}, u32[]{:S(2)}) copy-start(s32[8]{0:T(128)} %reach_ref.3) | copy-start | bytes 100
  34.3 8.6 %collective-permute-start.3 = (bf16[256,512]{1,0:T(8,128)(2,1)S(1)}, bf16[256,512]{1,0:T(8,128)(2,1)S(1)}, u32[]{:S(2)}, u32[]{:S(2)}) collective-permute-start(bf16[256,512]{1,0:T(8,128)(2,1)S(1)} %get-tuple-element.72.a_ref), channel_id=1, source_target_pairs={{0,1},{1,2},{2,3},{3,4},{4,5},{5,6},{6,7},{7,8},{8,9},{9,10},{10,1... | collective-permute-start | bytes 786440 | tf_op jit(solution)/shard_map/ppermute | solution.py:585
  44.9 1.2 %collective-permute-start.4 = (bf16[16,512]{1,0:T(8,128)(2,1)S(1)}, bf16[16,512]{1,0:T(8,128)(2,1)S(1)}, u32[]{:S(2)}, u32[]{:S(2)}) collective-permute-start(bf16[16,512]{1,0:T(8,128)(2,1)S(1)} %get-tuple-element.80), channel_id=1, source_target_pairs={{0,1},{1,0},{2,3},{3,2},{4,5},{5,4},{6,7},{7,6},{8,9},{9,8},{10,11... | collective-permute-start | bytes 49160 | tf_op jit(solution)/shard_map/ppermute | solution.py:574
  49.1 1.5 %collective-permute-start.5 = (bf16[8,80,128]{2,1,0:T(8,128)(2,1)S(1)}, bf16[8,80,128]{2,1,0:T(8,128)(2,1)S(1)}, u32[]{:S(2)}, u32[]{:S(2)}) collective-permute-start(bf16[8,80,128]{2,1,0:T(8,128)(2,1)S(1)} %get-tuple-element.82), channel_id=1, source_target_pairs={{0,1},{1,0},{2,3},{3,2},{4,5},{5,4},{6,7},{7,6},{8,9},{9,8},{10,11... | collective-permute-start | bytes 491528 | tf_op jit(solution)/shard_map/ppermute | solution.py:574
  71.4 1.5 %collective-permute-start.6 = (bf16[8,80,128]{2,1,0:T(8,128)(2,1)S(1)}, bf16[8,80,128]{2,1,0:T(8,128)(2,1)S(1)}, u32[]{:S(2)}, u32[]{:S(2)}) collective-permute-start(bf16[8,80,128]{2,1,0:T(8,128)(2,1)S(1)} %get-tuple-element.94), channel_id=1, source_target_pairs={{0,1},{1,0},{2,3},{3,2},{4,5},{5,4},{6,7},{7,6},{8,9},{9,8},{10,11... | collective-permute-start | bytes 491528 | tf_op jit(solution)/shard_map/ppermute | solution.py:574
  75.1 8.6 %collective-permute-start.7 = (bf16[256,512]{1,0:T(8,128)(2,1)S(1)}, bf16[256,512]{1,0:T(8,128)(2,1)S(1)}, u32[]{:S(2)}, u32[]{:S(2)}) collective-permute-start(bf16[256,512]{1,0:T(8,128)(2,1)S(1)} %get-tuple-element.96.a_ref), channel_id=1, source_target_pairs={{0,1},{1,2},{2,3},{3,4},{4,5},{5,6},{6,7},{7,8},{8,9},{9,10},{10,1... | collective-permute-start | bytes 786440 | tf_op jit(solution)/shard_map/ppermute | solution.py:585

commit v8 on v7

--- a/solution.py
+++ b/solution.py
@@ -38,10 +38,14 @@
     return (normed * (1.0 + scale) + shift).astype(BF16)
 
 
-def spread(per_head, sel):
+def split(per_head):
     high = per_head.astype(BF16)
     low = (per_head - high.astype(F32)).astype(BF16)
-    return dot(jnp.concatenate([high, low], axis=1), sel)
+    return jnp.concatenate([high, low], axis=1)
+
+
+def spread(per_head, sel):
+    return dot(split(per_head), sel)
 
 
 def spread_row(per_head, sel):
@@ -106,6 +110,7 @@
     tail_ref,
     pad_ref,
     send_ref,
+    scaled_ref,
 ):
     rows = u_ref.shape[0]
     u = u_ref[...]
@@ -133,8 +138,9 @@
             edge_ref[...] = edge[0:TAIL, :]
             edge = jnp.where(whole_tokens, edge, 0.0)
         ends.append(end)
-        edges.append(spread(edge, sel))
-
+        edges.append(edge)
+
+    edges = split(jnp.concatenate(edges, axis=0))
     chunk = 256
     for slot in range(2):
         ext_ref[slot, TAIL + rows :, :] = jnp.zeros((TAIL, chunk), F32)
@@ -151,7 +157,11 @@
             next_term = taps * ext_ref[slot, start + rows : start + rows + 8, :]
             total = term if total is None else total + term
             after = next_term if after is None else after + next_term
-        act_ref[:, c : c + chunk] = (total * jax.nn.sigmoid(total)).astype(BF16)
+        act = (total * jax.nn.sigmoid(total)).astype(BF16)
+        act_ref[:, c : c + chunk] = act
+        if c < INNER:
+            scale = dot(edges, sel_ref[:, c : c + chunk])
+            scaled_ref[:, c : c + chunk] = (act.astype(F32) * scale).astype(BF16)
         own_ref[:, c : c + chunk] = total[0:8, :]
         tail_ref[:, c : c + chunk] = after
 
@@ -159,8 +169,7 @@
     for b in range(rows // SPAN):
         r = slice(b * SPAN, (b + 1) * SPAN)
         in_map = act_ref[r, INNER : INNER + STATE]
-        scaled = (act_ref[r, 0:INNER].astype(F32) * edges[b]).astype(BF16)
-        term = dot(in_map, scaled, ((0,), (0,)))
+        term = dot(in_map, scaled_ref[r, :], ((0,), (0,)))
         if state is None:
             state = term
         else:
@@ -317,13 +326,16 @@
     return dot(both, stacked) + skip * values.astype(F32)
 
 
-def later_kernel(layer, act_ref, cum_ref, shifted_ref, skip_ref, sel_ref, y_ref):
+def later_kernel(layer, act_ref, cum_ref, shifted_ref, skip_ref, sel_ref, y_ref, decay_ref):
     skip = spread_row(skip_ref[layer : layer + 1, :], sel_ref[...])
     for b in range(1, act_ref.shape[0] // SPAN):
         r = slice(b * SPAN, (b + 1) * SPAN)
         maps = act_ref[r, INNER:]
         affinity = dot(maps[:, STATE:], maps[:, :STATE], ((1,), (1,)))
         cum, shifted = cum_ref[r, :], shifted_ref[:, r]
+        decays = split(jnp.exp(cum))
+        for c in range(0, INNER, 256):
+            decay_ref[(b - 1) * SPAN : b * SPAN, c : c + 256] = dot(decays, sel_ref[:, c : c + 256])
         for pair in range(HEADS // 2):
             cols = slice(pair * LANES, (pair + 1) * LANES)
             y_ref[(b - 1) * SPAN : b * SPAN, cols] = mixed_values(
@@ -331,17 +343,27 @@
             )
 
 
-def gate_kernel(layer, u_ref, w_ref, gate_ref):
+def gate_kernel(layer, u_ref, w_ref, cum_ref, sel_ref, gate_ref, wide_ref):
     chunk = 256
+    before = jnp.zeros((1, HEADS), F32)
+    scales = []
+    for b in range(u_ref.shape[0] // SPAN):
+        cum = cum_ref[b * SPAN : (b + 1) * SPAN, :]
+        scales.append(jnp.exp(cum + before))
+        before = before + cum[SPAN - 1 : SPAN, :]
+    scales = split(jnp.concatenate(scales, axis=0))
     for c in range(0, INNER, chunk):
         cols = slice(c, c + chunk)
+        wide_ref[:, cols] = dot(scales, sel_ref[:, cols])
         gate_ref[:, cols] = silu(dot(u_ref[...], w_ref[layer, :, cols]).astype(BF16).astype(F32))
 
 
 def finish_kernel(
     layer,
     gate_ref,
+    wide_ref,
     later_ref,
+    decay_ref,
     act_ref,
     own_ref,
     cum_ref,
@@ -393,20 +415,15 @@
         return jnp.concatenate([first_ref[:, cols], act_ref[TAIL:SPAN, cols]], axis=0)
 
     first_tokens = lax.broadcasted_iota(jnp.int32, (TAIL, HEADS), 0) < CONV - 1
-    early = spread(jnp.where(first_tokens, edge_ref[...], 0.0) * start, sel)
-    early = (first_ref[:, 0:INNER].astype(F32) * early).astype(BF16)
-    late = dot(first_ref[:, INNER : INNER + STATE], early, ((0,), (0,)))
-
+    early_scale = split(jnp.where(first_tokens, edge_ref[...], 0.0) * start)
+    early_map = first_ref[:, INNER : INNER + STATE]
     spans = rows // SPAN
     out_maps = [acts(b, slice(INNER + STATE, INNER + 2 * STATE)) for b in range(spans)]
     out_map = jnp.concatenate(out_maps, axis=0)
-    before = jnp.zeros((1, HEADS), F32)
-    scales = []
-    for b in range(spans):
-        cum = cum_ref[b * SPAN : (b + 1) * SPAN, :]
-        scales.append(jnp.exp(cum + before))
-        before = before + cum[SPAN - 1 : SPAN, :]
-    wide = spread(jnp.concatenate(scales, axis=0), sel)
+    decayed = [jnp.ones((1, INNER), F32)]
+    for b in range(1, spans - 1):
+        end = (b + 1) * SPAN - 1
+        decayed.append(decayed[-1] * spread_row(jnp.exp(cum_ref[end : end + 1, :]), sel))
     chunk = 256
     for c in range(0, INNER, chunk):
         cols = slice(c, c + chunk)
@@ -414,16 +431,15 @@
             [enter_ref[h, 0:HEAD_DIM, :] for h in range(c // HEAD_DIM, (c + chunk) // HEAD_DIM)],
             axis=0,
         )
-        y_ref[:, cols] = dot(out_map, entering, ((1,), (1,))) * wide[:, cols]
-    decayed = jnp.ones((1, HEADS), F32)
+        y_ref[:, cols] = dot(out_map, entering, ((1,), (1,))) * wide_ref[:, cols]
+    early = (first_ref[:, 0:INNER].astype(F32) * dot(early_scale, sel)).astype(BF16)
+    late = dot(early_map, early, ((0,), (0,)))
     for b in range(1, spans):
-        r = slice(b * SPAN, (b + 1) * SPAN)
-        state = state_ref[(b - 1) * STATE : b * STATE, :] + spread_row(decayed, sel) * late
-        cum = cum_ref[r, :]
-        decayed = decayed * jnp.exp(cum[SPAN - 1 : SPAN, :])
-        own = later_ref[(b - 1) * SPAN : b * SPAN, :]
-        own = own + dot(out_maps[b], state.astype(BF16)) * spread(jnp.exp(cum), sel)
-        y_ref[r, :] = (y_ref[r, :] + own) * gate_ref[r, :]
+        r, own = slice(b * SPAN, (b + 1) * SPAN), slice((b - 1) * SPAN, b * SPAN)
+        state = late if b == 1 else decayed[b - 1] * late
+        state = state_ref[(b - 1) * STATE : b * STATE, :] + state
+        within = later_ref[own, :] + dot(out_maps[b], state.astype(BF16)) * decay_ref[own, :]
+        y_ref[r, :] = (y_ref[r, :] + within) * gate_ref[r, :]
 
     skip = spread_row(skip_ref[layer : layer + 1, :], sel)
     r = slice(0, SPAN)
@@ -456,7 +472,7 @@
     one = jnp.ones((k_rows.stop - k_rows.start, LANES), BF16)
     zero = jnp.zeros((half, LANES), BF16)
     seen = jnp.concatenate([seen, seen], axis=0)
-    together = 2
+    together = 4
     for group in range(0, ATT_HEADS // 2, together):
         columns = [slice(p * LANES, (p + 1) * LANES) for p in range(group, group + together)]
         scores = []
@@ -647,19 +663,20 @@
                 pltpu.VMEM((8, mixed), F32),
                 pltpu.VMEM((HEADS, PAD, LANES), F32),
                 pltpu.VMEM((HEADS, BLOCK, LANES), BF16),
+                pltpu.VMEM((rows, INNER), BF16),
             ],
             name="local",
             flops=2 * rows * width * mixed,
         )
         got = swapped(give, "frames")
-        (later,) = run(
+        later, decays = run(
             functools.partial(later_kernel, layer),
             (act, cum, shifted, skip_gain, sel),
-            [shape((max(spans - 1, 1) * SPAN, INNER), F32)],
+            [shape((max(spans - 1, 1) * SPAN, INNER), F32)] * 2,
             name="later",
             flops=2 * rows * SPAN * INNER,
         )
-        got, later = lax.optimization_barrier((got, later))
+        got, later, decays = lax.optimization_barrier((got, later, decays))
         (send,) = run(
             chip_kernel,
             (keep, got),
@@ -688,16 +705,16 @@
         )
         give, u = lax.optimization_barrier((give, u))
         other = swapped(give, "frames")
-        (gate,) = run(
+        gate, wide = run(
             functools.partial(gate_kernel, layer),
-            (u, input_weight),
-            [shape((rows, INNER), F32)],
+            (u, input_weight, cum, sel),
+            [shape((rows, INNER), F32)] * 2,
             name="gate",
             flops=2 * rows * width * INNER,
         )
         hidden, a = run(
             functools.partial(finish_kernel, layer),
-            (gate, later, act, own, cum, shifted, edge, state, skip_gain, sel)
+            (gate, wide, later, decays, act, own, cum, shifted, edge, state, skip_gain, sel)
             + (mine, other, resid, output_weight, norm_gain, mods),
             [shape((rows, width), F32), shape((rows, width), BF16)],
             [

time: 86.7 us -> 84.6 us (0.976)
  Pallas kernels: 24.4 us -> 21.8 us
    pallas_call x20, Pallas kernels: 24.4 us -> 21.8 us  [run(): pl.pallas_call(kernel, in_specs=[SCALARS] * len(scalars) + [WHOLE] * len(...]
    ppermute x2, waiting for transfers between devices: 7.99 us -> 9.03 us  [from_behind(): return lax.ppermute(value, axis, [(i, i + 1) for i in range(count - 1)])]
where the time goes in v8:
time: 84.6 us; the launch traced here: 84.2 us
  blocking collectives  41.9 us (50%)
  Pallas kernels  21.8 us (26%)
  waiting for transfers between devices  14 us (17%)
  starting transfers between devices  5.02 us (6%)
  local copies, waits for them, and re-layouts  1.12 us (1%)
    all_to_all x4, blocking collectives, over_chips(): return lax.all_to_all(value, axis, 0, 0, axis_index_groups=groups)  41.9 us
    pallas_call x20, Pallas kernels, run(): pl.pallas_call(kernel, in_specs=[SCALARS] * len(scalars) + [WHOLE] * len(...  21.8 us
    ppermute x2, waiting for transfers between devices, from_behind(): return lax.ppermute(value, axis, [(i, i + 1) for i in range(count - 1)])  9.03 us
    ppermute x6, waiting for transfers between devices, swapped(): return lax.ppermute(value, axis, [(i, i ^ 1) for i in range(count)])  5 us
    ppermute x2, starting transfers between devices, from_behind(): return lax.ppermute(value, axis, [(i, i + 1) for i in range(count - 1)])  4.29 us
  transfers between devices with their start and end apart: 8, of which 8 were waited for; matrix products, arithmetic and copies ran while one was open for 0% of the time, Pallas kernels for 8%

profile of v8, /device:TPU:8, one launch (start us, length us, event | category | flops | bytes accessed | tf_op | source)
XLA Modules:
  0.0 84.2 jit_solution(5044276683268555328)
XLA Ops:
  0.0 0.0 copy-start.12
  0.0 0.0 copy-start.11
  0.0 0.0 copy-start.4
  0.0 0.0 slice-start
  0.1 0.7 copy-done.12
  0.7 0.3 copy-done.11
  1.0 0.0 copy-done.13
  1.0 0.1 copy-done.4
  1.1 0.0 copy-start.8
  1.1 0.7 first.1
  1.9 0.1 collective-permute-start
  1.9 1.2 %collective-permute-done.before_ref = bf16[16,512]{1,0:T(8,128)(2,1)S(1)} collective-permute-done((bf16[16,512]{1,0:T(8,128)(2,1)S(1)}, bf16[16,512]{1,0:T(8,128)(2,1)S(1)}, u32[]{:S(2)}, u32[]{:S(2)}) %collective-permute-start) | collective-permute-done | bytes 16416 | tf_op jit(solution)/shard_map/ppermute | solution.py:590
  3.1 0.0 slice-done
  3.1 0.0 slice-done.1
  3.1 0.0 copy-done.5
  3.1 0.0 copy-done.6
  3.1 0.0 copy-done.9
  3.1 0.0 copy-start
  3.2 0.0 copy-start.1
  3.2 0.0 copy-start.3
  3.2 0.0 copy-start.7
  3.2 2.5 %local.2 = (bf16[256,1280]{1,0:T(8,128)(2,1)S(1)}, f32[8,1280]{1,0:T(8,128)S(1)}, f32[256,16]{1,0:T(8,128)S(1)}, f32[16,256]{1,0:T(8,128)S(1)}, f32[16,16]{1,0:T...) custom-call(bf16[256,512]{1,0:T(8,128)(2,1)S(1)} %get-tuple-element.76.u_ref,, ...), custom_call_target="tpu_custom_call" | custom-call | flops 335544320 | bytes 6719616 | tf_op jit(solution)/shard_map/local/pallas_call | solution.py:572
  5.7 0.2 collective-permute-start.1
  5.9 0.0 copy-done.8
  5.9 0.6 later.2
  6.6 0.6 collective-permute-done.1.got_ref
  7.2 0.1 chip.2
  7.3 11.7 %all_to_all.20.got_ref = bf16[8,80,128]{2,1,0:T(8,128)(2,1)S(1)} all-to-all(bf16[8,80,128]{2,1,0:T(8,128)(2,1)S(1)} %chip.2), channel_id=1, replica_groups={{0,2,4,6,8,10,12,14},{1,3,5,7,9,11,13,15},{16,18,20,22,24,26,28,30},{17..., dimensions={0} | all-to-all | bytes 327680 | tf_op jit(solution)/shard_map/all_to_all | solution.py:596
  19.0 0.0 copy-done
  19.0 0.0 copy-done.1
  19.0 0.0 copy-done.3
  19.1 0.0 copy-done.7
  19.1 0.0 copy-done.2
  19.1 0.4 scan.2
  19.5 10.3 %all_to_all.21.back_ref = bf16[8,80,128]{2,1,0:T(8,128)(2,1)S(1)} all-to-all(bf16[8,80,128]{2,1,0:T(8,128)(2,1)S(1)} %scan.2), channel_id=1, replica_groups={{0,2,4,6,8,10,12,14},{1,3,5,7,9,11,13,15},{16,18,20,22,24,26,28,30},{17..., dimensions={0} | all-to-all | bytes 327680 | tf_op jit(solution)/shard_map/all_to_all | solution.py:596
  29.8 0.5 enter.2
  30.2 0.1 collective-permute-start.2
  30.3 0.6 gate.2
  30.9 0.7 collective-permute-done.2.other_ref
  31.7 1.9 %finish.2 = (f32[256,512]{1,0:T(8,128)S(1)}, bf16[256,512]{1,0:T(8,128)(2,1)S(1)}) custom-call(f32[256,1024]{1,0:T(8,128)S(1)} %get-tuple-element.77.gate_ref, f32[256,1024]{1,0:T(8,128)S(1)} %get-tuple-element.78.wide_ref, f32[128,1024]{1,0:T(8,128)S(1)} %get-tuple-element.79.later_ref, f32[128,1024]{1,0:T(8,128)S(1)} %get-tuple-element.80.decay_ref, ...), custom_call_target="tpu_custom_call" | custom-call | bytes 7963776 | tf_op jit(solution)/shard_map/finish/pallas_call | solution.py:572
  33.6 2.2 %collective-permute-start.3 = (bf16[256,512]{1,0:T(8,128)(2,1)S(1)}, bf16[256,512]{1,0:T(8,128)(2,1)S(1)}, u32[]{:S(2)}, u32[]{:S(2)}) collective-permute-start(bf16[256,512]{1,0:T(8,128)(2,1)S(1)} %get-tuple-element.87.a_ref), channel_id=1, source_target_pairs={{0,1},{1,2},{2,3},{3,4},{4,5},{5,6},{6,7},{7,8},{8,9},{9,10},{10,1... | collective-permute-start | bytes 786440 | tf_op jit(solution)/shard_map/ppermute | solution.py:601
  35.8 0.0 copy-done.10
  35.9 1.9 %memory.2 = (bf16[256,512]{1,0:T(8,128)(2,1)S(1)}, f32[256,512]{1,0:T(8,128)S(1)}, f32[256,512]{1,0:T(8,128)S(1)}, f32[256,512]{1,0:T(8,128)S(1)}, f32[256,512]{1,0:T(8,128)S(1)}) custom-call(s32[8]{0:T(128)S(1)} %copy-done.10, bf16[256,512]{1,0:T(8,128)(2,1)S(1)} %get-tuple-element.87.a_ref, bf16[2,512,512]{2,1,0:T(8,128)(2,1)S(1)} %copy-done.2, ...), custom_call_target="tpu_custom_call" | custom-call | flops 402653184 | bytes 5767168 | tf_op jit(solution)/shard_map/memory/pallas_call | solution.py:572
  37.8 4.4 %collective-permute-done.3.prev_ref = bf16[256,512]{1,0:T(8,128)(2,1)S(1)} collective-permute-done((bf16[256,512]{1,0:T(8,128)(2,1)S(1)}, bf16[256,512]{1,0:T(8,128)(2,1)S(1)}, u32[]{:S(2)}, u32[]{:S(2)}) %collective-permute-start.3) | collective-permute-done | bytes 262176 | tf_op jit(solution)/shard_map/ppermute | solution.py:601
  42.2 1.6 %attend.2 = (f32[256,512]{1,0:T(8,128)S(1)}, bf16[256,512]{1,0:T(8,128)(2,1)S(1)}, bf16[16,512]{1,0:T(8,128)(2,1)S(1)}) custom-call(bf16[256,512]{1,0:T(8,128)(2,1)S(1)} %get-tuple-element.88.q_ref, f32[256,512]{1,0:T(8,128)S(1)} %get-tuple-element.89.number_ref, f32[256,512]{1,0:T(8,128)S(1)} %get-tuple-element.90.total_ref, ...), custom_call_target="tpu_custom_call" | custom-call | bytes 7110656 | tf_op jit(solution)/shard_map/attend/pallas_call | solution.py:572
  43.8 0.1 collective-permute-start.4
  43.9 1.2 %collective-permute-done.4.before_ref = bf16[16,512]{1,0:T(8,128)(2,1)S(1)} collective-permute-done((bf16[16,512]{1,0:T(8,128)(2,1)S(1)}, bf16[16,512]{1,0:T(8,128)(2,1)S(1)}, u32[]{:S(2)}, u32[]{:S(2)}) %collective-permute-start.4) | collective-permute-done | bytes 16416 | tf_op jit(solution)/shard_map/ppermute | solution.py:590
  45.1 2.5 %local.3 = (bf16[256,1280]{1,0:T(8,128)(2,1)S(1)}, f32[8,1280]{1,0:T(8,128)S(1)}, f32[256,16]{1,0:T(8,128)S(1)}, f32[16,256]{1,0:T(8,128)S(1)}, f32[16,16]{1,0:T...) custom-call(bf16[256,512]{1,0:T(8,128)(2,1)S(1)} %get-tuple-element.105.u_ref, ...), custom_call_target="tpu_custom_call" | custom-call | flops 335544320 | bytes 6719616 | tf_op jit(solution)/shard_map/local/pallas_call | solution.py:572
  47.5 0.2 collective-permute-start.5
  47.8 0.6 later.3
  48.4 0.6 collective-permute-done.5.got_ref
  49.0 0.1 chip.3
  49.1 9.6 %all_to_all.22.got_ref = bf16[8,80,128]{2,1,0:T(8,128)(2,1)S(1)} all-to-all(bf16[8,80,128]{2,1,0:T(8,128)(2,1)S(1)} %chip.3), channel_id=1, replica_groups={{0,2,4,6,8,10,12,14},{1,3,5,7,9,11,13,15},{16,18,20,22,24,26,28,30},{17..., dimensions={0} | all-to-all | bytes 327680 | tf_op jit(solution)/shard_map/all_to_all | solution.py:596
  58.8 0.4 scan.3
  59.2 10.3 %all_to_all.23.back_ref = bf16[8,80,128]{2,1,0:T(8,128)(2,1)S(1)} all-to-all(bf16[8,80,128]{2,1,0:T(8,128)(2,1)S(1)} %scan.3), channel_id=1, replica_groups={{0,2,4,6,8,10,12,14},{1,3,5,7,9,11,13,15},{16,18,20,22,24,26,28,30},{17..., dimensions={0} | all-to-all | bytes 327680 | tf_op jit(solution)/shard_map/all_to_all | solution.py:596
  69.5 0.5 enter.3
  69.9 0.1 collective-permute-start.6
  70.0 0.6 gate.3
  70.6 0.7 collective-permute-done.6.other_ref
  71.4 2.0 %finish.3 = (f32[256,512]{1,0:T(8,128)S(1)}, bf16[256,512]{1,0:T(8,128)(2,1)S(1)}) custom-call(f32[256,1024]{1,0:T(8,128)S(1)} %get-tuple-element.106.gate_ref, f32[256,1024]{1,0:T(8,128)S(1)} %get-tuple-element.107.wide_ref, f32[128,1024]{1,0:T(8,128)S(1)} %get-tuple-element.108.later_ref, f32[128,1024]{1,0:T(8,128)S(1)} %get-tuple-element.109.decay_ref, ...), custom_call_target="tpu_custom_call" | custom-call | bytes 8225920 | tf_op jit(solution)/shard_map/finish/pallas_call | solution.py:572
  73.3 2.1 %collective-permute-start.7 = (bf16[256,512]{1,0:T(8,128)(2,1)S(1)}, bf16[256,512]{1,0:T(8,128)(2,1)S(1)}, u32[]{:S(2)}, u32[]{:S(2)}) collective-permute-start(bf16[256,512]{1,0:T(8,128)(2,1)S(1)} %get-tuple-element.116.a_ref), channel_id=1, source_target_pairs={{0,1},{1,2},{2,3},{3,4},{4,5},{5,6},{6,7},{7,8},{8,9},{9,10},{10,1... | collective-permute-start | bytes 786440 | tf_op jit(solution)/shard_map/ppermute | solution.py:601
  75.4 1.9 %memory.3 = (bf16[256,512]{1,0:T(8,128)(2,1)S(1)}, f32[256,512]{1,0:T(8,128)S(1)}, f32[256,512]{1,0:T(8,128)S(1)}, f32[256,512]{1,0:T(8,128)S(1)}, f32[256,512]{1,0:T(8,128)S(1)}) custom-call(s32[8]{0:T(128)S(1)} %copy-done.10, bf16[256,512]{1,0:T(8,128)(2,1)S(1)} %get-tuple-element.116.a_ref, bf16[2,512,512]{2,1,0:T(8,128)(2,1)S(1)} %copy-done.2, ...), custom_call_target="tpu_custom_call" | custom-call | flops 402653184 | bytes 5767168 | tf_op jit(solution)/shard_map/memory/pallas_call | solution.py:572
  77.3 4.6 %collective-permute-done.7.prev_ref = bf16[256,512]{1,0:T(8,128)(2,1)S(1)} collective-permute-done((bf16[256,512]{1,0:T(8,128)(2,1)S(1)}, bf16[256,512]{1,0:T(8,128)(2,1)S(1)}, u32[]{:S(2)}, u32[]{:S(2)}) %collective-permute-start.7) | collective-permute-done | bytes 262176 | tf_op jit(solution)/shard_map/ppermute | solution.py:601
  81.9 2.3 %attend.3 = f32[256,512]{1,0:T(8,128)} custom-call(bf16[256,512]{1,0:T(8,128)(2,1)S(1)} %get-tuple-element.117.q_ref, f32[256,512]{1,0:T(8,128)S(1)} %get-tuple-element.118.number_ref, f32[256,512]{1,0:T(8,128)S(1)} %get-tuple-element.119.total_ref, f32[256,512]{1,0:T(8,128)S(1)} %get-tuple-element.120.top_ref, f32[256,512]{1,0:T(8,128)S(1)} %get-tuple-element.121.seen_ref, ...), custom_call_target="tpu_custom_call" | custom-call | bytes 6832128 | tf_op jit(solution)/shard_map/attend/pallas_call | solution.py:572
  (9 shorter events, 0.0 us)
Async XLA Ops:
  0.0 0.7 copy-start.12
  0.0 1.0 %copy-start.11 = (bf16[2,50,4,512]{3,2,1,0:T(4,128)(2,1)S(1)}, bf16[2,50,4,512]{3,2,1,0:T(4,128)(2,1)}, u32[]{:S(2)}) copy-start(bf16[2,50,4,512]{3,2,1,0:T(4,128)(2,1)} %all_mods_ref.1) | copy-start | bytes 1228804
  0.0 1.0 %copy-start.13 = (s32[8]{0:T(128)S(1)}, s32[8]{0:T(128)}, u32[]{:S(2)}) copy-start(s32[8]{0:T(128)} %step_ref.1) | copy-start | bytes 100
  0.0 1.1 %copy-start.4 = (bf16[8,32,512]{2,1,0:T(8,128)(2,1)S(1)}, bf16[8,32,512]{2,1,0:T(8,128)(2,1)}, u32[]{:S(2)}) copy-start(bf16[8,32,512]{2,1,0:T(8,128)(2,1)} %param.15) | copy-start | bytes 786436
  0.0 3.1 %slice-start = ((s8[4718592]{0:T(1024)(128)(4,1)}), s8[4194304]{0:T(1024)(128)(4,1)S(1)}, s32[]{:S(2)}) async-start(s8[4718592]{0:T(1024)(128)(4,1)} %bitcast.4), calls=%async_computation.4 | async-start | bytes 8388608
  1.1 2.0 %slice-start.1 = ((s8[4718592]{0:T(1024)(128)(4,1)}), s8[524288]{0:T(1024)(128)(4,1)S(1)}, s32[]{:S(2)}) async-start(s8[4718592]{0:T(1024)(128)(4,1)} %bitcast.4), calls=%async_computation.5 | async-start | bytes 1048576
  1.1 2.0 %copy-start.5 = (f32[2,4,1280]{2,1,0:T(4,128)S(1)}, f32[2,4,1280]{2,1,0:T(4,128)}, u32[]{:S(2)}) copy-start(f32[2,4,1280]{2,1,0:T(4,128)} %conv_ref.3) | copy-start | bytes 122884
  1.1 2.0 %copy-start.6 = (bf16[2,512,16]{1,2,0:T(8,128)(2,1)S(1)}, bf16[2,512,16]{1,2,0:T(8,128)(2,1)}, u32[]{:S(2)}) copy-start(bf16[2,512,16]{1,2,0:T(8,128)(2,1)} %param.20) | copy-start | bytes 98308
  1.1 2.0 %copy-start.9 = (f32[2,16]{1,0:T(2,128)S(1)}, f32[2,16]{1,0:T(2,128)}, u32[]{:S(2)}) copy-start(f32[2,16]{1,0:T(2,128)} %decay_ref.3) | copy-start | bytes 388
  1.1 4.8 %copy-start.8 = (f32[2,16]{1,0:T(2,128)S(1)}, f32[2,16]{1,0:T(2,128)}, u32[]{:S(2)}) copy-start(f32[2,16]{1,0:T(2,128)} %skip_ref.7) | copy-start | bytes 388
  1.9 1.2 %collective-permute-start = (bf16[16,512]{1,0:T(8,128)(2,1)S(1)}, bf16[16,512]{1,0:T(8,128)(2,1)S(1)}, u32[]{:S(2)}, u32[]{:S(2)}) collective-permute-start(bf16[16,512]{1,0:T(8,128)(2,1)S(1)} %get-tuple-element.65), channel_id=1, source_target_pairs={{0,1},{1,0},{2,3},{3,2},{4,5},{5,4},{6,7},{7,6},{8,9},{9,8},{10,11... | collective-permute-start | bytes 49160 | tf_op jit(solution)/shard_map/ppermute | solution.py:590
  3.1 15.9 %copy-start = (bf16[2,512,1024]{2,1,0:T(8,128)(2,1)S(1)}, bf16[2,512,1024]{2,1,0:T(8,128)(2,1)}, u32[]{:S(2)}) copy-start(bf16[2,512,1024]{2,1,0:T(8,128)(2,1)} %wm_ref.7) | copy-start | bytes 6291460
  3.2 15.9 %copy-start.1 = (bf16[2,1024,512]{2,1,0:T(8,128)(2,1)S(1)}, bf16[2,1024,512]{2,1,0:T(8,128)(2,1)}, u32[]{:S(2)}) copy-start(bf16[2,1024,512]{2,1,0:T(8,128)(2,1)} %wo_ref.3) | copy-start | bytes 6291460
  3.2 15.9 %copy-start.3 = (bf16[2,512,512]{2,1,0:T(8,128)(2,1)S(1)}, bf16[2,512,512]{2,1,0:T(8,128)(2,1)}, u32[]{:S(2)}) copy-start(bf16[2,512,512]{2,1,0:T(8,128)(2,1)} %merge_ref.3) | copy-start | bytes 3145732
  3.2 15.9 %copy-start.7 = (f32[2,1024]{1,0:T(2,128)S(1)}, f32[2,1024]{1,0:T(2,128)}, u32[]{:S(2)}) copy-start(f32[2,1024]{1,0:T(2,128)} %gain_ref.3) | copy-start | bytes 24580
  5.7 13.4 %copy-start.2 = (bf16[2,512,512]{2,1,0:T(8,128)(2,1)S(1)}, bf16[2,512,512]{2,1,0:T(8,128)(2,1)}, u32[]{:S(2)}) copy-start(bf16[2,512,512]{2,1,0:T(8,128)(2,1)} %wq_ref.3) | copy-start | bytes 3145732
  5.7 1.5 %collective-permute-start.1 = (bf16[8,80,128]{2,1,0:T(8,128)(2,1)S(1)}, bf16[8,80,128]{2,1,0:T(8,128)(2,1)S(1)}, u32[]{:S(2)}, u32[]{:S(2)}) collective-permute-start(bf16[8,80,128]{2,1,0:T(8,128)(2,1)S(1)} %get-tuple-element.68), channel_id=1, source_target_pairs={{0,1},{1,0},{2,3},{3,2},{4,5},{5,4},{6,7},{7,6},{8,9},{9,8},{10,11... | collective-permute-start | bytes 491528 | tf_op jit(solution)/shard_map/ppermute | solution.py:590
  30.2 1.5 %collective-permute-start.2 = (bf16[8,80,128]{2,1,0:T(8,128)(2,1)S(1)}, bf16[8,80,128]{2,1,0:T(8,128)(2,1)S(1)}, u32[]{:S(2)}, u32[]{:S(2)}) collective-permute-start(bf16[8,80,128]{2,1,0:T(8,128)(2,1)S(1)} %get-tuple-element.85), channel_id=1, source_target_pairs={{0,1},{1,0},{2,3},{3,2},{4,5},{5,4},{6,7},{7,6},{8,9},{9,8},{10,11... | collective-permute-start | bytes 491528 | tf_op jit(solution)/shard_map/ppermute | solution.py:590
  31.7 4.2 %copy-start.10 = (s32[8]{0:T(128)S(1)}, s32[8]{0:T(128)}, u32[]{:S(2)}) copy-start(s32[8]{0:T(128)} %reach_ref.3) | copy-start | bytes 100
  33.6 8.6 %collective-permute-start.3 = (bf16[256,512]{1,0:T(8,128)(2,1)S(1)}, bf16[256,512]{1,0:T(8,128)(2,1)S(1)}, u32[]{:S(2)}, u32[]{:S(2)}) collective-permute-start(bf16[256,512]{1,0:T(8,128)(2,1)S(1)} %get-tuple-element.87.a_ref), channel_id=1, source_target_pairs={{0,1},{1,2},{2,3},{3,4},{4,5},{5,6},{6,7},{7,8},{8,9},{9,10},{10,1... | collective-permute-start | bytes 786440 | tf_op jit(solution)/shard_map/ppermute | solution.py:601
  43.8 1.2 %collective-permute-start.4 = (bf16[16,512]{1,0:T(8,128)(2,1)S(1)}, bf16[16,512]{1,0:T(8,128)(2,1)S(1)}, u32[]{:S(2)}, u32[]{:S(2)}) collective-permute-start(bf16[16,512]{1,0:T(8,128)(2,1)S(1)} %get-tuple-element.95), channel_id=1, source_target_pairs={{0,1},{1,0},{2,3},{3,2},{4,5},{5,4},{6,7},{7,6},{8,9},{9,8},{10,11... | collective-permute-start | bytes 49160 | tf_op jit(solution)/shard_map/ppermute | solution.py:590
  47.5 1.5 %collective-permute-start.5 = (bf16[8,80,128]{2,1,0:T(8,128)(2,1)S(1)}, bf16[8,80,128]{2,1,0:T(8,128)(2,1)S(1)}, u32[]{:S(2)}, u32[]{:S(2)}) collective-permute-start(bf16[8,80,128]{2,1,0:T(8,128)(2,1)S(1)} %get-tuple-element.97), channel_id=1, source_target_pairs={{0,1},{1,0},{2,3},{3,2},{4,5},{5,4},{6,7},{7,6},{8,9},{9,8},{10,11... | collective-permute-start | bytes 491528 | tf_op jit(solution)/shard_map/ppermute | solution.py:590
  69.9 1.5 %collective-permute-start.6 = (bf16[8,80,128]{2,1,0:T(8,128)(2,1)S(1)}, bf16[8,80,128]{2,1,0:T(8,128)(2,1)S(1)}, u32[]{:S(2)}, u32[]{:S(2)}) collective-permute-start(bf16[8,80,128]{2,1,0:T(8,128)(2,1)S(1)} %get-tuple-element.114), channel_id=1, source_target_pairs={{0,1},{1,0},{2,3},{3,2},{4,5},{5,4},{6,7},{7,6},{8,9},{9,8},{10,11... | collective-permute-start | bytes 491528 | tf_op jit(solution)/shard_map/ppermute | solution.py:590
  73.3 8.6 %collective-permute-start.7 = (bf16[256,512]{1,0:T(8,128)(2,1)S(1)}, bf16[256,512]{1,0:T(8,128)(2,1)S(1)}, u32[]{:S(2)}, u32[]{:S(2)}) collective-permute-start(bf16[256,512]{1,0:T(8,128)(2,1)S(1)} %get-tuple-element.116.a_ref), channel_id=1, source_target_pairs={{0,1},{1,2},{2,3},{3,4},{4,5},{5,6},{6,7},{7,8},{8,9},{9,10},{10,1... | collective-permute-start | bytes 786440 | tf_op jit(solution)/shard_map/ppermute | solution.py:601

commit v9 on v8

--- a/solution.py
+++ b/solution.py
@@ -117,7 +117,7 @@
     sel = sel_ref[...]
     core = core_index()
     tail_rows = before_ref[...].astype(F32) * core.astype(F32)
-    tail_rows = tail_rows.astype(BF16)
+    with_tail = jnp.concatenate([tail_rows.astype(BF16), u], axis=0)
     raw = dot(u, sw_ref[layer], ((1,), (1,))) + bias_ref[layer, 0:1, :]
     step = jnp.maximum(raw, 0.0) + jnp.log1p(jnp.exp(-jnp.abs(raw)))
     log_decay = -jnp.exp(decay_ref[layer : layer + 1, :]) * step
@@ -147,8 +147,7 @@
     for c in [INNER] + list(range(0, INNER, chunk)):
         w = w_ref[layer, :, INNER + c : INNER + c + chunk]
         slot = c // chunk % 2
-        ext_ref[slot, 0:TAIL, :] = dot(tail_rows, w).astype(BF16).astype(F32)
-        ext_ref[slot, TAIL : TAIL + rows, :] = dot(u, w).astype(BF16).astype(F32)
+        ext_ref[slot, 0 : TAIL + rows, :] = dot(with_tail, w).astype(BF16).astype(F32)
         total, after = None, None
         for k in range(CONV):
             start = TAIL - (CONV - 1) + k
@@ -520,9 +519,28 @@
         partial_attention(q_ref, seen, kv_ref, half, r, k_rows, done)
 
 
-def attend_kernel(
+def attend_half(part, q_ref, own_refs, seen_ref, kv_ref, first_key, out_ref):
+    number_ref, total_ref, top_ref = own_refs
+    rows = q_ref.shape[0]
+    half = rows // 2
+    r = slice(part * half, (part + 1) * half)
+    keys = slice(part * half, rows)
+
+    def done(cols, number, total, top):
+        top_own = top_ref[r, cols]
+        highest = jnp.maximum(top, top_own)
+        mine, own = jnp.exp(top - highest), jnp.exp(top_own - highest)
+        number = number * mine + number_ref[r, cols] * own
+        total = total * mine + total_ref[r, cols] * own
+        out_ref[r, cols] = (number / total).astype(BF16)
+
+    k_rows = slice(keys.start - first_key, keys.stop - first_key)
+    partial_attention(q_ref, seen_ref[r, keys], kv_ref, half, r, k_rows, done)
+    return r
+
+
+def last_rows_kernel(
     layer,
-    last,
     q_ref,
     number_ref,
     total_ref,
@@ -533,46 +551,92 @@
     merge_ref,
     hidden_ref,
     mods_ref,
-    *rest,
+    resid_ref,
+    u_ref,
+    tail_ref,
+    kv_ref,
+    out_ref,
 ):
-    if last:
-        resid_ref, kv_ref, out_ref = rest
-    else:
-        resid_ref, u_ref, tail_ref, kv_ref, out_ref = rest
-    rows = q_ref.shape[0]
-    half = rows // 2
+    half = q_ref.shape[0] // 2
+    kv_ref[...] = dot(prev_ref[half:, :], wm_ref[layer]).astype(BF16)
+    r = attend_half(1, q_ref, (number_ref, total_ref, top_ref), seen_ref, kv_ref, half, out_ref)
+    resid = hidden_ref[r, :] + dot(out_ref[r, :], merge_ref[layer])
+    resid_ref[...] = resid
+    u = rms_mod(resid, mods_ref[layer + 1, 0:1, :], mods_ref[layer + 1, 1:2, :])
+    u_ref[...] = u
+    tail_ref[...] = u[half - TAIL :]
+
+
+def first_rows_kernel(
+    layer,
+    q_ref,
+    number_ref,
+    total_ref,
+    top_ref,
+    seen_ref,
+    prev_ref,
+    wm_ref,
+    merge_ref,
+    hidden_ref,
+    mods_ref,
+    late_resid_ref,
+    late_u_ref,
+    late_kv_ref,
+    resid_ref,
+    u_ref,
+    kv_ref,
+    out_ref,
+):
+    half = q_ref.shape[0] // 2
+    kv_ref[0:half, :] = dot(prev_ref[0:half, :], wm_ref[layer]).astype(BF16)
+    kv_ref[half:, :] = late_kv_ref[...]
+    r = attend_half(0, q_ref, (number_ref, total_ref, top_ref), seen_ref, kv_ref, 0, out_ref)
+    resid = hidden_ref[r, :] + dot(out_ref[r, :], merge_ref[layer])
+    resid_ref[r, :] = resid
+    resid_ref[half:, :] = late_resid_ref[...]
+    u_ref[r, :] = rms_mod(resid, mods_ref[layer + 1, 0:1, :], mods_ref[layer + 1, 1:2, :])
+    u_ref[half:, :] = late_u_ref[...]
+
+
+def closing_kernel(
+    layer,
+    q_ref,
+    number_ref,
+    total_ref,
+    top_ref,
+    seen_ref,
+    prev_ref,
+    wm_ref,
+    merge_ref,
+    hidden_ref,
+    out_hbm,
+    kv_ref,
+    out_ref,
+    resid_ref,
+    sems,
+):
     kv_ref[...] = dot(prev_ref[...], wm_ref[layer]).astype(BF16)
+    copies = []
     for part in range(2):
-        r = slice(part * half, (part + 1) * half)
-        k_rows = slice(part * half, rows)
-
-        def done(cols, number, total, top):
-            top_own = top_ref[r, cols]
-            highest = jnp.maximum(top, top_own)
-            mine, own = jnp.exp(top - highest), jnp.exp(top_own - highest)
-            number = number * mine + number_ref[r, cols] * own
-            total = total * mine + total_ref[r, cols] * own
-            out_ref[r, cols] = (number / total).astype(BF16)
-
-        partial_attention(q_ref, seen_ref[r, k_rows], kv_ref, half, r, k_rows, done)
-    resid = hidden_ref[...] + dot(out_ref[...], merge_ref[layer])
-    resid_ref[...] = resid
-    if not last:
-        u = rms_mod(resid, mods_ref[layer + 1, 0:1, :], mods_ref[layer + 1, 1:2, :])
-        u_ref[...] = u
-        tail_ref[...] = u[rows - TAIL :]
+        own_refs = (number_ref, total_ref, top_ref)
+        r = attend_half(part, q_ref, own_refs, seen_ref, kv_ref, 0, out_ref)
+        resid_ref[part] = hidden_ref[r, :] + dot(out_ref[r, :], merge_ref[layer])
+        copies.append(pltpu.make_async_copy(resid_ref.at[part], out_hbm.at[part], sems.at[part]))
+        copies[-1].start()
+    for copy in copies:
+        copy.wait()
 
 
 WHOLE = pl.BlockSpec(memory_space=pltpu.VMEM)
 SCALARS = pl.BlockSpec(memory_space=pltpu.SMEM)
 
 
-def run(kernel, operands, outs, scratch=(), name=None, flops=0, scalars=()):
+def run(kernel, operands, outs, scratch=(), name=None, flops=0, scalars=(), out_spec=WHOLE):
     moved = sum(o.size * o.dtype.itemsize for o in list(operands) + list(outs))
     return pl.pallas_call(
         kernel,
         in_specs=[SCALARS] * len(scalars) + [WHOLE] * len(operands),
-        out_specs=[WHOLE] * len(outs),
+        out_specs=[out_spec] * len(outs),
         out_shape=list(outs),
         scratch_shapes=list(scratch),
         compiler_params=pltpu.CompilerParams(vmem_limit_bytes=20 * 1024 * 1024),
@@ -737,20 +801,43 @@
             scalars=(lookback,),
             flops=2 * rows * width * 3 * ATTN,
         )
-        last = layer == LAYERS - 1
-        outs = [shape((rows, width), F32)]
-        if not last:
-            outs += [shape((rows, width), BF16), shape((TAIL, width), BF16)]
-        result = run(
-            functools.partial(attend_kernel, layer, last),
-            (q, number, total, top, seen, prev, memory_weight, merge_weight, hidden, mods),
-            outs,
-            [pltpu.VMEM((rows, 2 * ATTN), BF16), pltpu.VMEM((rows, ATTN), BF16)],
-            name="attend",
-        )
-        resid = result[0]
-        if not last:
-            u, tail = result[1:]
+        half = rows // 2
+        attention = (q, number, total, top, seen, prev, memory_weight, merge_weight, hidden)
+        if layer == LAYERS - 1:
+            (resid,) = run(
+                functools.partial(closing_kernel, layer),
+                attention,
+                [shape((2, half, width), F32)],
+                [
+                    pltpu.VMEM((rows, 2 * ATTN), BF16),
+                    pltpu.VMEM((rows, ATTN), BF16),
+                    pltpu.VMEM((2, half, width), F32),
+                    pltpu.SemaphoreType.DMA((2,)),
+                ],
+                name="closing",
+                out_spec=pl.BlockSpec(memory_space=pl.ANY),
+            )
+        else:
+            late_resid, late_u, tail, late_kv = run(
+                functools.partial(last_rows_kernel, layer),
+                attention + (mods,),
+                [
+                    shape((half, width), F32),
+                    shape((half, width), BF16),
+                    shape((TAIL, width), BF16),
+                    shape((half, 2 * ATTN), BF16),
+                ],
+                [pltpu.VMEM((rows, ATTN), BF16)],
+                name="last_rows",
+            )
+            resid, u = run(
+                functools.partial(first_rows_kernel, layer),
+                attention + (mods, late_resid, late_u, late_kv),
+                [shape((rows, width), F32), shape((rows, width), BF16)],
+                [pltpu.VMEM((rows, 2 * ATTN), BF16), pltpu.VMEM((rows, ATTN), BF16)],
+                name="first_rows",
+                flops=2 * half * width * 4 * ATTN,
+            )
     return resid.reshape(latents.shape)
 
 

time: 84.6 us -> 84.7 us (level)
  waiting for transfers between devices: 14 us -> 12.7 us
    ppermute x6, waiting for transfers between devices: 5 us -> 3.64 us  [swapped(): return lax.ppermute(value, axis, [(i, i ^ 1) for i in range(count)])]
    pallas_call x20 -> x21, Pallas kernels: 21.8 us -> 22.5 us  [run(): pl.pallas_call(kernel, in_specs=[SCALARS] * len(scalars) + [WHOLE] * len(...]
  transfers between devices with their start and end apart: 8 -> 8, of which waited for: 8 -> 7; matrix products, arithmetic and copies ran while one was open for 0% -> 0% of each run, Pallas kernels for 8% -> 9%
where the time goes in v9:
time: 84.7 us; the launch traced here: 84.3 us
  blocking collectives  42.1 us (50%)
  Pallas kernels  22.5 us (27%)
  waiting for transfers between devices  12.7 us (15%)
  starting transfers between devices  5.34 us (6%)
  local copies, waits for them, and re-layouts  1.12 us (1%)
    all_to_all x4, blocking collectives, over_chips(): return lax.all_to_all(value, axis, 0, 0, axis_index_groups=groups)  42.1 us
    pallas_call x21, Pallas kernels, run(): pl.pallas_call(kernel, in_specs=[SCALARS] * len(scalars) + [WHOLE] * len(...  22.5 us
    ppermute x2, waiting for transfers between devices, from_behind(): return lax.ppermute(value, axis, [(i, i + 1) for i in range(count - 1)])  9.05 us
    ppermute x2, starting transfers between devices, from_behind(): return lax.ppermute(value, axis, [(i, i + 1) for i in range(count - 1)])  4.29 us
    ppermute x6, waiting for transfers between devices, swapped(): return lax.ppermute(value, axis, [(i, i ^ 1) for i in range(count)])  3.64 us
  transfers between devices with their start and end apart: 8, of which 7 were waited for; matrix products, arithmetic and copies ran while one was open for 0% of the time, Pallas kernels for 9%

profile of v9, /device:TPU:8, one launch (start us, length us, event | category | flops | bytes accessed | tf_op | source)
XLA Modules:
  0.0 84.3 jit_solution(11468160438935247778)
XLA Ops:
  0.0 0.0 copy-start.12
  0.0 0.0 copy-start.4
  0.0 0.0 slice-start
  0.1 0.7 copy-done.12
  0.7 0.3 copy-done.11
  1.0 0.0 copy-done.13
  1.0 0.1 copy-done.4
  1.1 0.0 copy-start.8
  1.1 0.7 first.1
  1.9 0.1 collective-permute-start
  1.9 1.2 %collective-permute-done.before_ref = bf16[16,512]{1,0:T(8,128)(2,1)S(1)} collective-permute-done((bf16[16,512]{1,0:T(8,128)(2,1)S(1)}, bf16[16,512]{1,0:T(8,128)(2,1)S(1)}, u32[]{:S(2)}, u32[]{:S(2)}) %collective-permute-start) | collective-permute-done | bytes 16416 | tf_op jit(solution)/shard_map/ppermute | solution.py:654
  3.1 0.0 slice-done
  3.1 0.0 slice-done.1
  3.1 0.0 copy-done.5
  3.1 0.0 copy-done.6
  3.1 0.0 copy-done.9
  3.1 0.0 copy-start
  3.2 0.0 copy-start.1
  3.2 0.0 copy-start.3
  3.2 0.0 copy-start.7
  3.2 2.5 %local.2 = (bf16[256,1280]{1,0:T(8,128)(2,1)S(1)}, f32[8,1280]{1,0:T(8,128)S(1)}, f32[256,16]{1,0:T(8,128)S(1)}, f32[16,256]{1,0:T(8,128)S(1)}, f32[16,16]{1,0:T...) custom-call(bf16[256,512]{1,0:T(8,128)(2,1)S(1)} %get-tuple-element.79.u_ref,, ...), custom_call_target="tpu_custom_call" | custom-call | flops 335544320 | bytes 6719616 | tf_op jit(solution)/shard_map/local/pallas_call | solution.py:636
  5.7 0.2 collective-permute-start.1
  5.9 0.0 copy-done.8
  5.9 0.6 later.2
  6.5 0.6 collective-permute-done.1.got_ref
  7.1 0.1 chip.2
  7.3 11.7 %all_to_all.20.got_ref = bf16[8,80,128]{2,1,0:T(8,128)(2,1)S(1)} all-to-all(bf16[8,80,128]{2,1,0:T(8,128)(2,1)S(1)} %chip.2), channel_id=1, replica_groups={{0,2,4,6,8,10,12,14},{1,3,5,7,9,11,13,15},{16,18,20,22,24,26,28,30},{17..., dimensions={0} | all-to-all | bytes 327680 | tf_op jit(solution)/shard_map/all_to_all | solution.py:660
  19.0 0.0 copy-done
  19.0 0.0 copy-done.1
  19.0 0.0 copy-done.3
  19.0 0.0 copy-done.7
  19.0 0.0 copy-done.2
  19.0 0.4 scan.2
  19.5 10.3 %all_to_all.21.back_ref = bf16[8,80,128]{2,1,0:T(8,128)(2,1)S(1)} all-to-all(bf16[8,80,128]{2,1,0:T(8,128)(2,1)S(1)} %scan.2), channel_id=1, replica_groups={{0,2,4,6,8,10,12,14},{1,3,5,7,9,11,13,15},{16,18,20,22,24,26,28,30},{17..., dimensions={0} | all-to-all | bytes 327680 | tf_op jit(solution)/shard_map/all_to_all | solution.py:660
  29.7 0.5 enter.2
  30.2 0.1 collective-permute-start.2
  30.3 0.6 gate.2
  30.9 0.7 collective-permute-done.2.other_ref
  31.6 1.9 %finish.2 = (f32[256,512]{1,0:T(8,128)S(1)}, bf16[256,512]{1,0:T(8,128)(2,1)S(1)}) custom-call(f32[256,1024]{1,0:T(8,128)S(1)} %get-tuple-element.80.gate_ref, f32[256,1024]{1,0:T(8,128)S(1)} %get-tuple-element.81.wide_ref, f32[128,1024]{1,0:T(8,128)S(1)} %get-tuple-element.82.later_ref, f32[128,1024]{1,0:T(8,128)S(1)} %get-tuple-element.83.decay_ref, ...), custom_call_target="tpu_custom_call" | custom-call | bytes 7963776 | tf_op jit(solution)/shard_map/finish/pallas_call | solution.py:636
  33.6 2.2 %collective-permute-start.3 = (bf16[256,512]{1,0:T(8,128)(2,1)S(1)}, bf16[256,512]{1,0:T(8,128)(2,1)S(1)}, u32[]{:S(2)}, u32[]{:S(2)}) collective-permute-start(bf16[256,512]{1,0:T(8,128)(2,1)S(1)} %get-tuple-element.90.a_ref), channel_id=1, source_target_pairs={{0,1},{1,2},{2,3},{3,4},{4,5},{5,6},{6,7},{7,8},{8,9},{9,10},{10,1... | collective-permute-start | bytes 786440 | tf_op jit(solution)/shard_map/ppermute | solution.py:665
  35.8 0.0 copy-done.10
  35.8 1.9 %memory.2 = (bf16[256,512]{1,0:T(8,128)(2,1)S(1)}, f32[256,512]{1,0:T(8,128)S(1)}, f32[256,512]{1,0:T(8,128)S(1)}, f32[256,512]{1,0:T(8,128)S(1)}, f32[256,512]{1,0:T(8,128)S(1)}) custom-call(s32[8]{0:T(128)S(1)} %copy-done.10, bf16[256,512]{1,0:T(8,128)(2,1)S(1)} %get-tuple-element.90.a_ref, bf16[2,512,512]{2,1,0:T(8,128)(2,1)S(1)} %copy-done.3, ...), custom_call_target="tpu_custom_call" | custom-call | flops 402653184 | bytes 5767168 | tf_op jit(solution)/shard_map/memory/pallas_call | solution.py:636
  37.7 4.4 %collective-permute-done.3.prev_ref = bf16[256,512]{1,0:T(8,128)(2,1)S(1)} collective-permute-done((bf16[256,512]{1,0:T(8,128)(2,1)S(1)}, bf16[256,512]{1,0:T(8,128)(2,1)S(1)}, u32[]{:S(2)}, u32[]{:S(2)}) %collective-permute-start.3) | collective-permute-done | bytes 262176 | tf_op jit(solution)/shard_map/ppermute | solution.py:665
  42.2 1.1 %last_rows.1 = (f32[128,512]{1,0:T(8,128)S(1)}, bf16[128,512]{1,0:T(8,128)(2,1)S(1)}, bf16[16,512]{1,0:T(8,128)(2,1)S(1)}, bf16[128,1024]{1,0:T(8,128)(2,1)S(1)}) custom-call(bf16[256,512]{1,0:T(8,128)(2,1)S(1)} %get-tuple-element.91.q_ref, f32[256,512]{1,0:T(8,128)S(1)} %get-tuple-element.92.number_ref, f32[256,512]{1,0:T(8,128)S(1)} %get-tuple-element.93.total_ref, ...), custom_call_target="tpu_custom_call" | custom-call | bytes 6979584 | tf_op jit(solution)/shard_map/last_rows/pallas_call | solution.py:636
  43.3 0.1 collective-permute-start.4
  43.4 1.2 %first_rows.1 = (f32[256,512]{1,0:T(8,128)S(1)}, bf16[256,512]{1,0:T(8,128)(2,1)S(1)}) custom-call(bf16[256,512]{1,0:T(8,128)(2,1)S(1)} %get-tuple-element.91.q_ref, f32[256,512]{1,0:T(8,128)S(1)} %get-tuple-element.92.number_ref, f32[256,512]{1,0:T(8,128)S(1)} %get-tuple-element.93.total_ref, f32[256,512]{1,0:T(8,128)S(1)} %get-tuple-element.94.top_ref, ...), custom_call_target="tpu_custom_call" | custom-call | flops 268435456 | bytes 7749632 | tf_op jit(solution)/shard_map/first_rows/pallas_call | solution.py:636
  44.5 0.0 collective-permute-done.4.before_ref
  44.5 2.5 %local.3 = (bf16[256,1280]{1,0:T(8,128)(2,1)S(1)}, f32[8,1280]{1,0:T(8,128)S(1)}, f32[256,16]{1,0:T(8,128)S(1)}, f32[16,256]{1,0:T(8,128)S(1)}, f32[16,16]{1,0:T...) custom-call(bf16[256,512]{1,0:T(8,128)(2,1)S(1)} %get-tuple-element.111.u_ref, ...), custom_call_target="tpu_custom_call" | custom-call | flops 335544320 | bytes 6719616 | tf_op jit(solution)/shard_map/local/pallas_call | solution.py:636
  47.0 0.5 collective-permute-start.5
  47.5 0.6 later.3
  48.2 0.4 collective-permute-done.5.got_ref
  48.6 0.1 chip.3
  48.7 9.8 %all_to_all.22.got_ref = bf16[8,80,128]{2,1,0:T(8,128)(2,1)S(1)} all-to-all(bf16[8,80,128]{2,1,0:T(8,128)(2,1)S(1)} %chip.3), channel_id=1, replica_groups={{0,2,4,6,8,10,12,14},{1,3,5,7,9,11,13,15},{16,18,20,22,24,26,28,30},{17..., dimensions={0} | all-to-all | bytes 327680 | tf_op jit(solution)/shard_map/all_to_all | solution.py:660
  58.5 0.4 scan.3
  58.9 10.3 %all_to_all.23.back_ref = bf16[8,80,128]{2,1,0:T(8,128)(2,1)S(1)} all-to-all(bf16[8,80,128]{2,1,0:T(8,128)(2,1)S(1)} %scan.3), channel_id=1, replica_groups={{0,2,4,6,8,10,12,14},{1,3,5,7,9,11,13,15},{16,18,20,22,24,26,28,30},{17..., dimensions={0} | all-to-all | bytes 327680 | tf_op jit(solution)/shard_map/all_to_all | solution.py:660
  69.2 0.4 enter.3
  69.7 0.1 collective-permute-start.6
  69.7 0.6 gate.3
  70.4 0.7 collective-permute-done.6.other_ref
  71.1 2.0 %finish.3 = (f32[256,512]{1,0:T(8,128)S(1)}, bf16[256,512]{1,0:T(8,128)(2,1)S(1)}) custom-call(f32[256,1024]{1,0:T(8,128)S(1)} %get-tuple-element.112.gate_ref, f32[256,1024]{1,0:T(8,128)S(1)} %get-tuple-element.113.wide_ref, f32[128,1024]{1,0:T(8,128)S(1)} %get-tuple-element.114.later_ref, f32[128,1024]{1,0:T(8,128)S(1)} %get-tuple-element.115.decay_ref, ...), custom_call_target="tpu_custom_call" | custom-call | bytes 8225920 | tf_op jit(solution)/shard_map/finish/pallas_call | solution.py:636
  73.1 2.1 %collective-permute-start.7 = (bf16[256,512]{1,0:T(8,128)(2,1)S(1)}, bf16[256,512]{1,0:T(8,128)(2,1)S(1)}, u32[]{:S(2)}, u32[]{:S(2)}) collective-permute-start(bf16[256,512]{1,0:T(8,128)(2,1)S(1)} %get-tuple-element.122.a_ref), channel_id=1, source_target_pairs={{0,1},{1,2},{2,3},{3,4},{4,5},{5,6},{6,7},{7,8},{8,9},{9,10},{10,1... | collective-permute-start | bytes 786440 | tf_op jit(solution)/shard_map/ppermute | solution.py:665
  75.2 1.9 %memory.3 = (bf16[256,512]{1,0:T(8,128)(2,1)S(1)}, f32[256,512]{1,0:T(8,128)S(1)}, f32[256,512]{1,0:T(8,128)S(1)}, f32[256,512]{1,0:T(8,128)S(1)}, f32[256,512]{1,0:T(8,128)S(1)}) custom-call(s32[8]{0:T(128)S(1)} %copy-done.10, bf16[256,512]{1,0:T(8,128)(2,1)S(1)} %get-tuple-element.122.a_ref, bf16[2,512,512]{2,1,0:T(8,128)(2,1)S(1)} %copy-done.3, ...), custom_call_target="tpu_custom_call" | custom-call | flops 402653184 | bytes 5767168 | tf_op jit(solution)/shard_map/memory/pallas_call | solution.py:636
  77.1 4.6 %collective-permute-done.7.prev_ref = bf16[256,512]{1,0:T(8,128)(2,1)S(1)} collective-permute-done((bf16[256,512]{1,0:T(8,128)(2,1)S(1)}, bf16[256,512]{1,0:T(8,128)(2,1)S(1)}, u32[]{:S(2)}, u32[]{:S(2)}) %collective-permute-start.7) | collective-permute-done | bytes 262176 | tf_op jit(solution)/shard_map/ppermute | solution.py:665
  81.7 2.4 %closing.1 = f32[2,128,512]{2,1,0:T(8,128)} custom-call(bf16[256,512]{1,0:T(8,128)(2,1)S(1)} %get-tuple-element.123.q_ref, f32[256,512]{1,0:T(8,128)S(1)} %get-tuple-element.124.number_ref, f32[256,512]{1,0:T(8,128)S(1)} %get-tuple-element.125.total_ref, f32[256,512]{1,0:T(8,128)S(1)} %get-tuple-element.126.top_ref, ...), custom_call_target="tpu_custom_call" | custom-call | bytes 6815744 | tf_op jit(solution)/shard_map/closing/pallas_call | solution.py:636
  (10 shorter events, 0.0 us)
Async XLA Ops:
  0.0 0.7 copy-start.12
  0.0 1.0 %copy-start.11 = (bf16[2,50,4,512]{3,2,1,0:T(4,128)(2,1)S(1)}, bf16[2,50,4,512]{3,2,1,0:T(4,128)(2,1)}, u32[]{:S(2)}) copy-start(bf16[2,50,4,512]{3,2,1,0:T(4,128)(2,1)} %all_mods_ref.1) | copy-start | bytes 1228804
  0.0 1.0 %copy-start.13 = (s32[8]{0:T(128)S(1)}, s32[8]{0:T(128)}, u32[]{:S(2)}) copy-start(s32[8]{0:T(128)} %step_ref.1) | copy-start | bytes 100
  0.0 1.1 %copy-start.4 = (bf16[8,32,512]{2,1,0:T(8,128)(2,1)S(1)}, bf16[8,32,512]{2,1,0:T(8,128)(2,1)}, u32[]{:S(2)}) copy-start(bf16[8,32,512]{2,1,0:T(8,128)(2,1)} %param.15) | copy-start | bytes 786436
  0.0 3.1 %slice-start = ((s8[4718592]{0:T(1024)(128)(4,1)}), s8[4194304]{0:T(1024)(128)(4,1)S(1)}, s32[]{:S(2)}) async-start(s8[4718592]{0:T(1024)(128)(4,1)} %bitcast.4), calls=%async_computation.4 | async-start | bytes 8388608
  1.1 2.0 %slice-start.1 = ((s8[4718592]{0:T(1024)(128)(4,1)}), s8[524288]{0:T(1024)(128)(4,1)S(1)}, s32[]{:S(2)}) async-start(s8[4718592]{0:T(1024)(128)(4,1)} %bitcast.4), calls=%async_computation.5 | async-start | bytes 1048576
  1.1 2.0 %copy-start.5 = (f32[2,4,1280]{2,1,0:T(4,128)S(1)}, f32[2,4,1280]{2,1,0:T(4,128)}, u32[]{:S(2)}) copy-start(f32[2,4,1280]{2,1,0:T(4,128)} %conv_ref.3) | copy-start | bytes 122884
  1.1 2.0 %copy-start.6 = (bf16[2,512,16]{1,2,0:T(8,128)(2,1)S(1)}, bf16[2,512,16]{1,2,0:T(8,128)(2,1)}, u32[]{:S(2)}) copy-start(bf16[2,512,16]{1,2,0:T(8,128)(2,1)} %param.20) | copy-start | bytes 98308
  1.1 2.0 %copy-start.9 = (f32[2,16]{1,0:T(2,128)S(1)}, f32[2,16]{1,0:T(2,128)}, u32[]{:S(2)}) copy-start(f32[2,16]{1,0:T(2,128)} %decay_ref.3) | copy-start | bytes 388
  1.1 4.8 %copy-start.8 = (f32[2,16]{1,0:T(2,128)S(1)}, f32[2,16]{1,0:T(2,128)}, u32[]{:S(2)}) copy-start(f32[2,16]{1,0:T(2,128)} %skip_ref.7) | copy-start | bytes 388
  1.9 1.2 %collective-permute-start = (bf16[16,512]{1,0:T(8,128)(2,1)S(1)}, bf16[16,512]{1,0:T(8,128)(2,1)S(1)}, u32[]{:S(2)}, u32[]{:S(2)}) collective-permute-start(bf16[16,512]{1,0:T(8,128)(2,1)S(1)} %get-tuple-element.68), channel_id=1, source_target_pairs={{0,1},{1,0},{2,3},{3,2},{4,5},{5,4},{6,7},{7,6},{8,9},{9,8},{10,11... | collective-permute-start | bytes 49160 | tf_op jit(solution)/shard_map/ppermute | solution.py:654
  3.1 15.9 %copy-start = (bf16[2,512,1024]{2,1,0:T(8,128)(2,1)S(1)}, bf16[2,512,1024]{2,1,0:T(8,128)(2,1)}, u32[]{:S(2)}) copy-start(bf16[2,512,1024]{2,1,0:T(8,128)(2,1)} %wm_ref.9) | copy-start | bytes 6291460
  3.2 15.9 %copy-start.1 = (bf16[2,1024,512]{2,1,0:T(8,128)(2,1)S(1)}, bf16[2,1024,512]{2,1,0:T(8,128)(2,1)}, u32[]{:S(2)}) copy-start(bf16[2,1024,512]{2,1,0:T(8,128)(2,1)} %wo_ref.3) | copy-start | bytes 6291460
  3.2 15.9 %copy-start.3 = (bf16[2,512,512]{2,1,0:T(8,128)(2,1)S(1)}, bf16[2,512,512]{2,1,0:T(8,128)(2,1)}, u32[]{:S(2)}) copy-start(bf16[2,512,512]{2,1,0:T(8,128)(2,1)} %wq_ref.3) | copy-start | bytes 3145732
  3.2 15.9 %copy-start.7 = (f32[2,1024]{1,0:T(2,128)S(1)}, f32[2,1024]{1,0:T(2,128)}, u32[]{:S(2)}) copy-start(f32[2,1024]{1,0:T(2,128)} %gain_ref.3) | copy-start | bytes 24580
  5.7 13.4 %copy-start.2 = (bf16[2,512,512]{2,1,0:T(8,128)(2,1)S(1)}, bf16[2,512,512]{2,1,0:T(8,128)(2,1)}, u32[]{:S(2)}) copy-start(bf16[2,512,512]{2,1,0:T(8,128)(2,1)} %merge_ref.5) | copy-start | bytes 3145732
  5.7 1.5 %collective-permute-start.1 = (bf16[8,80,128]{2,1,0:T(8,128)(2,1)S(1)}, bf16[8,80,128]{2,1,0:T(8,128)(2,1)S(1)}, u32[]{:S(2)}, u32[]{:S(2)}) collective-permute-start(bf16[8,80,128]{2,1,0:T(8,128)(2,1)S(1)} %get-tuple-element.71), channel_id=1, source_target_pairs={{0,1},{1,0},{2,3},{3,2},{4,5},{5,4},{6,7},{7,6},{8,9},{9,8},{10,11... | collective-permute-start | bytes 491528 | tf_op jit(solution)/shard_map/ppermute | solution.py:654
  30.2 1.5 %collective-permute-start.2 = (bf16[8,80,128]{2,1,0:T(8,128)(2,1)S(1)}, bf16[8,80,128]{2,1,0:T(8,128)(2,1)S(1)}, u32[]{:S(2)}, u32[]{:S(2)}) collective-permute-start(bf16[8,80,128]{2,1,0:T(8,128)(2,1)S(1)} %get-tuple-element.88), channel_id=1, source_target_pairs={{0,1},{1,0},{2,3},{3,2},{4,5},{5,4},{6,7},{7,6},{8,9},{9,8},{10,11... | collective-permute-start | bytes 491528 | tf_op jit(solution)/shard_map/ppermute | solution.py:654
  31.6 4.2 %copy-start.10 = (s32[8]{0:T(128)S(1)}, s32[8]{0:T(128)}, u32[]{:S(2)}) copy-start(s32[8]{0:T(128)} %reach_ref.3) | copy-start | bytes 100
  33.6 8.6 %collective-permute-start.3 = (bf16[256,512]{1,0:T(8,128)(2,1)S(1)}, bf16[256,512]{1,0:T(8,128)(2,1)S(1)}, u32[]{:S(2)}, u32[]{:S(2)}) collective-permute-start(bf16[256,512]{1,0:T(8,128)(2,1)S(1)} %get-tuple-element.90.a_ref), channel_id=1, source_target_pairs={{0,1},{1,2},{2,3},{3,4},{4,5},{5,6},{6,7},{7,8},{8,9},{9,10},{10,1... | collective-permute-start | bytes 786440 | tf_op jit(solution)/shard_map/ppermute | solution.py:665
  43.3 1.2 %collective-permute-start.4 = (bf16[16,512]{1,0:T(8,128)(2,1)S(1)}, bf16[16,512]{1,0:T(8,128)(2,1)S(1)}, u32[]{:S(2)}, u32[]{:S(2)}) collective-permute-start(bf16[16,512]{1,0:T(8,128)(2,1)S(1)} %get-tuple-element.101), channel_id=1, source_target_pairs={{0,1},{1,0},{2,3},{3,2},{4,5},{5,4},{6,7},{7,6},{8,9},{9,8},{10,11... | collective-permute-start | bytes 49160 | tf_op jit(solution)/shard_map/ppermute | solution.py:654
  47.0 1.6 %collective-permute-start.5 = (bf16[8,80,128]{2,1,0:T(8,128)(2,1)S(1)}, bf16[8,80,128]{2,1,0:T(8,128)(2,1)S(1)}, u32[]{:S(2)}, u32[]{:S(2)}) collective-permute-start(bf16[8,80,128]{2,1,0:T(8,128)(2,1)S(1)} %get-tuple-element.103), channel_id=1, source_target_pairs={{0,1},{1,0},{2,3},{3,2},{4,5},{5,4},{6,7},{7,6},{8,9},{9,8},{10,11... | collective-permute-start | bytes 491528 | tf_op jit(solution)/shard_map/ppermute | solution.py:654
  69.7 1.5 %collective-permute-start.6 = (bf16[8,80,128]{2,1,0:T(8,128)(2,1)S(1)}, bf16[8,80,128]{2,1,0:T(8,128)(2,1)S(1)}, u32[]{:S(2)}, u32[]{:S(2)}) collective-permute-start(bf16[8,80,128]{2,1,0:T(8,128)(2,1)S(1)} %get-tuple-element.120), channel_id=1, source_target_pairs={{0,1},{1,0},{2,3},{3,2},{4,5},{5,4},{6,7},{7,6},{8,9},{9,8},{10,11... | collective-permute-start | bytes 491528 | tf_op jit(solution)/shard_map/ppermute | solution.py:654
  73.1 8.6 %collective-permute-start.7 = (bf16[256,512]{1,0:T(8,128)(2,1)S(1)}, bf16[256,512]{1,0:T(8,128)(2,1)S(1)}, u32[]{:S(2)}, u32[]{:S(2)}) collective-permute-start(bf16[256,512]{1,0:T(8,128)(2,1)S(1)} %get-tuple-element.122.a_ref), channel_id=1, source_target_pairs={{0,1},{1,2},{2,3},{3,4},{4,5},{5,6},{6,7},{7,8},{8,9},{9,10},{10,1... | collective-permute-start | bytes 786440 | tf_op jit(solution)/shard_map/ppermute | solution.py:665

commit v10 on v9

--- a/solution.py
+++ b/solution.py
@@ -609,34 +609,27 @@
     wm_ref,
     merge_ref,
     hidden_ref,
-    out_hbm,
+    resid_ref,
     kv_ref,
     out_ref,
-    resid_ref,
-    sems,
 ):
     kv_ref[...] = dot(prev_ref[...], wm_ref[layer]).astype(BF16)
-    copies = []
     for part in range(2):
         own_refs = (number_ref, total_ref, top_ref)
-        r = attend_half(part, q_ref, own_refs, seen_ref, kv_ref, 0, out_ref)
-        resid_ref[part] = hidden_ref[r, :] + dot(out_ref[r, :], merge_ref[layer])
-        copies.append(pltpu.make_async_copy(resid_ref.at[part], out_hbm.at[part], sems.at[part]))
-        copies[-1].start()
-    for copy in copies:
-        copy.wait()
+        attend_half(part, q_ref, own_refs, seen_ref, kv_ref, 0, out_ref)
+    resid_ref[...] = hidden_ref[...] + dot(out_ref[...], merge_ref[layer])
 
 
 WHOLE = pl.BlockSpec(memory_space=pltpu.VMEM)
 SCALARS = pl.BlockSpec(memory_space=pltpu.SMEM)
 
 
-def run(kernel, operands, outs, scratch=(), name=None, flops=0, scalars=(), out_spec=WHOLE):
+def run(kernel, operands, outs, scratch=(), name=None, flops=0, scalars=()):
     moved = sum(o.size * o.dtype.itemsize for o in list(operands) + list(outs))
     return pl.pallas_call(
         kernel,
         in_specs=[SCALARS] * len(scalars) + [WHOLE] * len(operands),
-        out_specs=[out_spec] * len(outs),
+        out_specs=[WHOLE] * len(outs),
         out_shape=list(outs),
         scratch_shapes=list(scratch),
         compiler_params=pltpu.CompilerParams(vmem_limit_bytes=20 * 1024 * 1024),
@@ -807,15 +800,9 @@
             (resid,) = run(
                 functools.partial(closing_kernel, layer),
                 attention,
-                [shape((2, half, width), F32)],
-                [
-                    pltpu.VMEM((rows, 2 * ATTN), BF16),
-                    pltpu.VMEM((rows, ATTN), BF16),
-                    pltpu.VMEM((2, half, width), F32),
-                    pltpu.SemaphoreType.DMA((2,)),
-                ],
+                [shape((rows, width), F32)],
+                [pltpu.VMEM((rows, 2 * ATTN), BF16), pltpu.VMEM((rows, ATTN), BF16)],
                 name="closing",
-                out_spec=pl.BlockSpec(memory_space=pl.ANY),
             )
         else:
             late_resid, late_u, tail, late_kv = run(

time: 84.7 us -> 84.4 us (level)
  no operation moved by 1% of the time
where the time goes in v10:
time: 84.4 us; the launch traced here: 84 us
  blocking collectives  42.1 us (50%)
  Pallas kernels  22.4 us (27%)
  waiting for transfers between devices  12.7 us (15%)
  starting transfers between devices  5.34 us (6%)
  local copies, waits for them, and re-layouts  1.12 us (1%)
    all_to_all x4, blocking collectives, over_chips(): return lax.all_to_all(value, axis, 0, 0, axis_index_groups=groups)  42.1 us
    pallas_call x21, Pallas kernels, run(): pl.pallas_call(kernel, in_specs=[SCALARS] * len(scalars) + [WHOLE] * len(...  22.4 us
    ppermute x2, waiting for transfers between devices, from_behind(): return lax.ppermute(value, axis, [(i, i + 1) for i in range(count - 1)])  9.05 us
    ppermute x2, starting transfers between devices, from_behind(): return lax.ppermute(value, axis, [(i, i + 1) for i in range(count - 1)])  4.29 us
    ppermute x6, waiting for transfers between devices, swapped(): return lax.ppermute(value, axis, [(i, i ^ 1) for i in range(count)])  3.64 us
  transfers between devices with their start and end apart: 8, of which 7 were waited for; matrix products, arithmetic and copies ran while one was open for 0% of the time, Pallas kernels for 9%

profile of v10, /device:TPU:8, one launch (start us, length us, event | category | flops | bytes accessed | tf_op | source)
XLA Modules:
  0.0 84.0 jit_solution(17019366452882640700)
XLA Ops:
  0.0 0.0 copy-start.12
  0.0 0.0 copy-start.4
  0.0 0.0 slice-start
  0.1 0.7 copy-done.12
  0.7 0.3 copy-done.11
  1.0 0.0 copy-done.13
  1.0 0.1 copy-done.4
  1.1 0.0 copy-start.8
  1.1 0.7 first.1
  1.9 0.1 collective-permute-start
  1.9 1.2 %collective-permute-done.before_ref = bf16[16,512]{1,0:T(8,128)(2,1)S(1)} collective-permute-done((bf16[16,512]{1,0:T(8,128)(2,1)S(1)}, bf16[16,512]{1,0:T(8,128)(2,1)S(1)}, u32[]{:S(2)}, u32[]{:S(2)}) %collective-permute-start) | collective-permute-done | bytes 16416 | tf_op jit(solution)/shard_map/ppermute | solution.py:647
  3.1 0.0 slice-done
  3.1 0.0 slice-done.1
  3.1 0.0 copy-done.5
  3.1 0.0 copy-done.6
  3.1 0.0 copy-done.9
  3.1 0.0 copy-start
  3.2 0.0 copy-start.1
  3.2 0.0 copy-start.3
  3.2 0.0 copy-start.7
  3.2 2.5 %local.2 = (bf16[256,1280]{1,0:T(8,128)(2,1)S(1)}, f32[8,1280]{1,0:T(8,128)S(1)}, f32[256,16]{1,0:T(8,128)S(1)}, f32[16,256]{1,0:T(8,128)S(1)}, f32[16,16]{1,0:T...) custom-call(bf16[256,512]{1,0:T(8,128)(2,1)S(1)} %get-tuple-element.79.u_ref,, ...), custom_call_target="tpu_custom_call" | custom-call | flops 335544320 | bytes 6719616 | tf_op jit(solution)/shard_map/local/pallas_call | solution.py:629
  5.7 0.2 collective-permute-start.1
  5.9 0.0 copy-done.8
  5.9 0.6 later.2
  6.5 0.6 collective-permute-done.1.got_ref
  7.1 0.1 chip.2
  7.3 11.7 %all_to_all.20.got_ref = bf16[8,80,128]{2,1,0:T(8,128)(2,1)S(1)} all-to-all(bf16[8,80,128]{2,1,0:T(8,128)(2,1)S(1)} %chip.2), channel_id=1, replica_groups={{0,2,4,6,8,10,12,14},{1,3,5,7,9,11,13,15},{16,18,20,22,24,26,28,30},{17..., dimensions={0} | all-to-all | bytes 327680 | tf_op jit(solution)/shard_map/all_to_all | solution.py:653
  19.0 0.0 copy-done
  19.0 0.0 copy-done.1
  19.0 0.0 copy-done.3
  19.0 0.0 copy-done.7
  19.0 0.0 copy-done.2
  19.0 0.4 scan.2
  19.5 10.3 %all_to_all.21.back_ref = bf16[8,80,128]{2,1,0:T(8,128)(2,1)S(1)} all-to-all(bf16[8,80,128]{2,1,0:T(8,128)(2,1)S(1)} %scan.2), channel_id=1, replica_groups={{0,2,4,6,8,10,12,14},{1,3,5,7,9,11,13,15},{16,18,20,22,24,26,28,30},{17..., dimensions={0} | all-to-all | bytes 327680 | tf_op jit(solution)/shard_map/all_to_all | solution.py:653
  29.7 0.5 enter.2
  30.2 0.1 collective-permute-start.2
  30.3 0.6 gate.2
  30.9 0.7 collective-permute-done.2.other_ref
  31.6 1.9 %finish.2 = (f32[256,512]{1,0:T(8,128)S(1)}, bf16[256,512]{1,0:T(8,128)(2,1)S(1)}) custom-call(f32[256,1024]{1,0:T(8,128)S(1)} %get-tuple-element.80.gate_ref, f32[256,1024]{1,0:T(8,128)S(1)} %get-tuple-element.81.wide_ref, f32[128,1024]{1,0:T(8,128)S(1)} %get-tuple-element.82.later_ref, f32[128,1024]{1,0:T(8,128)S(1)} %get-tuple-element.83.decay_ref, ...), custom_call_target="tpu_custom_call" | custom-call | bytes 7963776 | tf_op jit(solution)/shard_map/finish/pallas_call | solution.py:629
  33.6 2.2 %collective-permute-start.3 = (bf16[256,512]{1,0:T(8,128)(2,1)S(1)}, bf16[256,512]{1,0:T(8,128)(2,1)S(1)}, u32[]{:S(2)}, u32[]{:S(2)}) collective-permute-start(bf16[256,512]{1,0:T(8,128)(2,1)S(1)} %get-tuple-element.90.a_ref), channel_id=1, source_target_pairs={{0,1},{1,2},{2,3},{3,4},{4,5},{5,6},{6,7},{7,8},{8,9},{9,10},{10,1... | collective-permute-start | bytes 786440 | tf_op jit(solution)/shard_map/ppermute | solution.py:658
  35.8 0.0 copy-done.10
  35.8 1.9 %memory.2 = (bf16[256,512]{1,0:T(8,128)(2,1)S(1)}, f32[256,512]{1,0:T(8,128)S(1)}, f32[256,512]{1,0:T(8,128)S(1)}, f32[256,512]{1,0:T(8,128)S(1)}, f32[256,512]{1,0:T(8,128)S(1)}) custom-call(s32[8]{0:T(128)S(1)} %copy-done.10, bf16[256,512]{1,0:T(8,128)(2,1)S(1)} %get-tuple-element.90.a_ref, bf16[2,512,512]{2,1,0:T(8,128)(2,1)S(1)} %copy-done.3, ...), custom_call_target="tpu_custom_call" | custom-call | flops 402653184 | bytes 5767168 | tf_op jit(solution)/shard_map/memory/pallas_call | solution.py:629
  37.7 4.4 %collective-permute-done.3.prev_ref = bf16[256,512]{1,0:T(8,128)(2,1)S(1)} collective-permute-done((bf16[256,512]{1,0:T(8,128)(2,1)S(1)}, bf16[256,512]{1,0:T(8,128)(2,1)S(1)}, u32[]{:S(2)}, u32[]{:S(2)}) %collective-permute-start.3) | collective-permute-done | bytes 262176 | tf_op jit(solution)/shard_map/ppermute | solution.py:658
  42.2 1.1 %last_rows.1 = (f32[128,512]{1,0:T(8,128)S(1)}, bf16[128,512]{1,0:T(8,128)(2,1)S(1)}, bf16[16,512]{1,0:T(8,128)(2,1)S(1)}, bf16[128,1024]{1,0:T(8,128)(2,1)S(1)}) custom-call(bf16[256,512]{1,0:T(8,128)(2,1)S(1)} %get-tuple-element.91.q_ref, f32[256,512]{1,0:T(8,128)S(1)} %get-tuple-element.92.number_ref, f32[256,512]{1,0:T(8,128)S(1)} %get-tuple-element.93.total_ref, ...), custom_call_target="tpu_custom_call" | custom-call | bytes 6979584 | tf_op jit(solution)/shard_map/last_rows/pallas_call | solution.py:629
  43.3 0.1 collective-permute-start.4
  43.4 1.2 %first_rows.1 = (f32[256,512]{1,0:T(8,128)S(1)}, bf16[256,512]{1,0:T(8,128)(2,1)S(1)}) custom-call(bf16[256,512]{1,0:T(8,128)(2,1)S(1)} %get-tuple-element.91.q_ref, f32[256,512]{1,0:T(8,128)S(1)} %get-tuple-element.92.number_ref, f32[256,512]{1,0:T(8,128)S(1)} %get-tuple-element.93.total_ref, f32[256,512]{1,0:T(8,128)S(1)} %get-tuple-element.94.top_ref, ...), custom_call_target="tpu_custom_call" | custom-call | flops 268435456 | bytes 7749632 | tf_op jit(solution)/shard_map/first_rows/pallas_call | solution.py:629
  44.5 0.0 collective-permute-done.4.before_ref
  44.5 2.5 %local.3 = (bf16[256,1280]{1,0:T(8,128)(2,1)S(1)}, f32[8,1280]{1,0:T(8,128)S(1)}, f32[256,16]{1,0:T(8,128)S(1)}, f32[16,256]{1,0:T(8,128)S(1)}, f32[16,16]{1,0:T...) custom-call(bf16[256,512]{1,0:T(8,128)(2,1)S(1)} %get-tuple-element.111.u_ref, ...), custom_call_target="tpu_custom_call" | custom-call | flops 335544320 | bytes 6719616 | tf_op jit(solution)/shard_map/local/pallas_call | solution.py:629
  47.0 0.5 collective-permute-start.5
  47.5 0.6 later.3
  48.2 0.4 collective-permute-done.5.got_ref
  48.6 0.1 chip.3
  48.7 9.8 %all_to_all.22.got_ref = bf16[8,80,128]{2,1,0:T(8,128)(2,1)S(1)} all-to-all(bf16[8,80,128]{2,1,0:T(8,128)(2,1)S(1)} %chip.3), channel_id=1, replica_groups={{0,2,4,6,8,10,12,14},{1,3,5,7,9,11,13,15},{16,18,20,22,24,26,28,30},{17..., dimensions={0} | all-to-all | bytes 327680 | tf_op jit(solution)/shard_map/all_to_all | solution.py:653
  58.5 0.4 scan.3
  58.9 10.3 %all_to_all.23.back_ref = bf16[8,80,128]{2,1,0:T(8,128)(2,1)S(1)} all-to-all(bf16[8,80,128]{2,1,0:T(8,128)(2,1)S(1)} %scan.3), channel_id=1, replica_groups={{0,2,4,6,8,10,12,14},{1,3,5,7,9,11,13,15},{16,18,20,22,24,26,28,30},{17..., dimensions={0} | all-to-all | bytes 327680 | tf_op jit(solution)/shard_map/all_to_all | solution.py:653
  69.2 0.4 enter.3
  69.7 0.1 collective-permute-start.6
  69.7 0.6 gate.3
  70.4 0.7 collective-permute-done.6.other_ref
  71.1 2.0 %finish.3 = (f32[256,512]{1,0:T(8,128)S(1)}, bf16[256,512]{1,0:T(8,128)(2,1)S(1)}) custom-call(f32[256,1024]{1,0:T(8,128)S(1)} %get-tuple-element.112.gate_ref, f32[256,1024]{1,0:T(8,128)S(1)} %get-tuple-element.113.wide_ref, f32[128,1024]{1,0:T(8,128)S(1)} %get-tuple-element.114.later_ref, f32[128,1024]{1,0:T(8,128)S(1)} %get-tuple-element.115.decay_ref, ...), custom_call_target="tpu_custom_call" | custom-call | bytes 8225920 | tf_op jit(solution)/shard_map/finish/pallas_call | solution.py:629
  73.1 2.1 %collective-permute-start.7 = (bf16[256,512]{1,0:T(8,128)(2,1)S(1)}, bf16[256,512]{1,0:T(8,128)(2,1)S(1)}, u32[]{:S(2)}, u32[]{:S(2)}) collective-permute-start(bf16[256,512]{1,0:T(8,128)(2,1)S(1)} %get-tuple-element.122.a_ref), channel_id=1, source_target_pairs={{0,1},{1,2},{2,3},{3,4},{4,5},{5,6},{6,7},{7,8},{8,9},{9,10},{10,1... | collective-permute-start | bytes 786440 | tf_op jit(solution)/shard_map/ppermute | solution.py:658
  75.2 1.9 %memory.3 = (bf16[256,512]{1,0:T(8,128)(2,1)S(1)}, f32[256,512]{1,0:T(8,128)S(1)}, f32[256,512]{1,0:T(8,128)S(1)}, f32[256,512]{1,0:T(8,128)S(1)}, f32[256,512]{1,0:T(8,128)S(1)}) custom-call(s32[8]{0:T(128)S(1)} %copy-done.10, bf16[256,512]{1,0:T(8,128)(2,1)S(1)} %get-tuple-element.122.a_ref, bf16[2,512,512]{2,1,0:T(8,128)(2,1)S(1)} %copy-done.3, ...), custom_call_target="tpu_custom_call" | custom-call | flops 402653184 | bytes 5767168 | tf_op jit(solution)/shard_map/memory/pallas_call | solution.py:629
  77.1 4.6 %collective-permute-done.7.prev_ref = bf16[256,512]{1,0:T(8,128)(2,1)S(1)} collective-permute-done((bf16[256,512]{1,0:T(8,128)(2,1)S(1)}, bf16[256,512]{1,0:T(8,128)(2,1)S(1)}, u32[]{:S(2)}, u32[]{:S(2)}) %collective-permute-start.7) | collective-permute-done | bytes 262176 | tf_op jit(solution)/shard_map/ppermute | solution.py:658
  81.7 2.3 %closing.1 = f32[256,512]{1,0:T(8,128)} custom-call(bf16[256,512]{1,0:T(8,128)(2,1)S(1)} %get-tuple-element.123.q_ref, f32[256,512]{1,0:T(8,128)S(1)} %get-tuple-element.124.number_ref, f32[256,512]{1,0:T(8,128)S(1)} %get-tuple-element.125.total_ref, f32[256,512]{1,0:T(8,128)S(1)} %get-tuple-element.126.top_ref, f32[256,512]{1,0:T(8,128)S(1)} %get-tuple-element.127.seen_ref, ...), custom_call_target="tpu_custom_call" | custom-call | bytes 6815744 | tf_op jit(solution)/shard_map/closing/pallas_call | solution.py:629
  (10 shorter events, 0.0 us)
Async XLA Ops:
  0.0 0.7 copy-start.12
  0.0 1.0 %copy-start.11 = (bf16[2,50,4,512]{3,2,1,0:T(4,128)(2,1)S(1)}, bf16[2,50,4,512]{3,2,1,0:T(4,128)(2,1)}, u32[]{:S(2)}) copy-start(bf16[2,50,4,512]{3,2,1,0:T(4,128)(2,1)} %all_mods_ref.1) | copy-start | bytes 1228804
  0.0 1.0 %copy-start.13 = (s32[8]{0:T(128)S(1)}, s32[8]{0:T(128)}, u32[]{:S(2)}) copy-start(s32[8]{0:T(128)} %step_ref.1) | copy-start | bytes 100
  0.0 1.1 %copy-start.4 = (bf16[8,32,512]{2,1,0:T(8,128)(2,1)S(1)}, bf16[8,32,512]{2,1,0:T(8,128)(2,1)}, u32[]{:S(2)}) copy-start(bf16[8,32,512]{2,1,0:T(8,128)(2,1)} %param.15) | copy-start | bytes 786436
  0.0 3.1 %slice-start = ((s8[4718592]{0:T(1024)(128)(4,1)}), s8[4194304]{0:T(1024)(128)(4,1)S(1)}, s32[]{:S(2)}) async-start(s8[4718592]{0:T(1024)(128)(4,1)} %bitcast.4), calls=%async_computation.4 | async-start | bytes 8388608
  1.1 2.0 %slice-start.1 = ((s8[4718592]{0:T(1024)(128)(4,1)}), s8[524288]{0:T(1024)(128)(4,1)S(1)}, s32[]{:S(2)}) async-start(s8[4718592]{0:T(1024)(128)(4,1)} %bitcast.4), calls=%async_computation.5 | async-start | bytes 1048576
  1.1 2.0 %copy-start.5 = (f32[2,4,1280]{2,1,0:T(4,128)S(1)}, f32[2,4,1280]{2,1,0:T(4,128)}, u32[]{:S(2)}) copy-start(f32[2,4,1280]{2,1,0:T(4,128)} %conv_ref.3) | copy-start | bytes 122884
  1.1 2.0 %copy-start.6 = (bf16[2,512,16]{1,2,0:T(8,128)(2,1)S(1)}, bf16[2,512,16]{1,2,0:T(8,128)(2,1)}, u32[]{:S(2)}) copy-start(bf16[2,512,16]{1,2,0:T(8,128)(2,1)} %param.20) | copy-start | bytes 98308
  1.1 2.0 %copy-start.9 = (f32[2,16]{1,0:T(2,128)S(1)}, f32[2,16]{1,0:T(2,128)}, u32[]{:S(2)}) copy-start(f32[2,16]{1,0:T(2,128)} %decay_ref.3) | copy-start | bytes 388
  1.1 4.8 %copy-start.8 = (f32[2,16]{1,0:T(2,128)S(1)}, f32[2,16]{1,0:T(2,128)}, u32[]{:S(2)}) copy-start(f32[2,16]{1,0:T(2,128)} %skip_ref.7) | copy-start | bytes 388
  1.9 1.2 %collective-permute-start = (bf16[16,512]{1,0:T(8,128)(2,1)S(1)}, bf16[16,512]{1,0:T(8,128)(2,1)S(1)}, u32[]{:S(2)}, u32[]{:S(2)}) collective-permute-start(bf16[16,512]{1,0:T(8,128)(2,1)S(1)} %get-tuple-element.68), channel_id=1, source_target_pairs={{0,1},{1,0},{2,3},{3,2},{4,5},{5,4},{6,7},{7,6},{8,9},{9,8},{10,11... | collective-permute-start | bytes 49160 | tf_op jit(solution)/shard_map/ppermute | solution.py:647
  3.1 15.9 %copy-start = (bf16[2,512,1024]{2,1,0:T(8,128)(2,1)S(1)}, bf16[2,512,1024]{2,1,0:T(8,128)(2,1)}, u32[]{:S(2)}) copy-start(bf16[2,512,1024]{2,1,0:T(8,128)(2,1)} %wm_ref.9) | copy-start | bytes 6291460
  3.2 15.9 %copy-start.1 = (bf16[2,1024,512]{2,1,0:T(8,128)(2,1)S(1)}, bf16[2,1024,512]{2,1,0:T(8,128)(2,1)}, u32[]{:S(2)}) copy-start(bf16[2,1024,512]{2,1,0:T(8,128)(2,1)} %wo_ref.3) | copy-start | bytes 6291460
  3.2 15.9 %copy-start.3 = (bf16[2,512,512]{2,1,0:T(8,128)(2,1)S(1)}, bf16[2,512,512]{2,1,0:T(8,128)(2,1)}, u32[]{:S(2)}) copy-start(bf16[2,512,512]{2,1,0:T(8,128)(2,1)} %wq_ref.3) | copy-start | bytes 3145732
  3.2 15.9 %copy-start.7 = (f32[2,1024]{1,0:T(2,128)S(1)}, f32[2,1024]{1,0:T(2,128)}, u32[]{:S(2)}) copy-start(f32[2,1024]{1,0:T(2,128)} %gain_ref.3) | copy-start | bytes 24580
  5.7 13.4 %copy-start.2 = (bf16[2,512,512]{2,1,0:T(8,128)(2,1)S(1)}, bf16[2,512,512]{2,1,0:T(8,128)(2,1)}, u32[]{:S(2)}) copy-start(bf16[2,512,512]{2,1,0:T(8,128)(2,1)} %merge_ref.5) | copy-start | bytes 3145732
  5.7 1.5 %collective-permute-start.1 = (bf16[8,80,128]{2,1,0:T(8,128)(2,1)S(1)}, bf16[8,80,128]{2,1,0:T(8,128)(2,1)S(1)}, u32[]{:S(2)}, u32[]{:S(2)}) collective-permute-start(bf16[8,80,128]{2,1,0:T(8,128)(2,1)S(1)} %get-tuple-element.71), channel_id=1, source_target_pairs={{0,1},{1,0},{2,3},{3,2},{4,5},{5,4},{6,7},{7,6},{8,9},{9,8},{10,11... | collective-permute-start | bytes 491528 | tf_op jit(solution)/shard_map/ppermute | solution.py:647
  30.2 1.5 %collective-permute-start.2 = (bf16[8,80,128]{2,1,0:T(8,128)(2,1)S(1)}, bf16[8,80,128]{2,1,0:T(8,128)(2,1)S(1)}, u32[]{:S(2)}, u32[]{:S(2)}) collective-permute-start(bf16[8,80,128]{2,1,0:T(8,128)(2,1)S(1)} %get-tuple-element.88), channel_id=1, source_target_pairs={{0,1},{1,0},{2,3},{3,2},{4,5},{5,4},{6,7},{7,6},{8,9},{9,8},{10,11... | collective-permute-start | bytes 491528 | tf_op jit(solution)/shard_map/ppermute | solution.py:647
  31.6 4.2 %copy-start.10 = (s32[8]{0:T(128)S(1)}, s32[8]{0:T(128)}, u32[]{:S(2)}) copy-start(s32[8]{0:T(128)} %reach_ref.3) | copy-start | bytes 100
  33.6 8.6 %collective-permute-start.3 = (bf16[256,512]{1,0:T(8,128)(2,1)S(1)}, bf16[256,512]{1,0:T(8,128)(2,1)S(1)}, u32[]{:S(2)}, u32[]{:S(2)}) collective-permute-start(bf16[256,512]{1,0:T(8,128)(2,1)S(1)} %get-tuple-element.90.a_ref), channel_id=1, source_target_pairs={{0,1},{1,2},{2,3},{3,4},{4,5},{5,6},{6,7},{7,8},{8,9},{9,10},{10,1... | collective-permute-start | bytes 786440 | tf_op jit(solution)/shard_map/ppermute | solution.py:658
  43.3 1.2 %collective-permute-start.4 = (bf16[16,512]{1,0:T(8,128)(2,1)S(1)}, bf16[16,512]{1,0:T(8,128)(2,1)S(1)}, u32[]{:S(2)}, u32[]{:S(2)}) collective-permute-start(bf16[16,512]{1,0:T(8,128)(2,1)S(1)} %get-tuple-element.101), channel_id=1, source_target_pairs={{0,1},{1,0},{2,3},{3,2},{4,5},{5,4},{6,7},{7,6},{8,9},{9,8},{10,11... | collective-permute-start | bytes 49160 | tf_op jit(solution)/shard_map/ppermute | solution.py:647
  47.0 1.6 %collective-permute-start.5 = (bf16[8,80,128]{2,1,0:T(8,128)(2,1)S(1)}, bf16[8,80,128]{2,1,0:T(8,128)(2,1)S(1)}, u32[]{:S(2)}, u32[]{:S(2)}) collective-permute-start(bf16[8,80,128]{2,1,0:T(8,128)(2,1)S(1)} %get-tuple-element.103), channel_id=1, source_target_pairs={{0,1},{1,0},{2,3},{3,2},{4,5},{5,4},{6,7},{7,6},{8,9},{9,8},{10,11... | collective-permute-start | bytes 491528 | tf_op jit(solution)/shard_map/ppermute | solution.py:647
  69.7 1.5 %collective-permute-start.6 = (bf16[8,80,128]{2,1,0:T(8,128)(2,1)S(1)}, bf16[8,80,128]{2,1,0:T(8,128)(2,1)S(1)}, u32[]{:S(2)}, u32[]{:S(2)}) collective-permute-start(bf16[8,80,128]{2,1,0:T(8,128)(2,1)S(1)} %get-tuple-element.120), channel_id=1, source_target_pairs={{0,1},{1,0},{2,3},{3,2},{4,5},{5,4},{6,7},{7,6},{8,9},{9,8},{10,11... | collective-permute-start | bytes 491528 | tf_op jit(solution)/shard_map/ppermute | solution.py:647
  73.1 8.6 %collective-permute-start.7 = (bf16[256,512]{1,0:T(8,128)(2,1)S(1)}, bf16[256,512]{1,0:T(8,128)(2,1)S(1)}, u32[]{:S(2)}, u32[]{:S(2)}) collective-permute-start(bf16[256,512]{1,0:T(8,128)(2,1)S(1)} %get-tuple-element.122.a_ref), channel_id=1, source_target_pairs={{0,1},{1,2},{2,3},{3,4},{4,5},{5,6},{6,7},{7,8},{8,9},{9,10},{10,1... | collective-permute-start | bytes 786440 | tf_op jit(solution)/shard_map/ppermute | solution.py:658

commit v11 on v8

--- a/solution.py
+++ b/solution.py
@@ -117,7 +117,7 @@
     sel = sel_ref[...]
     core = core_index()
     tail_rows = before_ref[...].astype(F32) * core.astype(F32)
-    tail_rows = tail_rows.astype(BF16)
+    with_tail = jnp.concatenate([tail_rows.astype(BF16), u], axis=0)
     raw = dot(u, sw_ref[layer], ((1,), (1,))) + bias_ref[layer, 0:1, :]
     step = jnp.maximum(raw, 0.0) + jnp.log1p(jnp.exp(-jnp.abs(raw)))
     log_decay = -jnp.exp(decay_ref[layer : layer + 1, :]) * step
@@ -147,8 +147,7 @@
     for c in [INNER] + list(range(0, INNER, chunk)):
         w = w_ref[layer, :, INNER + c : INNER + c + chunk]
         slot = c // chunk % 2
-        ext_ref[slot, 0:TAIL, :] = dot(tail_rows, w).astype(BF16).astype(F32)
-        ext_ref[slot, TAIL : TAIL + rows, :] = dot(u, w).astype(BF16).astype(F32)
+        ext_ref[slot, 0 : TAIL + rows, :] = dot(with_tail, w).astype(BF16).astype(F32)
         total, after = None, None
         for k in range(CONV):
             start = TAIL - (CONV - 1) + k

time: 84.6 us -> 84.6 us (level)
  no operation moved by 1% of the time
where the time goes in v11:
time: 84.6 us; the launch traced here: 84.2 us
  blocking collectives  41.9 us (50%)
  Pallas kernels  21.8 us (26%)
  waiting for transfers between devices  14 us (17%)
  starting transfers between devices  5.02 us (6%)
  local copies, waits for them, and re-layouts  1.12 us (1%)
    all_to_all x4, blocking collectives, over_chips(): return lax.all_to_all(value, axis, 0, 0, axis_index_groups=groups)  41.9 us
    pallas_call x20, Pallas kernels, run(): pl.pallas_call(kernel, in_specs=[SCALARS] * len(scalars) + [WHOLE] * len(...  21.8 us
    ppermute x2, waiting for transfers between devices, from_behind(): return lax.ppermute(value, axis, [(i, i + 1) for i in range(count - 1)])  9.03 us
    ppermute x6, waiting for transfers between devices, swapped(): return lax.ppermute(value, axis, [(i, i ^ 1) for i in range(count)])  5 us
    ppermute x2, starting transfers between devices, from_behind(): return lax.ppermute(value, axis, [(i, i + 1) for i in range(count - 1)])  4.29 us
  transfers between devices with their start and end apart: 8, of which 8 were waited for; matrix products, arithmetic and copies ran while one was open for 0% of the time, Pallas kernels for 8%

profile of v11, /device:TPU:8, one launch (start us, length us, event | category | flops | bytes accessed | tf_op | source)
XLA Modules:
  0.0 84.2 jit_solution(17396075235224228172)
XLA Ops:
  0.0 0.0 copy-start.12
  0.0 0.0 copy-start.11
  0.0 0.0 copy-start.4
  0.0 0.0 slice-start
  0.1 0.7 copy-done.12
  0.7 0.3 copy-done.11
  1.0 0.0 copy-done.13
  1.0 0.1 copy-done.4
  1.1 0.0 copy-start.8
  1.1 0.7 first.1
  1.9 0.1 collective-permute-start
  1.9 1.2 %collective-permute-done.before_ref = bf16[16,512]{1,0:T(8,128)(2,1)S(1)} collective-permute-done((bf16[16,512]{1,0:T(8,128)(2,1)S(1)}, bf16[16,512]{1,0:T(8,128)(2,1)S(1)}, u32[]{:S(2)}, u32[]{:S(2)}) %collective-permute-start) | collective-permute-done | bytes 16416 | tf_op jit(solution)/shard_map/ppermute | solution.py:589
  3.1 0.0 slice-done
  3.1 0.0 slice-done.1
  3.1 0.0 copy-done.5
  3.1 0.0 copy-done.6
  3.1 0.0 copy-done.9
  3.1 0.0 copy-start
  3.2 0.0 copy-start.1
  3.2 0.0 copy-start.3
  3.2 0.0 copy-start.7
  3.2 2.5 %local.2 = (bf16[256,1280]{1,0:T(8,128)(2,1)S(1)}, f32[8,1280]{1,0:T(8,128)S(1)}, f32[256,16]{1,0:T(8,128)S(1)}, f32[16,256]{1,0:T(8,128)S(1)}, f32[16,16]{1,0:T...) custom-call(bf16[256,512]{1,0:T(8,128)(2,1)S(1)} %get-tuple-element.76.u_ref,, ...), custom_call_target="tpu_custom_call" | custom-call | flops 335544320 | bytes 6719616 | tf_op jit(solution)/shard_map/local/pallas_call | solution.py:571
  5.7 0.2 collective-permute-start.1
  5.9 0.0 copy-done.8
  5.9 0.6 later.2
  6.5 0.6 collective-permute-done.1.got_ref
  7.1 0.1 chip.2
  7.3 11.7 %all_to_all.20.got_ref = bf16[8,80,128]{2,1,0:T(8,128)(2,1)S(1)} all-to-all(bf16[8,80,128]{2,1,0:T(8,128)(2,1)S(1)} %chip.2), channel_id=1, replica_groups={{0,2,4,6,8,10,12,14},{1,3,5,7,9,11,13,15},{16,18,20,22,24,26,28,30},{17..., dimensions={0} | all-to-all | bytes 327680 | tf_op jit(solution)/shard_map/all_to_all | solution.py:595
  19.0 0.0 copy-done
  19.0 0.0 copy-done.1
  19.0 0.0 copy-done.3
  19.0 0.0 copy-done.7
  19.0 0.0 copy-done.2
  19.1 0.4 scan.2
  19.5 10.3 %all_to_all.21.back_ref = bf16[8,80,128]{2,1,0:T(8,128)(2,1)S(1)} all-to-all(bf16[8,80,128]{2,1,0:T(8,128)(2,1)S(1)} %scan.2), channel_id=1, replica_groups={{0,2,4,6,8,10,12,14},{1,3,5,7,9,11,13,15},{16,18,20,22,24,26,28,30},{17..., dimensions={0} | all-to-all | bytes 327680 | tf_op jit(solution)/shard_map/all_to_all | solution.py:595
  29.7 0.5 enter.2
  30.2 0.1 collective-permute-start.2
  30.3 0.6 gate.2
  30.9 0.7 collective-permute-done.2.other_ref
  31.7 1.9 %finish.2 = (f32[256,512]{1,0:T(8,128)S(1)}, bf16[256,512]{1,0:T(8,128)(2,1)S(1)}) custom-call(f32[256,1024]{1,0:T(8,128)S(1)} %get-tuple-element.77.gate_ref, f32[256,1024]{1,0:T(8,128)S(1)} %get-tuple-element.78.wide_ref, f32[128,1024]{1,0:T(8,128)S(1)} %get-tuple-element.79.later_ref, f32[128,1024]{1,0:T(8,128)S(1)} %get-tuple-element.80.decay_ref, ...), custom_call_target="tpu_custom_call" | custom-call | bytes 7963776 | tf_op jit(solution)/shard_map/finish/pallas_call | solution.py:571
  33.6 2.2 %collective-permute-start.3 = (bf16[256,512]{1,0:T(8,128)(2,1)S(1)}, bf16[256,512]{1,0:T(8,128)(2,1)S(1)}, u32[]{:S(2)}, u32[]{:S(2)}) collective-permute-start(bf16[256,512]{1,0:T(8,128)(2,1)S(1)} %get-tuple-element.87.a_ref), channel_id=1, source_target_pairs={{0,1},{1,2},{2,3},{3,4},{4,5},{5,6},{6,7},{7,8},{8,9},{9,10},{10,1... | collective-permute-start | bytes 786440 | tf_op jit(solution)/shard_map/ppermute | solution.py:600
  35.8 0.0 copy-done.10
  35.8 1.9 %memory.2 = (bf16[256,512]{1,0:T(8,128)(2,1)S(1)}, f32[256,512]{1,0:T(8,128)S(1)}, f32[256,512]{1,0:T(8,128)S(1)}, f32[256,512]{1,0:T(8,128)S(1)}, f32[256,512]{1,0:T(8,128)S(1)}) custom-call(s32[8]{0:T(128)S(1)} %copy-done.10, bf16[256,512]{1,0:T(8,128)(2,1)S(1)} %get-tuple-element.87.a_ref, bf16[2,512,512]{2,1,0:T(8,128)(2,1)S(1)} %copy-done.2, ...), custom_call_target="tpu_custom_call" | custom-call | flops 402653184 | bytes 5767168 | tf_op jit(solution)/shard_map/memory/pallas_call | solution.py:571
  37.8 4.4 %collective-permute-done.3.prev_ref = bf16[256,512]{1,0:T(8,128)(2,1)S(1)} collective-permute-done((bf16[256,512]{1,0:T(8,128)(2,1)S(1)}, bf16[256,512]{1,0:T(8,128)(2,1)S(1)}, u32[]{:S(2)}, u32[]{:S(2)}) %collective-permute-start.3) | collective-permute-done | bytes 262176 | tf_op jit(solution)/shard_map/ppermute | solution.py:600
  42.2 1.6 %attend.2 = (f32[256,512]{1,0:T(8,128)S(1)}, bf16[256,512]{1,0:T(8,128)(2,1)S(1)}, bf16[16,512]{1,0:T(8,128)(2,1)S(1)}) custom-call(bf16[256,512]{1,0:T(8,128)(2,1)S(1)} %get-tuple-element.88.q_ref, f32[256,512]{1,0:T(8,128)S(1)} %get-tuple-element.89.number_ref, f32[256,512]{1,0:T(8,128)S(1)} %get-tuple-element.90.total_ref, ...), custom_call_target="tpu_custom_call" | custom-call | bytes 7110656 | tf_op jit(solution)/shard_map/attend/pallas_call | solution.py:571
  43.8 0.1 collective-permute-start.4
  43.9 1.2 %collective-permute-done.4.before_ref = bf16[16,512]{1,0:T(8,128)(2,1)S(1)} collective-permute-done((bf16[16,512]{1,0:T(8,128)(2,1)S(1)}, bf16[16,512]{1,0:T(8,128)(2,1)S(1)}, u32[]{:S(2)}, u32[]{:S(2)}) %collective-permute-start.4) | collective-permute-done | bytes 16416 | tf_op jit(solution)/shard_map/ppermute | solution.py:589
  45.1 2.5 %local.3 = (bf16[256,1280]{1,0:T(8,128)(2,1)S(1)}, f32[8,1280]{1,0:T(8,128)S(1)}, f32[256,16]{1,0:T(8,128)S(1)}, f32[16,256]{1,0:T(8,128)S(1)}, f32[16,16]{1,0:T...) custom-call(bf16[256,512]{1,0:T(8,128)(2,1)S(1)} %get-tuple-element.105.u_ref, ...), custom_call_target="tpu_custom_call" | custom-call | flops 335544320 | bytes 6719616 | tf_op jit(solution)/shard_map/local/pallas_call | solution.py:571
  47.5 0.2 collective-permute-start.5
  47.7 0.6 later.3
  48.4 0.6 collective-permute-done.5.got_ref
  49.0 0.1 chip.3
  49.1 9.6 %all_to_all.22.got_ref = bf16[8,80,128]{2,1,0:T(8,128)(2,1)S(1)} all-to-all(bf16[8,80,128]{2,1,0:T(8,128)(2,1)S(1)} %chip.3), channel_id=1, replica_groups={{0,2,4,6,8,10,12,14},{1,3,5,7,9,11,13,15},{16,18,20,22,24,26,28,30},{17..., dimensions={0} | all-to-all | bytes 327680 | tf_op jit(solution)/shard_map/all_to_all | solution.py:595
  58.7 0.4 scan.3
  59.1 10.3 %all_to_all.23.back_ref = bf16[8,80,128]{2,1,0:T(8,128)(2,1)S(1)} all-to-all(bf16[8,80,128]{2,1,0:T(8,128)(2,1)S(1)} %scan.3), channel_id=1, replica_groups={{0,2,4,6,8,10,12,14},{1,3,5,7,9,11,13,15},{16,18,20,22,24,26,28,30},{17..., dimensions={0} | all-to-all | bytes 327680 | tf_op jit(solution)/shard_map/all_to_all | solution.py:595
  69.4 0.5 enter.3
  69.9 0.1 collective-permute-start.6
  69.9 0.6 gate.3
  70.6 0.7 collective-permute-done.6.other_ref
  71.3 2.0 %finish.3 = (f32[256,512]{1,0:T(8,128)S(1)}, bf16[256,512]{1,0:T(8,128)(2,1)S(1)}) custom-call(f32[256,1024]{1,0:T(8,128)S(1)} %get-tuple-element.106.gate_ref, f32[256,1024]{1,0:T(8,128)S(1)} %get-tuple-element.107.wide_ref, f32[128,1024]{1,0:T(8,128)S(1)} %get-tuple-element.108.later_ref, f32[128,1024]{1,0:T(8,128)S(1)} %get-tuple-element.109.decay_ref, ...), custom_call_target="tpu_custom_call" | custom-call | bytes 8225920 | tf_op jit(solution)/shard_map/finish/pallas_call | solution.py:571
  73.3 2.1 %collective-permute-start.7 = (bf16[256,512]{1,0:T(8,128)(2,1)S(1)}, bf16[256,512]{1,0:T(8,128)(2,1)S(1)}, u32[]{:S(2)}, u32[]{:S(2)}) collective-permute-start(bf16[256,512]{1,0:T(8,128)(2,1)S(1)} %get-tuple-element.116.a_ref), channel_id=1, source_target_pairs={{0,1},{1,2},{2,3},{3,4},{4,5},{5,6},{6,7},{7,8},{8,9},{9,10},{10,1... | collective-permute-start | bytes 786440 | tf_op jit(solution)/shard_map/ppermute | solution.py:600
  75.4 1.9 %memory.3 = (bf16[256,512]{1,0:T(8,128)(2,1)S(1)}, f32[256,512]{1,0:T(8,128)S(1)}, f32[256,512]{1,0:T(8,128)S(1)}, f32[256,512]{1,0:T(8,128)S(1)}, f32[256,512]{1,0:T(8,128)S(1)}) custom-call(s32[8]{0:T(128)S(1)} %copy-done.10, bf16[256,512]{1,0:T(8,128)(2,1)S(1)} %get-tuple-element.116.a_ref, bf16[2,512,512]{2,1,0:T(8,128)(2,1)S(1)} %copy-done.2, ...), custom_call_target="tpu_custom_call" | custom-call | flops 402653184 | bytes 5767168 | tf_op jit(solution)/shard_map/memory/pallas_call | solution.py:571
  77.3 4.6 %collective-permute-done.7.prev_ref = bf16[256,512]{1,0:T(8,128)(2,1)S(1)} collective-permute-done((bf16[256,512]{1,0:T(8,128)(2,1)S(1)}, bf16[256,512]{1,0:T(8,128)(2,1)S(1)}, u32[]{:S(2)}, u32[]{:S(2)}) %collective-permute-start.7) | collective-permute-done | bytes 262176 | tf_op jit(solution)/shard_map/ppermute | solution.py:600
  81.9 2.3 %attend.3 = f32[256,512]{1,0:T(8,128)} custom-call(bf16[256,512]{1,0:T(8,128)(2,1)S(1)} %get-tuple-element.117.q_ref, f32[256,512]{1,0:T(8,128)S(1)} %get-tuple-element.118.number_ref, f32[256,512]{1,0:T(8,128)S(1)} %get-tuple-element.119.total_ref, f32[256,512]{1,0:T(8,128)S(1)} %get-tuple-element.120.top_ref, f32[256,512]{1,0:T(8,128)S(1)} %get-tuple-element.121.seen_ref, ...), custom_call_target="tpu_custom_call" | custom-call | bytes 6832128 | tf_op jit(solution)/shard_map/attend/pallas_call | solution.py:571
  (9 shorter events, 0.0 us)
Async XLA Ops:
  0.0 0.7 copy-start.12
  0.0 1.0 %copy-start.11 = (bf16[2,50,4,512]{3,2,1,0:T(4,128)(2,1)S(1)}, bf16[2,50,4,512]{3,2,1,0:T(4,128)(2,1)}, u32[]{:S(2)}) copy-start(bf16[2,50,4,512]{3,2,1,0:T(4,128)(2,1)} %all_mods_ref.1) | copy-start | bytes 1228804
  0.0 1.0 %copy-start.13 = (s32[8]{0:T(128)S(1)}, s32[8]{0:T(128)}, u32[]{:S(2)}) copy-start(s32[8]{0:T(128)} %step_ref.1) | copy-start | bytes 100
  0.0 1.1 %copy-start.4 = (bf16[8,32,512]{2,1,0:T(8,128)(2,1)S(1)}, bf16[8,32,512]{2,1,0:T(8,128)(2,1)}, u32[]{:S(2)}) copy-start(bf16[8,32,512]{2,1,0:T(8,128)(2,1)} %param.15) | copy-start | bytes 786436
  0.0 3.1 %slice-start = ((s8[4718592]{0:T(1024)(128)(4,1)}), s8[4194304]{0:T(1024)(128)(4,1)S(1)}, s32[]{:S(2)}) async-start(s8[4718592]{0:T(1024)(128)(4,1)} %bitcast.4), calls=%async_computation.4 | async-start | bytes 8388608
  1.1 2.0 %slice-start.1 = ((s8[4718592]{0:T(1024)(128)(4,1)}), s8[524288]{0:T(1024)(128)(4,1)S(1)}, s32[]{:S(2)}) async-start(s8[4718592]{0:T(1024)(128)(4,1)} %bitcast.4), calls=%async_computation.5 | async-start | bytes 1048576
  1.1 2.0 %copy-start.5 = (f32[2,4,1280]{2,1,0:T(4,128)S(1)}, f32[2,4,1280]{2,1,0:T(4,128)}, u32[]{:S(2)}) copy-start(f32[2,4,1280]{2,1,0:T(4,128)} %conv_ref.3) | copy-start | bytes 122884
  1.1 2.0 %copy-start.6 = (bf16[2,512,16]{1,2,0:T(8,128)(2,1)S(1)}, bf16[2,512,16]{1,2,0:T(8,128)(2,1)}, u32[]{:S(2)}) copy-start(bf16[2,512,16]{1,2,0:T(8,128)(2,1)} %param.20) | copy-start | bytes 98308
  1.1 2.0 %copy-start.9 = (f32[2,16]{1,0:T(2,128)S(1)}, f32[2,16]{1,0:T(2,128)}, u32[]{:S(2)}) copy-start(f32[2,16]{1,0:T(2,128)} %decay_ref.3) | copy-start | bytes 388
  1.1 4.8 %copy-start.8 = (f32[2,16]{1,0:T(2,128)S(1)}, f32[2,16]{1,0:T(2,128)}, u32[]{:S(2)}) copy-start(f32[2,16]{1,0:T(2,128)} %skip_ref.7) | copy-start | bytes 388
  1.9 1.2 %collective-permute-start = (bf16[16,512]{1,0:T(8,128)(2,1)S(1)}, bf16[16,512]{1,0:T(8,128)(2,1)S(1)}, u32[]{:S(2)}, u32[]{:S(2)}) collective-permute-start(bf16[16,512]{1,0:T(8,128)(2,1)S(1)} %get-tuple-element.65), channel_id=1, source_target_pairs={{0,1},{1,0},{2,3},{3,2},{4,5},{5,4},{6,7},{7,6},{8,9},{9,8},{10,11... | collective-permute-start | bytes 49160 | tf_op jit(solution)/shard_map/ppermute | solution.py:589
  3.1 15.9 %copy-start = (bf16[2,512,1024]{2,1,0:T(8,128)(2,1)S(1)}, bf16[2,512,1024]{2,1,0:T(8,128)(2,1)}, u32[]{:S(2)}) copy-start(bf16[2,512,1024]{2,1,0:T(8,128)(2,1)} %wm_ref.7) | copy-start | bytes 6291460
  3.2 15.9 %copy-start.1 = (bf16[2,1024,512]{2,1,0:T(8,128)(2,1)S(1)}, bf16[2,1024,512]{2,1,0:T(8,128)(2,1)}, u32[]{:S(2)}) copy-start(bf16[2,1024,512]{2,1,0:T(8,128)(2,1)} %wo_ref.3) | copy-start | bytes 6291460
  3.2 15.9 %copy-start.3 = (bf16[2,512,512]{2,1,0:T(8,128)(2,1)S(1)}, bf16[2,512,512]{2,1,0:T(8,128)(2,1)}, u32[]{:S(2)}) copy-start(bf16[2,512,512]{2,1,0:T(8,128)(2,1)} %merge_ref.3) | copy-start | bytes 3145732
  3.2 15.9 %copy-start.7 = (f32[2,1024]{1,0:T(2,128)S(1)}, f32[2,1024]{1,0:T(2,128)}, u32[]{:S(2)}) copy-start(f32[2,1024]{1,0:T(2,128)} %gain_ref.3) | copy-start | bytes 24580
  5.7 13.4 %copy-start.2 = (bf16[2,512,512]{2,1,0:T(8,128)(2,1)S(1)}, bf16[2,512,512]{2,1,0:T(8,128)(2,1)}, u32[]{:S(2)}) copy-start(bf16[2,512,512]{2,1,0:T(8,128)(2,1)} %wq_ref.3) | copy-start | bytes 3145732
  5.7 1.5 %collective-permute-start.1 = (bf16[8,80,128]{2,1,0:T(8,128)(2,1)S(1)}, bf16[8,80,128]{2,1,0:T(8,128)(2,1)S(1)}, u32[]{:S(2)}, u32[]{:S(2)}) collective-permute-start(bf16[8,80,128]{2,1,0:T(8,128)(2,1)S(1)} %get-tuple-element.68), channel_id=1, source_target_pairs={{0,1},{1,0},{2,3},{3,2},{4,5},{5,4},{6,7},{7,6},{8,9},{9,8},{10,11... | collective-permute-start | bytes 491528 | tf_op jit(solution)/shard_map/ppermute | solution.py:589
  30.2 1.5 %collective-permute-start.2 = (bf16[8,80,128]{2,1,0:T(8,128)(2,1)S(1)}, bf16[8,80,128]{2,1,0:T(8,128)(2,1)S(1)}, u32[]{:S(2)}, u32[]{:S(2)}) collective-permute-start(bf16[8,80,128]{2,1,0:T(8,128)(2,1)S(1)} %get-tuple-element.85), channel_id=1, source_target_pairs={{0,1},{1,0},{2,3},{3,2},{4,5},{5,4},{6,7},{7,6},{8,9},{9,8},{10,11... | collective-permute-start | bytes 491528 | tf_op jit(solution)/shard_map/ppermute | solution.py:589
  31.7 4.2 %copy-start.10 = (s32[8]{0:T(128)S(1)}, s32[8]{0:T(128)}, u32[]{:S(2)}) copy-start(s32[8]{0:T(128)} %reach_ref.3) | copy-start | bytes 100
  33.6 8.6 %collective-permute-start.3 = (bf16[256,512]{1,0:T(8,128)(2,1)S(1)}, bf16[256,512]{1,0:T(8,128)(2,1)S(1)}, u32[]{:S(2)}, u32[]{:S(2)}) collective-permute-start(bf16[256,512]{1,0:T(8,128)(2,1)S(1)} %get-tuple-element.87.a_ref), channel_id=1, source_target_pairs={{0,1},{1,2},{2,3},{3,4},{4,5},{5,6},{6,7},{7,8},{8,9},{9,10},{10,1... | collective-permute-start | bytes 786440 | tf_op jit(solution)/shard_map/ppermute | solution.py:600
  43.8 1.2 %collective-permute-start.4 = (bf16[16,512]{1,0:T(8,128)(2,1)S(1)}, bf16[16,512]{1,0:T(8,128)(2,1)S(1)}, u32[]{:S(2)}, u32[]{:S(2)}) collective-permute-start(bf16[16,512]{1,0:T(8,128)(2,1)S(1)} %get-tuple-element.95), channel_id=1, source_target_pairs={{0,1},{1,0},{2,3},{3,2},{4,5},{5,4},{6,7},{7,6},{8,9},{9,8},{10,11... | collective-permute-start | bytes 49160 | tf_op jit(solution)/shard_map/ppermute | solution.py:589
  47.5 1.5 %collective-permute-start.5 = (bf16[8,80,128]{2,1,0:T(8,128)(2,1)S(1)}, bf16[8,80,128]{2,1,0:T(8,128)(2,1)S(1)}, u32[]{:S(2)}, u32[]{:S(2)}) collective-permute-start(bf16[8,80,128]{2,1,0:T(8,128)(2,1)S(1)} %get-tuple-element.97), channel_id=1, source_target_pairs={{0,1},{1,0},{2,3},{3,2},{4,5},{5,4},{6,7},{7,6},{8,9},{9,8},{10,11... | collective-permute-start | bytes 491528 | tf_op jit(solution)/shard_map/ppermute | solution.py:589
  69.9 1.5 %collective-permute-start.6 = (bf16[8,80,128]{2,1,0:T(8,128)(2,1)S(1)}, bf16[8,80,128]{2,1,0:T(8,128)(2,1)S(1)}, u32[]{:S(2)}, u32[]{:S(2)}) collective-permute-start(bf16[8,80,128]{2,1,0:T(8,128)(2,1)S(1)} %get-tuple-element.114), channel_id=1, source_target_pairs={{0,1},{1,0},{2,3},{3,2},{4,5},{5,4},{6,7},{7,6},{8,9},{9,8},{10,11... | collective-permute-start | bytes 491528 | tf_op jit(solution)/shard_map/ppermute | solution.py:589
  73.3 8.6 %collective-permute-start.7 = (bf16[256,512]{1,0:T(8,128)(2,1)S(1)}, bf16[256,512]{1,0:T(8,128)(2,1)S(1)}, u32[]{:S(2)}, u32[]{:S(2)}) collective-permute-start(bf16[256,512]{1,0:T(8,128)(2,1)S(1)} %get-tuple-element.116.a_ref), channel_id=1, source_target_pairs={{0,1},{1,2},{2,3},{3,4},{4,5},{5,6},{6,7},{7,8},{8,9},{9,10},{10,1... | collective-permute-start | bytes 786440 | tf_op jit(solution)/shard_map/ppermute | solution.py:600

commit v12 on v8

--- a/solution.py
+++ b/solution.py
@@ -457,9 +457,7 @@
         cols = slice(c, c + chunk)
         total = y_ref[:, cols]
         square = total * total
-        high = square.astype(BF16)
-        low = (square - high.astype(F32)).astype(BF16)
-        mean = dot(high, same) + dot(low, same)
+        mean = dot(square.astype(BF16), same)
         gain = gain_ref[layer : layer + 1, cols]
         normed_ref[:, cols] = (total * lax.rsqrt(mean + HEAD_EPS) * gain).astype(BF16)
     hidden = resid_ref[...].astype(F32) + dot(normed_ref[...], wo_ref[layer])

time: 84.6 us -> 84.3 us (level)
  no operation moved by 1% of the time
where the time goes in v12:
time: 84.3 us; the launch traced here: 84 us
  blocking collectives  41.9 us (50%)
  Pallas kernels  21.6 us (26%)
  waiting for transfers between devices  14 us (17%)
  starting transfers between devices  5.02 us (6%)
  local copies, waits for them, and re-layouts  1.12 us (1%)
    all_to_all x4, blocking collectives, over_chips(): return lax.all_to_all(value, axis, 0, 0, axis_index_groups=groups)  41.9 us
    pallas_call x20, Pallas kernels, run(): pl.pallas_call(kernel, in_specs=[SCALARS] * len(scalars) + [WHOLE] * len(...  21.6 us
    ppermute x2, waiting for transfers between devices, from_behind(): return lax.ppermute(value, axis, [(i, i + 1) for i in range(count - 1)])  9.03 us
    ppermute x6, waiting for transfers between devices, swapped(): return lax.ppermute(value, axis, [(i, i ^ 1) for i in range(count)])  5 us
    ppermute x2, starting transfers between devices, from_behind(): return lax.ppermute(value, axis, [(i, i + 1) for i in range(count - 1)])  4.29 us
  transfers between devices with their start and end apart: 8, of which 8 were waited for; matrix products, arithmetic and copies ran while one was open for 0% of the time, Pallas kernels for 8%

profile of v12, /device:TPU:8, one launch (start us, length us, event | category | flops | bytes accessed | tf_op | source)
XLA Modules:
  0.0 84.0 jit_solution(5032496278007036421)
XLA Ops:
  0.0 0.0 copy-start.12
  0.0 0.0 copy-start.11
  0.0 0.0 copy-start.4
  0.0 0.0 slice-start
  0.1 0.7 copy-done.12
  0.7 0.3 copy-done.11
  1.0 0.0 copy-done.13
  1.0 0.1 copy-done.4
  1.1 0.0 copy-start.8
  1.1 0.7 first.1
  1.9 0.1 collective-permute-start
  1.9 1.2 %collective-permute-done.before_ref = bf16[16,512]{1,0:T(8,128)(2,1)S(1)} collective-permute-done((bf16[16,512]{1,0:T(8,128)(2,1)S(1)}, bf16[16,512]{1,0:T(8,128)(2,1)S(1)}, u32[]{:S(2)}, u32[]{:S(2)}) %collective-permute-start) | collective-permute-done | bytes 16416 | tf_op jit(solution)/shard_map/ppermute | solution.py:588
  3.1 0.0 slice-done
  3.1 0.0 slice-done.1
  3.1 0.0 copy-done.5
  3.1 0.0 copy-done.6
  3.1 0.0 copy-done.9
  3.1 0.0 copy-start
  3.2 0.0 copy-start.1
  3.2 0.0 copy-start.3
  3.2 0.0 copy-start.7
  3.2 2.5 %local.2 = (bf16[256,1280]{1,0:T(8,128)(2,1)S(1)}, f32[8,1280]{1,0:T(8,128)S(1)}, f32[256,16]{1,0:T(8,128)S(1)}, f32[16,256]{1,0:T(8,128)S(1)}, f32[16,16]{1,0:T...) custom-call(bf16[256,512]{1,0:T(8,128)(2,1)S(1)} %get-tuple-element.76.u_ref,, ...), custom_call_target="tpu_custom_call" | custom-call | flops 335544320 | bytes 6719616 | tf_op jit(solution)/shard_map/local/pallas_call | solution.py:570
  5.7 0.2 collective-permute-start.1
  5.9 0.0 copy-done.8
  5.9 0.6 later.2
  6.6 0.6 collective-permute-done.1.got_ref
  7.2 0.1 chip.2
  7.3 11.7 %all_to_all.20.got_ref = bf16[8,80,128]{2,1,0:T(8,128)(2,1)S(1)} all-to-all(bf16[8,80,128]{2,1,0:T(8,128)(2,1)S(1)} %chip.2), channel_id=1, replica_groups={{0,2,4,6,8,10,12,14},{1,3,5,7,9,11,13,15},{16,18,20,22,24,26,28,30},{17..., dimensions={0} | all-to-all | bytes 327680 | tf_op jit(solution)/shard_map/all_to_all | solution.py:594
  19.0 0.0 copy-done
  19.0 0.0 copy-done.1
  19.0 0.0 copy-done.3
  19.1 0.0 copy-done.7
  19.1 0.0 copy-done.2
  19.1 0.4 scan.2
  19.5 10.3 %all_to_all.21.back_ref = bf16[8,80,128]{2,1,0:T(8,128)(2,1)S(1)} all-to-all(bf16[8,80,128]{2,1,0:T(8,128)(2,1)S(1)} %scan.2), channel_id=1, replica_groups={{0,2,4,6,8,10,12,14},{1,3,5,7,9,11,13,15},{16,18,20,22,24,26,28,30},{17..., dimensions={0} | all-to-all | bytes 327680 | tf_op jit(solution)/shard_map/all_to_all | solution.py:594
  29.8 0.5 enter.2
  30.2 0.1 collective-permute-start.2
  30.3 0.6 gate.2
  30.9 0.7 collective-permute-done.2.other_ref
  31.7 1.8 %finish.2 = (f32[256,512]{1,0:T(8,128)S(1)}, bf16[256,512]{1,0:T(8,128)(2,1)S(1)}) custom-call(f32[256,1024]{1,0:T(8,128)S(1)} %get-tuple-element.77.gate_ref, f32[256,1024]{1,0:T(8,128)S(1)} %get-tuple-element.78.wide_ref, f32[128,1024]{1,0:T(8,128)S(1)} %get-tuple-element.79.later_ref, f32[128,1024]{1,0:T(8,128)S(1)} %get-tuple-element.80.decay_ref, ...), custom_call_target="tpu_custom_call" | custom-call | bytes 7963776 | tf_op jit(solution)/shard_map/finish/pallas_call | solution.py:570
  33.5 2.2 %collective-permute-start.3 = (bf16[256,512]{1,0:T(8,128)(2,1)S(1)}, bf16[256,512]{1,0:T(8,128)(2,1)S(1)}, u32[]{:S(2)}, u32[]{:S(2)}) collective-permute-start(bf16[256,512]{1,0:T(8,128)(2,1)S(1)} %get-tuple-element.87.a_ref), channel_id=1, source_target_pairs={{0,1},{1,2},{2,3},{3,4},{4,5},{5,6},{6,7},{7,8},{8,9},{9,10},{10,1... | collective-permute-start | bytes 786440 | tf_op jit(solution)/shard_map/ppermute | solution.py:599
  35.7 0.0 copy-done.10
  35.7 1.9 %memory.2 = (bf16[256,512]{1,0:T(8,128)(2,1)S(1)}, f32[256,512]{1,0:T(8,128)S(1)}, f32[256,512]{1,0:T(8,128)S(1)}, f32[256,512]{1,0:T(8,128)S(1)}, f32[256,512]{1,0:T(8,128)S(1)}) custom-call(s32[8]{0:T(128)S(1)} %copy-done.10, bf16[256,512]{1,0:T(8,128)(2,1)S(1)} %get-tuple-element.87.a_ref, bf16[2,512,512]{2,1,0:T(8,128)(2,1)S(1)} %copy-done.2, ...), custom_call_target="tpu_custom_call" | custom-call | flops 402653184 | bytes 5767168 | tf_op jit(solution)/shard_map/memory/pallas_call | solution.py:570
  37.7 4.4 %collective-permute-done.3.prev_ref = bf16[256,512]{1,0:T(8,128)(2,1)S(1)} collective-permute-done((bf16[256,512]{1,0:T(8,128)(2,1)S(1)}, bf16[256,512]{1,0:T(8,128)(2,1)S(1)}, u32[]{:S(2)}, u32[]{:S(2)}) %collective-permute-start.3) | collective-permute-done | bytes 262176 | tf_op jit(solution)/shard_map/ppermute | solution.py:599
  42.1 1.6 %attend.2 = (f32[256,512]{1,0:T(8,128)S(1)}, bf16[256,512]{1,0:T(8,128)(2,1)S(1)}, bf16[16,512]{1,0:T(8,128)(2,1)S(1)}) custom-call(bf16[256,512]{1,0:T(8,128)(2,1)S(1)} %get-tuple-element.88.q_ref, f32[256,512]{1,0:T(8,128)S(1)} %get-tuple-element.89.number_ref, f32[256,512]{1,0:T(8,128)S(1)} %get-tuple-element.90.total_ref, ...), custom_call_target="tpu_custom_call" | custom-call | bytes 7110656 | tf_op jit(solution)/shard_map/attend/pallas_call | solution.py:570
  43.7 0.1 collective-permute-start.4
  43.8 1.2 %collective-permute-done.4.before_ref = bf16[16,512]{1,0:T(8,128)(2,1)S(1)} collective-permute-done((bf16[16,512]{1,0:T(8,128)(2,1)S(1)}, bf16[16,512]{1,0:T(8,128)(2,1)S(1)}, u32[]{:S(2)}, u32[]{:S(2)}) %collective-permute-start.4) | collective-permute-done | bytes 16416 | tf_op jit(solution)/shard_map/ppermute | solution.py:588
  44.9 2.5 %local.3 = (bf16[256,1280]{1,0:T(8,128)(2,1)S(1)}, f32[8,1280]{1,0:T(8,128)S(1)}, f32[256,16]{1,0:T(8,128)S(1)}, f32[16,256]{1,0:T(8,128)S(1)}, f32[16,16]{1,0:T...) custom-call(bf16[256,512]{1,0:T(8,128)(2,1)S(1)} %get-tuple-element.105.u_ref, ...), custom_call_target="tpu_custom_call" | custom-call | flops 335544320 | bytes 6719616 | tf_op jit(solution)/shard_map/local/pallas_call | solution.py:570
  47.4 0.2 collective-permute-start.5
  47.6 0.6 later.3
  48.3 0.6 collective-permute-done.5.got_ref
  48.9 0.1 chip.3
  49.0 9.6 %all_to_all.22.got_ref = bf16[8,80,128]{2,1,0:T(8,128)(2,1)S(1)} all-to-all(bf16[8,80,128]{2,1,0:T(8,128)(2,1)S(1)} %chip.3), channel_id=1, replica_groups={{0,2,4,6,8,10,12,14},{1,3,5,7,9,11,13,15},{16,18,20,22,24,26,28,30},{17..., dimensions={0} | all-to-all | bytes 327680 | tf_op jit(solution)/shard_map/all_to_all | solution.py:594
  58.6 0.4 scan.3
  59.0 10.3 %all_to_all.23.back_ref = bf16[8,80,128]{2,1,0:T(8,128)(2,1)S(1)} all-to-all(bf16[8,80,128]{2,1,0:T(8,128)(2,1)S(1)} %scan.3), channel_id=1, replica_groups={{0,2,4,6,8,10,12,14},{1,3,5,7,9,11,13,15},{16,18,20,22,24,26,28,30},{17..., dimensions={0} | all-to-all | bytes 327680 | tf_op jit(solution)/shard_map/all_to_all | solution.py:594
  69.3 0.5 enter.3
  69.8 0.1 collective-permute-start.6
  69.8 0.6 gate.3
  70.5 0.7 collective-permute-done.6.other_ref
  71.2 1.8 %finish.3 = (f32[256,512]{1,0:T(8,128)S(1)}, bf16[256,512]{1,0:T(8,128)(2,1)S(1)}) custom-call(f32[256,1024]{1,0:T(8,128)S(1)} %get-tuple-element.106.gate_ref, f32[256,1024]{1,0:T(8,128)S(1)} %get-tuple-element.107.wide_ref, f32[128,1024]{1,0:T(8,128)S(1)} %get-tuple-element.108.later_ref, f32[128,1024]{1,0:T(8,128)S(1)} %get-tuple-element.109.decay_ref, ...), custom_call_target="tpu_custom_call" | custom-call | bytes 8225920 | tf_op jit(solution)/shard_map/finish/pallas_call | solution.py:570
  73.1 2.1 %collective-permute-start.7 = (bf16[256,512]{1,0:T(8,128)(2,1)S(1)}, bf16[256,512]{1,0:T(8,128)(2,1)S(1)}, u32[]{:S(2)}, u32[]{:S(2)}) collective-permute-start(bf16[256,512]{1,0:T(8,128)(2,1)S(1)} %get-tuple-element.116.a_ref), channel_id=1, source_target_pairs={{0,1},{1,2},{2,3},{3,4},{4,5},{5,6},{6,7},{7,8},{8,9},{9,10},{10,1... | collective-permute-start | bytes 786440 | tf_op jit(solution)/shard_map/ppermute | solution.py:599
  75.1 1.9 %memory.3 = (bf16[256,512]{1,0:T(8,128)(2,1)S(1)}, f32[256,512]{1,0:T(8,128)S(1)}, f32[256,512]{1,0:T(8,128)S(1)}, f32[256,512]{1,0:T(8,128)S(1)}, f32[256,512]{1,0:T(8,128)S(1)}) custom-call(s32[8]{0:T(128)S(1)} %copy-done.10, bf16[256,512]{1,0:T(8,128)(2,1)S(1)} %get-tuple-element.116.a_ref, bf16[2,512,512]{2,1,0:T(8,128)(2,1)S(1)} %copy-done.2, ...), custom_call_target="tpu_custom_call" | custom-call | flops 402653184 | bytes 5767168 | tf_op jit(solution)/shard_map/memory/pallas_call | solution.py:570
  77.0 4.6 %collective-permute-done.7.prev_ref = bf16[256,512]{1,0:T(8,128)(2,1)S(1)} collective-permute-done((bf16[256,512]{1,0:T(8,128)(2,1)S(1)}, bf16[256,512]{1,0:T(8,128)(2,1)S(1)}, u32[]{:S(2)}, u32[]{:S(2)}) %collective-permute-start.7) | collective-permute-done | bytes 262176 | tf_op jit(solution)/shard_map/ppermute | solution.py:599
  81.7 2.3 %attend.3 = f32[256,512]{1,0:T(8,128)} custom-call(bf16[256,512]{1,0:T(8,128)(2,1)S(1)} %get-tuple-element.117.q_ref, f32[256,512]{1,0:T(8,128)S(1)} %get-tuple-element.118.number_ref, f32[256,512]{1,0:T(8,128)S(1)} %get-tuple-element.119.total_ref, f32[256,512]{1,0:T(8,128)S(1)} %get-tuple-element.120.top_ref, f32[256,512]{1,0:T(8,128)S(1)} %get-tuple-element.121.seen_ref, ...), custom_call_target="tpu_custom_call" | custom-call | bytes 6832128 | tf_op jit(solution)/shard_map/attend/pallas_call | solution.py:570
  (9 shorter events, 0.0 us)
Async XLA Ops:
  0.0 0.7 copy-start.12
  0.0 1.0 %copy-start.11 = (bf16[2,50,4,512]{3,2,1,0:T(4,128)(2,1)S(1)}, bf16[2,50,4,512]{3,2,1,0:T(4,128)(2,1)}, u32[]{:S(2)}) copy-start(bf16[2,50,4,512]{3,2,1,0:T(4,128)(2,1)} %all_mods_ref.1) | copy-start | bytes 1228804
  0.0 1.0 %copy-start.13 = (s32[8]{0:T(128)S(1)}, s32[8]{0:T(128)}, u32[]{:S(2)}) copy-start(s32[8]{0:T(128)} %step_ref.1) | copy-start | bytes 100
  0.0 1.1 %copy-start.4 = (bf16[8,32,512]{2,1,0:T(8,128)(2,1)S(1)}, bf16[8,32,512]{2,1,0:T(8,128)(2,1)}, u32[]{:S(2)}) copy-start(bf16[8,32,512]{2,1,0:T(8,128)(2,1)} %param.15) | copy-start | bytes 786436
  0.0 3.1 %slice-start = ((s8[4718592]{0:T(1024)(128)(4,1)}), s8[4194304]{0:T(1024)(128)(4,1)S(1)}, s32[]{:S(2)}) async-start(s8[4718592]{0:T(1024)(128)(4,1)} %bitcast.4), calls=%async_computation.4 | async-start | bytes 8388608
  1.1 2.0 %slice-start.1 = ((s8[4718592]{0:T(1024)(128)(4,1)}), s8[524288]{0:T(1024)(128)(4,1)S(1)}, s32[]{:S(2)}) async-start(s8[4718592]{0:T(1024)(128)(4,1)} %bitcast.4), calls=%async_computation.5 | async-start | bytes 1048576
  1.1 2.0 %copy-start.5 = (f32[2,4,1280]{2,1,0:T(4,128)S(1)}, f32[2,4,1280]{2,1,0:T(4,128)}, u32[]{:S(2)}) copy-start(f32[2,4,1280]{2,1,0:T(4,128)} %conv_ref.3) | copy-start | bytes 122884
  1.1 2.0 %copy-start.6 = (bf16[2,512,16]{1,2,0:T(8,128)(2,1)S(1)}, bf16[2,512,16]{1,2,0:T(8,128)(2,1)}, u32[]{:S(2)}) copy-start(bf16[2,512,16]{1,2,0:T(8,128)(2,1)} %param.20) | copy-start | bytes 98308
  1.1 2.0 %copy-start.9 = (f32[2,16]{1,0:T(2,128)S(1)}, f32[2,16]{1,0:T(2,128)}, u32[]{:S(2)}) copy-start(f32[2,16]{1,0:T(2,128)} %decay_ref.3) | copy-start | bytes 388
  1.1 4.8 %copy-start.8 = (f32[2,16]{1,0:T(2,128)S(1)}, f32[2,16]{1,0:T(2,128)}, u32[]{:S(2)}) copy-start(f32[2,16]{1,0:T(2,128)} %skip_ref.7) | copy-start | bytes 388
  1.9 1.2 %collective-permute-start = (bf16[16,512]{1,0:T(8,128)(2,1)S(1)}, bf16[16,512]{1,0:T(8,128)(2,1)S(1)}, u32[]{:S(2)}, u32[]{:S(2)}) collective-permute-start(bf16[16,512]{1,0:T(8,128)(2,1)S(1)} %get-tuple-element.65), channel_id=1, source_target_pairs={{0,1},{1,0},{2,3},{3,2},{4,5},{5,4},{6,7},{7,6},{8,9},{9,8},{10,11... | collective-permute-start | bytes 49160 | tf_op jit(solution)/shard_map/ppermute | solution.py:588
  3.1 15.9 %copy-start = (bf16[2,512,1024]{2,1,0:T(8,128)(2,1)S(1)}, bf16[2,512,1024]{2,1,0:T(8,128)(2,1)}, u32[]{:S(2)}) copy-start(bf16[2,512,1024]{2,1,0:T(8,128)(2,1)} %wm_ref.7) | copy-start | bytes 6291460
  3.2 15.9 %copy-start.1 = (bf16[2,1024,512]{2,1,0:T(8,128)(2,1)S(1)}, bf16[2,1024,512]{2,1,0:T(8,128)(2,1)}, u32[]{:S(2)}) copy-start(bf16[2,1024,512]{2,1,0:T(8,128)(2,1)} %wo_ref.3) | copy-start | bytes 6291460
  3.2 15.9 %copy-start.3 = (bf16[2,512,512]{2,1,0:T(8,128)(2,1)S(1)}, bf16[2,512,512]{2,1,0:T(8,128)(2,1)}, u32[]{:S(2)}) copy-start(bf16[2,512,512]{2,1,0:T(8,128)(2,1)} %merge_ref.3) | copy-start | bytes 3145732
  3.2 15.9 %copy-start.7 = (f32[2,1024]{1,0:T(2,128)S(1)}, f32[2,1024]{1,0:T(2,128)}, u32[]{:S(2)}) copy-start(f32[2,1024]{1,0:T(2,128)} %gain_ref.3) | copy-start | bytes 24580
  5.7 13.4 %copy-start.2 = (bf16[2,512,512]{2,1,0:T(8,128)(2,1)S(1)}, bf16[2,512,512]{2,1,0:T(8,128)(2,1)}, u32[]{:S(2)}) copy-start(bf16[2,512,512]{2,1,0:T(8,128)(2,1)} %wq_ref.3) | copy-start | bytes 3145732
  5.7 1.5 %collective-permute-start.1 = (bf16[8,80,128]{2,1,0:T(8,128)(2,1)S(1)}, bf16[8,80,128]{2,1,0:T(8,128)(2,1)S(1)}, u32[]{:S(2)}, u32[]{:S(2)}) collective-permute-start(bf16[8,80,128]{2,1,0:T(8,128)(2,1)S(1)} %get-tuple-element.68), channel_id=1, source_target_pairs={{0,1},{1,0},{2,3},{3,2},{4,5},{5,4},{6,7},{7,6},{8,9},{9,8},{10,11... | collective-permute-start | bytes 491528 | tf_op jit(solution)/shard_map/ppermute | solution.py:588
  30.2 1.5 %collective-permute-start.2 = (bf16[8,80,128]{2,1,0:T(8,128)(2,1)S(1)}, bf16[8,80,128]{2,1,0:T(8,128)(2,1)S(1)}, u32[]{:S(2)}, u32[]{:S(2)}) collective-permute-start(bf16[8,80,128]{2,1,0:T(8,128)(2,1)S(1)} %get-tuple-element.85), channel_id=1, source_target_pairs={{0,1},{1,0},{2,3},{3,2},{4,5},{5,4},{6,7},{7,6},{8,9},{9,8},{10,11... | collective-permute-start | bytes 491528 | tf_op jit(solution)/shard_map/ppermute | solution.py:588
  31.7 4.0 %copy-start.10 = (s32[8]{0:T(128)S(1)}, s32[8]{0:T(128)}, u32[]{:S(2)}) copy-start(s32[8]{0:T(128)} %reach_ref.3) | copy-start | bytes 100
  33.5 8.6 %collective-permute-start.3 = (bf16[256,512]{1,0:T(8,128)(2,1)S(1)}, bf16[256,512]{1,0:T(8,128)(2,1)S(1)}, u32[]{:S(2)}, u32[]{:S(2)}) collective-permute-start(bf16[256,512]{1,0:T(8,128)(2,1)S(1)} %get-tuple-element.87.a_ref), channel_id=1, source_target_pairs={{0,1},{1,2},{2,3},{3,4},{4,5},{5,6},{6,7},{7,8},{8,9},{9,10},{10,1... | collective-permute-start | bytes 786440 | tf_op jit(solution)/shard_map/ppermute | solution.py:599
  43.7 1.2 %collective-permute-start.4 = (bf16[16,512]{1,0:T(8,128)(2,1)S(1)}, bf16[16,512]{1,0:T(8,128)(2,1)S(1)}, u32[]{:S(2)}, u32[]{:S(2)}) collective-permute-start(bf16[16,512]{1,0:T(8,128)(2,1)S(1)} %get-tuple-element.95), channel_id=1, source_target_pairs={{0,1},{1,0},{2,3},{3,2},{4,5},{5,4},{6,7},{7,6},{8,9},{9,8},{10,11... | collective-permute-start | bytes 49160 | tf_op jit(solution)/shard_map/ppermute | solution.py:588
  47.4 1.5 %collective-permute-start.5 = (bf16[8,80,128]{2,1,0:T(8,128)(2,1)S(1)}, bf16[8,80,128]{2,1,0:T(8,128)(2,1)S(1)}, u32[]{:S(2)}, u32[]{:S(2)}) collective-permute-start(bf16[8,80,128]{2,1,0:T(8,128)(2,1)S(1)} %get-tuple-element.97), channel_id=1, source_target_pairs={{0,1},{1,0},{2,3},{3,2},{4,5},{5,4},{6,7},{7,6},{8,9},{9,8},{10,11... | collective-permute-start | bytes 491528 | tf_op jit(solution)/shard_map/ppermute | solution.py:588
  69.8 1.5 %collective-permute-start.6 = (bf16[8,80,128]{2,1,0:T(8,128)(2,1)S(1)}, bf16[8,80,128]{2,1,0:T(8,128)(2,1)S(1)}, u32[]{:S(2)}, u32[]{:S(2)}) collective-permute-start(bf16[8,80,128]{2,1,0:T(8,128)(2,1)S(1)} %get-tuple-element.114), channel_id=1, source_target_pairs={{0,1},{1,0},{2,3},{3,2},{4,5},{5,4},{6,7},{7,6},{8,9},{9,8},{10,11... | collective-permute-start | bytes 491528 | tf_op jit(solution)/shard_map/ppermute | solution.py:588
  73.1 8.6 %collective-permute-start.7 = (bf16[256,512]{1,0:T(8,128)(2,1)S(1)}, bf16[256,512]{1,0:T(8,128)(2,1)S(1)}, u32[]{:S(2)}, u32[]{:S(2)}) collective-permute-start(bf16[256,512]{1,0:T(8,128)(2,1)S(1)} %get-tuple-element.116.a_ref), channel_id=1, source_target_pairs={{0,1},{1,2},{2,3},{3,4},{4,5},{5,6},{6,7},{7,8},{8,9},{9,10},{10,1... | collective-permute-start | bytes 786440 | tf_op jit(solution)/shard_map/ppermute | solution.py:599
